TPU v7x, 32 devices: a whole 2x2x4 slice. The times are simulated.
32 devices in a mesh: orbits: 4 (over z), rows: 2 (over x), cols: 4 (over y, core).
Axes of the slice: x: 2, y: 2, z: 4, core: 2. Of those that a mesh axis runs over, the one named last changes fastest.
Arguments:
- obs_feat: bfloat16 [131072, 128], P(('orbits', 'rows', 'cols')), may hold values from -6 to 6
- obs_offset: bfloat16 [2, 131072], P(None, ('orbits', 'rows', 'cols')), may hold values from -0.5 to 0.5
- obs_cells: int32 [16, 131072], P(None, ('orbits', 'rows', 'cols')), may hold values from 0 to 255, as said below
- block_tile: int32 [1024], P(('orbits', 'rows', 'cols')), may hold values from 0 to 7, as said below
- block_patch: int32 [1024], P(('orbits', 'rows', 'cols')), may hold values from 0 to 31
- w_embed: bfloat16 [128, 128], replicated, may hold values from -0.5 to 0.5
- b_embed: float32 [128], replicated, may hold values from -3 to 3
- w_proj: bfloat16 [128, 128], replicated, may hold values from -0.5 to 0.5
- b_proj: float32 [128], replicated, may hold values from -3 to 3
- density_weight: float32 [128], replicated, may hold values from -4 to 4
- w_first: bfloat16 [3, 3, 128, 128], replicated, may hold values from -0.1875 to 0.1875
- b_first: float32 [128], replicated, may hold values from -3 to 3
- w_second: bfloat16 [3, 3, 128, 128], replicated, may hold values from -0.1875 to 0.1875
- b_second: float32 [128], replicated, may hold values from -3 to 3
Outputs:
- obs_out: bfloat16 [131072, 128], P(('orbits', 'rows', 'cols'))
- grid_out: bfloat16 [128, 512, 128], P(('orbits', 'rows'), 'cols')
Inputs may be any that keep to these rules, and one draw needn't show every extreme that they name: `obs_cells`: column o is a 4 by 4 window of cells of a 8 by 32 patch: entry k is (a + k // 4) * 32 + b + k % 4 with 0 <= a <= 4 and 0 <= b <= 28. `block_tile`: tile t is the grid block of the devices with rows index t // 4 and cols index t % 4. Of the 32 blocks of one device, at most 8 name one tile, so one tile gets at most 64 blocks from the devices of one orbits index.
All inputs are finite; a program needn't handle non-finite values.
Results may differ from a plain program's by a relative error of at most 0.013.
Values may be sent and summed in bfloat16 or wider, within the bound.
No kernel may reach another device: no remote copies, remote signals or barrier semaphores. Data moves between devices by JAX's collectives and lax.ppermute only.
A program may use at most 64 MiB of HBM per device.

v0:
```python
import jax
import jax.numpy as jnp
from jax import lax
from jax.sharding import PartitionSpec as P

KN = 16
PH = 8
PW = 32
SR = 16
TC = 128


inverse_width = 0.5


def extended(x, sides, width):
    for axis, dim in sides:
        size, length = (lax.axis_size(axis), x.shape[dim])
        up = [(i, (i + 1) % size) for i in range(size - 1)]
        down = [(j, i) for i, j in up]
        last = lax.slice_in_dim(x, length - width, length, axis=dim)
        initial = lax.slice_in_dim(x, 0, width, axis=dim)
        before = lax.ppermute(last, axis, up)
        after = lax.ppermute(initial, axis, down)
        x = jnp.concatenate([before, x, after], axis=dim)
    return x


def tap_weights(offsets):
    offsets_wide = offsets.astype(jnp.float32)
    tap_ids = jnp.arange(KN)
    tap_row = (tap_ids // 4).astype(jnp.float32)
    tap_col = (tap_ids % 4).astype(jnp.float32)
    delta_row = tap_row[None, :, None] - 1.5 - offsets_wide[:, 0:1, :]
    delta_col = tap_col[None, :, None] - 1.5 - offsets_wide[:, 1:2, :]
    return jnp.exp(-(delta_row * delta_row + delta_col * delta_col) * inverse_width).astype(
        jnp.bfloat16
    )


def kernel_matrix(cells, weights):
    slot_count, tap_count, obs_count = cells.shape
    slot_ids = jnp.broadcast_to(jnp.arange(slot_count, dtype=jnp.int32)[:, None, None], cells.shape)
    obs_ids = jnp.broadcast_to(jnp.arange(obs_count, dtype=jnp.int32)[None, None, :], cells.shape)
    blank = jnp.zeros((slot_count, PH * PW, obs_count), jnp.bfloat16)
    return blank.at[slot_ids, cells, obs_ids].set(weights)


def convolve(padded, weight, bias_vec):
    height = padded.shape[-3] - 2
    breadth = padded.shape[-2] - 2
    channels = padded.shape[-1]
    leading = padded.shape[:-3]
    summed = None
    for row_shift in range(3):
        rows_part = padded[..., row_shift : row_shift + height, :, :]
        stacked = jnp.concatenate(
            [rows_part[..., col_shift : col_shift + breadth, :] for col_shift in range(3)], axis=-1
        )
        product_term = jnp.dot(
            stacked.reshape(-1, 3 * channels),
            weight[row_shift].reshape(3 * channels, channels),
            preferred_element_type=jnp.float32,
        )
        summed = product_term if summed is None else summed + product_term
    return summed.reshape(leading + (height, breadth, channels)) + bias_vec


def grid_input(spread, density, density_weight):
    return (
        spread / jnp.maximum(density, 1.0)[..., None]
        + density_weight * (density / (1.0 + density))[..., None]
    ).astype(jnp.bfloat16)


def patches_to_tile(patches, tile_height, tile_width):
    trailing = patches.shape[2:]
    shaped = patches.reshape((tile_height // PH, tile_width // PW, PH, PW) + trailing)
    axes_order = (0, 2, 1, 3) + tuple(range(4, 4 + len(trailing)))
    return shaped.transpose(axes_order).reshape((tile_height, tile_width) + trailing)


def tile_to_patches(tile):
    tile_height, tile_width = (tile.shape[0], tile.shape[1])
    trailing = tile.shape[2:]
    shaped = tile.reshape((tile_height // PH, PH, tile_width // PW, PW) + trailing)
    axes_order = (0, 2, 1, 3) + tuple(range(4, 4 + len(trailing)))
    return shaped.transpose(axes_order).reshape(
        (tile_height // PH * (tile_width // PW), PH * PW) + trailing
    )


def plain_edges(stripe):
    return extended(stripe, ((("orbits", "rows"), 0), ("cols", 1)), 1)


def local(
    obs_feat,
    obs_offset,
    obs_cells,
    block_tile,
    block_patch,
    w_embed,
    b_embed,
    w_proj,
    b_proj,
    density_weight,
    w_first,
    b_first,
    w_second,
    b_second,
):
    channels = obs_feat.shape[1]
    block_count = block_tile.shape[0]
    block_size = obs_feat.shape[0] // block_count
    tiles = lax.axis_size("rows") * lax.axis_size("cols")
    orbit_count = lax.axis_size("orbits")
    most = max(2, 2 * block_count // tiles)
    slots = tiles * most
    tile_height = orbit_count * SR
    patch_count = tile_height // PH * (TC // PW)
    group_size = 16
    group_count = slots // group_size
    hidden = jax.nn.silu(
        jnp.dot(obs_feat, w_embed, preferred_element_type=jnp.float32) + b_embed
    ).astype(jnp.bfloat16)
    features = (jnp.dot(hidden, w_proj, preferred_element_type=jnp.float32) + b_proj).astype(
        jnp.bfloat16
    )
    positions = jnp.arange(block_count)
    same_tile = block_tile[:, None] == block_tile[None, :]
    earlier = positions[:, None] > positions[None, :]
    rank_in_tile = jnp.sum(same_tile & earlier, axis=1)
    slot_of = block_tile * most + rank_in_tile
    blocks = features.reshape(block_count, block_size, channels)
    send_feats = (
        jnp.zeros((slots, block_size, channels), jnp.bfloat16)
        .at[slot_of]
        .set(blocks)
        .reshape(tiles, most, block_size, channels)
    )
    local_offsets = obs_offset.reshape(2, block_count, block_size).transpose(1, 0, 2)
    send_offsets = (
        jnp.zeros((slots, 2, block_size), jnp.bfloat16)
        .at[slot_of]
        .set(local_offsets)
        .reshape(tiles, most, 2, block_size)
    )
    send_patch = jnp.full((slots,), -1, jnp.int32).at[slot_of].set(block_patch).reshape(tiles, most)
    local_cells = obs_cells.reshape(KN, block_count, block_size).transpose(1, 0, 2)
    send_corner = (
        jnp.zeros((slots, block_size), jnp.int32)
        .at[slot_of]
        .set(local_cells[:, 0, :])
        .reshape(tiles, most, block_size)
    )
    got_feats, got_offsets, got_corner, got_patch = (
        lax.all_to_all(send_feats, ("rows", "cols"), split_axis=0, concat_axis=0, tiled=True),
        lax.all_to_all(send_offsets, ("rows", "cols"), split_axis=0, concat_axis=0, tiled=True),
        lax.all_to_all(send_corner, ("rows", "cols"), split_axis=0, concat_axis=0, tiled=True),
        lax.all_to_all(send_patch, ("rows", "cols"), split_axis=0, concat_axis=0, tiled=True),
    )
    tap_ids = jnp.arange(KN, dtype=jnp.int32)
    tap_step = tap_ids // 4 * PW + tap_ids % 4
    got_cells = got_corner.reshape(slots, 1, block_size) + tap_step[None, :, None]
    got_feats = got_feats.reshape(slots, block_size, channels)
    got_offsets = got_offsets.reshape(slots, 2, block_size)
    got_patch = got_patch.reshape(slots)
    live = got_patch >= 0
    safe_patch = jnp.where(live, got_patch, 0)
    weights = tap_weights(got_offsets)
    live_weights = jnp.where(live[:, None, None], weights, jnp.zeros_like(weights))

    def regroup(array):
        return array.reshape((group_count, group_size) + array.shape[1:])

    patch_ids = jnp.arange(patch_count, dtype=jnp.int32)

    def spread_group(carry, parts):
        spread_sum, density_sum = carry
        feats_part, cells_part, weights_part, patch_part = parts
        matrix = kernel_matrix(cells_part, weights_part)
        contrib = jnp.einsum("sco,sod->scd", matrix, feats_part, preferred_element_type=jnp.float32)
        cell_weight = jnp.sum(matrix.astype(jnp.float32), axis=2)
        one_hot = (patch_part[None, :] == patch_ids[:, None]).astype(jnp.float32)
        spread_sum = spread_sum + jnp.einsum(
            "ps,scd->pcd", one_hot, contrib, precision=lax.Precision.HIGHEST
        )
        density_sum = density_sum + jnp.dot(one_hot, cell_weight, precision=lax.Precision.HIGHEST)
        return ((spread_sum, density_sum), None)

    start = (
        jnp.zeros((patch_count, PH * PW, channels), jnp.float32),
        jnp.zeros((patch_count, PH * PW), jnp.float32),
    )
    (spread_patches, density_patches), unused = lax.scan(
        spread_group,
        start,
        (regroup(got_feats), regroup(got_cells), regroup(live_weights), regroup(safe_patch)),
    )
    spread_tile = patches_to_tile(spread_patches, tile_height, TC)
    density_tile = patches_to_tile(density_patches, tile_height, TC)
    spread_part, density_part = (
        lax.psum_scatter(
            spread_tile.astype(jnp.bfloat16), "orbits", scatter_dimension=0, tiled=True
        ).astype(jnp.float32),
        lax.psum_scatter(
            density_tile.astype(jnp.bfloat16), "orbits", scatter_dimension=0, tiled=True
        ).astype(jnp.float32),
    )
    grid_in = grid_input(spread_part, density_part, density_weight)
    first = jax.nn.silu(convolve(plain_edges(grid_in), w_first, b_first)).astype(jnp.bfloat16)
    grid_out = (
        grid_in.astype(jnp.float32) + convolve(plain_edges(first), w_second, b_second)
    ).astype(jnp.bfloat16)
    full_out = lax.all_gather(grid_out, "orbits", axis=0, tiled=True)
    tile_values = tile_to_patches(full_out)

    def read_group(carry, parts):
        cells_part, weights_part, patch_part = parts
        matrix = kernel_matrix(cells_part, weights_part)
        values = tile_values[patch_part]
        summed = jnp.einsum("sco,scd->sod", matrix, values, preferred_element_type=jnp.float32)
        tap_total = jnp.sum(weights_part.astype(jnp.float32), axis=1)
        return (carry, (summed / tap_total[:, :, None]).astype(jnp.bfloat16))

    unused_carry, readings = lax.scan(
        read_group, 0, (regroup(got_cells), regroup(weights), regroup(safe_patch))
    )
    returned = lax.all_to_all(
        readings.reshape(tiles, most, block_size, channels),
        ("rows", "cols"),
        split_axis=0,
        concat_axis=0,
        tiled=True,
    )
    mine = returned.reshape(slots, block_size, channels)[slot_of].reshape(
        block_count * block_size, channels
    )
    obs_out = (features.astype(jnp.float32) + mine.astype(jnp.float32)).astype(jnp.bfloat16)
    return (obs_out, grid_out)


def solution(mesh):
    in_specs = (
        P(("orbits", "rows", "cols"), None),
        P(None, ("orbits", "rows", "cols")),
        P(None, ("orbits", "rows", "cols")),
        P(("orbits", "rows", "cols")),
        P(("orbits", "rows", "cols")),
        P(),
        P(),
        P(),
        P(),
        P(),
        P(),
        P(),
        P(),
        P(),
    )
    out_specs = (P(("orbits", "rows", "cols"), None), P(("orbits", "rows"), "cols", None))
    return jax.shard_map(local, mesh=mesh, in_specs=in_specs, out_specs=out_specs, check_vma=False)
```

profile of v0, /device:TPU:0, one launch (start us, length us, event | category | flops | bytes accessed | tf_op | source)
XLA Modules:
  0.0 2135.4 jit_solution(7228297084363839567)
XLA Ops:
  10.3 5.2 all-to-all-start.2
  16.1 3.7 scatter_fusion
  20.0 3.9 all-to-all-start.1
  26.2 2.5 all-to-all-done.1
  28.7 3.3 all-to-all-start
  33.7 1.8 broadcast_in_dim.61
  35.5 4.6 scatter_fusion.1
  40.2 4.5 all-to-all-start.3
  47.5 22.9 %all-to-all-done.3 = bf16[8,8,128,128]{3,2,1,0:T(8,128)(2,1)} async-done(((bf16[8,8,128,128]{3,2,1,0:T(8,128)(2,1)}), bf16[8,8,128,128]{3,2,1,0:T(8,128)(2,1)}, u32[]{:S(2)}, u32[]{:S(2)}) %all-to-all-start.3) | async-done | bytes 2097184 | tf_op jit(solution)/shard_map/all_to_all | solution.py:158
  70.4 947.7 %while.24 = (s32[]{:T(128)}, f32[32,256,128]{2,0,1:T(8,128)}, f32[32,256]{1,0:T(8,128)S(1)}, s32[4,16]{1,0:T(4,128)S(1)}, s32[4,16,16,128]{3,2,1,0:T(8,128)}, /*...) while((s32[]{:T(128)}, f32[32,256,128]{2,0,1:T(8,128)}, ...), condition=%wide.region_8.9_spmd.clone, body=%wide.region_5.8_spmd.clone.sunk | while | flops 341324800 | bytes 18252708 | solution.py:196
  71.6 224.7 %scatter_custom_fusion.18 = bf16[524288]{0:T(1024)(128)(2,1)S(1)} fusion(s32[32768]{0:T(1024)S(1)} %bitcast.152, bf16[32768]{0:T(1024)(128)(2,1)S(1)} %bitcast.156, bf16[]{:T(256)} %constant.105.clone.1..sunk.1), kind=kCustom, calls=%fused_computation.33.clone.1 | custom fusion | bytes 1048578 | tf_op jit(solution)/shard_map/while
  296.4 2.8 fusion.93
  299.2 6.5 select_add_fusion.2
  307.6 224.7 %scatter_custom_fusion.18 = bf16[524288]{0:T(1024)(128)(2,1)S(1)} fusion(s32[32768]{0:T(1024)S(1)} %bitcast.152, bf16[32768]{0:T(1024)(128)(2,1)S(1)} %bitcast.156, bf16[]{:T(256)} %constant.105.clone.1..sunk.1), kind=kCustom, calls=%fused_computation.33.clone.1 | custom fusion | bytes 1048578 | tf_op jit(solution)/shard_map/while
  532.3 2.8 fusion.93
  535.2 7.8 select_add_fusion.2
  544.8 224.7 %scatter_custom_fusion.18 = bf16[524288]{0:T(1024)(128)(2,1)S(1)} fusion(s32[32768]{0:T(1024)S(1)} %bitcast.152, bf16[32768]{0:T(1024)(128)(2,1)S(1)} %bitcast.156, bf16[]{:T(256)} %constant.105.clone.1..sunk.1), kind=kCustom, calls=%fused_computation.33.clone.1 | custom fusion | bytes 1048578 | tf_op jit(solution)/shard_map/while
  769.6 2.8 fusion.93
  772.4 7.8 select_add_fusion.2
  782.0 224.7 %scatter_custom_fusion.18 = bf16[524288]{0:T(1024)(128)(2,1)S(1)} fusion(s32[32768]{0:T(1024)S(1)} %bitcast.152, bf16[32768]{0:T(1024)(128)(2,1)S(1)} %bitcast.156, bf16[]{:T(256)} %constant.105.clone.1..sunk.1), kind=kCustom, calls=%fused_computation.33.clone.1 | custom fusion | bytes 1048578 | tf_op jit(solution)/shard_map/while
  1006.8 2.8 fusion.93
  1009.6 7.8 select_add_fusion.2
  1019.0 2.7 convert_element_type.107
  1021.6 2.7 copy.36
  1024.4 13.9 reduce-scatter.5.cloned.1.call-done
  1039.0 43.8 %reduce-scatter.3.cloned.1.call-done = bf16[16,128,128]{2,1,0:T(8,128)(2,1)} async-done(((bf16[64,128,128]{2,1,0:T(8,128)(2,1)}), bf16[16,128,128]{2,1,0:T(8,128)(2,1)}) %reduce-scatter.3.cloned.1.call-update) | async-done | bytes 524304 | tf_op jit(solution)/shard_map/reduce_scatter | solution.py:204
  1084.4 3.4 collective-permute-start
  1089.4 4.2 collective-permute-done.1
  1096.5 3.2 collective-permute-done.3
  1103.7 2.8 collective-permute-start.4
  1108.1 4.2 collective-permute-done.5
  1112.4 2.9 collective-permute-start.6
  1116.6 2.7 collective-permute-done.7
  1125.1 46.9 %all-gather.2.cloned.1.call-done = bf16[64,128,128]{2,1,0:T(8,128)(2,1)} async-done(((bf16[16,128,128]{2,1,0:T(8,128)(2,1)}), bf16[64,128,128]{2,1,0:T(8,128)(2,1)}) %all-gather.2.cloned.1.call-update) | async-done | bytes 2097168 | tf_op jit(solution)/shard_map/all_gather | solution.py:216
  1172.0 3.5 copy.38
  1175.5 919.6 %while.23 = (s32[]{:T(128)}, bf16[4,16,128,128]{3,2,1,0:T(8,128)(2,1)}, s32[4,16,16,128]{3,2,1,0:T(8,128)}, bf16[4,16,16,128]{3,2,1,0:T(8,128)(2,1)S(1)}, s32[4,...) while((s32[]{:T(128)}, ...), condition=%wide.region_14.15_spmd, body=%wide.region_11.14_spmd.sunk | while | flops 135855152 | bytes 7689099 | solution.py:227
  1176.7 224.7 %scatter_custom_fusion.16 = bf16[524288]{0:T(1024)(128)(2,1)S(1)} fusion(s32[32768]{0:T(1024)S(1)} %bitcast.151, bf16[32768]{0:T(1024)(128)(2,1)S(1)} %bitcast.155, bf16[]{:T(256)} %constant.105.clone.1..sunk), kind=kCustom, calls=%fused_computation.13.clone.1 | custom fusion | bytes 1048578 | tf_op jit(solution)/shard_map/while
  1401.5 2.3 gather_fusion
  1406.6 224.7 %scatter_custom_fusion.16 = bf16[524288]{0:T(1024)(128)(2,1)S(1)} fusion(s32[32768]{0:T(1024)S(1)} %bitcast.151, bf16[32768]{0:T(1024)(128)(2,1)S(1)} %bitcast.155, bf16[]{:T(256)} %constant.105.clone.1..sunk), kind=kCustom, calls=%fused_computation.13.clone.1 | custom fusion | bytes 1048578 | tf_op jit(solution)/shard_map/while
  1631.4 2.3 gather_fusion
  1636.6 224.7 %scatter_custom_fusion.16 = bf16[524288]{0:T(1024)(128)(2,1)S(1)} fusion(s32[32768]{0:T(1024)S(1)} %bitcast.151, bf16[32768]{0:T(1024)(128)(2,1)S(1)} %bitcast.155, bf16[]{:T(256)} %constant.105.clone.1..sunk), kind=kCustom, calls=%fused_computation.13.clone.1 | custom fusion | bytes 1048578 | tf_op jit(solution)/shard_map/while
  1861.3 2.3 gather_fusion
  1866.5 224.7 %scatter_custom_fusion.16 = bf16[524288]{0:T(1024)(128)(2,1)S(1)} fusion(s32[32768]{0:T(1024)S(1)} %bitcast.151, bf16[32768]{0:T(1024)(128)(2,1)S(1)} %bitcast.155, bf16[]{:T(256)} %constant.105.clone.1..sunk), kind=kCustom, calls=%fused_computation.13.clone.1 | custom fusion | bytes 1048578 | tf_op jit(solution)/shard_map/while
  2091.2 2.3 gather_fusion
  2095.1 3.6 all-to-all-start.4
  2098.7 25.7 %all-to-all-done.4 = bf16[8,8,128,128]{3,2,1,0:T(8,128)(2,1)S(1)} async-done(((bf16[8,8,128,128]{3,2,1,0:T(8,128)(2,1)}), bf16[8,8,128,128]{3,2,1,0:T(8,128)(2,1)S(1)}, u32[]{:S(2)}, u32[]{:S(2)}) %all-to-all-start.4) | async-done | bytes 2097184 | tf_op jit(solution)/shard_map/all_to_all | solution.py:230
  2124.4 1.7 gather_fusion.1
  2126.1 2.8 fusion.22
  (169 shorter events, 49.3 us)
Async XLA Ops:
  7.2 24.9 %copy-start = (bf16[4096,128]{1,0:T(8,128)(2,1)S(1)}, bf16[4096,128]{1,0:T(8,128)(2,1)}, u32[]{:S(2)}) copy-start(bf16[4096,128]{1,0:T(8,128)(2,1)} %param.18) | copy-start | bytes 3145732
  10.3 9.7 all-to-all-start.2
  20.0 8.7 all-to-all-start.1
  28.7 11.4 all-to-all-start
  33.7 6.4 copy-start.1
  40.1 30.2 %copy-start.5 = (s32[3]{0:T(128)S(1)}, s32[3]{0:T(128)}, u32[]{:S(2)}) copy-start(s32[3]{0:T(128)} %constant.234) | copy-start | bytes 40
  40.1 30.2 %copy-start.6 = (s32[3]{0:T(128)S(1)}, s32[3]{0:T(128)}, u32[]{:S(2)}) copy-start(s32[3]{0:T(128)} %constant.235) | copy-start | bytes 40
  40.2 30.2 %all-to-all-start.3 = ((bf16[8,8,128,128]{3,2,1,0:T(8,128)(2,1)}), bf16[8,8,128,128]{3,2,1,0:T(8,128)(2,1)}, u32[]{:S(2)}, u32[]{:S(2)}) async-start(bf16[8,8,128,128]{3,2,1,0:T(8,128)(2,1)} %bitcast.20), calls=%async_computation.3 | async-start | bytes 4194304 | tf_op jit(solution)/shard_map/all_to_all | solution.py:158
  44.7 993.6 %reduce-scatter.5.cloned.1.call-start = ((), (), s32[]{:S(2)}) async-start(), calls=%async_computation.8 | async-start | bytes 20480 | tf_op jit(solution)/shard_map/reduce_scatter | solution.py:207
  1018.9 63.8 %reduce-scatter.3.cloned.1.call-start = ((), (), s32[]{:S(2)}) async-start(), calls=%async_computation.7 | async-start | bytes 2621440 | tf_op jit(solution)/shard_map/reduce_scatter | solution.py:204
  1024.3 58.4 %copy-start.7 = (f32[128]{0:T(128)S(1)}, f32[128]{0:T(128)}, u32[]{:S(2)}) copy-start(f32[128]{0:T(128)} %param.27) | copy-start | bytes 1540
  1024.3 72.1 %copy-start.3 = (bf16[3,3,128,128]{3,2,1,0:T(8,128)(2,1)S(1)}, bf16[3,3,128,128]{3,2,1,0:T(8,128)(2,1)}, u32[]{:S(2)}) copy-start(bf16[3,3,128,128]{3,2,1,0:T(8,128)(2,1)} %param.28) | copy-start | bytes 884740
  1024.4 147.6 %all-gather.2.cloned.1.call-start = ((), (), s32[]{:S(2)}) async-start(), calls=%async_computation.9 | async-start | bytes 2621440 | tf_op jit(solution)/shard_map/all_gather | solution.py:216
  1084.4 4.9 collective-permute-start
  1087.8 5.8 collective-permute-start.1
  1093.6 2.9 collective-permute-start.2
  1094.9 4.8 collective-permute-start.3
  1102.8 0.7 copy-start.8
  1103.4 13.2 copy-start.4
  1103.7 4.4 collective-permute-start.4
  1106.5 5.8 collective-permute-start.5
  1112.4 4.2 collective-permute-start.6
  1115.3 4.0 collective-permute-start.7
  1122.4 1.0 copy-start.2
  1122.4 1.0 copy-start.9
  2095.1 29.3 %all-to-all-start.4 = ((bf16[8,8,128,128]{3,2,1,0:T(8,128)(2,1)}), bf16[8,8,128,128]{3,2,1,0:T(8,128)(2,1)S(1)}, u32[]{:S(2)}, u32[]{:S(2)}) async-start(bf16[8,8,128,128]{3,2,1,0:T(8,128)(2,1)} %bitcast.153), calls=%async_computation.6 | async-start | bytes 4194304 | tf_op jit(solution)/shard_map/all_to_all | solution.py:230
Sparse Core Ops, SparseCore 0:
  1019.0 19.2 reduce-scatter.4
  1040.7 42.0 reduce-scatter.2
  1125.0 46.9 all-gather.1
where the time goes:
time: 2140 us
  local copies, waits for them, and re-layouts  1830 us (86%)
  waiting for transfers between devices  171 us (8%)
  matrix products  53.3 us (2%)
  starting transfers between devices  36.6 us (2%)
  other arithmetic  26.5 us (1%)
    while x8, local copies, waits for them, and re-layouts  1800 us
    all_gather x1, waiting for transfers between devices, local(): full_out = lax.all_gather(grid_out, 'orbits', axis=0, tiled=True)  46.9 us
    reduce_scatter x1, waiting for transfers between devices, local(): lax.psum_scatter(spread_tile.astype(jnp.bfloat16), 'orbits', scatter_dime...  43.8 us
  transfers between devices with their start and end apart: 16, of which 13 were waited for; matrix products, arithmetic and copies ran while one was open for 1% of the time, Pallas kernels for 0%

commit v1 on v0

v1 whole, which is shorter than its diff:
```python
import functools

import jax
import jax.numpy as jnp
from jax import lax
from jax.experimental import pallas as pl
from jax.experimental.pallas import tpu as pltpu
from jax.sharding import PartitionSpec as P

KN = 16
PH = 8
PW = 32
SR = 16
TC = 128
SIDE = 4
PAD = 8
META = 4
F32 = jnp.float32
BF16 = jnp.bfloat16

VMEM = pl.BlockSpec(memory_space=pltpu.VMEM)
SMEM = pl.BlockSpec(memory_space=pltpu.SMEM)
LIMIT = 48 * 1024 * 1024


def call(kernel, out_shape, in_specs, scratch, flops, moved):
    single = not isinstance(out_shape, (tuple, list))
    return pl.pallas_call(
        kernel,
        out_shape=out_shape,
        in_specs=in_specs,
        out_specs=VMEM if single else [VMEM] * len(out_shape),
        scratch_shapes=scratch,
        compiler_params=pltpu.CompilerParams(vmem_limit_bytes=LIMIT),
        cost_estimate=pl.CostEstimate(flops=flops, bytes_accessed=moved, transcendentals=0),
    )


def silu(v):
    half = 0.5 * v
    return half + half * jnp.tanh(half)


def each_slot(tile_ref, count_ref, most, body):
    for t in range(count_ref.shape[0]):
        count_ref[t] = 0
    for b in range(tile_ref.shape[0]):
        t = tile_ref[b]
        n = count_ref[t]
        count_ref[t] = n + 1
        body(b, t * most + n)


def meta_kernel(most, tile_ref, patch_ref, offset_ref, cells_ref, out_ref, count_ref):
    size = out_ref.shape[1]
    row = lax.broadcasted_iota(jnp.int32, out_ref.shape, 0) % META
    out_ref[...] = jnp.where(row == META - 1, 0.0, jnp.where(row == META - 2, -65536.0, 0.0))

    def put(b, slot):
        part = slice(b * size, (b + 1) * size)
        out_ref[pl.ds(slot * META, 2), :] = offset_ref[:, part].astype(F32)
        out_ref[pl.ds(slot * META + 2, 1), :] = cells_ref[0:1, part].astype(F32)
        out_ref[pl.ds(slot * META + 3, 1), :] = jnp.full((1, size), patch_ref[b], jnp.int32).astype(F32)

    each_slot(tile_ref, count_ref, most, put)


def embed_kernel(most, tile_ref, x_ref, we_ref, be_ref, wp_ref, bp_ref, feat_ref, send_ref, count_ref):
    blocks, size, channels = feat_ref.shape
    send_ref[...] = jnp.zeros(send_ref.shape, BF16)
    step = 4

    def some(i, unused):
        rows = pl.ds(pl.multiple_of(i * step * size, step * size), step * size)
        hidden = silu(jnp.dot(x_ref[rows, :], we_ref[...], preferred_element_type=F32) + be_ref[...])
        out = jnp.dot(hidden.astype(BF16), wp_ref[...], preferred_element_type=F32) + bp_ref[...]
        feat_ref[pl.ds(i * step, step)] = out.astype(BF16).reshape(step, size, channels)
        return unused

    lax.fori_loop(0, blocks // step, some, 0)

    def put(b, slot):
        send_ref[slot] = feat_ref[b]

    each_slot(tile_ref, count_ref, most, put)


def factors(meta, normal):
    off_row, off_col, corner = meta[0:1, :], meta[1:2, :], meta[2:3, :]
    first_row = jnp.floor(corner * (1.0 / PW))
    first_col = corner - first_row * PW

    def factor(count, start, off):
        at = lax.broadcasted_iota(jnp.int32, (count, meta.shape[1]), 0).astype(F32) - start
        delta = at - 1.5 - off
        value = jnp.exp(delta * delta * -0.5)
        return jnp.where((at >= 0.0) & (at < SIDE), value, 0.0)

    def total(off):
        at = lax.broadcasted_iota(jnp.int32, (SIDE, meta.shape[1]), 0).astype(F32)
        delta = at - 1.5 - off
        return jnp.sum(jnp.exp(delta * delta * -0.5), axis=0, keepdims=True)

    rows, cols = factor(PH, first_row, off_row), factor(PW, first_col, off_col)
    if normal:
        rows = rows / (total(off_row) * total(off_col))
    return rows, cols


def outer(rows, cols):
    return (rows[:, None, :] * cols[None, :, :]).reshape(PH * PW, rows.shape[1]).astype(BF16)


def spread_kernel(patch_ref, meta_ref, feat_ref, out_ref, acc_ref, dens_ref):
    slots = feat_ref.shape[0]
    across = TC // PW
    orbits = out_ref.shape[0]
    acc_ref[...] = jnp.zeros(acc_ref.shape, F32)
    dens_ref[...] = jnp.zeros(dens_ref.shape, F32)

    def pair(i, unused):
        metas = meta_ref[pl.ds(pl.multiple_of(i * 2 * META, 2 * META), 2 * META), :]
        for k in range(2):
            slot = i * 2 + k
            rows, cols = factors(metas[k * META : (k + 1) * META], False)
            matrix = outer(rows, cols)
            patch = patch_ref[slot]
            part = jnp.dot(matrix, feat_ref[slot], preferred_element_type=F32)
            at = (
                pl.ds(pl.multiple_of(patch // across * PH, PH), PH),
                pl.ds(pl.multiple_of(patch % across * PW, PW), PW),
            )
            acc_ref[at] += part.reshape(PH, PW, part.shape[1])
            dens_ref[patch] += lax.dot_general(
                rows.astype(BF16), cols.astype(BF16), (((1,), (1,)), ((), ())), preferred_element_type=F32
            )
        return unused

    lax.fori_loop(0, slots // 2, pair, 0)
    channels = acc_ref.shape[2]
    for z in range(orbits):
        out_ref[z, 0 : SR * TC, :] = acc_ref[z * SR : (z + 1) * SR].reshape(SR * TC, channels).astype(BF16)
        bands = []
        for band in range(SR // PH):
            first = (z * (SR // PH) + band) * across
            bands.append(jnp.concatenate([dens_ref[first + c] for c in range(across)], axis=1))
        out_ref[z, SR * TC :, :] = jnp.concatenate(bands, axis=0).astype(BF16)


def grid_kernel(part_ref, weight_ref, out_ref):
    density = part_ref[SR * TC :, :].astype(F32).T
    for i in range(SR):
        d = jnp.broadcast_to(density[:, i : i + 1], (TC, out_ref.shape[2]))
        spread = part_ref[i * TC : (i + 1) * TC, :].astype(F32)
        out_ref[i] = (spread / jnp.maximum(d, 1.0) + weight_ref[...] * (d / (1.0 + d))).astype(BF16)


def conv_kernel(
    edge_ref, x_ref, up_ref, down_ref, left_ref, right_ref, w1_ref, b1_ref, w2_ref, b2_ref,
    out_ref, wide_ref, x16_ref, first_ref, wc1_ref, wc2_ref,
):
    channels = out_ref.shape[2]
    width = x16_ref.shape[1]
    for a in range(3):
        for b in range(3):
            at = (slice(a * channels, (a + 1) * channels), slice(b * channels, (b + 1) * channels))
            wc1_ref[at] = w1_ref[a, b]
            wc2_ref[at] = w2_ref[a, b]
    body = slice(PAD, PAD + TC)
    wide_ref[...] = jnp.zeros(wide_ref.shape, F32)
    wide_ref[0:2, body] = up_ref[...].astype(F32)
    wide_ref[2 : 2 + SR, body] = x_ref[...].astype(F32)
    wide_ref[2 + SR :, body] = down_ref[...].astype(F32)
    wide_ref[:, PAD - 2 : PAD] = left_ref[...].astype(F32)
    wide_ref[:, PAD + TC : PAD + TC + 2] = right_ref[...].astype(F32)
    x16_ref[...] = wide_ref[...].astype(BF16)

    def taps(source, i, weights):
        rows = jnp.concatenate([source[i], source[i + 1], source[i + 2]], axis=1)
        all_taps = jnp.dot(rows, weights[...], preferred_element_type=F32)
        return (
            pltpu.roll(all_taps[:, :channels], 1, 0)
            + all_taps[:, channels : 2 * channels]
            + pltpu.roll(all_taps[:, 2 * channels :], width - 1, 0)
        )

    col = lax.broadcasted_iota(jnp.int32, (width, channels), 0)
    inside = (col >= PAD - edge_ref[2]) & (col < PAD + TC + edge_ref[3])

    def first_row(i, unused):
        value = silu(taps(x16_ref, i, wc1_ref) + b1_ref[...])
        low = jnp.where(edge_ref[0] == 1, 0, 1)
        high = jnp.where(edge_ref[1] == 1, SR + 2, SR + 1)
        keep = inside & (i >= low) & (i < high)
        first_ref[i] = jnp.where(keep, value, 0.0).astype(BF16)
        return unused

    lax.fori_loop(0, SR + 2, first_row, 0)

    def second_row(i, unused):
        value = taps(first_ref, i, wc2_ref) + b2_ref[...]
        out_ref[i] = (value[PAD : PAD + TC] + x_ref[i].astype(F32)).astype(BF16)
        return unused

    lax.fori_loop(0, SR, second_row, 0)


def read_kernel(patch_ref, meta_ref, grid_ref, out_ref):
    slots = out_ref.shape[0]
    across = TC // PW

    def pair(i, unused):
        metas = meta_ref[pl.ds(pl.multiple_of(i * 2 * META, 2 * META), 2 * META), :]
        for k in range(2):
            slot = i * 2 + k
            rows, cols = factors(metas[k * META : (k + 1) * META], True)
            matrix = outer(rows, cols)
            patch = patch_ref[slot]
            values = grid_ref[
                pl.ds(pl.multiple_of(patch // across * PH, PH), PH),
                pl.ds(pl.multiple_of(patch % across * PW, PW), PW),
            ].reshape(PH * PW, grid_ref.shape[2])
            out_ref[slot] = lax.dot_general(
                matrix, values, (((0,), (0,)), ((), ())), preferred_element_type=F32
            ).astype(BF16)
        return unused

    lax.fori_loop(0, slots // 2, pair, 0)


def final_kernel(most, tile_ref, feat_ref, got_ref, out_ref, count_ref):
    def put(b, slot):
        out_ref[b] = (feat_ref[b].astype(F32) + got_ref[slot].astype(F32)).astype(BF16)

    each_slot(tile_ref, count_ref, most, put)


def shifts(axis):
    size = lax.axis_size(axis)
    up = [(i, i + 1) for i in range(size - 1)]
    return up, [(j, i) for i, j in up]


def halo(x, axis, dim, width):
    up, down = shifts(axis)
    length = x.shape[dim]
    before = lax.ppermute(lax.slice_in_dim(x, length - width, length, axis=dim), axis, up)
    after = lax.ppermute(lax.slice_in_dim(x, 0, width, axis=dim), axis, down)
    return before, after


def local(
    obs_feat, obs_offset, obs_cells, block_tile, block_patch, w_embed, b_embed, w_proj, b_proj,
    density_weight, w_first, b_first, w_second, b_second,
):
    channels = obs_feat.shape[1]
    blocks = block_tile.shape[0]
    size = obs_feat.shape[0] // blocks
    plane = ("rows", "cols")
    tiles = lax.axis_size(plane)
    orbits = lax.axis_size("orbits")
    most = max(2, 2 * blocks // tiles)
    slots = tiles * most
    height = orbits * SR
    patches = height // PH * (TC // PW)
    counts = pltpu.SMEM((tiles,), jnp.int32)
    shape = jax.ShapeDtypeStruct
    bias = lambda b: b.reshape(1, channels)

    meta = call(
        functools.partial(meta_kernel, most),
        shape((slots * META, size), F32),
        [SMEM, SMEM, VMEM, VMEM],
        [counts],
        1000000,
        obs_cells.size * 4,
    )(block_tile, block_patch, obs_offset, obs_cells)
    got_meta = lax.all_to_all(
        meta.reshape(tiles, most * META, size), plane, split_axis=0, concat_axis=0, tiled=True
    ).reshape(slots * META, size)
    features, send = call(
        functools.partial(embed_kernel, most),
        (shape((blocks, size, channels), BF16), shape((slots, size, channels), BF16)),
        [SMEM, VMEM, VMEM, VMEM, VMEM, VMEM],
        [counts],
        4 * obs_feat.size * channels,
        8 * obs_feat.size,
    )(block_tile, obs_feat, w_embed, bias(b_embed), w_proj, bias(b_proj))
    got = lax.all_to_all(
        send.reshape(tiles, most, size, channels), plane, split_axis=0, concat_axis=0, tiled=True
    ).reshape(slots, size, channels)
    got_patch = got_meta.reshape(slots, META, size)[:, META - 1, 0].astype(jnp.int32)

    matmul_flops = 2 * slots * size * channels * PH * PW
    partial = call(
        spread_kernel,
        shape((orbits, SR * TC + SR, channels), BF16),
        [SMEM, VMEM, VMEM],
        [pltpu.VMEM((height, TC, channels), F32), pltpu.VMEM((patches, PH, PW), F32)],
        matmul_flops,
        8 * slots * size * channels,
    )(got_patch, got_meta, got)
    part = lax.psum_scatter(
        partial.reshape(orbits * (SR * TC + SR), channels), "orbits", scatter_dimension=0, tiled=True
    )
    grid_in = call(
        grid_kernel, shape((SR, TC, channels), BF16), [VMEM, VMEM], [], 10000000, 4 * part.size
    )(part, bias(density_weight))

    stripe = ("orbits", "rows")
    above, below = halo(grid_in, stripe, 0, 2)
    extended = jnp.concatenate(
        [jnp.concatenate([above[:, c], grid_in[:, c], below[:, c]], axis=0) for c in (slice(0, 2), slice(TC - 2, TC))],
        axis=1,
    )
    left, right = halo(extended, "cols", 1, 2)
    at_row, at_col = lax.axis_index(stripe), lax.axis_index("cols")
    edges = jnp.stack(
        [
            at_row > 0,
            at_row < lax.axis_size(stripe) - 1,
            at_col > 0,
            at_col < lax.axis_size("cols") - 1,
        ]
    ).astype(jnp.int32)
    width = TC + 2 * PAD
    grid_out = call(
        conv_kernel,
        shape((SR, TC, channels), BF16),
        [SMEM] + [VMEM] * 9,
        [
            pltpu.VMEM((SR + 4, width, channels), F32),
            pltpu.VMEM((SR + 4, width, channels), BF16),
            pltpu.VMEM((SR + 2, width, channels), BF16),
            pltpu.VMEM((3 * channels, 3 * channels), BF16),
            pltpu.VMEM((3 * channels, 3 * channels), BF16),
        ],
        4 * 9 * SR * TC * channels * channels,
        4 * grid_in.size,
    )(edges, grid_in, above, below, left, right, w_first, bias(b_first), w_second, bias(b_second))

    whole = lax.all_gather(grid_out, "orbits", axis=0, tiled=True)
    readings = call(
        read_kernel,
        shape((slots, size, channels), BF16),
        [SMEM, VMEM, VMEM],
        [],
        matmul_flops,
        8 * slots * size * channels,
    )(got_patch, got_meta, whole)
    returned = lax.all_to_all(
        readings.reshape(tiles, most, size, channels), plane, split_axis=0, concat_axis=0, tiled=True
    ).reshape(slots, size, channels)
    obs_out = call(
        functools.partial(final_kernel, most),
        shape((blocks, size, channels), BF16),
        [SMEM, VMEM, VMEM],
        [counts],
        1000000,
        8 * obs_feat.size,
    )(block_tile, features, returned)
    return obs_out.reshape(obs_feat.shape), grid_out


def solution(mesh):
    spread_out = ("orbits", "rows", "cols")
    in_specs = (
        P(spread_out, None),
        P(None, spread_out),
        P(None, spread_out),
        P(spread_out),
        P(spread_out),
    ) + (P(),) * 9
    out_specs = (P(spread_out, None), P(("orbits", "rows"), "cols", None))
    return jax.shard_map(local, mesh=mesh, in_specs=in_specs, out_specs=out_specs, check_vma=False)
```

time: 2140 us -> 234 us (0.11)
  local copies, waits for them, and re-layouts: 1830 us -> 11.7 us
  matrix products: 53.3 us -> 0 us
  waiting for transfers between devices: 171 us -> 124 us
  Pallas kernels: 0 us -> 35.2 us
  blocking collectives: 0 us -> 29.4 us
  other arithmetic: 26.5 us -> 1.35 us
    while x8 -> x0, local copies, waits for them, and re-layouts: 1800 us -> none
    dot_general x23 -> x0, matrix products: 53.3 us -> none  [the longest x4 29.8 us: spread_group(): jnp.einsum('ps,scd->pcd', one_hot, contrib, precision=lax.Precision.HIGHEST)]
    pallas_call x0 -> x7, Pallas kernels: none -> 35.2 us  [the longest x1 9.97 us: local(): call(conv_kernel, shape((SR, TC, channels), BF16), [SMEM] + [VMEM] * 9, [...]
    all_to_all x0 -> x1, blocking collectives: none -> 29.4 us  [local(): lax.all_to_all(readings.reshape(tiles, most, size, channels), plane, spli...]
    all_to_all x5 -> x2, waiting for transfers between devices: 51.3 us -> 24.4 us  [the longest x1 24.4 us: local(): lax.all_to_all(send.reshape(tiles, most, size, channels), plane, split_ax...]
    reduce_scatter x2 -> x1, waiting for transfers between devices: 57.6 us -> 44.7 us  [local(): lax.psum_scatter(partial.reshape(orbits * (SR * TC + SR), channels), 'orb...]
  transfers between devices with their start and end apart: 16 -> 8, of which waited for: 13 -> 6; matrix products, arithmetic and copies ran while one was open for 1% -> 1% of each run, Pallas kernels for 0% -> 2%
where the time goes in v1:
time: 234 us
  waiting for transfers between devices  124 us (53%)
  Pallas kernels  35.2 us (15%)
  blocking collectives  29.4 us (13%)
  starting transfers between devices  17.9 us (8%)
  between operations  14.2 us (6%)
  local copies, waits for them, and re-layouts  11.7 us (5%)
    all_gather x1, waiting for transfers between devices, local(): whole = lax.all_gather(grid_out, 'orbits', axis=0, tiled=True)  49.3 us
    reduce_scatter x1, waiting for transfers between devices, local(): lax.psum_scatter(partial.reshape(orbits * (SR * TC + SR), channels), 'orb...  44.7 us
    all_to_all x1, blocking collectives, local(): lax.all_to_all(readings.reshape(tiles, most, size, channels), plane, spli...  29.4 us
    all_to_all x1, waiting for transfers between devices, local(): lax.all_to_all(send.reshape(tiles, most, size, channels), plane, split_ax...  24.4 us
    unnamed x38, local copies, waits for them, and re-layouts  11.7 us
    pallas_call x1, Pallas kernels, local(): call(conv_kernel, shape((SR, TC, channels), BF16), [SMEM] + [VMEM] * 9, [...  9.97 us
    pallas_call x1, Pallas kernels, local(): call(read_kernel, shape((slots, size, channels), BF16), [SMEM, VMEM, VMEM...  9.1 us
    pallas_call x1, Pallas kernels, local(): call(spread_kernel, shape((orbits, SR * TC + SR, channels), BF16), [SMEM,...  8.95 us
  transfers between devices with their start and end apart: 8, of which 6 were waited for; matrix products, arithmetic and copies ran while one was open for 1% of the time, Pallas kernels for 2%

profile of v1, /device:TPU:0, one launch (start us, length us, event | category | flops | bytes accessed | tf_op | source)
XLA Modules:
  0.0 233.5 jit_solution(525527266755812878)
XLA Ops:
  7.2 0.0 copy-start.4
  7.2 0.9 copy-done.4
  8.1 0.7 copy-done.7
  8.8 0.7 copy-done.8
  9.5 0.7 copy-done.11
  10.1 1.3 shard_map.150
  11.5 5.2 %all-to-all-start = ((f32[8,32,128]{2,1,0:T(8,128)}), f32[8,32,128]{2,1,0:T(8,128)S(1)}, u32[]{:S(2)}, u32[]{:S(2)}) async-start(f32[8,32,128]{2,1,0:T(8,128)} %bitcast.2), calls=%async_computation | async-start | bytes 262144 | tf_op jit(solution)/shard_map/all_to_all | solution.py:278
  16.7 1.2 copy-done.2
  17.9 0.8 copy-done.5
  18.6 0.8 copy-done.6
  19.4 0.7 copy-done.9
  20.1 0.7 copy-done.12
  20.7 0.7 copy-done.13
  21.4 3.6 %shard_map.149 = (bf16[32,128,128]{2,1,0:T(8,128)(2,1)S(1)}, bf16[64,128,128]{2,1,0:T(8,128)(2,1)S(1)}) custom-call(s32[32]{0:T(128)S(1)} %copy-done.9, bf16[4096,128]{1,0:T(8,128)(2,1)S(1)} %copy-done.2, bf16[128,128]{1,0:T(8,128)(2,1)S(1)} %copy-done.5, f32[1,128]{1,0:T(1,128)S(1)} %bitcast.25, bf16[128,128]{1,0:T(8,128)(2,1)S(1)} %copy-done.6, ...), custom_call_target="tpu_custom_call" | custom-call | flops 268435456 | bytes 4194304 | tf_op jit(solution)/shard_map/pallas_call | solution.py:281
  24.9 0.0 copy-start
  25.0 1.4 copy-done
  26.3 0.0 all-to-all-done
  26.3 4.2 %all-to-all-start.1 = ((bf16[8,8,128,128]{3,2,1,0:T(8,128)(2,1)}), bf16[8,8,128,128]{3,2,1,0:T(8,128)(2,1)S(1)}, u32[]{:S(2)}, u32[]{:S(2)}) async-start(bf16[8,8,128,128]{3,2,1,0:T(8,128)(2,1)} %bitcast.21), calls=%async_computation.1 | async-start | bytes 4194304 | tf_op jit(solution)/shard_map/all_to_all | solution.py:289
  30.5 0.0 reduce-scatter.2.cloned.1.call-start
  30.6 1.2 fusion.patch_ref
  31.8 24.4 %all-to-all-done.1 = bf16[8,8,128,128]{3,2,1,0:T(8,128)(2,1)S(1)} async-done(((bf16[8,8,128,128]{3,2,1,0:T(8,128)(2,1)}), bf16[8,8,128,128]{3,2,1,0:T(8,128)(2,1)S(1)}, u32[]{:S(2)}, u32[]{:S(2)}) %all-to-all-start.1) | async-done | bytes 2097184 | tf_op jit(solution)/shard_map/all_to_all | solution.py:289
  56.2 8.9 %shard_map.151 = bf16[4,2064,128]{2,1,0:T(8,128)(2,1)} custom-call(s32[64]{0:T(128)S(1)} %fusion.patch_ref, f32[256,128]{1,0:T(8,128)S(1)} %bitcast.23, bf16[64,128,128]{2,1,0:T(8,128)(2,1)S(1)} %bitcast.18), custom_call_target="tpu_custom_call" | custom-call | flops 536870912 | bytes 8388608 | tf_op jit(solution)/shard_map/pallas_call | solution.py:295
  65.2 0.0 copy-start.18
  65.2 0.0 reduce-scatter.2.cloned.1.call-update
  65.2 0.0 all-gather.2.cloned.1.call-start
  65.3 44.7 %reduce-scatter.2.cloned.1.call-done.part_ref = bf16[2064,128]{1,0:T(8,128)(2,1)} async-done(((bf16[8256,128]{1,0:T(8,128)(2,1)}), bf16[2064,128]{1,0:T(8,128)(2,1)}) %reduce-scatter.2.cloned.1.call-update) | async-done | bytes 528400 | tf_op jit(solution)/shard_map/reduce_scatter | solution.py:303
  110.0 0.0 copy-done.14
  110.0 1.0 copy-done.3
  111.0 0.5 shard_map.152.x_ref
  111.6 1.3 collective-permute-start.1
  112.9 4.5 %collective-permute-start = (bf16[2,128,128]{2,1,0:T(8,128)(2,1)S(1)}, bf16[2,128,128]{2,1,0:T(8,128)(2,1)S(1)}, u32[]{:S(2)}, u32[]{:S(2)}) collective-permute-start(bf16[2,128,128]{2,1,0:T(8,128)(2,1)S(1)} %get-tuple-element.9), channel_id=1, source_target_pairs={{0,4},{4,8},{8,12},{12,16},{16,20},{20,24},{24,28},{1,5},{5,9},{9,... | collective-permute-start | bytes 196616 | tf_op jit(solution)/shard_map/ppermute | solution.py:247
  117.4 0.3 collective-permute-done.1.down_ref
  117.7 1.6 collective-permute-done.up_ref
  119.4 1.3 collective-permute-start.2
  120.7 1.3 collective-permute-start.3
  122.0 0.1 add_convert_fusion.edge_ref
  122.1 0.0 collective-permute-done.2.left_ref
  122.1 3.4 %collective-permute-done.3.right_ref = bf16[20,2,128]{2,1,0:T(2,128)(2,1)S(1)} collective-permute-done((bf16[20,2,128]{2,1,0:T(2,128)(2,1)S(1)}, bf16[20,2,128]{2,1,0:T(2,128)(2,1)S(1)}, u32[]{:S(2)}, u32[]{:S(2)}) %collective-permute-start.3) | collective-permute-done | bytes 10272 | tf_op jit(solution)/shard_map/ppermute | solution.py:248
  125.5 0.0 copy-done.18
  125.5 10.0 %shard_map.153 = bf16[16,128,128]{2,1,0:T(8,128)(2,1)} custom-call(s32[4]{0:T(128)S(1)} %add_convert_fusion.edge_ref, bf16[16,128,128]{2,1,0:T(8,128)(2,1)S(1)} %shard_map.152.x_ref, bf16[2,128,128]{2,1,0:T(8,128)(2,1)S(1)} %collective-permute-done.up_ref, bf16[2,128,128]{2,1,0:T(8,128)(2,1)S(1)} %collective-permute-done.1.down_ref, ...), custom_call_target="tpu_custom_call" | custom-call | flops 1207959552 | bytes 1048576 | tf_op jit(solution)/shard_map/pallas_call | solution.py:327
  135.4 0.0 all-gather.2.cloned.1.call-update
  135.5 49.3 %all-gather.2.cloned.1.call-done.grid_ref = bf16[64,128,128]{2,1,0:T(8,128)(2,1)} async-done(((bf16[16,128,128]{2,1,0:T(8,128)(2,1)}), bf16[64,128,128]{2,1,0:T(8,128)(2,1)}) %all-gather.2.cloned.1.call-update) | async-done | bytes 2097168 | tf_op jit(solution)/shard_map/all_gather | solution.py:342
  184.8 1.6 copy-done.1
  186.3 9.1 %shard_map.154 = bf16[64,128,128]{2,1,0:T(8,128)(2,1)S(1)} custom-call(s32[64]{0:T(128)S(1)} %fusion.patch_ref, f32[256,128]{1,0:T(8,128)S(1)} %bitcast.24, bf16[64,128,128]{2,1,0:T(8,128)(2,1)S(1)} %copy-done.1), custom_call_target="tpu_custom_call" | custom-call | flops 536870912 | bytes 8388608 | tf_op jit(solution)/shard_map/pallas_call | solution.py:343
  195.5 0.0 copy-start.10
  195.5 29.4 %all_to_all.15 = bf16[8,8,128,128]{3,2,1,0:T(8,128)(2,1)S(1)} all-to-all(bf16[8,8,128,128]{3,2,1,0:T(8,128)(2,1)S(1)} %bitcast.19), channel_id=1, replica_groups=mesh['orbits'=4,'rows'=2,'cols'=4] {'rows','cols'}, dimensions={0} | all-to-all | bytes 4194304 | tf_op jit(solution)/shard_map/all_to_all | solution.py:351
  224.9 0.0 copy-done.10
  224.9 1.8 shard_map.155
  (24 shorter events, 0.1 us)
Async XLA Ops:
  7.2 1.0 copy-start.4
  8.1 0.7 copy-start.7
  8.8 0.7 copy-start.8
  9.5 0.7 copy-start.11
  11.5 14.8 %all-to-all-start = ((f32[8,32,128]{2,1,0:T(8,128)}), f32[8,32,128]{2,1,0:T(8,128)S(1)}, u32[]{:S(2)}, u32[]{:S(2)}) async-start(f32[8,32,128]{2,1,0:T(8,128)} %bitcast.2), calls=%async_computation | async-start | bytes 262144 | tf_op jit(solution)/shard_map/all_to_all | solution.py:278
  16.7 1.2 copy-start.2
  17.9 0.8 copy-start.5
  18.6 0.8 copy-start.6
  19.4 0.7 copy-start.9
  20.1 0.7 copy-start.12
  20.7 0.7 copy-start.13
  24.9 1.4 copy-start
  26.3 29.9 %all-to-all-start.1 = ((bf16[8,8,128,128]{3,2,1,0:T(8,128)(2,1)}), bf16[8,8,128,128]{3,2,1,0:T(8,128)(2,1)S(1)}, u32[]{:S(2)}, u32[]{:S(2)}) async-start(bf16[8,8,128,128]{3,2,1,0:T(8,128)(2,1)} %bitcast.21), calls=%async_computation.1 | async-start | bytes 4194304 | tf_op jit(solution)/shard_map/all_to_all | solution.py:289
  30.5 79.5 %reduce-scatter.2.cloned.1.call-start = ((), (), s32[]{:S(2)}) async-start(), calls=%async_computation.4 | async-start | bytes 2641920 | tf_op jit(solution)/shard_map/reduce_scatter | solution.py:303
  65.2 44.8 %copy-start.14 = (f32[128]{0:T(128)S(1)}, f32[128]{0:T(128)}, u32[]{:S(2)}) copy-start(f32[128]{0:T(128)} %param.23) | copy-start | bytes 1540
  65.2 60.3 %copy-start.15 = (bf16[3,3,128,128]{3,2,1,0:T(8,128)(2,1)S(1)}, bf16[3,3,128,128]{3,2,1,0:T(8,128)(2,1)}, u32[]{:S(2)}) copy-start(bf16[3,3,128,128]{3,2,1,0:T(8,128)(2,1)} %w1_ref.1) | copy-start | bytes 884740
  65.2 60.3 %copy-start.16 = (bf16[3,3,128,128]{3,2,1,0:T(8,128)(2,1)S(1)}, bf16[3,3,128,128]{3,2,1,0:T(8,128)(2,1)}, u32[]{:S(2)}) copy-start(bf16[3,3,128,128]{3,2,1,0:T(8,128)(2,1)} %w2_ref.1) | copy-start | bytes 884740
  65.2 60.3 %copy-start.17 = (f32[128]{0:T(128)S(1)}, f32[128]{0:T(128)}, u32[]{:S(2)}) copy-start(f32[128]{0:T(128)} %param.25) | copy-start | bytes 1540
  65.2 60.3 %copy-start.18 = (f32[128]{0:T(128)S(1)}, f32[128]{0:T(128)}, u32[]{:S(2)}) copy-start(f32[128]{0:T(128)} %param.27) | copy-start | bytes 1540
  65.2 119.5 %all-gather.2.cloned.1.call-start = ((), (), s32[]{:S(2)}) async-start(), calls=%async_computation.5 | async-start | bytes 2621440 | tf_op jit(solution)/shard_map/all_gather | solution.py:342
  110.0 1.0 copy-start.3
  111.6 6.2 %collective-permute-start.1 = (bf16[2,128,128]{2,1,0:T(8,128)(2,1)S(1)}, bf16[2,128,128]{2,1,0:T(8,128)(2,1)S(1)}, u32[]{:S(2)}, u32[]{:S(2)}) collective-permute-start(bf16[2,128,128]{2,1,0:T(8,128)(2,1)S(1)} %get-tuple-element.8), channel_id=1, source_target_pairs={{4,0},{8,4},{12,8},{16,12},{20,16},{24,20},{28,24},{5,1},{9,5},{13... | collective-permute-start | bytes 196616 | tf_op jit(solution)/shard_map/ppermute | solution.py:248
  112.9 6.4 %collective-permute-start = (bf16[2,128,128]{2,1,0:T(8,128)(2,1)S(1)}, bf16[2,128,128]{2,1,0:T(8,128)(2,1)S(1)}, u32[]{:S(2)}, u32[]{:S(2)}) collective-permute-start(bf16[2,128,128]{2,1,0:T(8,128)(2,1)S(1)} %get-tuple-element.9), channel_id=1, source_target_pairs={{0,4},{4,8},{8,12},{12,16},{16,20},{20,24},{24,28},{1,5},{5,9},{9,... | collective-permute-start | bytes 196616 | tf_op jit(solution)/shard_map/ppermute | solution.py:247
  119.4 2.7 %collective-permute-start.2 = (bf16[20,2,128]{2,1,0:T(2,128)(2,1)S(1)}, bf16[20,2,128]{2,1,0:T(2,128)(2,1)S(1)}, u32[]{:S(2)}, u32[]{:S(2)}) collective-permute-start(bf16[20,2,128]{2,1,0:T(2,128)(2,1)S(1)} %pad_maximum_fusion), channel_id=1, source_target_pairs={{0,1},{1,2},{2,3},{4,5},{5,6},{6,7},{8,9},{9,10},{10,11},{12,13},{... | collective-permute-start | bytes 30728 | tf_op jit(solution)/shard_map/ppermute | solution.py:247
  120.7 4.8 %collective-permute-start.3 = (bf16[20,2,128]{2,1,0:T(2,128)(2,1)S(1)}, bf16[20,2,128]{2,1,0:T(2,128)(2,1)S(1)}, u32[]{:S(2)}, u32[]{:S(2)}) collective-permute-start(bf16[20,2,128]{2,1,0:T(2,128)(2,1)S(1)} %pad_maximum_fusion.1), channel_id=1, source_target_pairs={{1,0},{2,1},{3,2},{5,4},{6,5},{7,6},{9,8},{10,9},{11,10},{13,12},{... | collective-permute-start | bytes 30728 | tf_op jit(solution)/shard_map/ppermute | solution.py:248
  184.8 1.6 copy-start.1
  195.5 29.4 %copy-start.10 = (s32[32]{0:T(128)S(1)}, s32[32]{0:T(128)}, u32[]{:S(2)}) copy-start(s32[32]{0:T(128)} %tile_ref.5) | copy-start | bytes 388
Sparse Core Ops, SparseCore 0:
  65.3 44.6 reduce-scatter.1
  135.6 49.1 all-gather.1

commit v2 on v1

v2 whole, which is shorter than its diff:
```python
import functools

import jax
import jax.numpy as jnp
from jax import lax
from jax.experimental import pallas as pl
from jax.experimental.pallas import tpu as pltpu
from jax.sharding import PartitionSpec as P

KN = 16
PH = 8
PW = 32
SR = 16
TC = 128
SIDE = 4
PAD = 8
META = 4
ACROSS = TC // PW
F32 = jnp.float32
BF16 = jnp.bfloat16

SMEM = pl.BlockSpec(memory_space=pltpu.SMEM)
LIMIT = 48 * 1024 * 1024


def whole(shape):
    zeros = (0,) * len(shape)
    return pl.BlockSpec(tuple(shape), lambda i: zeros)


def part(shape, *rest):
    tail = rest or (0,) * (len(shape) - 1)
    return pl.BlockSpec(tuple(shape), lambda i: (i,) + tuple(tail))


def call(kernel, grid, in_specs, out_specs, out_shape, scratch, flops, moved, *args):
    return pl.pallas_call(
        kernel,
        grid=(grid,),
        in_specs=in_specs,
        out_specs=out_specs,
        out_shape=out_shape,
        scratch_shapes=scratch,
        compiler_params=pltpu.CompilerParams(vmem_limit_bytes=LIMIT),
        cost_estimate=pl.CostEstimate(flops=flops, bytes_accessed=moved, transcendentals=0),
    )(*args)


def silu(v):
    half = 0.5 * v
    return half + half * jnp.tanh(half)


def swap(x):
    axis = x.ndim - 1
    return pltpu.roll(x.astype(F32), x.shape[axis] // 2, axis).astype(x.dtype)


def lanes(shape):
    return lax.broadcasted_iota(jnp.int32, shape, len(shape) - 1) // (shape[-1] // 2)


def next_slot(tile_ref, count_ref, b):
    t = tile_ref[b]
    n = count_ref[t]
    count_ref[t] = n + 1
    return t, n


def clear(count_ref):
    for t in range(count_ref.shape[0]):
        count_ref[t] = 0


def embed_kernel(
    tile_ref, patch_ref, offset_ref, cells_ref, x_ref, we_ref, be_ref, wp_ref, bp_ref,
    feat_ref, send0_ref, send1_ref, count_ref, meta_ref, wide_ref, bias_ref,
):
    step = pl.program_id(0)
    per, size, channels = feat_ref.shape
    tiles = send0_ref.shape[0]
    meta_rows = meta_ref.shape[0] // tiles

    @pl.when(step == 0)
    def _():
        clear(count_ref)
        send0_ref[...] = jnp.zeros(send0_ref.shape, BF16)
        send1_ref[...] = jnp.zeros(send1_ref.shape, BF16)
        row = lax.broadcasted_iota(jnp.int32, meta_ref.shape, 0) % META
        meta_ref[...] = jnp.where(row == 2, -65536.0, 0.0)
        wide_ref[:, :channels] = wp_ref[...]
        wide_ref[:, channels:] = swap(wp_ref[...])
        bias_ref[:, :channels] = bp_ref[...]
        bias_ref[:, channels:] = swap(bp_ref[...])

    hidden = silu(jnp.dot(x_ref[...], we_ref[...], preferred_element_type=F32) + be_ref[...])
    both = jnp.dot(hidden.astype(BF16), wide_ref[...], preferred_element_type=F32) + bias_ref[...]
    feat_ref[...] = both[:, :channels].astype(BF16).reshape(feat_ref.shape)
    group = lanes((size, channels))
    for k in range(per):
        b = step * per + k
        t, n = next_slot(tile_ref, count_ref, b)
        odd = lax.rem(n, 2)
        at = pl.ds(pl.multiple_of(n // 2 * size, size), size)
        straight = both[k * size : (k + 1) * size, :channels]
        turned = both[k * size : (k + 1) * size, channels:]
        keep = group == odd
        low = jnp.where(keep, jnp.where(odd == 0, straight, turned), 0.0).astype(BF16)
        high = jnp.where(keep, jnp.where(odd == 0, turned, straight), 0.0).astype(BF16)
        send0_ref[t, at, :] += low
        send1_ref[t, at, :] += high
        first = t * meta_rows + n * META
        obs = pl.ds(pl.multiple_of(b * size, size), size)
        meta_ref[pl.ds(first, 2), :] = offset_ref[:, obs].astype(F32)
        meta_ref[pl.ds(first + 2, 1), :] = cells_ref[0:1, obs].astype(F32)
        meta_ref[pl.ds(first + 3, 1), :] = jnp.full((1, size), patch_ref[b], jnp.int32).astype(F32)

    @pl.when(step == pl.num_programs(0) - 1)
    def _():
        base = send1_ref.shape[1]
        extra = send0_ref.shape[1] - base - meta_rows
        for t in range(tiles):
            rows = meta_ref[t * meta_rows : (t + 1) * meta_rows, :]
            if extra:
                rows = jnp.concatenate([rows, jnp.zeros((extra, size), F32)], axis=0)
            send0_ref[t, base:, :] = rows.astype(BF16)


def factors(meta, normal):
    off_row, off_col, corner = meta[0:1, :], meta[1:2, :], meta[2:3, :]
    first_row = jnp.floor(corner * (1.0 / PW))
    first_col = corner - first_row * PW

    def factor(count, start, off):
        at = lax.broadcasted_iota(jnp.int32, (count, meta.shape[1]), 0).astype(F32) - start
        delta = at - 1.5 - off
        value = jnp.exp(delta * delta * -0.5)
        return jnp.where((at >= 0.0) & (at < SIDE), value, 0.0)

    def total(off):
        at = lax.broadcasted_iota(jnp.int32, (SIDE, meta.shape[1]), 0).astype(F32)
        delta = at - 1.5 - off
        return jnp.sum(jnp.exp(delta * delta * -0.5), axis=0, keepdims=True)

    rows, cols = factor(PH, first_row, off_row), factor(PW, first_col, off_col)
    if normal:
        rows = rows / (total(off_row) * total(off_col))
    return rows, cols


def outer(rows, cols):
    return (rows[:, None, :] * cols[None, :, :]).reshape(PH * PW, rows.shape[1])


def place(patch):
    row, col = patch // ACROSS, lax.rem(patch, ACROSS)
    halves = ACROSS // 2
    return (
        pl.ds(pl.multiple_of(row * PH, PH), PH),
        pl.ds(pl.multiple_of(lax.rem(col, halves) * PW, PW), PW),
        col // halves,
    )


def add_slot(acc_ref, matrix, packed, turned, odd, patch):
    at_row, at_col, half = place(patch)
    keep = lanes((1, packed.shape[1])) == half
    values = jnp.where(half == odd, packed, turned) * jnp.where(keep, 1.0, 0.0).astype(BF16)
    result = jnp.dot(matrix, values, preferred_element_type=F32)
    acc_ref[at_row, at_col, :] += result.reshape(PH, PW, result.shape[1])


def write_stripes(ring_ref, acc_ref, outs):
    for k, out_ref in enumerate(outs):
        z = ring_ref[k]
        stripe = acc_ref[pl.ds(z * SR, SR)].astype(BF16)
        out_ref[0 : SR * TC // 2, :] = stripe.reshape(SR * TC // 2, stripe.shape[2])


def spread0_kernel(orbits, most, ring_ref, got_ref, *refs):
    outs, (matrix_ref, patch_ref, acc_ref, dens_ref) = refs[:orbits], refs[orbits:]
    t = pl.program_id(0)
    size = got_ref.shape[2]

    @pl.when(t == 0)
    def _():
        acc_ref[...] = jnp.zeros(acc_ref.shape, F32)
        dens_ref[...] = jnp.zeros(dens_ref.shape, F32)

    base = most // 2 * size
    metas = got_ref[0, base:, :].astype(F32)
    patches = [jnp.max(metas[n * META + 3 : n * META + 4, :]).astype(jnp.int32) for n in range(most)]
    for pair in range(most // 2):
        packed = got_ref[0, pair * size : (pair + 1) * size, :]
        turned = swap(packed)
        for odd in range(2):
            n = pair * 2 + odd
            patch = patches[n]
            patch_ref[t * most + n] = patch
            rows, cols = factors(metas[n * META : (n + 1) * META], False)
            matrix = outer(rows, cols).astype(BF16)
            matrix_ref[n] = matrix
            add_slot(acc_ref, matrix, packed, turned, odd, patch)
            dens_ref[patch] += lax.dot_general(
                rows.astype(BF16), cols.astype(BF16), (((1,), (1,)), ((), ())), preferred_element_type=F32
            )

    @pl.when(t == pl.num_programs(0) - 1)
    def _():
        write_stripes(ring_ref, acc_ref, outs)
        for k, out_ref in enumerate(outs):
            bands = []
            for band in range(SR // PH):
                first = (ring_ref[k] * (SR // PH) + band) * ACROSS
                bands.append(jnp.concatenate([dens_ref[first + c] for c in range(ACROSS)], axis=1))
            out_ref[SR * TC // 2 :, :] = jnp.concatenate(bands, axis=0).astype(BF16)


def spread1_kernel(orbits, most, ring_ref, patch_ref, matrix_ref, got_ref, *refs):
    outs, (acc_ref,) = refs[:orbits], refs[orbits:]
    t = pl.program_id(0)
    size = got_ref.shape[2]

    @pl.when(t == 0)
    def _():
        acc_ref[...] = jnp.zeros(acc_ref.shape, F32)

    for pair in range(most // 2):
        packed = got_ref[0, pair * size : (pair + 1) * size, :]
        turned = swap(packed)
        for odd in range(2):
            n = pair * 2 + odd
            add_slot(acc_ref, matrix_ref[n], packed, turned, odd, patch_ref[t * most + n])

    @pl.when(t == pl.num_programs(0) - 1)
    def _():
        write_stripes(ring_ref, acc_ref, outs)


def weights_kernel(most, meta_ref, out_ref):
    metas = meta_ref[0].astype(F32)
    for n in range(most):
        rows, cols = factors(metas[n * META : (n + 1) * META], True)
        out_ref[n] = outer(rows, cols).T.astype(BF16)


def grid_kernel(own0_ref, sum0_ref, own1_ref, sum1_ref, weight_ref, out_ref):
    half = TC // 2
    channels = out_ref.shape[2]
    tail = slice(SR * half, SR * half + SR)
    density = (own0_ref[tail, :].astype(F32) + sum0_ref[tail, :].astype(F32)).T
    low = lanes((half, channels)) == 0
    for i in range(SR):
        at = slice(i * half, (i + 1) * half)
        a = own0_ref[at, :].astype(F32) + sum0_ref[at, :].astype(F32)
        b = own1_ref[at, :].astype(F32) + sum1_ref[at, :].astype(F32)
        spread = jnp.concatenate([jnp.where(low, a, swap(b)), jnp.where(low, swap(a), b)], axis=0)
        d = jnp.broadcast_to(density[:, i : i + 1], (TC, channels))
        out_ref[i] = (spread / jnp.maximum(d, 1.0) + weight_ref[...] * (d / (1.0 + d))).astype(BF16)


def conv_kernel(
    edge_ref, x_ref, up_ref, down_ref, left_ref, right_ref, w1_ref, b1_ref, w2_ref, b2_ref,
    out_ref, out0_ref, out1_ref, wide_ref, x16_ref, first_ref, wc1_ref, wc2_ref,
):
    channels = out_ref.shape[2]
    width = x16_ref.shape[1]
    half = TC // 2
    for a in range(3):
        for b in range(3):
            at = (slice(a * channels, (a + 1) * channels), slice(b * channels, (b + 1) * channels))
            wc1_ref[at] = w1_ref[a, b]
            wc2_ref[at] = w2_ref[a, b]
    body = slice(PAD, PAD + TC)
    wide_ref[...] = jnp.zeros(wide_ref.shape, F32)
    wide_ref[0:2, body] = up_ref[...].astype(F32)
    wide_ref[2 : 2 + SR, body] = x_ref[...].astype(F32)
    wide_ref[2 + SR :, body] = down_ref[...].astype(F32)
    wide_ref[:, PAD - 2 : PAD] = left_ref[...].astype(F32)
    wide_ref[:, PAD + TC : PAD + TC + 2] = right_ref[...].astype(F32)
    x16_ref[...] = wide_ref[...].astype(BF16)

    def taps(source, i, weights):
        rows = jnp.concatenate([source[i], source[i + 1], source[i + 2]], axis=1)
        all_taps = jnp.dot(rows, weights[...], preferred_element_type=F32)
        return (
            pltpu.roll(all_taps[:, :channels], 1, 0)
            + all_taps[:, channels : 2 * channels]
            + pltpu.roll(all_taps[:, 2 * channels :], width - 1, 0)
        )

    col = lax.broadcasted_iota(jnp.int32, (width, channels), 0)
    inside = (col >= PAD - edge_ref[2]) & (col < PAD + TC + edge_ref[3])

    def first_row(i, unused):
        value = silu(taps(x16_ref, i, wc1_ref) + b1_ref[...])
        low = jnp.where(edge_ref[0] == 1, 0, 1)
        high = jnp.where(edge_ref[1] == 1, SR + 2, SR + 1)
        keep = inside & (i >= low) & (i < high)
        first_ref[i] = jnp.where(keep, value, 0.0).astype(BF16)
        return unused

    lax.fori_loop(0, SR + 2, first_row, 0)
    group = lanes((half, channels)) == 0

    def second_row(i, unused):
        value = taps(first_ref, i, wc2_ref) + b2_ref[...]
        value = value[PAD : PAD + TC] + x_ref[i].astype(F32)
        left, right = value[:half], value[half:]
        out_ref[i] = value.astype(BF16)
        out0_ref[i] = jnp.where(group, left, swap(right)).astype(BF16)
        out1_ref[i] = jnp.where(group, swap(left), right).astype(BF16)
        return unused

    lax.fori_loop(0, SR, second_row, 0)


def read_kernel(orbits, most, ring_ref, patch_ref, weights_ref, *refs):
    pieces, (out_ref, grid_ref) = refs[:orbits], refs[orbits:]
    t = pl.program_id(0)
    size = out_ref.shape[2]

    @pl.when(t == 0)
    def _():
        for k, piece_ref in enumerate(pieces):
            at = pl.ds(ring_ref[k] * SR, SR)
            grid_ref[0, at] = piece_ref[...]
            grid_ref[1, at] = swap(piece_ref[...])

    low = lanes((size, out_ref.shape[2])) == 0
    for pair in range(most // 2):
        sums = []
        for odd in range(2):
            n = pair * 2 + odd
            at_row, at_col, half = place(patch_ref[t * most + n])
            turn = jnp.where(half == odd, 0, 1)
            values = grid_ref[turn, at_row, at_col, :].reshape(PH * PW, grid_ref.shape[3])
            sums.append(jnp.dot(weights_ref[n], values, preferred_element_type=F32))
        out_ref[0, pair * size : (pair + 1) * size, :] = jnp.where(low, sums[0], sums[1]).astype(BF16)


def final_kernel(tile_ref, feat_ref, got0_ref, got1_ref, out_ref, count_ref):
    step = pl.program_id(0)
    per, size, channels = feat_ref.shape

    @pl.when(step == 0)
    def _():
        clear(count_ref)

    low = lanes((size, channels)) == 0
    for k in range(per):
        t, n = next_slot(tile_ref, count_ref, step * per + k)
        odd = lax.rem(n, 2)
        at = pl.ds(pl.multiple_of(n // 2 * size, size), size)
        a, b = got0_ref[t, at, :].astype(F32), got1_ref[t, at, :].astype(F32)
        turn = swap(jnp.where(odd == 0, b, a))
        mine = jnp.where(odd == 0, jnp.where(low, a, turn), jnp.where(low, turn, b))
        out_ref[k] = (feat_ref[k].astype(F32) + mine).astype(BF16)


def shifts(axis):
    size = lax.axis_size(axis)
    up = [(i, i + 1) for i in range(size - 1)]
    return up, [(j, i) for i, j in up]


def halo(x, axis, dim, width):
    up, down = shifts(axis)
    length = x.shape[dim]
    before = lax.ppermute(lax.slice_in_dim(x, length - width, length, axis=dim), axis, up)
    after = lax.ppermute(lax.slice_in_dim(x, 0, width, axis=dim), axis, down)
    return before, after


def turn(x, way):
    size = lax.axis_size("orbits")
    return lax.ppermute(x, "orbits", [(i, (i + way) % size) for i in range(size)])


def ring_sum(stripes, way):
    total = None
    for stripe in stripes[:-1]:
        total = turn(stripe if total is None else stripe + total, way)
    return total


def ring_gather(x, way):
    pieces = [x]
    for _ in range(lax.axis_size("orbits") - 1):
        pieces.append(turn(pieces[-1], way))
    return pieces


def local(
    obs_feat, obs_offset, obs_cells, block_tile, block_patch, w_embed, b_embed, w_proj, b_proj,
    density_weight, w_first, b_first, w_second, b_second,
):
    channels = obs_feat.shape[1]
    blocks = block_tile.shape[0]
    size = obs_feat.shape[0] // blocks
    plane = ("rows", "cols")
    tiles = lax.axis_size(plane)
    orbits = lax.axis_size("orbits")
    most = max(2, 2 * blocks // tiles)
    slots = tiles * most
    height = orbits * SR
    patches = height // PH * ACROSS
    half = TC // 2
    pairs = most // 2 * size
    meta_rows = max(16, most * META)
    per = 4
    counts = pltpu.SMEM((tiles,), jnp.int32)
    shape = jax.ShapeDtypeStruct
    bias = lambda b: b.reshape(1, channels)
    me = lax.axis_index("orbits")
    order = jnp.arange(orbits, dtype=jnp.int32)
    exchange = lambda x: lax.all_to_all(x, plane, split_axis=0, concat_axis=0, tiled=True)

    features, send0, send1 = call(
        embed_kernel,
        blocks // per,
        [SMEM, SMEM, whole(obs_offset.shape), whole((8, obs_cells.shape[1])), part((per * size, channels))]
        + [whole((channels, channels)), whole((1, channels))] * 2,
        [
            part((per, size, channels)),
            whole((tiles, pairs + meta_rows, channels)),
            whole((tiles, pairs, channels)),
        ],
        (
            shape((blocks, size, channels), BF16),
            shape((tiles, pairs + meta_rows, channels), BF16),
            shape((tiles, pairs, channels), BF16),
        ),
        [
            counts,
            pltpu.VMEM((slots * META, size), F32),
            pltpu.VMEM((channels, 2 * channels), BF16),
            pltpu.VMEM((1, 2 * channels), F32),
        ],
        6 * obs_feat.size * channels,
        8 * obs_feat.size,
        block_tile, block_patch, obs_offset, obs_cells, obs_feat, w_embed, bias(b_embed), w_proj, bias(b_proj),
    )
    got0 = exchange(send0)
    got1 = exchange(send1)

    flops = 2 * slots * size * channels * PH * PW
    stripe_shape = shape((SR * half, channels), BF16)
    dense_shape = shape((SR * half + SR, channels), BF16)
    acc = pltpu.VMEM((height, half, channels), F32)
    *out0, matrices, patch_of = call(
        functools.partial(spread0_kernel, orbits, most),
        tiles,
        [SMEM, part((1, pairs + meta_rows, channels))],
        [whole(dense_shape.shape)] * orbits + [part((most, PH * PW, size)), SMEM],
        [dense_shape] * orbits + [shape((slots, PH * PW, size), BF16), shape((slots,), jnp.int32)],
        [acc, pltpu.VMEM((patches, PH, PW), F32)],
        flops,
        12 * slots * size * channels,
        (me - 1 - order) % orbits, got0,
    )
    sum0 = ring_sum(out0, 1)
    out1 = call(
        functools.partial(spread1_kernel, orbits, most),
        tiles,
        [SMEM, SMEM, part((most, PH * PW, size)), part((1, pairs, channels))],
        [whole(stripe_shape.shape)] * orbits,
        [stripe_shape] * orbits,
        [acc],
        flops,
        8 * slots * size * channels,
        (me + 1 + order) % orbits, patch_of, matrices, got1,
    )
    sum1 = ring_sum(out1, -1)
    weights = call(
        functools.partial(weights_kernel, most),
        tiles,
        [part((1, meta_rows, channels), pairs // meta_rows, 0)],
        part((most, size, PH * PW)),
        shape((slots, size, PH * PW), BF16),
        [],
        flops,
        4 * slots * size * channels,
        got0,
    )
    grid_in = call(
        grid_kernel,
        1,
        [whole(dense_shape.shape)] * 2 + [whole(stripe_shape.shape)] * 2 + [whole((1, channels))],
        whole((SR, TC, channels)),
        shape((SR, TC, channels), BF16),
        [],
        10000000,
        8 * SR * TC * channels,
        out0[-1], sum0, out1[-1], sum1, bias(density_weight),
    )

    stripe = ("orbits", "rows")
    above, below = halo(grid_in, stripe, 0, 2)
    extended = jnp.concatenate(
        [
            jnp.concatenate([above[:, c], grid_in[:, c], below[:, c]], axis=0)
            for c in (slice(0, 2), slice(TC - 2, TC))
        ],
        axis=1,
    )
    left, right = halo(extended, "cols", 1, 2)
    at_row, at_col = lax.axis_index(stripe), lax.axis_index("cols")
    edges = jnp.stack(
        [
            at_row > 0,
            at_row < lax.axis_size(stripe) - 1,
            at_col > 0,
            at_col < lax.axis_size("cols") - 1,
        ]
    ).astype(jnp.int32)
    width = TC + 2 * PAD
    weight_spec = whole(w_first.shape)
    grid_out, half0, half1 = call(
        conv_kernel,
        1,
        [SMEM]
        + [whole(a.shape) for a in (grid_in, above, below, left, right)]
        + [weight_spec, whole((1, channels))] * 2,
        [whole((SR, TC, channels)), whole((SR, half, channels)), whole((SR, half, channels))],
        [shape((SR, TC, channels), BF16)] + [shape((SR, half, channels), BF16)] * 2,
        [
            pltpu.VMEM((SR + 4, width, channels), F32),
            pltpu.VMEM((SR + 4, width, channels), BF16),
            pltpu.VMEM((SR + 2, width, channels), BF16),
            pltpu.VMEM((3 * channels, 3 * channels), BF16),
            pltpu.VMEM((3 * channels, 3 * channels), BF16),
        ],
        4 * 9 * SR * TC * channels * channels,
        8 * grid_in.size,
        edges, grid_in, above, below, left, right, w_first, bias(b_first), w_second, bias(b_second),
    )

    def readings(pieces, ring):
        return call(
            functools.partial(read_kernel, orbits, most),
            tiles,
            [SMEM, SMEM, part((most, size, PH * PW))] + [whole((SR, half, channels))] * orbits,
            part((1, pairs, channels)),
            shape((tiles, pairs, channels), BF16),
            [pltpu.VMEM((2, height, half, channels), BF16)],
            flops,
            8 * slots * size * channels,
            ring, patch_of, weights, *pieces,
        )

    back0 = exchange(readings(ring_gather(half0, 1), (me - order) % orbits))
    back1 = exchange(readings(ring_gather(half1, -1), (me + order) % orbits))
    block = part((per, size, channels))
    obs_out = call(
        final_kernel,
        blocks // per,
        [SMEM, block] + [whole((tiles, pairs, channels))] * 2,
        block,
        shape((blocks, size, channels), BF16),
        [counts],
        1000000,
        8 * obs_feat.size,
        block_tile, features, back0, back1,
    )
    return obs_out.reshape(obs_feat.shape), grid_out


def solution(mesh):
    spread_out = ("orbits", "rows", "cols")
    in_specs = (
        P(spread_out, None),
        P(None, spread_out),
        P(None, spread_out),
        P(spread_out),
        P(spread_out),
    ) + (P(),) * 9
    out_specs = (P(spread_out, None), P(("orbits", "rows"), "cols", None))
    return jax.shard_map(local, mesh=mesh, in_specs=in_specs, out_specs=out_specs, check_vma=False)
```

time: 234 us -> 219 us (0.936)
  waiting for transfers between devices: 124 us -> 70.4 us
  starting transfers between devices: 17.9 us -> 42.5 us
  Pallas kernels: 35.2 us -> 49.3 us
  between operations: 14.2 us -> 0.9 us
  blocking collectives: 29.4 us -> 39 us
    ppermute x0 -> x12, waiting for transfers between devices: none -> 60.2 us  [turn(): lax.ppermute(x, 'orbits', [(i, (i + way) % size) for i in range(size)])]
    all_gather x1 -> x0, waiting for transfers between devices: 49.3 us -> none  [local(): whole = lax.all_gather(grid_out, 'orbits', axis=0, tiled=True)]
    reduce_scatter x1 -> x0, waiting for transfers between devices: 44.7 us -> none  [local(): lax.psum_scatter(partial.reshape(orbits * (SR * TC + SR), channels), 'orb...]
    ppermute x0 -> x12, starting transfers between devices: none -> 27.2 us  [turn(): lax.ppermute(x, 'orbits', [(i, (i + way) % size) for i in range(size)])]
    all_to_all x2, waiting for transfers between devices: 24.4 us -> 4.66 us  [local(): lax.all_to_all(x, plane, split_axis=0, concat_axis=0, tiled=True)]
    pallas_call x7 -> x9, Pallas kernels: 35.2 us -> 49.3 us  [call(): pl.pallas_call(kernel, grid=(grid,), in_specs=in_specs, out_specs=out_spe...]
    all_to_all x1 -> x2, blocking collectives: 29.4 us -> 39 us  [local(): lax.all_to_all(x, plane, split_axis=0, concat_axis=0, tiled=True)]
    unnamed x38 -> x46, local copies, waits for them, and re-layouts: 11.7 us -> 13.3 us
  transfers between devices with their start and end apart: 8 -> 18, of which waited for: 6 -> 14; matrix products, arithmetic and copies ran while one was open for 1% -> 1% of each run, Pallas kernels for 2% -> 10%
where the time goes in v2:
time: 219 us; the launch traced here: 217 us
  waiting for transfers between devices  70.4 us (32%)
  Pallas kernels  49.3 us (23%)
  starting transfers between devices  42.5 us (19%)
  blocking collectives  39 us (18%)
  local copies, waits for them, and re-layouts  13.3 us (6%)
    ppermute x12, waiting for transfers between devices, turn(): lax.ppermute(x, 'orbits', [(i, (i + way) % size) for i in range(size)])  60.2 us
    pallas_call x9, Pallas kernels, call(): pl.pallas_call(kernel, grid=(grid,), in_specs=in_specs, out_specs=out_spe...  49.3 us
    all_to_all x2, blocking collectives, local(): lax.all_to_all(x, plane, split_axis=0, concat_axis=0, tiled=True)  39 us
    ppermute x12, starting transfers between devices, turn(): lax.ppermute(x, 'orbits', [(i, (i + way) % size) for i in range(size)])  27.2 us
    unnamed x46, local copies, waits for them, and re-layouts  13.3 us
    all_to_all x2, starting transfers between devices, local(): lax.all_to_all(x, plane, split_axis=0, concat_axis=0, tiled=True)  7.12 us
    ppermute x2, starting transfers between devices, halo(): lax.ppermute(lax.slice_in_dim(x, length - width, length, axis=dim), axis,...  5.54 us
    all_to_all x2, waiting for transfers between devices, local(): lax.all_to_all(x, plane, split_axis=0, concat_axis=0, tiled=True)  4.66 us
  transfers between devices with their start and end apart: 18, of which 14 were waited for; matrix products, arithmetic and copies ran while one was open for 1% of the time, Pallas kernels for 10%

profile of v2, /device:TPU:0, one launch (start us, length us, event | category | flops | bytes accessed | tf_op | source)
XLA Modules:
  0.0 217.5 jit_solution(3909121522008339914)
XLA Ops:
  1.3 1.2 copy-done.11
  2.5 0.9 copy-done.14
  3.5 0.8 copy-done.15
  4.2 0.8 copy-done.16
  7.7 4.2 %shard_map.149 = (bf16[32,128,128]{2,1,0:T(8,128)(2,1)S(1)}, bf16[8,544,128]{2,1,0:T(8,128)(2,1)S(1)}, bf16[8,512,128]{2,1,0:T(8,128)(2,1)S(1)}) custom-call(s32[32]{0:T(128)S(1)} %copy-done.9, s32[32]{0:T(128)S(1)} %copy-done.18, bf16[2,4096]{1,0:T(2,128)(2,1)S(1)} %copy-done.17, s32[16,4096]{1,0:T(8,128)S(1)} %copy-done.14, ...), custom_call_target="tpu_custom_call" | custom-call | flops 402653184 | bytes 4194304 | tf_op jit(solution)/shard_map/pallas_call | solution.py:37
  11.9 21.0 %all_to_all.20.got_ref.meta_ref = bf16[8,544,128]{2,1,0:T(8,128)(2,1)S(1)} all-to-all(bf16[8,544,128]{2,1,0:T(8,128)(2,1)S(1)} %get-tuple-element.19), channel_id=1, replica_groups=mesh['orbits'=4,'rows'=2,'cols'=4] {'rows','cols'}, dimensions={0} | all-to-all | bytes 2228224 | tf_op jit(solution)/shard_map/all_to_all | solution.py:417
  32.9 3.6 %all-to-all-start.1 = ((bf16[8,512,128]{2,1,0:T(8,128)(2,1)}), bf16[8,512,128]{2,1,0:T(8,128)(2,1)S(1)}, u32[]{:S(2)}, u32[]{:S(2)}) async-start(bf16[8,512,128]{2,1,0:T(8,128)(2,1)} %copy-done.1), calls=%async_computation.1 | async-start | bytes 2097152 | tf_op jit(solution)/shard_map/all_to_all | solution.py:417
  36.5 6.7 %shard_map.150 = (bf16[1040,128]{1,0:T(8,128)(2,1)}, bf16[1040,128]{1,0:T(8,128)(2,1)S(1)}, bf16[1040,128]{1,0:T(8,128)(2,1)S(1)}, bf16[1040,128]{1,0:T(8,128)(2...) custom-call(s32[4]{0:T(128)S(1)} %and_select_fusion.2.ring_ref, bf16[8,544,128]{2,1,0:T(8,128)(2,1)S(1)} %all_to_all.20.got_ref.meta_ref), custom_call_target="tpu_custom_call" | custom-call | flops 536870912 | bytes 12582912 | tf_op jit(solution)/shard_map/pallas_call | solution.py:37
  44.6 1.6 collective-permute-start
  46.2 4.7 %all-to-all-done.1.got_ref = bf16[8,512,128]{2,1,0:T(8,128)(2,1)S(1)} async-done(((bf16[8,512,128]{2,1,0:T(8,128)(2,1)}), bf16[8,512,128]{2,1,0:T(8,128)(2,1)S(1)}, u32[]{:S(2)}, u32[]{:S(2)}) %all-to-all-start.1) | async-done | bytes 1048608 | tf_op jit(solution)/shard_map/all_to_all | solution.py:417
  50.9 6.6 %shard_map.152 = (bf16[1024,128]{1,0:T(8,128)(2,1)S(1)}, bf16[1024,128]{1,0:T(8,128)(2,1)S(1)}, bf16[1024,128]{1,0:T(8,128)(2,1)S(1)}, bf16[1024,128]{1,0:T(8,128)(2,1)S(1)}) custom-call(s32[4]{0:T(128)S(1)} %and_select_fusion.1.ring_ref, s32[64]{0:T(128)S(1)} %get-tuple-element.20.patch_ref, bf16[64,256,128]{2,1,0:T(8,128)(2,1)} %get-tuple-element.25.matrix_ref, ...), custom_call_target="tpu_custom_call" | custom-call | flops 536870912 | bytes 8388608 | tf_op jit(solution)/shard_map/pallas_call | solution.py:37
  57.5 3.7 %collective-permute-start.3 = (bf16[1024,128]{1,0:T(8,128)(2,1)S(1)}, bf16[1024,128]{1,0:T(8,128)(2,1)S(1)}, u32[]{:S(2)}, u32[]{:S(2)}) collective-permute-start(bf16[1024,128]{1,0:T(8,128)(2,1)S(1)} %get-tuple-element.30), channel_id=1, source_target_pairs={{0,24},{8,0},{16,8},{24,16},{1,25},{9,1},{17,9},{25,17},{2,26},{10... | collective-permute-start | bytes 786440 | tf_op jit(solution)/shard_map/ppermute | solution.py:377
  61.1 1.0 add.50
  62.2 5.6 %collective-permute-done.3 = bf16[1024,128]{1,0:T(8,128)(2,1)S(1)} collective-permute-done((bf16[1024,128]{1,0:T(8,128)(2,1)S(1)}, bf16[1024,128]{1,0:T(8,128)(2,1)S(1)}, u32[]{:S(2)}, u32[]{:S(2)}) %collective-permute-start.3) | collective-permute-done | bytes 262176 | tf_op jit(solution)/shard_map/ppermute | solution.py:377
  67.9 4.3 %collective-permute-start.4 = (bf16[1024,128]{1,0:T(8,128)(2,1)S(1)}, bf16[1024,128]{1,0:T(8,128)(2,1)S(1)}, u32[]{:S(2)}, u32[]{:S(2)}) collective-permute-start(bf16[1024,128]{1,0:T(8,128)(2,1)S(1)} %add.56), channel_id=1, source_target_pairs={{0,24},{8,0},{16,8},{24,16},{1,25},{9,1},{17,9},{25,17},{2,26},{10... | collective-permute-start | bytes 786440 | tf_op jit(solution)/shard_map/ppermute | solution.py:377
  72.3 2.2 %collective-permute-done.1 = bf16[1040,128]{1,0:T(8,128)(2,1)S(1)} collective-permute-done((bf16[1040,128]{1,0:T(8,128)(2,1)S(1)}, bf16[1040,128]{1,0:T(8,128)(2,1)S(1)}, u32[]{:S(2)}, u32[]{:S(2)}) %collective-permute-start.1) | collective-permute-done | bytes 266272 | tf_op jit(solution)/shard_map/ppermute | solution.py:377
  74.5 0.8 add.51
  75.3 1.5 collective-permute-start.2
  76.8 2.7 %collective-permute-done.4 = bf16[1024,128]{1,0:T(8,128)(2,1)S(1)} collective-permute-done((bf16[1024,128]{1,0:T(8,128)(2,1)S(1)}, bf16[1024,128]{1,0:T(8,128)(2,1)S(1)}, u32[]{:S(2)}, u32[]{:S(2)}) %collective-permute-start.4) | collective-permute-done | bytes 262176 | tf_op jit(solution)/shard_map/ppermute | solution.py:377
  79.7 4.0 %collective-permute-start.5 = (bf16[1024,128]{1,0:T(8,128)(2,1)S(1)}, bf16[1024,128]{1,0:T(8,128)(2,1)S(1)}, u32[]{:S(2)}, u32[]{:S(2)}) collective-permute-start(bf16[1024,128]{1,0:T(8,128)(2,1)S(1)} %add.57), channel_id=1, source_target_pairs={{0,24},{8,0},{16,8},{24,16},{1,25},{9,1},{17,9},{25,17},{2,26},{10... | collective-permute-start | bytes 786440 | tf_op jit(solution)/shard_map/ppermute | solution.py:377
  83.6 6.6 %collective-permute-done.5.sum1_ref = bf16[1024,128]{1,0:T(8,128)(2,1)S(1)} collective-permute-done((bf16[1024,128]{1,0:T(8,128)(2,1)S(1)}, bf16[1024,128]{1,0:T(8,128)(2,1)S(1)}, u32[]{:S(2)}, u32[]{:S(2)}) %collective-permute-start.5) | collective-permute-done | bytes 262176 | tf_op jit(solution)/shard_map/ppermute | solution.py:377
  90.3 0.9 copy-done.5
  91.2 0.9 copy-done.7
  92.2 0.8 shard_map.153.x_ref
  92.9 2.5 %collective-permute-start.6 = (bf16[2,128,128]{2,1,0:T(8,128)(2,1)S(1)}, bf16[2,128,128]{2,1,0:T(8,128)(2,1)S(1)}, u32[]{:S(2)}, u32[]{:S(2)}) collective-permute-start(bf16[2,128,128]{2,1,0:T(8,128)(2,1)S(1)} %get-tuple-element.37), channel_id=1, source_target_pairs={{0,4},{4,8},{8,12},{12,16},{16,20},{20,24},{24,28},{1,5},{5,9},{9,... | collective-permute-start | bytes 196616 | tf_op jit(solution)/shard_map/ppermute | solution.py:370
  95.5 1.3 collective-permute-start.7
  97.4 4.3 %collective-permute-done.7.down_ref = bf16[2,128,128]{2,1,0:T(8,128)(2,1)S(1)} collective-permute-done((bf16[2,128,128]{2,1,0:T(8,128)(2,1)S(1)}, bf16[2,128,128]{2,1,0:T(8,128)(2,1)S(1)}, u32[]{:S(2)}, u32[]{:S(2)}) %collective-permute-start.7) | collective-permute-done | bytes 65568 | tf_op jit(solution)/shard_map/ppermute | solution.py:371
  101.7 1.3 collective-permute-start.9
  103.0 3.0 %collective-permute-start.8 = (bf16[20,2,128]{2,1,0:T(2,128)(2,1)S(1)}, bf16[20,2,128]{2,1,0:T(2,128)(2,1)S(1)}, u32[]{:S(2)}, u32[]{:S(2)}) collective-permute-start(bf16[20,2,128]{2,1,0:T(2,128)(2,1)S(1)} %pad_maximum_fusion), channel_id=1, source_target_pairs={{0,1},{1,2},{2,3},{4,5},{5,6},{6,7},{8,9},{9,10},{10,11},{12,13},{... | collective-permute-start | bytes 30728 | tf_op jit(solution)/shard_map/ppermute | solution.py:370
  106.1 0.7 collective-permute-done.8.left_ref
  106.9 1.0 copy-done.13
  107.8 11.0 %shard_map.154 = (bf16[16,128,128]{2,1,0:T(8,128)(2,1)}, bf16[16,64,128]{2,1,0:T(8,128)(2,1)S(1)}, bf16[16,64,128]{2,1,0:T(8,128)(2,1)S(1)}) custom-call(s32[4]{0:T(128)S(1)} %add_convert_fusion.edge_ref, bf16[16,128,128]{2,1,0:T(8,128)(2,1)S(1)} %shard_map.153.x_ref, bf16[2,128,128]{2,1,0:T(8,128)(2,1)S(1)} %collective-permute-done.6.up_ref, ...), custom_call_target="tpu_custom_call" | custom-call | flops 1207959552 | bytes 2097152 | tf_op jit(solution)/shard_map/pallas_call | solution.py:37
  118.8 3.4 %collective-permute-start.13 = (bf16[16,64,128]{2,1,0:T(8,128)(2,1)S(1)}, bf16[16,64,128]{2,1,0:T(8,128)(2,1)S(1)}, u32[]{:S(2)}, u32[]{:S(2)}) collective-permute-start(bf16[16,64,128]{2,1,0:T(8,128)(2,1)S(1)} %get-tuple-element.32.refs_0_), channel_id=1, source_target_pairs={{0,24},{8,0},{16,8},{24,16},{1,25},{9,1},{17,9},{25,17},{2,26},{10... | collective-permute-start | bytes 786440 | tf_op jit(solution)/shard_map/ppermute | solution.py:377
  122.3 6.7 %collective-permute-done.13.refs_1_ = bf16[16,64,128]{2,1,0:T(8,128)(2,1)S(1)} collective-permute-done((bf16[16,64,128]{2,1,0:T(8,128)(2,1)S(1)}, bf16[16,64,128]{2,1,0:T(8,128)(2,1)S(1)}, u32[]{:S(2)}, u32[]{:S(2)}) %collective-permute-start.13) | collective-permute-done | bytes 262176 | tf_op jit(solution)/shard_map/ppermute | solution.py:377
  128.9 4.3 %collective-permute-start.14 = (bf16[16,64,128]{2,1,0:T(8,128)(2,1)S(1)}, bf16[16,64,128]{2,1,0:T(8,128)(2,1)S(1)}, u32[]{:S(2)}, u32[]{:S(2)}) collective-permute-start(bf16[16,64,128]{2,1,0:T(8,128)(2,1)S(1)} %collective-permute-done.13.refs_1_), channel_id=1, source_target_pairs={{0,24},{8,0},{16,8},{24,16},{1,25},{9,1},{17,9},{25,17},{2,26},{10... | collective-permute-start | bytes 786440 | tf_op jit(solution)/shard_map/ppermute | solution.py:377
  133.2 5.8 %collective-permute-done.14.refs_2_ = bf16[16,64,128]{2,1,0:T(8,128)(2,1)S(1)} collective-permute-done((bf16[16,64,128]{2,1,0:T(8,128)(2,1)S(1)}, bf16[16,64,128]{2,1,0:T(8,128)(2,1)S(1)}, u32[]{:S(2)}, u32[]{:S(2)}) %collective-permute-start.14) | collective-permute-done | bytes 262176 | tf_op jit(solution)/shard_map/ppermute | solution.py:377
  139.0 4.3 %collective-permute-start.15 = (bf16[16,64,128]{2,1,0:T(8,128)(2,1)S(1)}, bf16[16,64,128]{2,1,0:T(8,128)(2,1)S(1)}, u32[]{:S(2)}, u32[]{:S(2)}) collective-permute-start(bf16[16,64,128]{2,1,0:T(8,128)(2,1)S(1)} %collective-permute-done.14.refs_2_), channel_id=1, source_target_pairs={{0,24},{8,0},{16,8},{24,16},{1,25},{9,1},{17,9},{25,17},{2,26},{10... | collective-permute-start | bytes 786440 | tf_op jit(solution)/shard_map/ppermute | solution.py:377
  143.3 2.3 %shard_map.151.weights_ref = bf16[64,128,256]{2,1,0:T(8,128)(2,1)S(1)} custom-call(bf16[8,544,128]{2,1,0:T(8,128)(2,1)S(1)} %all_to_all.20.got_ref.meta_ref), custom_call_target="tpu_custom_call" | custom-call | flops 536870912 | bytes 4194304 | tf_op jit(solution)/shard_map/pallas_call | solution.py:37
  145.7 1.9 copy-done
  147.6 0.7 collective-permute-done.15.refs_3_
  148.3 7.4 %shard_map.156 = bf16[8,512,128]{2,1,0:T(8,128)(2,1)} custom-call(s32[4]{0:T(128)S(1)} %and_select_fusion.ring_ref, s32[64]{0:T(128)S(1)} %get-tuple-element.20.patch_ref, bf16[64,128,256]{2,1,0:T(8,128)(2,1)} %copy-done, bf16[16,64,128]{2,1,0:T(8,128)(2,1)S(1)} %get-tuple-element.32.refs_0_, bf16[16,64,128]{2,1,0:T(8,128)(2,1)S(1)} %collective-permute-done.13.refs_1_, ...), custom_call_target="tpu_custom_call" | custom-call | flops 536870912 | bytes 8388608 | tf_op jit(solution)/shard_map/pallas_call | solution.py:37
  155.7 3.6 %all-to-all-start.3 = ((bf16[8,512,128]{2,1,0:T(8,128)(2,1)}), bf16[8,512,128]{2,1,0:T(8,128)(2,1)S(1)}, u32[]{:S(2)}, u32[]{:S(2)}) async-start(bf16[8,512,128]{2,1,0:T(8,128)(2,1)} %shard_map.156), calls=%async_computation.3 | async-start | bytes 2097152 | tf_op jit(solution)/shard_map/all_to_all | solution.py:417
  159.3 11.1 %collective-permute-done.10.refs_1_ = bf16[16,64,128]{2,1,0:T(8,128)(2,1)S(1)} collective-permute-done((bf16[16,64,128]{2,1,0:T(8,128)(2,1)S(1)}, bf16[16,64,128]{2,1,0:T(8,128)(2,1)S(1)}, u32[]{:S(2)}, u32[]{:S(2)}) %collective-permute-start.10) | collective-permute-done | bytes 262176 | tf_op jit(solution)/shard_map/ppermute | solution.py:377
  170.4 9.8 %collective-permute-done.11.refs_2_ = bf16[16,64,128]{2,1,0:T(8,128)(2,1)S(1)} collective-permute-done((bf16[16,64,128]{2,1,0:T(8,128)(2,1)S(1)}, bf16[16,64,128]{2,1,0:T(8,128)(2,1)S(1)}, u32[]{:S(2)}, u32[]{:S(2)}) %collective-permute-start.11) | collective-permute-done | bytes 262176 | tf_op jit(solution)/shard_map/ppermute | solution.py:377
  180.2 8.9 %collective-permute-done.12.refs_3_ = bf16[16,64,128]{2,1,0:T(8,128)(2,1)S(1)} collective-permute-done((bf16[16,64,128]{2,1,0:T(8,128)(2,1)S(1)}, bf16[16,64,128]{2,1,0:T(8,128)(2,1)S(1)}, u32[]{:S(2)}, u32[]{:S(2)}) %collective-permute-start.12) | collective-permute-done | bytes 262176 | tf_op jit(solution)/shard_map/ppermute | solution.py:377
  189.1 6.3 %shard_map.155 = bf16[8,512,128]{2,1,0:T(8,128)(2,1)S(1)} custom-call(s32[4]{0:T(128)S(1)} %and_select_fusion.3.ring_ref, s32[64]{0:T(128)S(1)} %get-tuple-element.20.patch_ref, bf16[64,128,256]{2,1,0:T(8,128)(2,1)} %copy-done, bf16[16,64,128]{2,1,0:T(8,128)(2,1)S(1)} %get-tuple-element.31.refs_0_, bf16[16,64,128]{2,1,0:T(8,128)(2,1)S(1)} %collective-permute-done.10.refs_1_, ...), custom_call_target="tpu_custom_call" | custom-call | flops 536870912 | bytes 8388608 | tf_op jit(solution)/shard_map/pallas_call | solution.py:37
  195.5 18.0 %all_to_all.21.got0_ref = bf16[8,512,128]{2,1,0:T(8,128)(2,1)S(1)} all-to-all(bf16[8,512,128]{2,1,0:T(8,128)(2,1)S(1)} %shard_map.155), channel_id=1, replica_groups=mesh['orbits'=4,'rows'=2,'cols'=4] {'rows','cols'}, dimensions={0} | all-to-all | bytes 2097152 | tf_op jit(solution)/shard_map/all_to_all | solution.py:417
  213.5 4.0 %shard_map.157 = bf16[32,128,128]{2,1,0:T(8,128)(2,1)} custom-call(s32[32]{0:T(128)S(1)} %copy-done.10, bf16[32,128,128]{2,1,0:T(8,128)(2,1)S(1)} %get-tuple-element.18.feat_ref, bf16[8,512,128]{2,1,0:T(8,128)(2,1)S(1)} %all_to_all.21.got0_ref, bf16[8,512,128]{2,1,0:T(8,128)(2,1)S(1)} %all-to-all-done.3.got1_ref), custom_call_target="tpu_custom_call" | custom-call | flops 1000000 | bytes 4194304 | tf_op jit(solution)/shard_map/pallas_call | solution.py:37
  (60 shorter events, 5.8 us)
Async XLA Ops:
  0.6 0.7 copy-start.9
  1.3 1.2 copy-start.11
  2.5 0.9 copy-start.14
  3.5 0.8 copy-start.15
  4.2 0.8 copy-start.16
  5.0 0.7 copy-start.17
  5.7 0.7 copy-start.18
  6.4 0.7 copy-start.19
  7.0 0.7 copy-start.20
  11.9 21.1 %copy-start.1 = (bf16[8,512,128]{2,1,0:T(8,128)(2,1)}, bf16[8,512,128]{2,1,0:T(8,128)(2,1)S(1)}, u32[]{:S(2)}) copy-start(bf16[8,512,128]{2,1,0:T(8,128)(2,1)S(1)} %get-tuple-element.26) | copy-start | bytes 3145732
  32.9 17.9 %all-to-all-start.1 = ((bf16[8,512,128]{2,1,0:T(8,128)(2,1)}), bf16[8,512,128]{2,1,0:T(8,128)(2,1)S(1)}, u32[]{:S(2)}, u32[]{:S(2)}) async-start(bf16[8,512,128]{2,1,0:T(8,128)(2,1)} %copy-done.1), calls=%async_computation.1 | async-start | bytes 2097152 | tf_op jit(solution)/shard_map/all_to_all | solution.py:417
  43.2 0.7 copy-start.2
  43.9 0.7 copy-start.4
  44.6 16.5 %collective-permute-start = (bf16[1040,128]{1,0:T(8,128)(2,1)}, bf16[1040,128]{1,0:T(8,128)(2,1)}, u32[]{:S(2)}, u32[]{:S(2)}) collective-permute-start(bf16[1040,128]{1,0:T(8,128)(2,1)} %get-tuple-element.24), channel_id=1, source_target_pairs={{0,8},{8,16},{16,24},{24,0},{1,9},{9,17},{17,25},{25,1},{2,10},{10... | collective-permute-start | bytes 798728 | tf_op jit(solution)/shard_map/ppermute | solution.py:377
  50.9 10.3 %copy-start.3 = (bf16[1040,128]{1,0:T(8,128)(2,1)S(1)}, bf16[1040,128]{1,0:T(8,128)(2,1)}, u32[]{:S(2)}) copy-start(bf16[1040,128]{1,0:T(8,128)(2,1)} %copy-done.2) | copy-start | bytes 798724
  50.9 39.4 %copy-start.8 = (f32[128]{0:T(128)S(1)}, f32[128]{0:T(128)}, u32[]{:S(2)}) copy-start(f32[128]{0:T(128)} %param.23) | copy-start | bytes 1540
  50.9 56.0 %copy-start.21 = (f32[128]{0:T(128)S(1)}, f32[128]{0:T(128)}, u32[]{:S(2)}) copy-start(f32[128]{0:T(128)} %param.25) | copy-start | bytes 1540
  50.9 56.0 %copy-start.22 = (f32[128]{0:T(128)S(1)}, f32[128]{0:T(128)}, u32[]{:S(2)}) copy-start(f32[128]{0:T(128)} %param.27) | copy-start | bytes 1540
  57.5 22.2 %copy-start.6 = (bf16[1024,128]{1,0:T(8,128)(2,1)}, bf16[1024,128]{1,0:T(8,128)(2,1)S(1)}, u32[]{:S(2)}) copy-start(bf16[1024,128]{1,0:T(8,128)(2,1)S(1)} %get-tuple-element.27.own1_ref) | copy-start | bytes 786436
  57.5 49.4 %copy-start.12 = (bf16[3,3,128,128]{3,2,1,0:T(8,128)(2,1)S(1)}, bf16[3,3,128,128]{3,2,1,0:T(8,128)(2,1)}, u32[]{:S(2)}) copy-start(bf16[3,3,128,128]{3,2,1,0:T(8,128)(2,1)} %w1_ref.1) | copy-start | bytes 884740
  57.5 10.4 %collective-permute-start.3 = (bf16[1024,128]{1,0:T(8,128)(2,1)S(1)}, bf16[1024,128]{1,0:T(8,128)(2,1)S(1)}, u32[]{:S(2)}, u32[]{:S(2)}) collective-permute-start(bf16[1024,128]{1,0:T(8,128)(2,1)S(1)} %get-tuple-element.30), channel_id=1, source_target_pairs={{0,24},{8,0},{16,8},{24,16},{1,25},{9,1},{17,9},{25,17},{2,26},{10... | collective-permute-start | bytes 786440 | tf_op jit(solution)/shard_map/ppermute | solution.py:377
  62.2 12.3 %collective-permute-start.1 = (bf16[1040,128]{1,0:T(8,128)(2,1)S(1)}, bf16[1040,128]{1,0:T(8,128)(2,1)S(1)}, u32[]{:S(2)}, u32[]{:S(2)}) collective-permute-start(bf16[1040,128]{1,0:T(8,128)(2,1)S(1)} %add.50), channel_id=1, source_target_pairs={{0,8},{8,16},{16,24},{24,0},{1,9},{9,17},{17,25},{25,1},{2,10},{10... | collective-permute-start | bytes 798728 | tf_op jit(solution)/shard_map/ppermute | solution.py:377
  67.9 11.6 %collective-permute-start.4 = (bf16[1024,128]{1,0:T(8,128)(2,1)S(1)}, bf16[1024,128]{1,0:T(8,128)(2,1)S(1)}, u32[]{:S(2)}, u32[]{:S(2)}) collective-permute-start(bf16[1024,128]{1,0:T(8,128)(2,1)S(1)} %add.56), channel_id=1, source_target_pairs={{0,24},{8,0},{16,8},{24,16},{1,25},{9,1},{17,9},{25,17},{2,26},{10... | collective-permute-start | bytes 786440 | tf_op jit(solution)/shard_map/ppermute | solution.py:377
  75.3 14.9 %collective-permute-start.2 = (bf16[1040,128]{1,0:T(8,128)(2,1)}, bf16[1040,128]{1,0:T(8,128)(2,1)S(1)}, u32[]{:S(2)}, u32[]{:S(2)}) collective-permute-start(bf16[1040,128]{1,0:T(8,128)(2,1)} %add.51), channel_id=1, source_target_pairs={{0,8},{8,16},{16,24},{24,0},{1,9},{9,17},{17,25},{25,1},{2,10},{10... | collective-permute-start | bytes 798728 | tf_op jit(solution)/shard_map/ppermute | solution.py:377
  79.7 10.6 %collective-permute-start.5 = (bf16[1024,128]{1,0:T(8,128)(2,1)S(1)}, bf16[1024,128]{1,0:T(8,128)(2,1)S(1)}, u32[]{:S(2)}, u32[]{:S(2)}) collective-permute-start(bf16[1024,128]{1,0:T(8,128)(2,1)S(1)} %add.57), channel_id=1, source_target_pairs={{0,24},{8,0},{16,8},{24,16},{1,25},{9,1},{17,9},{25,17},{2,26},{10... | collective-permute-start | bytes 786440 | tf_op jit(solution)/shard_map/ppermute | solution.py:377
  90.2 1.0 copy-start.5
  91.2 0.9 copy-start.7
  92.9 4.4 %collective-permute-start.6 = (bf16[2,128,128]{2,1,0:T(8,128)(2,1)S(1)}, bf16[2,128,128]{2,1,0:T(8,128)(2,1)S(1)}, u32[]{:S(2)}, u32[]{:S(2)}) collective-permute-start(bf16[2,128,128]{2,1,0:T(8,128)(2,1)S(1)} %get-tuple-element.37), channel_id=1, source_target_pairs={{0,4},{4,8},{8,12},{12,16},{16,20},{20,24},{24,28},{1,5},{5,9},{9,... | collective-permute-start | bytes 196616 | tf_op jit(solution)/shard_map/ppermute | solution.py:370
  95.5 6.2 %collective-permute-start.7 = (bf16[2,128,128]{2,1,0:T(8,128)(2,1)S(1)}, bf16[2,128,128]{2,1,0:T(8,128)(2,1)S(1)}, u32[]{:S(2)}, u32[]{:S(2)}) collective-permute-start(bf16[2,128,128]{2,1,0:T(8,128)(2,1)S(1)} %get-tuple-element.36), channel_id=1, source_target_pairs={{4,0},{8,4},{12,8},{16,12},{20,16},{24,20},{28,24},{5,1},{9,5},{13... | collective-permute-start | bytes 196616 | tf_op jit(solution)/shard_map/ppermute | solution.py:371
  101.7 4.5 %collective-permute-start.9 = (bf16[20,2,128]{2,1,0:T(2,128)(2,1)S(1)}, bf16[20,2,128]{2,1,0:T(2,128)(2,1)S(1)}, u32[]{:S(2)}, u32[]{:S(2)}) collective-permute-start(bf16[20,2,128]{2,1,0:T(2,128)(2,1)S(1)} %pad_maximum_fusion.1), channel_id=1, source_target_pairs={{1,0},{2,1},{3,2},{5,4},{6,5},{7,6},{9,8},{10,9},{11,10},{13,12},{... | collective-permute-start | bytes 30728 | tf_op jit(solution)/shard_map/ppermute | solution.py:371
  103.0 3.9 %collective-permute-start.8 = (bf16[20,2,128]{2,1,0:T(2,128)(2,1)S(1)}, bf16[20,2,128]{2,1,0:T(2,128)(2,1)S(1)}, u32[]{:S(2)}, u32[]{:S(2)}) collective-permute-start(bf16[20,2,128]{2,1,0:T(2,128)(2,1)S(1)} %pad_maximum_fusion), channel_id=1, source_target_pairs={{0,1},{1,2},{2,3},{4,5},{5,6},{6,7},{8,9},{9,10},{10,11},{12,13},{... | collective-permute-start | bytes 30728 | tf_op jit(solution)/shard_map/ppermute | solution.py:370
  106.9 1.0 copy-start.13
  118.8 10.1 %collective-permute-start.13 = (bf16[16,64,128]{2,1,0:T(8,128)(2,1)S(1)}, bf16[16,64,128]{2,1,0:T(8,128)(2,1)S(1)}, u32[]{:S(2)}, u32[]{:S(2)}) collective-permute-start(bf16[16,64,128]{2,1,0:T(8,128)(2,1)S(1)} %get-tuple-element.32.refs_0_), channel_id=1, source_target_pairs={{0,24},{8,0},{16,8},{24,16},{1,25},{9,1},{17,9},{25,17},{2,26},{10... | collective-permute-start | bytes 786440 | tf_op jit(solution)/shard_map/ppermute | solution.py:377
  128.9 10.1 %collective-permute-start.14 = (bf16[16,64,128]{2,1,0:T(8,128)(2,1)S(1)}, bf16[16,64,128]{2,1,0:T(8,128)(2,1)S(1)}, u32[]{:S(2)}, u32[]{:S(2)}) collective-permute-start(bf16[16,64,128]{2,1,0:T(8,128)(2,1)S(1)} %collective-permute-done.13.refs_1_), channel_id=1, source_target_pairs={{0,24},{8,0},{16,8},{24,16},{1,25},{9,1},{17,9},{25,17},{2,26},{10... | collective-permute-start | bytes 786440 | tf_op jit(solution)/shard_map/ppermute | solution.py:377
  139.0 9.3 %collective-permute-start.15 = (bf16[16,64,128]{2,1,0:T(8,128)(2,1)S(1)}, bf16[16,64,128]{2,1,0:T(8,128)(2,1)S(1)}, u32[]{:S(2)}, u32[]{:S(2)}) collective-permute-start(bf16[16,64,128]{2,1,0:T(8,128)(2,1)S(1)} %collective-permute-done.14.refs_2_), channel_id=1, source_target_pairs={{0,24},{8,0},{16,8},{24,16},{1,25},{9,1},{17,9},{25,17},{2,26},{10... | collective-permute-start | bytes 786440 | tf_op jit(solution)/shard_map/ppermute | solution.py:377
  145.6 2.0 copy-start
  155.7 39.7 %all-to-all-start.3 = ((bf16[8,512,128]{2,1,0:T(8,128)(2,1)}), bf16[8,512,128]{2,1,0:T(8,128)(2,1)S(1)}, u32[]{:S(2)}, u32[]{:S(2)}) async-start(bf16[8,512,128]{2,1,0:T(8,128)(2,1)} %shard_map.156), calls=%async_computation.3 | async-start | bytes 2097152 | tf_op jit(solution)/shard_map/all_to_all | solution.py:417
  159.3 11.2 %collective-permute-start.10 = (bf16[16,64,128]{2,1,0:T(8,128)(2,1)S(1)}, bf16[16,64,128]{2,1,0:T(8,128)(2,1)S(1)}, u32[]{:S(2)}, u32[]{:S(2)}) collective-permute-start(bf16[16,64,128]{2,1,0:T(8,128)(2,1)S(1)} %get-tuple-element.31.refs_0_), channel_id=1, source_target_pairs={{0,8},{8,16},{16,24},{24,0},{1,9},{9,17},{17,25},{25,1},{2,10},{10... | collective-permute-start | bytes 786440 | tf_op jit(solution)/shard_map/ppermute | solution.py:377
  170.4 9.8 %collective-permute-start.11 = (bf16[16,64,128]{2,1,0:T(8,128)(2,1)S(1)}, bf16[16,64,128]{2,1,0:T(8,128)(2,1)S(1)}, u32[]{:S(2)}, u32[]{:S(2)}) collective-permute-start(bf16[16,64,128]{2,1,0:T(8,128)(2,1)S(1)} %collective-permute-done.10.refs_1_), channel_id=1, source_target_pairs={{0,8},{8,16},{16,24},{24,0},{1,9},{9,17},{17,25},{25,1},{2,10},{10... | collective-permute-start | bytes 786440 | tf_op jit(solution)/shard_map/ppermute | solution.py:377
  180.2 8.9 %collective-permute-start.12 = (bf16[16,64,128]{2,1,0:T(8,128)(2,1)S(1)}, bf16[16,64,128]{2,1,0:T(8,128)(2,1)S(1)}, u32[]{:S(2)}, u32[]{:S(2)}) collective-permute-start(bf16[16,64,128]{2,1,0:T(8,128)(2,1)S(1)} %collective-permute-done.11.refs_2_), channel_id=1, source_target_pairs={{0,8},{8,16},{16,24},{24,0},{1,9},{9,17},{17,25},{25,1},{2,10},{10... | collective-permute-start | bytes 786440 | tf_op jit(solution)/shard_map/ppermute | solution.py:377
  180.2 33.2 %copy-start.10 = (s32[32]{0:T(128)S(1)}, s32[32]{0:T(128)}, u32[]{:S(2)}) copy-start(s32[32]{0:T(128)} %tile_ref.3) | copy-start | bytes 388

commit v3 on v2

v3 whole, which is shorter than its diff:
```python
import functools

import jax
import jax.numpy as jnp
from jax import lax
from jax.experimental import pallas as pl
from jax.experimental.pallas import tpu as pltpu
from jax.sharding import PartitionSpec as P

KN = 16
PH = 8
PW = 32
SR = 16
TC = 128
SIDE = 4
PAD = 8
META = 4
ACROSS = TC // PW
F32 = jnp.float32
BF16 = jnp.bfloat16

VMEM = pl.BlockSpec(memory_space=pltpu.VMEM)
SMEM = pl.BlockSpec(memory_space=pltpu.SMEM)
HBM = pl.BlockSpec(memory_space=pltpu.HBM)
LIMIT = 56 * 1024 * 1024


def call(kernel, in_specs, out_specs, out_shape, scratch, flops, moved, *args):
    return pl.pallas_call(
        kernel,
        in_specs=in_specs,
        out_specs=out_specs,
        out_shape=out_shape,
        scratch_shapes=scratch,
        compiler_params=pltpu.CompilerParams(vmem_limit_bytes=LIMIT),
        cost_estimate=pl.CostEstimate(flops=flops, bytes_accessed=moved, transcendentals=0),
    )(*args)


def silu(v):
    half = 0.5 * v
    return half + half * jnp.tanh(half)


def swap(x):
    axis = x.ndim - 1
    return pltpu.roll(x.astype(F32), x.shape[axis] // 2, axis).astype(x.dtype)


def lanes(shape):
    return lax.broadcasted_iota(jnp.int32, shape, len(shape) - 1) // (shape[-1] // 2)


def next_slot(tile_ref, count_ref, b):
    t = tile_ref[b]
    n = count_ref[t]
    count_ref[t] = n + 1
    return t, n


def clear(count_ref):
    for t in range(count_ref.shape[0]):
        count_ref[t] = 0


def embed_kernel(
    tile_hbm, patch_hbm, offset_hbm, cells_hbm, x_hbm, we_hbm, be_hbm, wp_hbm, bp_hbm,
    feat_ref, send0_ref, send1_ref,
    tile_ref, patch_ref, offset_ref, cells_ref, x_ref, we_ref, be_ref, wp_ref, bp_ref,
    count_ref, meta_ref, wide_ref, bias_ref, sems, x_sems,
):
    blocks, size, channels = feat_ref.shape
    chunks = x_sems.shape[0]
    per = blocks // chunks
    tiles = send0_ref.shape[0]
    meta_rows = meta_ref.shape[0] // tiles
    pairs = (
        (we_hbm, we_ref), (be_hbm, be_ref), (wp_hbm, wp_ref), (bp_hbm, bp_ref), (tile_hbm, tile_ref),
        (patch_hbm, patch_ref), (offset_hbm, offset_ref), (cells_hbm.at[0:8], cells_ref),
    )
    copies = [pltpu.make_async_copy(a, b, sems.at[i]) for i, (a, b) in enumerate(pairs)]

    def fetch(c):
        rows = pl.ds(pl.multiple_of(c * per * size, per * size), per * size)
        return pltpu.make_async_copy(x_hbm.at[rows], x_ref.at[rows], x_sems.at[c])

    for copy in copies:
        copy.start()
    for c in range(chunks):
        fetch(c).start()
    clear(count_ref)
    send0_ref[...] = jnp.zeros(send0_ref.shape, BF16)
    send1_ref[...] = jnp.zeros(send1_ref.shape, BF16)
    row = lax.broadcasted_iota(jnp.int32, meta_ref.shape, 0) % META
    meta_ref[...] = jnp.where(row == 2, -65536.0, 0.0)
    for copy in copies:
        copy.wait()
    wide_ref[:, :channels] = wp_ref[...]
    wide_ref[:, channels:] = swap(wp_ref[...])
    bias_ref[:, :channels] = bp_ref[...]
    bias_ref[:, channels:] = swap(bp_ref[...])
    group = lanes((size, channels))

    def chunk(c, unused):
        fetch(c).wait()
        rows = pl.ds(pl.multiple_of(c * per * size, per * size), per * size)
        hidden = silu(jnp.dot(x_ref[rows, :], we_ref[...], preferred_element_type=F32) + be_ref[...])
        both = jnp.dot(hidden.astype(BF16), wide_ref[...], preferred_element_type=F32) + bias_ref[...]
        feat_ref[pl.ds(c * per, per)] = both[:, :channels].astype(BF16).reshape(per, size, channels)
        for k in range(per):
            b = c * per + k
            t, n = next_slot(tile_ref, count_ref, b)
            odd = lax.rem(n, 2)
            at = pl.ds(pl.multiple_of(n // 2 * size, size), size)
            straight = both[k * size : (k + 1) * size, :channels]
            turned = both[k * size : (k + 1) * size, channels:]
            keep = group == odd
            low = jnp.where(keep, jnp.where(odd == 0, straight, turned), 0.0).astype(BF16)
            high = jnp.where(keep, jnp.where(odd == 0, turned, straight), 0.0).astype(BF16)
            send0_ref[t, at, :] += low
            send1_ref[t, at, :] += high
            first = t * meta_rows + n * META
            obs = pl.ds(pl.multiple_of(b * size, size), size)
            meta_ref[pl.ds(first, 2), :] = offset_ref[:, obs].astype(F32)
            meta_ref[pl.ds(first + 2, 1), :] = cells_ref[0:1, obs].astype(F32)
            meta_ref[pl.ds(first + 3, 1), :] = jnp.full((1, size), patch_ref[b], jnp.int32).astype(F32)
        return unused

    lax.fori_loop(0, chunks, chunk, 0)
    base = send1_ref.shape[1]
    extra = send0_ref.shape[1] - base - meta_rows
    for t in range(tiles):
        rows = meta_ref[t * meta_rows : (t + 1) * meta_rows, :]
        if extra:
            rows = jnp.concatenate([rows, jnp.zeros((extra, size), F32)], axis=0)
        send0_ref[t, base:, :] = rows.astype(BF16)


def factors(meta, normal):
    off_row, off_col, corner = meta[0:1, :], meta[1:2, :], meta[2:3, :]
    first_row = jnp.floor(corner * (1.0 / PW))
    first_col = corner - first_row * PW

    def factor(count, start, off):
        at = lax.broadcasted_iota(jnp.int32, (count, meta.shape[1]), 0).astype(F32) - start
        delta = at - 1.5 - off
        value = jnp.exp(delta * delta * -0.5)
        return jnp.where((at >= 0.0) & (at < SIDE), value, 0.0)

    def total(off):
        at = lax.broadcasted_iota(jnp.int32, (SIDE, meta.shape[1]), 0).astype(F32)
        delta = at - 1.5 - off
        return jnp.sum(jnp.exp(delta * delta * -0.5), axis=0, keepdims=True)

    rows, cols = factor(PH, first_row, off_row), factor(PW, first_col, off_col)
    if normal:
        rows = rows / (total(off_row) * total(off_col))
    return rows, cols


def outer(rows, cols):
    return (rows[:, None, :] * cols[None, :, :]).reshape(PH * PW, rows.shape[1])


def place(patch):
    row, col = patch // ACROSS, lax.rem(patch, ACROSS)
    halves = ACROSS // 2
    return (
        pl.ds(pl.multiple_of(row * PH, PH), PH),
        pl.ds(pl.multiple_of(lax.rem(col, halves) * PW, PW), PW),
        col // halves,
    )


def add_slot(acc_ref, matrix, packed, turned, odd, patch):
    at_row, at_col, half = place(patch)
    keep = lanes((1, packed.shape[1])) == half
    values = jnp.where(half == odd, packed, turned) * jnp.where(keep, 1.0, 0.0).astype(BF16)
    result = jnp.dot(matrix, values, preferred_element_type=F32)
    acc_ref[at_row, at_col, :] += result.reshape(PH, PW, result.shape[1])


def stripe_at(k, way):
    orbits = lax.axis_size("orbits")
    return lax.rem(lax.axis_index("orbits") + way * (orbits - 1 - k) + orbits * orbits, orbits)


def write_stripes(acc_ref, outs, way):
    for k, out_ref in enumerate(outs):
        stripe = acc_ref[pl.ds(stripe_at(k, way) * SR, SR)].astype(BF16)
        out_ref[0 : SR * TC // 2, :] = stripe.reshape(SR * TC // 2, stripe.shape[2])


def spread0_kernel(orbits, most, got_ref, *refs):
    outs, (matrix_ref, patch_ref, acc_ref, dens_ref) = refs[:orbits], refs[orbits:]
    size = got_ref.shape[2]
    acc_ref[...] = jnp.zeros(acc_ref.shape, F32)
    dens_ref[...] = jnp.zeros(dens_ref.shape, F32)
    base = most // 2 * size

    def tile(t, unused):
        metas = got_ref[t, base:, :].astype(F32)
        patches = [jnp.max(metas[n * META + 3 : n * META + 4, :]).astype(jnp.int32) for n in range(most)]
        for pair in range(most // 2):
            packed = got_ref[t, pair * size : (pair + 1) * size, :]
            turned = swap(packed)
            for odd in range(2):
                n = pair * 2 + odd
                patch = patches[n]
                patch_ref[t * most + n] = patch
                rows, cols = factors(metas[n * META : (n + 1) * META], False)
                matrix = outer(rows, cols).astype(BF16)
                matrix_ref[t * most + n] = matrix
                add_slot(acc_ref, matrix, packed, turned, odd, patch)
                dens_ref[patch] += lax.dot_general(
                    rows.astype(BF16), cols.astype(BF16), (((1,), (1,)), ((), ())), preferred_element_type=F32
                )
        return unused

    lax.fori_loop(0, got_ref.shape[0], tile, 0)
    write_stripes(acc_ref, outs, 1)
    for k, out_ref in enumerate(outs):
        bands = []
        for band in range(SR // PH):
            first = (stripe_at(k, 1) * (SR // PH) + band) * ACROSS
            bands.append(jnp.concatenate([dens_ref[first + c] for c in range(ACROSS)], axis=1))
        out_ref[SR * TC // 2 :, :] = jnp.concatenate(bands, axis=0).astype(BF16)


def spread1_kernel(orbits, most, patch_ref, matrix_ref, got_ref, *refs):
    outs, (acc_ref,) = refs[:orbits], refs[orbits:]
    size = got_ref.shape[2]
    acc_ref[...] = jnp.zeros(acc_ref.shape, F32)

    def tile(t, unused):
        for pair in range(most // 2):
            packed = got_ref[t, pair * size : (pair + 1) * size, :]
            turned = swap(packed)
            for odd in range(2):
                slot = t * most + pair * 2 + odd
                add_slot(acc_ref, matrix_ref[slot], packed, turned, odd, patch_ref[slot])
        return unused

    lax.fori_loop(0, got_ref.shape[0], tile, 0)
    write_stripes(acc_ref, outs, -1)


def weights_kernel(most, got_ref, out_ref):
    base = most // 2 * got_ref.shape[2]

    def tile(t, unused):
        metas = got_ref[t, base:, :].astype(F32)
        for n in range(most):
            rows, cols = factors(metas[n * META : (n + 1) * META], True)
            out_ref[t * most + n] = outer(rows, cols).T.astype(BF16)
        return unused

    lax.fori_loop(0, got_ref.shape[0], tile, 0)


def grid_kernel(own0_ref, sum0_ref, own1_ref, sum1_ref, weight_ref, out_ref):
    half = TC // 2
    channels = out_ref.shape[2]
    tail = slice(SR * half, SR * half + SR)
    density = (own0_ref[tail, :].astype(F32) + sum0_ref[tail, :].astype(F32)).T
    low = lanes((half, channels)) == 0
    for i in range(SR):
        at = slice(i * half, (i + 1) * half)
        a = own0_ref[at, :].astype(F32) + sum0_ref[at, :].astype(F32)
        b = own1_ref[at, :].astype(F32) + sum1_ref[at, :].astype(F32)
        spread = jnp.concatenate([jnp.where(low, a, swap(b)), jnp.where(low, swap(a), b)], axis=0)
        d = jnp.broadcast_to(density[:, i : i + 1], (TC, channels))
        out_ref[i] = (spread / jnp.maximum(d, 1.0) + weight_ref[...] * (d / (1.0 + d))).astype(BF16)


def conv_kernel(
    x_ref, up_ref, down_ref, left_ref, right_ref, w1_ref, b1_ref, w2_ref, b2_ref,
    out_ref, out0_ref, out1_ref, wide_ref, x16_ref, first_ref, wc1_ref, wc2_ref,
):
    channels = out_ref.shape[2]
    width = x16_ref.shape[1]
    half = TC // 2
    for a in range(3):
        for b in range(3):
            at = (slice(a * channels, (a + 1) * channels), slice(b * channels, (b + 1) * channels))
            wc1_ref[at] = w1_ref[a, b]
            wc2_ref[at] = w2_ref[a, b]
    body = slice(PAD, PAD + TC)
    wide_ref[...] = jnp.zeros(wide_ref.shape, F32)
    wide_ref[0:2, body] = up_ref[...].astype(F32)
    wide_ref[2 : 2 + SR, body] = x_ref[...].astype(F32)
    wide_ref[2 + SR :, body] = down_ref[...].astype(F32)
    wide_ref[:, PAD - 2 : PAD] = left_ref[...].astype(F32)
    wide_ref[:, PAD + TC : PAD + TC + 2] = right_ref[...].astype(F32)
    x16_ref[...] = wide_ref[...].astype(BF16)

    def taps(source, first, count, weights):
        rows = [source[pl.ds(first + a, count)].reshape(count * width, channels) for a in range(3)]
        all_taps = jnp.dot(jnp.concatenate(rows, axis=1), weights[...], preferred_element_type=F32)
        return (
            pltpu.roll(all_taps[:, :channels], 1, 0)
            + all_taps[:, channels : 2 * channels]
            + pltpu.roll(all_taps[:, 2 * channels :], count * width - 1, 0)
        )

    at_row, at_col = lax.axis_index(("orbits", "rows")), lax.axis_index("cols")
    col = lax.broadcasted_iota(jnp.int32, (width, channels), 0)
    first_col = jnp.where(at_col > 0, PAD - 1, PAD)
    last_col = jnp.where(at_col < lax.axis_size("cols") - 1, PAD + TC, PAD + TC - 1)
    inside = (col >= first_col) & (col <= last_col)
    first_row = jnp.where(at_row > 0, 0, 1)
    last_row = jnp.where(at_row < lax.axis_size(("orbits", "rows")) - 1, SR + 1, SR)
    count = (SR + 2) // 3

    def first_rows(i, unused):
        value = silu(taps(x16_ref, i * count, count, wc1_ref) + b1_ref[...])
        for r in range(count):
            row = i * count + r
            keep = inside & (row >= first_row) & (row <= last_row)
            first_ref[row] = jnp.where(keep, value[r * width : (r + 1) * width], 0.0).astype(BF16)
        return unused

    lax.fori_loop(0, 3, first_rows, 0)
    group = lanes((half, channels)) == 0
    again = SR // 2

    def second_rows(i, unused):
        values = taps(first_ref, i * again, again, wc2_ref) + b2_ref[...]
        for r in range(again):
            row = i * again + r
            value = values[r * width + PAD : r * width + PAD + TC] + x_ref[row].astype(F32)
            left, right = value[:half], value[half:]
            out_ref[row] = value.astype(BF16)
            out0_ref[row] = jnp.where(group, left, swap(right)).astype(BF16)
            out1_ref[row] = jnp.where(group, swap(left), right).astype(BF16)
        return unused

    lax.fori_loop(0, 2, second_rows, 0)


def read_kernel(orbits, most, way, patch_ref, weights_ref, *refs):
    pieces, (out_ref, grid_ref) = refs[:orbits], refs[orbits:]
    size = out_ref.shape[2]
    for k, piece_ref in enumerate(pieces):
        at = pl.ds(stripe_at(orbits - 1 - k, -way) * SR, SR)
        grid_ref[0, at] = piece_ref[...]
        grid_ref[1, at] = swap(piece_ref[...])
    low = lanes((size, out_ref.shape[2])) == 0

    def tile(t, unused):
        for pair in range(most // 2):
            sums = []
            for odd in range(2):
                slot = t * most + pair * 2 + odd
                at_row, at_col, half = place(patch_ref[slot])
                turn = jnp.where(half == odd, 0, 1)
                values = grid_ref[turn, at_row, at_col, :].reshape(PH * PW, grid_ref.shape[3])
                sums.append(jnp.dot(weights_ref[slot], values, preferred_element_type=F32))
            out_ref[t, pair * size : (pair + 1) * size, :] = jnp.where(low, sums[0], sums[1]).astype(BF16)
        return unused

    lax.fori_loop(0, out_ref.shape[0], tile, 0)


def final_kernel(tile_ref, feat_ref, got0_ref, got1_ref, out_ref, count_ref):
    blocks, size, channels = feat_ref.shape
    clear(count_ref)
    low = lanes((size, channels)) == 0
    per = 4

    def chunk(c, unused):
        for k in range(per):
            b = c * per + k
            t, n = next_slot(tile_ref, count_ref, b)
            odd = lax.rem(n, 2)
            at = pl.ds(pl.multiple_of(n // 2 * size, size), size)
            a, b2 = got0_ref[t, at, :].astype(F32), got1_ref[t, at, :].astype(F32)
            turned = swap(jnp.where(odd == 0, b2, a))
            mine = jnp.where(odd == 0, jnp.where(low, a, turned), jnp.where(low, turned, b2))
            out_ref[b] = (feat_ref[b].astype(F32) + mine).astype(BF16)
        return unused

    lax.fori_loop(0, blocks // per, chunk, 0)


def shifts(axis):
    size = lax.axis_size(axis)
    up = [(i, i + 1) for i in range(size - 1)]
    return up, [(j, i) for i, j in up]


def halo(x, axis, dim, width):
    up, down = shifts(axis)
    length = x.shape[dim]
    before = lax.ppermute(lax.slice_in_dim(x, length - width, length, axis=dim), axis, up)
    after = lax.ppermute(lax.slice_in_dim(x, 0, width, axis=dim), axis, down)
    return before, after


def turn(x, way):
    size = lax.axis_size("orbits")
    return lax.ppermute(x, "orbits", [(i, (i + way) % size) for i in range(size)])


together = lax.optimization_barrier


def local(
    obs_feat, obs_offset, obs_cells, block_tile, block_patch, w_embed, b_embed, w_proj, b_proj,
    density_weight, w_first, b_first, w_second, b_second,
):
    channels = obs_feat.shape[1]
    blocks = block_tile.shape[0]
    size = obs_feat.shape[0] // blocks
    plane = ("rows", "cols")
    tiles = lax.axis_size(plane)
    orbits = lax.axis_size("orbits")
    most = max(2, 2 * blocks // tiles)
    slots = tiles * most
    height = orbits * SR
    patches = height // PH * ACROSS
    half = TC // 2
    pairs = most // 2 * size
    meta_rows = max(16, most * META)
    chunks = blocks // 4
    counts = pltpu.SMEM((tiles,), jnp.int32)
    shape = jax.ShapeDtypeStruct
    bias = lambda b: b.reshape(1, channels)
    exchange = lambda x: lax.all_to_all(x, plane, split_axis=0, concat_axis=0, tiled=True)
    vmem = lambda a: pltpu.VMEM(a.shape, a.dtype)

    b_embed, b_proj = bias(b_embed), bias(b_proj)
    features, send0, send1 = call(
        embed_kernel,
        [HBM] * 9,
        [VMEM] * 3,
        (
            shape((blocks, size, channels), BF16),
            shape((tiles, pairs + meta_rows, channels), BF16),
            shape((tiles, pairs, channels), BF16),
        ),
        [
            pltpu.SMEM((blocks,), jnp.int32),
            pltpu.SMEM((blocks,), jnp.int32),
            vmem(obs_offset),
            pltpu.VMEM((8, obs_cells.shape[1]), jnp.int32),
            vmem(obs_feat),
            vmem(w_embed),
            vmem(b_embed),
            vmem(w_proj),
            vmem(b_proj),
            counts,
            pltpu.VMEM((slots * META, size), F32),
            pltpu.VMEM((channels, 2 * channels), BF16),
            pltpu.VMEM((1, 2 * channels), F32),
            pltpu.SemaphoreType.DMA((8,)),
            pltpu.SemaphoreType.DMA((chunks,)),
        ],
        6 * obs_feat.size * channels,
        8 * obs_feat.size,
        block_tile, block_patch, obs_offset, obs_cells, obs_feat, w_embed, b_embed, w_proj, b_proj,
    )
    got0 = exchange(send0)
    got1 = exchange(send1)

    flops = 2 * slots * size * channels * PH * PW
    stripe_shape = shape((SR * half, channels), BF16)
    dense_shape = shape((SR * half + SR, channels), BF16)
    acc = pltpu.VMEM((height, half, channels), F32)
    *out0, matrices, patch_of = call(
        functools.partial(spread0_kernel, orbits, most),
        [VMEM],
        [VMEM] * (orbits + 1) + [SMEM],
        [dense_shape] * orbits + [shape((slots, PH * PW, size), BF16), shape((slots,), jnp.int32)],
        [acc, pltpu.VMEM((patches, PH, PW), F32)],
        flops,
        12 * slots * size * channels,
        got0,
    )
    sum0 = out0[0]
    for k in range(1, orbits):
        sum0 = turn(sum0, 1)
        if k < orbits - 1:
            sum0 = sum0 + out0[k]
        if k == 1:
            sum0, got1 = together((sum0, got1))
    out1 = call(
        functools.partial(spread1_kernel, orbits, most),
        [SMEM, VMEM, VMEM],
        [VMEM] * orbits,
        [stripe_shape] * orbits,
        [acc],
        flops,
        8 * slots * size * channels,
        patch_of, matrices, got1,
    )
    sum1 = out1[0]
    for k in range(1, orbits):
        sum1 = turn(sum1, -1)
        if k < orbits - 1:
            sum1 = sum1 + out1[k]
    weights = call(
        functools.partial(weights_kernel, most),
        [VMEM],
        VMEM,
        shape((slots, size, PH * PW), BF16),
        [],
        flops,
        4 * slots * size * channels,
        got0,
    )
    grid_in = call(
        grid_kernel,
        [VMEM] * 5,
        VMEM,
        shape((SR, TC, channels), BF16),
        [],
        10000000,
        8 * SR * TC * channels,
        out0[-1], sum0, out1[-1], sum1, bias(density_weight),
    )

    above, below = halo(grid_in, ("orbits", "rows"), 0, 2)
    extended = jnp.concatenate(
        [
            jnp.concatenate([above[:, c], grid_in[:, c], below[:, c]], axis=0)
            for c in (slice(0, 2), slice(TC - 2, TC))
        ],
        axis=1,
    )
    left, right = halo(extended, "cols", 1, 2)
    width = TC + 2 * PAD
    grid_out, half0, half1 = call(
        conv_kernel,
        [VMEM] * 9,
        [VMEM] * 3,
        [shape((SR, TC, channels), BF16)] + [shape((SR, half, channels), BF16)] * 2,
        [
            pltpu.VMEM((SR + 4, width, channels), F32),
            pltpu.VMEM((SR + 4, width, channels), BF16),
            pltpu.VMEM((SR + 2, width, channels), BF16),
            pltpu.VMEM((3 * channels, 3 * channels), BF16),
            pltpu.VMEM((3 * channels, 3 * channels), BF16),
        ],
        4 * 9 * SR * TC * channels * channels,
        8 * grid_in.size,
        grid_in, above, below, left, right, w_first, bias(b_first), w_second, bias(b_second),
    )

    def readings(pieces, way):
        return call(
            functools.partial(read_kernel, orbits, most, way),
            [SMEM, VMEM] + [VMEM] * orbits,
            VMEM,
            shape((tiles, pairs, channels), BF16),
            [pltpu.VMEM((2, height, half, channels), BF16)],
            flops,
            8 * slots * size * channels,
            patch_of, weights, *pieces,
        )

    pieces0, pieces1 = [half0, turn(half0, 1)], [half1]
    for k in range(2, orbits):
        both = together((turn(pieces0[-1], 1), turn(pieces1[-1], -1)))
        pieces0.append(both[0])
        pieces1.append(both[1])
    while len(pieces1) < orbits:
        pieces1.append(turn(pieces1[-1], -1))
    back0 = exchange(readings(pieces0, 1))
    back1 = exchange(readings(pieces1, -1))
    obs_out = call(
        final_kernel,
        [SMEM] + [VMEM] * 3,
        VMEM,
        shape((blocks, size, channels), BF16),
        [counts],
        1000000,
        8 * obs_feat.size,
        block_tile, features, back0, back1,
    )
    return obs_out.reshape(obs_feat.shape), grid_out


def solution(mesh):
    spread_out = ("orbits", "rows", "cols")
    in_specs = (
        P(spread_out, None),
        P(None, spread_out),
        P(None, spread_out),
        P(spread_out),
        P(spread_out),
    ) + (P(),) * 9
    out_specs = (P(spread_out, None), P(("orbits", "rows"), "cols", None))
    return jax.shard_map(local, mesh=mesh, in_specs=in_specs, out_specs=out_specs, check_vma=False)
```

time: 219 us -> 205 us (0.936)
  local copies, waits for them, and re-layouts: 13.3 us -> 4.68 us
  waiting for transfers between devices: 70.4 us -> 64.3 us
  starting transfers between devices: 42.5 us -> 39.2 us
  Pallas kernels: 49.3 us -> 51.9 us
    unnamed x46 -> x30, local copies, waits for them, and re-layouts: 13.3 us -> 2.99 us
    all_to_all x2, waiting for transfers between devices: 4.66 us -> 0.01 us  [local(): lax.all_to_all(x, plane, split_axis=0, concat_axis=0, tiled=True)]
    ppermute x12, starting transfers between devices: 27.2 us -> 22.8 us  [turn(): lax.ppermute(x, 'orbits', [(i, (i + way) % size) for i in range(size)])]
    pallas_call x9, Pallas kernels: 49.3 us -> 51.9 us  [call(): pl.pallas_call(kernel, in_specs=in_specs, out_specs=out_specs, out_shape=...]
  transfers between devices with their start and end apart: 18 -> 18, of which waited for: 14 -> 14; matrix products, arithmetic and copies ran while one was open for 1% -> 2% of each run, Pallas kernels for 10% -> 10%
where the time goes in v3:
time: 205 us; the launch traced here: 204 us
  waiting for transfers between devices  64.3 us (31%)
  Pallas kernels  51.9 us (25%)
  blocking collectives  40.2 us (20%)
  starting transfers between devices  39.2 us (19%)
  local copies, waits for them, and re-layouts  4.68 us (2%)
  other arithmetic  3.18 us (2%)
    ppermute x12, waiting for transfers between devices, turn(): lax.ppermute(x, 'orbits', [(i, (i + way) % size) for i in range(size)])  58.6 us
    pallas_call x9, Pallas kernels, call(): pl.pallas_call(kernel, in_specs=in_specs, out_specs=out_specs, out_shape=...  51.9 us
    all_to_all x2, blocking collectives, local(): lax.all_to_all(x, plane, split_axis=0, concat_axis=0, tiled=True)  40.2 us
    ppermute x12, starting transfers between devices, turn(): lax.ppermute(x, 'orbits', [(i, (i + way) % size) for i in range(size)])  22.8 us
    all_to_all x2, starting transfers between devices, local(): lax.all_to_all(x, plane, split_axis=0, concat_axis=0, tiled=True)  7.12 us
    ppermute x2, starting transfers between devices, halo(): lax.ppermute(lax.slice_in_dim(x, length - width, length, axis=dim), axis,...  6.78 us
    ppermute x2, waiting for transfers between devices, halo(): after = lax.ppermute(lax.slice_in_dim(x, 0, width, axis=dim), axis, down)  4.83 us
  transfers between devices with their start and end apart: 18, of which 14 were waited for; matrix products, arithmetic and copies ran while one was open for 2% of the time, Pallas kernels for 10%

profile of v3, /device:TPU:0, one launch (start us, length us, event | category | flops | bytes accessed | tf_op | source)
XLA Modules:
  0.0 204.3 jit_solution(10690764278224188817)
XLA Ops:
  0.6 6.4 %shard_map.149 = (bf16[32,128,128]{2,1,0:T(8,128)(2,1)}, bf16[8,544,128]{2,1,0:T(8,128)(2,1)}, bf16[8,512,128]{2,1,0:T(8,128)(2,1)}) custom-call(s32[32]{0:T(128)} %tile_ref.1, s32[32]{0:T(128)} %patch_hbm.1, bf16[2,4096]{1,0:T(2,128)(2,1)} %offset_hbm.1, s32[16,4096]{1,0:T(8,128)} %cells_hbm.1, bf16[4096,128]{1,0:T(8,128)(2,1)} %x_hbm.1, ...), custom_call_target="tpu_custom_call" | custom-call | flops 402653184 | bytes 4194304 | tf_op jit(solution)/shard_map/pallas_call | solution.py:29
  7.0 21.4 %all_to_all.20.got_ref = bf16[8,544,128]{2,1,0:T(8,128)(2,1)} all-to-all(bf16[8,544,128]{2,1,0:T(8,128)(2,1)} %get-tuple-element.25), channel_id=1, replica_groups=mesh['orbits'=4,'rows'=2,'cols'=4] {'rows','cols'}, dimensions={0} | all-to-all | bytes 2228224 | tf_op jit(solution)/shard_map/all_to_all | solution.py:429
  28.4 3.6 %all-to-all-start.1 = ((bf16[8,512,128]{2,1,0:T(8,128)(2,1)}), bf16[8,512,128]{2,1,0:T(8,128)(2,1)S(1)}, u32[]{:S(2)}, u32[]{:S(2)}) async-start(bf16[8,512,128]{2,1,0:T(8,128)(2,1)} %get-tuple-element.30), calls=%async_computation.1 | async-start | bytes 2097152 | tf_op jit(solution)/shard_map/all_to_all | solution.py:429
  31.9 7.8 %shard_map.150 = (bf16[1040,128]{1,0:T(8,128)(2,1)}, bf16[1040,128]{1,0:T(8,128)(2,1)}, bf16[1040,128]{1,0:T(8,128)(2,1)}, bf16[1040,128]{1,0:T(8,128)(2,1)}, bf16[64,256,128]{2,1,0:T(8,128)(2,1)}, /*index=5*/s32[64]{0:T(128)}) custom-call(bf16[8,544,128]{2,1,0:T(8,128)(2,1)} %all_to_all.20.got_ref), custom_call_target="tpu_custom_call" | custom-call | flops 536870912 | bytes 12582912 | tf_op jit(solution)/shard_map/pallas_call | solution.py:29
  39.8 2.0 %collective-permute-start = (bf16[1040,128]{1,0:T(8,128)(2,1)}, bf16[1040,128]{1,0:T(8,128)(2,1)S(1)}, u32[]{:S(2)}, u32[]{:S(2)}) collective-permute-start(bf16[1040,128]{1,0:T(8,128)(2,1)} %get-tuple-element.28), channel_id=1, source_target_pairs={{0,8},{8,16},{16,24},{24,0},{1,9},{9,17},{17,25},{25,1},{2,10},{10... | collective-permute-start | bytes 798728 | tf_op jit(solution)/shard_map/ppermute | solution.py:402
  41.8 9.2 %collective-permute-done = bf16[1040,128]{1,0:T(8,128)(2,1)S(1)} collective-permute-done((bf16[1040,128]{1,0:T(8,128)(2,1)}, bf16[1040,128]{1,0:T(8,128)(2,1)S(1)}, u32[]{:S(2)}, u32[]{:S(2)}) %collective-permute-start) | collective-permute-done | bytes 266272 | tf_op jit(solution)/shard_map/ppermute | solution.py:402
  51.0 1.0 add.12
  52.1 1.0 copy-done.1
  53.0 6.6 %shard_map.152 = (bf16[1024,128]{1,0:T(8,128)(2,1)}, bf16[1024,128]{1,0:T(8,128)(2,1)}, bf16[1024,128]{1,0:T(8,128)(2,1)}, bf16[1024,128]{1,0:T(8,128)(2,1)}) custom-call(s32[64]{0:T(128)} %get-tuple-element.26.patch_ref, bf16[64,256,128]{2,1,0:T(8,128)(2,1)} %get-tuple-element.33.matrix_ref, bf16[8,512,128]{2,1,0:T(8,128)(2,1)} %copy-done.1), custom_call_target="tpu_custom_call" | custom-call | flops 536870912 | bytes 8388608 | tf_op jit(solution)/shard_map/pallas_call | solution.py:29
  59.7 1.8 collective-permute-start.3
  61.7 7.6 %collective-permute-done.3 = bf16[1024,128]{1,0:T(8,128)(2,1)S(1)} collective-permute-done((bf16[1024,128]{1,0:T(8,128)(2,1)}, bf16[1024,128]{1,0:T(8,128)(2,1)S(1)}, u32[]{:S(2)}, u32[]{:S(2)}) %collective-permute-start.3) | collective-permute-done | bytes 262176 | tf_op jit(solution)/shard_map/ppermute | solution.py:402
  69.3 1.0 add.14
  70.3 3.4 %collective-permute-start.4 = (bf16[1024,128]{1,0:T(8,128)(2,1)S(1)}, bf16[1024,128]{1,0:T(8,128)(2,1)S(1)}, u32[]{:S(2)}, u32[]{:S(2)}) collective-permute-start(bf16[1024,128]{1,0:T(8,128)(2,1)S(1)} %add.14), channel_id=1, source_target_pairs={{0,24},{8,0},{16,8},{24,16},{1,25},{9,1},{17,9},{25,17},{2,26},{10... | collective-permute-start | bytes 786440 | tf_op jit(solution)/shard_map/ppermute | solution.py:402
  73.7 1.3 collective-permute-done.1
  75.1 1.6 collective-permute-start.2
  76.7 4.3 %collective-permute-done.4 = bf16[1024,128]{1,0:T(8,128)(2,1)S(1)} collective-permute-done((bf16[1024,128]{1,0:T(8,128)(2,1)S(1)}, bf16[1024,128]{1,0:T(8,128)(2,1)S(1)}, u32[]{:S(2)}, u32[]{:S(2)}) %collective-permute-start.4) | collective-permute-done | bytes 262176 | tf_op jit(solution)/shard_map/ppermute | solution.py:402
  81.0 1.0 add.15
  82.1 3.9 %collective-permute-start.5 = (bf16[1024,128]{1,0:T(8,128)(2,1)S(1)}, bf16[1024,128]{1,0:T(8,128)(2,1)S(1)}, u32[]{:S(2)}, u32[]{:S(2)}) collective-permute-start(bf16[1024,128]{1,0:T(8,128)(2,1)S(1)} %add.15), channel_id=1, source_target_pairs={{0,24},{8,0},{16,8},{24,16},{1,25},{9,1},{17,9},{25,17},{2,26},{10... | collective-permute-start | bytes 786440 | tf_op jit(solution)/shard_map/ppermute | solution.py:402
  85.9 0.8 collective-permute-done.2.sum0_ref
  86.7 4.0 %collective-permute-done.5.sum1_ref = bf16[1024,128]{1,0:T(8,128)(2,1)S(1)} collective-permute-done((bf16[1024,128]{1,0:T(8,128)(2,1)S(1)}, bf16[1024,128]{1,0:T(8,128)(2,1)S(1)}, u32[]{:S(2)}, u32[]{:S(2)}) %collective-permute-start.5) | collective-permute-done | bytes 262176 | tf_op jit(solution)/shard_map/ppermute | solution.py:402
  90.7 0.7 copy-done.10
  91.4 2.7 %shard_map.153.x_ref = bf16[16,128,128]{2,1,0:T(8,128)(2,1)} custom-call(bf16[1040,128]{1,0:T(8,128)(2,1)} %get-tuple-element.27.own0_ref, bf16[1040,128]{1,0:T(8,128)(2,1)} %copy-done.3, bf16[1024,128]{1,0:T(8,128)(2,1)} %get-tuple-element.35.own1_ref, bf16[1024,128]{1,0:T(8,128)(2,1)} %copy-done.10, f32[1,128]{1,0:T(1,128)} %bitcast.7), custom_call_target="tpu_custom_call" | custom-call | flops 10000000 | bytes 2097152 | tf_op jit(solution)/shard_map/pallas_call | solution.py:29
  94.1 0.9 fusion.1
  95.0 3.8 %collective-permute-start.6 = (bf16[2,128,128]{2,1,0:T(8,128)(2,1)S(1)}, bf16[2,128,128]{2,1,0:T(8,128)(2,1)S(1)}, u32[]{:S(2)}, u32[]{:S(2)}) collective-permute-start(bf16[2,128,128]{2,1,0:T(8,128)(2,1)S(1)} %get-tuple-element.49), channel_id=1, source_target_pairs={{0,4},{4,8},{8,12},{12,16},{16,20},{20,24},{24,28},{1,5},{5,9},{9,... | collective-permute-start | bytes 196616 | tf_op jit(solution)/shard_map/ppermute | solution.py:395
  98.7 0.8 fusion
  99.5 1.3 collective-permute-start.7
  100.9 4.8 %collective-permute-done.7.down_ref = bf16[2,128,128]{2,1,0:T(8,128)(2,1)S(1)} collective-permute-done((bf16[2,128,128]{2,1,0:T(8,128)(2,1)S(1)}, bf16[2,128,128]{2,1,0:T(8,128)(2,1)S(1)}, u32[]{:S(2)}, u32[]{:S(2)}) %collective-permute-start.7) | collective-permute-done | bytes 65568 | tf_op jit(solution)/shard_map/ppermute | solution.py:396
  105.7 1.3 collective-permute-start.9
  107.1 3.0 %collective-permute-start.8 = (bf16[20,2,128]{2,1,0:T(2,128)(2,1)S(1)}, bf16[20,2,128]{2,1,0:T(2,128)(2,1)S(1)}, u32[]{:S(2)}, u32[]{:S(2)}) collective-permute-start(bf16[20,2,128]{2,1,0:T(2,128)(2,1)S(1)} %pad_maximum_fusion), channel_id=1, source_target_pairs={{0,1},{1,2},{2,3},{4,5},{5,6},{6,7},{8,9},{9,10},{10,11},{12,13},{... | collective-permute-start | bytes 30728 | tf_op jit(solution)/shard_map/ppermute | solution.py:395
  110.1 0.8 collective-permute-done.8.left_ref
  110.9 0.6 copy-done.14
  111.5 6.1 %shard_map.154 = (bf16[16,128,128]{2,1,0:T(8,128)(2,1)}, bf16[16,64,128]{2,1,0:T(8,128)(2,1)}, bf16[16,64,128]{2,1,0:T(8,128)(2,1)}) custom-call(bf16[16,128,128]{2,1,0:T(8,128)(2,1)} %shard_map.153.x_ref, bf16[2,128,128]{2,1,0:T(8,128)(2,1)} %copy-done.11, bf16[2,128,128]{2,1,0:T(8,128)(2,1)} %copy-done.12, bf16[20,2,128]{2,1,0:T(2,128)(2,1)} %copy-done.14, ...), custom_call_target="tpu_custom_call" | custom-call | flops 1207959552 | bytes 2097152 | tf_op jit(solution)/shard_map/pallas_call | solution.py:29
  117.7 3.8 %collective-permute-start.12 = (bf16[16,64,128]{2,1,0:T(8,128)(2,1)}, bf16[16,64,128]{2,1,0:T(8,128)(2,1)S(1)}, u32[]{:S(2)}, u32[]{:S(2)}) collective-permute-start(bf16[16,64,128]{2,1,0:T(8,128)(2,1)} %get-tuple-element.40.refs_0_), channel_id=1, source_target_pairs={{0,24},{8,0},{16,8},{24,16},{1,25},{9,1},{17,9},{25,17},{2,26},{10... | collective-permute-start | bytes 786440 | tf_op jit(solution)/shard_map/ppermute | solution.py:402
  121.5 7.4 %collective-permute-done.10.refs_1_ = bf16[16,64,128]{2,1,0:T(8,128)(2,1)S(1)} collective-permute-done((bf16[16,64,128]{2,1,0:T(8,128)(2,1)}, bf16[16,64,128]{2,1,0:T(8,128)(2,1)S(1)}, u32[]{:S(2)}, u32[]{:S(2)}) %collective-permute-start.10) | collective-permute-done | bytes 262176 | tf_op jit(solution)/shard_map/ppermute | solution.py:402
  128.9 3.6 %collective-permute-done.12.refs_1_ = bf16[16,64,128]{2,1,0:T(8,128)(2,1)S(1)} collective-permute-done((bf16[16,64,128]{2,1,0:T(8,128)(2,1)}, bf16[16,64,128]{2,1,0:T(8,128)(2,1)S(1)}, u32[]{:S(2)}, u32[]{:S(2)}) %collective-permute-start.12) | collective-permute-done | bytes 262176 | tf_op jit(solution)/shard_map/ppermute | solution.py:402
  132.5 9.9 %collective-permute-done.11.refs_2_ = bf16[16,64,128]{2,1,0:T(8,128)(2,1)S(1)} collective-permute-done((bf16[16,64,128]{2,1,0:T(8,128)(2,1)S(1)}, bf16[16,64,128]{2,1,0:T(8,128)(2,1)S(1)}, u32[]{:S(2)}, u32[]{:S(2)}) %collective-permute-start.11) | collective-permute-done | bytes 262176 | tf_op jit(solution)/shard_map/ppermute | solution.py:402
  142.4 3.8 %collective-permute-start.14 = (bf16[16,64,128]{2,1,0:T(8,128)(2,1)S(1)}, bf16[16,64,128]{2,1,0:T(8,128)(2,1)S(1)}, u32[]{:S(2)}, u32[]{:S(2)}) collective-permute-start(bf16[16,64,128]{2,1,0:T(8,128)(2,1)S(1)} %collective-permute-done.12.refs_1_), channel_id=1, source_target_pairs={{0,24},{8,0},{16,8},{24,16},{1,25},{9,1},{17,9},{25,17},{2,26},{10... | collective-permute-start | bytes 786440 | tf_op jit(solution)/shard_map/ppermute | solution.py:402
  146.2 5.5 %shard_map.151.weights_ref = bf16[64,128,256]{2,1,0:T(8,128)(2,1)} custom-call(bf16[8,544,128]{2,1,0:T(8,128)(2,1)} %all_to_all.20.got_ref), custom_call_target="tpu_custom_call" | custom-call | flops 536870912 | bytes 4194304 | tf_op jit(solution)/shard_map/pallas_call | solution.py:29
  151.7 1.7 collective-permute-done.13.refs_3_
  153.4 2.4 %collective-permute-done.14.refs_2_ = bf16[16,64,128]{2,1,0:T(8,128)(2,1)S(1)} collective-permute-done((bf16[16,64,128]{2,1,0:T(8,128)(2,1)S(1)}, bf16[16,64,128]{2,1,0:T(8,128)(2,1)S(1)}, u32[]{:S(2)}, u32[]{:S(2)}) %collective-permute-start.14) | collective-permute-done | bytes 262176 | tf_op jit(solution)/shard_map/ppermute | solution.py:402
  155.9 6.3 %shard_map.155 = bf16[8,512,128]{2,1,0:T(8,128)(2,1)} custom-call(s32[64]{0:T(128)} %get-tuple-element.26.patch_ref, bf16[64,128,256]{2,1,0:T(8,128)(2,1)} %shard_map.151.weights_ref, bf16[16,64,128]{2,1,0:T(8,128)(2,1)} %get-tuple-element.39.refs_0_, bf16[16,64,128]{2,1,0:T(8,128)(2,1)} %copy-done.5, bf16[16,64,128]{2,1,0:T(8,128)(2,1)} %copy-done.7, ...), custom_call_target="tpu_custom_call" | custom-call | flops 536870912 | bytes 8388608 | tf_op jit(solution)/shard_map/pallas_call | solution.py:29
  162.2 3.6 %all-to-all-start.2 = ((bf16[8,512,128]{2,1,0:T(8,128)(2,1)}), bf16[8,512,128]{2,1,0:T(8,128)(2,1)S(1)}, u32[]{:S(2)}, u32[]{:S(2)}) async-start(bf16[8,512,128]{2,1,0:T(8,128)(2,1)} %shard_map.155), calls=%async_computation.2 | async-start | bytes 2097152 | tf_op jit(solution)/shard_map/all_to_all | solution.py:429
  165.8 2.1 %collective-permute-start.15 = (bf16[16,64,128]{2,1,0:T(8,128)(2,1)S(1)}, bf16[16,64,128]{2,1,0:T(8,128)(2,1)S(1)}, u32[]{:S(2)}, u32[]{:S(2)}) collective-permute-start(bf16[16,64,128]{2,1,0:T(8,128)(2,1)S(1)} %collective-permute-done.14.refs_2_), channel_id=1, source_target_pairs={{0,24},{8,0},{16,8},{24,16},{1,25},{9,1},{17,9},{25,17},{2,26},{10... | collective-permute-start | bytes 786440 | tf_op jit(solution)/shard_map/ppermute | solution.py:402
  167.9 6.5 %collective-permute-done.15.refs_3_ = bf16[16,64,128]{2,1,0:T(8,128)(2,1)S(1)} collective-permute-done((bf16[16,64,128]{2,1,0:T(8,128)(2,1)S(1)}, bf16[16,64,128]{2,1,0:T(8,128)(2,1)S(1)}, u32[]{:S(2)}, u32[]{:S(2)}) %collective-permute-start.15) | collective-permute-done | bytes 262176 | tf_op jit(solution)/shard_map/ppermute | solution.py:402
  174.4 0.7 copy-done.9
  175.1 6.3 %shard_map.156 = bf16[8,512,128]{2,1,0:T(8,128)(2,1)} custom-call(s32[64]{0:T(128)} %get-tuple-element.26.patch_ref, bf16[64,128,256]{2,1,0:T(8,128)(2,1)} %shard_map.151.weights_ref, bf16[16,64,128]{2,1,0:T(8,128)(2,1)} %get-tuple-element.40.refs_0_, bf16[16,64,128]{2,1,0:T(8,128)(2,1)} %copy-done.4, bf16[16,64,128]{2,1,0:T(8,128)(2,1)} %copy-done.6, ...), custom_call_target="tpu_custom_call" | custom-call | flops 536870912 | bytes 8388608 | tf_op jit(solution)/shard_map/pallas_call | solution.py:29
  181.4 18.8 %all_to_all.21.got1_ref = bf16[8,512,128]{2,1,0:T(8,128)(2,1)} all-to-all(bf16[8,512,128]{2,1,0:T(8,128)(2,1)} %shard_map.156), channel_id=1, replica_groups=mesh['orbits'=4,'rows'=2,'cols'=4] {'rows','cols'}, dimensions={0} | all-to-all | bytes 2097152 | tf_op jit(solution)/shard_map/all_to_all | solution.py:429
  200.2 4.1 %shard_map.157 = bf16[32,128,128]{2,1,0:T(8,128)(2,1)} custom-call(s32[32]{0:T(128)} %tile_ref.1, bf16[32,128,128]{2,1,0:T(8,128)(2,1)} %get-tuple-element.24.feat_ref, bf16[8,512,128]{2,1,0:T(8,128)(2,1)} %copy-done, bf16[8,512,128]{2,1,0:T(8,128)(2,1)} %all_to_all.21.got1_ref), custom_call_target="tpu_custom_call" | custom-call | flops 1000000 | bytes 4194304 | tf_op jit(solution)/shard_map/pallas_call | solution.py:29
  (39 shorter events, 0.5 us)
Async XLA Ops:
  28.4 23.7 %all-to-all-start.1 = ((bf16[8,512,128]{2,1,0:T(8,128)(2,1)}), bf16[8,512,128]{2,1,0:T(8,128)(2,1)S(1)}, u32[]{:S(2)}, u32[]{:S(2)}) async-start(bf16[8,512,128]{2,1,0:T(8,128)(2,1)} %get-tuple-element.30), calls=%async_computation.1 | async-start | bytes 2097152 | tf_op jit(solution)/shard_map/all_to_all | solution.py:429
  39.8 35.3 %copy-start.2 = (bf16[1040,128]{1,0:T(8,128)(2,1)S(1)}, bf16[1040,128]{1,0:T(8,128)(2,1)}, u32[]{:S(2)}) copy-start(bf16[1040,128]{1,0:T(8,128)(2,1)} %get-tuple-element.32) | copy-start | bytes 798724
  39.8 11.2 %collective-permute-start = (bf16[1040,128]{1,0:T(8,128)(2,1)}, bf16[1040,128]{1,0:T(8,128)(2,1)S(1)}, u32[]{:S(2)}, u32[]{:S(2)}) collective-permute-start(bf16[1040,128]{1,0:T(8,128)(2,1)} %get-tuple-element.28), channel_id=1, source_target_pairs={{0,8},{8,16},{16,24},{24,0},{1,9},{9,17},{17,25},{25,1},{2,10},{10... | collective-permute-start | bytes 798728 | tf_op jit(solution)/shard_map/ppermute | solution.py:402
  52.0 1.0 copy-start.1
  59.7 9.6 %collective-permute-start.3 = (bf16[1024,128]{1,0:T(8,128)(2,1)}, bf16[1024,128]{1,0:T(8,128)(2,1)S(1)}, u32[]{:S(2)}, u32[]{:S(2)}) collective-permute-start(bf16[1024,128]{1,0:T(8,128)(2,1)} %get-tuple-element.36), channel_id=1, source_target_pairs={{0,24},{8,0},{16,8},{24,16},{1,25},{9,1},{17,9},{25,17},{2,26},{10... | collective-permute-start | bytes 786440 | tf_op jit(solution)/shard_map/ppermute | solution.py:402
  61.4 13.6 %collective-permute-start.1 = (bf16[1040,128]{1,0:T(8,128)(2,1)S(1)}, bf16[1040,128]{1,0:T(8,128)(2,1)S(1)}, u32[]{:S(2)}, u32[]{:S(2)}) collective-permute-start(bf16[1040,128]{1,0:T(8,128)(2,1)S(1)} %add.12), channel_id=1, source_target_pairs={{0,8},{8,16},{16,24},{24,0},{1,9},{9,17},{17,25},{25,1},{2,10},{10... | collective-permute-start | bytes 798728 | tf_op jit(solution)/shard_map/ppermute | solution.py:402
  70.3 10.7 %collective-permute-start.4 = (bf16[1024,128]{1,0:T(8,128)(2,1)S(1)}, bf16[1024,128]{1,0:T(8,128)(2,1)S(1)}, u32[]{:S(2)}, u32[]{:S(2)}) collective-permute-start(bf16[1024,128]{1,0:T(8,128)(2,1)S(1)} %add.14), channel_id=1, source_target_pairs={{0,24},{8,0},{16,8},{24,16},{1,25},{9,1},{17,9},{25,17},{2,26},{10... | collective-permute-start | bytes 786440 | tf_op jit(solution)/shard_map/ppermute | solution.py:402
  75.1 11.6 %collective-permute-start.2 = (bf16[1040,128]{1,0:T(8,128)(2,1)S(1)}, bf16[1040,128]{1,0:T(8,128)(2,1)S(1)}, u32[]{:S(2)}, u32[]{:S(2)}) collective-permute-start(bf16[1040,128]{1,0:T(8,128)(2,1)S(1)} %add.13), channel_id=1, source_target_pairs={{0,8},{8,16},{16,24},{24,0},{1,9},{9,17},{17,25},{25,1},{2,10},{10... | collective-permute-start | bytes 798728 | tf_op jit(solution)/shard_map/ppermute | solution.py:402
  82.1 8.6 %collective-permute-start.5 = (bf16[1024,128]{1,0:T(8,128)(2,1)S(1)}, bf16[1024,128]{1,0:T(8,128)(2,1)S(1)}, u32[]{:S(2)}, u32[]{:S(2)}) collective-permute-start(bf16[1024,128]{1,0:T(8,128)(2,1)S(1)} %add.15), channel_id=1, source_target_pairs={{0,24},{8,0},{16,8},{24,16},{1,25},{9,1},{17,9},{25,17},{2,26},{10... | collective-permute-start | bytes 786440 | tf_op jit(solution)/shard_map/ppermute | solution.py:402
  86.7 4.0 %copy-start.3 = (bf16[1040,128]{1,0:T(8,128)(2,1)}, bf16[1040,128]{1,0:T(8,128)(2,1)S(1)}, u32[]{:S(2)}) copy-start(bf16[1040,128]{1,0:T(8,128)(2,1)S(1)} %collective-permute-done.2.sum0_ref) | copy-start | bytes 798724
  90.7 0.7 copy-start.10
  95.0 5.9 %collective-permute-start.6 = (bf16[2,128,128]{2,1,0:T(8,128)(2,1)S(1)}, bf16[2,128,128]{2,1,0:T(8,128)(2,1)S(1)}, u32[]{:S(2)}, u32[]{:S(2)}) collective-permute-start(bf16[2,128,128]{2,1,0:T(8,128)(2,1)S(1)} %get-tuple-element.49), channel_id=1, source_target_pairs={{0,4},{4,8},{8,12},{12,16},{16,20},{20,24},{24,28},{1,5},{5,9},{9,... | collective-permute-start | bytes 196616 | tf_op jit(solution)/shard_map/ppermute | solution.py:395
  99.5 6.2 %collective-permute-start.7 = (bf16[2,128,128]{2,1,0:T(8,128)(2,1)S(1)}, bf16[2,128,128]{2,1,0:T(8,128)(2,1)S(1)}, u32[]{:S(2)}, u32[]{:S(2)}) collective-permute-start(bf16[2,128,128]{2,1,0:T(8,128)(2,1)S(1)} %get-tuple-element.48), channel_id=1, source_target_pairs={{4,0},{8,4},{12,8},{16,12},{20,16},{24,20},{28,24},{5,1},{9,5},{13... | collective-permute-start | bytes 196616 | tf_op jit(solution)/shard_map/ppermute | solution.py:396
  100.8 10.1 %copy-start.11 = (bf16[2,128,128]{2,1,0:T(8,128)(2,1)}, bf16[2,128,128]{2,1,0:T(8,128)(2,1)S(1)}, u32[]{:S(2)}) copy-start(bf16[2,128,128]{2,1,0:T(8,128)(2,1)S(1)} %collective-permute-done.6.up_ref) | copy-start | bytes 196612
  105.7 5.2 %copy-start.12 = (bf16[2,128,128]{2,1,0:T(8,128)(2,1)}, bf16[2,128,128]{2,1,0:T(8,128)(2,1)S(1)}, u32[]{:S(2)}) copy-start(bf16[2,128,128]{2,1,0:T(8,128)(2,1)S(1)} %collective-permute-done.7.down_ref) | copy-start | bytes 196612
  105.7 4.4 %collective-permute-start.9 = (bf16[20,2,128]{2,1,0:T(2,128)(2,1)S(1)}, bf16[20,2,128]{2,1,0:T(2,128)(2,1)S(1)}, u32[]{:S(2)}, u32[]{:S(2)}) collective-permute-start(bf16[20,2,128]{2,1,0:T(2,128)(2,1)S(1)} %pad_maximum_fusion.1), channel_id=1, source_target_pairs={{1,0},{2,1},{3,2},{5,4},{6,5},{7,6},{9,8},{10,9},{11,10},{13,12},{... | collective-permute-start | bytes 30728 | tf_op jit(solution)/shard_map/ppermute | solution.py:396
  107.1 3.9 %collective-permute-start.8 = (bf16[20,2,128]{2,1,0:T(2,128)(2,1)S(1)}, bf16[20,2,128]{2,1,0:T(2,128)(2,1)S(1)}, u32[]{:S(2)}, u32[]{:S(2)}) collective-permute-start(bf16[20,2,128]{2,1,0:T(2,128)(2,1)S(1)} %pad_maximum_fusion), channel_id=1, source_target_pairs={{0,1},{1,2},{2,3},{4,5},{5,6},{6,7},{8,9},{9,10},{10,11},{12,13},{... | collective-permute-start | bytes 30728 | tf_op jit(solution)/shard_map/ppermute | solution.py:395
  110.1 0.8 copy-start.13
  110.9 0.6 copy-start.14
  117.6 11.2 %collective-permute-start.10 = (bf16[16,64,128]{2,1,0:T(8,128)(2,1)}, bf16[16,64,128]{2,1,0:T(8,128)(2,1)S(1)}, u32[]{:S(2)}, u32[]{:S(2)}) collective-permute-start(bf16[16,64,128]{2,1,0:T(8,128)(2,1)} %get-tuple-element.39.refs_0_), channel_id=1, source_target_pairs={{0,8},{8,16},{16,24},{24,0},{1,9},{9,17},{17,25},{25,1},{2,10},{10... | collective-permute-start | bytes 786440 | tf_op jit(solution)/shard_map/ppermute | solution.py:402
  117.7 14.8 %collective-permute-start.12 = (bf16[16,64,128]{2,1,0:T(8,128)(2,1)}, bf16[16,64,128]{2,1,0:T(8,128)(2,1)S(1)}, u32[]{:S(2)}, u32[]{:S(2)}) collective-permute-start(bf16[16,64,128]{2,1,0:T(8,128)(2,1)} %get-tuple-element.40.refs_0_), channel_id=1, source_target_pairs={{0,24},{8,0},{16,8},{24,16},{1,25},{9,1},{17,9},{25,17},{2,26},{10... | collective-permute-start | bytes 786440 | tf_op jit(solution)/shard_map/ppermute | solution.py:402
  128.9 27.0 %copy-start.5 = (bf16[16,64,128]{2,1,0:T(8,128)(2,1)}, bf16[16,64,128]{2,1,0:T(8,128)(2,1)S(1)}, u32[]{:S(2)}) copy-start(bf16[16,64,128]{2,1,0:T(8,128)(2,1)S(1)} %collective-permute-done.10.refs_1_) | copy-start | bytes 786436
  128.9 13.5 %collective-permute-start.11 = (bf16[16,64,128]{2,1,0:T(8,128)(2,1)S(1)}, bf16[16,64,128]{2,1,0:T(8,128)(2,1)S(1)}, u32[]{:S(2)}, u32[]{:S(2)}) collective-permute-start(bf16[16,64,128]{2,1,0:T(8,128)(2,1)S(1)} %collective-permute-done.10.refs_1_), channel_id=1, source_target_pairs={{0,8},{8,16},{16,24},{24,0},{1,9},{9,17},{17,25},{25,1},{2,10},{10... | collective-permute-start | bytes 786440 | tf_op jit(solution)/shard_map/ppermute | solution.py:402
  132.5 29.7 %copy-start.4 = (bf16[16,64,128]{2,1,0:T(8,128)(2,1)}, bf16[16,64,128]{2,1,0:T(8,128)(2,1)S(1)}, u32[]{:S(2)}) copy-start(bf16[16,64,128]{2,1,0:T(8,128)(2,1)S(1)} %collective-permute-done.12.refs_1_) | copy-start | bytes 786436
  142.4 13.4 %copy-start.7 = (bf16[16,64,128]{2,1,0:T(8,128)(2,1)}, bf16[16,64,128]{2,1,0:T(8,128)(2,1)S(1)}, u32[]{:S(2)}) copy-start(bf16[16,64,128]{2,1,0:T(8,128)(2,1)S(1)} %collective-permute-done.11.refs_2_) | copy-start | bytes 786436
  142.4 11.0 %collective-permute-start.13 = (bf16[16,64,128]{2,1,0:T(8,128)(2,1)S(1)}, bf16[16,64,128]{2,1,0:T(8,128)(2,1)S(1)}, u32[]{:S(2)}, u32[]{:S(2)}) collective-permute-start(bf16[16,64,128]{2,1,0:T(8,128)(2,1)S(1)} %collective-permute-done.11.refs_2_), channel_id=1, source_target_pairs={{0,8},{8,16},{16,24},{24,0},{1,9},{9,17},{17,25},{25,1},{2,10},{10... | collective-permute-start | bytes 786440 | tf_op jit(solution)/shard_map/ppermute | solution.py:402
  142.4 13.4 %collective-permute-start.14 = (bf16[16,64,128]{2,1,0:T(8,128)(2,1)S(1)}, bf16[16,64,128]{2,1,0:T(8,128)(2,1)S(1)}, u32[]{:S(2)}, u32[]{:S(2)}) collective-permute-start(bf16[16,64,128]{2,1,0:T(8,128)(2,1)S(1)} %collective-permute-done.12.refs_1_), channel_id=1, source_target_pairs={{0,24},{8,0},{16,8},{24,16},{1,25},{9,1},{17,9},{25,17},{2,26},{10... | collective-permute-start | bytes 786440 | tf_op jit(solution)/shard_map/ppermute | solution.py:402
  153.4 2.4 %copy-start.8 = (bf16[16,64,128]{2,1,0:T(8,128)(2,1)}, bf16[16,64,128]{2,1,0:T(8,128)(2,1)S(1)}, u32[]{:S(2)}) copy-start(bf16[16,64,128]{2,1,0:T(8,128)(2,1)S(1)} %collective-permute-done.13.refs_3_) | copy-start | bytes 786436
  155.8 9.9 %copy-start.6 = (bf16[16,64,128]{2,1,0:T(8,128)(2,1)}, bf16[16,64,128]{2,1,0:T(8,128)(2,1)S(1)}, u32[]{:S(2)}) copy-start(bf16[16,64,128]{2,1,0:T(8,128)(2,1)S(1)} %collective-permute-done.14.refs_2_) | copy-start | bytes 786436
  162.2 19.2 %all-to-all-start.2 = ((bf16[8,512,128]{2,1,0:T(8,128)(2,1)}), bf16[8,512,128]{2,1,0:T(8,128)(2,1)S(1)}, u32[]{:S(2)}, u32[]{:S(2)}) async-start(bf16[8,512,128]{2,1,0:T(8,128)(2,1)} %shard_map.155), calls=%async_computation.2 | async-start | bytes 2097152 | tf_op jit(solution)/shard_map/all_to_all | solution.py:429
  165.8 8.6 %collective-permute-start.15 = (bf16[16,64,128]{2,1,0:T(8,128)(2,1)S(1)}, bf16[16,64,128]{2,1,0:T(8,128)(2,1)S(1)}, u32[]{:S(2)}, u32[]{:S(2)}) collective-permute-start(bf16[16,64,128]{2,1,0:T(8,128)(2,1)S(1)} %collective-permute-done.14.refs_2_), channel_id=1, source_target_pairs={{0,24},{8,0},{16,8},{24,16},{1,25},{9,1},{17,9},{25,17},{2,26},{10... | collective-permute-start | bytes 786440 | tf_op jit(solution)/shard_map/ppermute | solution.py:402
  174.4 0.7 copy-start.9
  181.4 18.8 %copy-start = (bf16[8,512,128]{2,1,0:T(8,128)(2,1)}, bf16[8,512,128]{2,1,0:T(8,128)(2,1)S(1)}, u32[]{:S(2)}) copy-start(bf16[8,512,128]{2,1,0:T(8,128)(2,1)S(1)} %all-to-all-done.2.got0_ref) | copy-start | bytes 3145732

commit v4 on v3

v4 whole, which is shorter than its diff:
```python
import functools

import jax
import jax.numpy as jnp
from jax import lax
from jax.experimental import pallas as pl
from jax.experimental.pallas import tpu as pltpu
from jax.sharding import PartitionSpec as P

KN = 16
PH = 8
PW = 32
SR = 16
TC = 128
SIDE = 4
PAD = 8
META = 4
ACROSS = TC // PW
F32 = jnp.float32
BF16 = jnp.bfloat16

VMEM = pl.BlockSpec(memory_space=pltpu.VMEM)
SMEM = pl.BlockSpec(memory_space=pltpu.SMEM)
HBM = pl.BlockSpec(memory_space=pltpu.HBM)
LIMIT = 20 * 1024 * 1024
LARGE = 56 * 1024 * 1024


def call(kernel, in_specs, out_specs, out_shape, scratch, flops, moved, *args, limit=LIMIT):
    return pl.pallas_call(
        kernel,
        in_specs=in_specs,
        out_specs=out_specs,
        out_shape=out_shape,
        scratch_shapes=scratch,
        compiler_params=pltpu.CompilerParams(vmem_limit_bytes=limit),
        cost_estimate=pl.CostEstimate(flops=flops, bytes_accessed=moved, transcendentals=0),
    )(*args)


def silu(v):
    half = 0.5 * v
    return half + half * jnp.tanh(half)


def next_slot(tile_ref, count_ref, b):
    t = tile_ref[b]
    n = count_ref[t]
    count_ref[t] = n + 1
    return t, n


def clear(count_ref):
    for t in range(count_ref.shape[0]):
        count_ref[t] = 0


def embed_kernel(
    tile_hbm, patch_hbm, offset_hbm, cells_hbm, x_hbm, we_hbm, be_hbm, wp_hbm, bp_hbm,
    feat_ref, send_ref,
    tile_ref, patch_ref, offset_ref, cells_ref, x_ref, we_ref, be_ref, wp_ref, bp_ref,
    count_ref, meta_ref, sems, x_sems,
):
    blocks, size, channels = feat_ref.shape
    chunks = x_sems.shape[0]
    per = blocks // chunks
    tiles = send_ref.shape[0]
    meta_rows = meta_ref.shape[0] // tiles
    base = meta_rows // META * size
    pairs = (
        (we_hbm, we_ref), (be_hbm, be_ref), (wp_hbm, wp_ref), (bp_hbm, bp_ref), (tile_hbm, tile_ref),
        (patch_hbm, patch_ref), (offset_hbm, offset_ref), (cells_hbm.at[0:8], cells_ref),
    )
    copies = [pltpu.make_async_copy(a, b, sems.at[i]) for i, (a, b) in enumerate(pairs)]

    def fetch(c):
        rows = pl.ds(pl.multiple_of(c * per * size, per * size), per * size)
        return pltpu.make_async_copy(x_hbm.at[rows], x_ref.at[rows], x_sems.at[c])

    for copy in copies:
        copy.start()
    for c in range(chunks):
        fetch(c).start()
    clear(count_ref)
    send_ref[...] = jnp.zeros(send_ref.shape, BF16)
    row = lax.broadcasted_iota(jnp.int32, meta_ref.shape, 0) % META
    meta_ref[...] = jnp.where(row == 2, -65536.0, 0.0)
    for copy in copies:
        copy.wait()

    def chunk(c, unused):
        fetch(c).wait()
        rows = pl.ds(pl.multiple_of(c * per * size, per * size), per * size)
        hidden = silu(jnp.dot(x_ref[rows, :], we_ref[...], preferred_element_type=F32) + be_ref[...])
        out = jnp.dot(hidden.astype(BF16), wp_ref[...], preferred_element_type=F32) + bp_ref[...]
        out = out.astype(BF16)
        feat_ref[pl.ds(c * per, per)] = out.reshape(per, size, channels)
        for k in range(per):
            b = c * per + k
            t, n = next_slot(tile_ref, count_ref, b)
            send_ref[t, pl.ds(pl.multiple_of(n * size, size), size), :] = out[k * size : (k + 1) * size]
            first = t * meta_rows + n * META
            obs = pl.ds(pl.multiple_of(b * size, size), size)
            meta_ref[pl.ds(first, 2), :] = offset_ref[:, obs].astype(F32)
            meta_ref[pl.ds(first + 2, 1), :] = cells_ref[0:1, obs].astype(F32)
            meta_ref[pl.ds(first + 3, 1), :] = jnp.full((1, size), patch_ref[b], jnp.int32).astype(F32)
        return unused

    lax.fori_loop(0, chunks, chunk, 0)
    extra = send_ref.shape[1] - base - meta_rows
    for t in range(tiles):
        rows = meta_ref[t * meta_rows : (t + 1) * meta_rows, :]
        if extra:
            rows = jnp.concatenate([rows, jnp.zeros((extra, size), F32)], axis=0)
        send_ref[t, base:, :] = rows.astype(BF16)


def factors(meta, normal):
    off_row, off_col, corner = meta[0:1, :], meta[1:2, :], meta[2:3, :]
    first_row = jnp.floor(corner * (1.0 / PW))
    first_col = corner - first_row * PW

    def factor(count, start, off):
        at = lax.broadcasted_iota(jnp.int32, (count, meta.shape[1]), 0).astype(F32) - start
        delta = at - 1.5 - off
        value = jnp.exp(delta * delta * -0.5)
        return jnp.where((at >= 0.0) & (at < SIDE), value, 0.0)

    def total(off):
        at = lax.broadcasted_iota(jnp.int32, (SIDE, meta.shape[1]), 0).astype(F32)
        delta = at - 1.5 - off
        return jnp.sum(jnp.exp(delta * delta * -0.5), axis=0, keepdims=True)

    rows, cols = factor(PH, first_row, off_row), factor(PW, first_col, off_col)
    if normal:
        rows = rows / (total(off_row) * total(off_col))
    return rows, cols


def outer(rows, cols):
    return (rows[:, None, :] * cols[None, :, :]).reshape(PH * PW, rows.shape[1])


def place(patch):
    row, col = patch // ACROSS, lax.rem(patch, ACROSS)
    return pl.ds(pl.multiple_of(row * PH, PH), PH), pl.ds(pl.multiple_of(col * PW, PW), PW)


def stripe_at(k, way):
    orbits = lax.axis_size("orbits")
    return lax.rem(lax.axis_index("orbits") + way * (orbits - 1 - k) + orbits * orbits, orbits)


def spread_kernel(orbits, most, got_ref, *refs):
    up, down, (patch_ref, acc_ref, dens_ref) = refs[:orbits], refs[orbits : 2 * orbits], refs[2 * orbits :]
    size, channels = got_ref.shape[2], acc_ref.shape[2]
    acc_ref[...] = jnp.zeros(acc_ref.shape, F32)
    dens_ref[...] = jnp.zeros(dens_ref.shape, F32)
    base = most * size

    def tile(t, unused):
        metas = got_ref[t, base:, :].astype(F32)
        patches = [jnp.max(metas[n * META + 3 : n * META + 4, :]).astype(jnp.int32) for n in range(most)]
        for n in range(most):
            patch = patches[n]
            patch_ref[t * most + n] = patch
            rows, cols = factors(metas[n * META : (n + 1) * META], False)
            values = got_ref[t, n * size : (n + 1) * size, :]
            result = jnp.dot(outer(rows, cols).astype(BF16), values, preferred_element_type=F32)
            at_row, at_col = place(patch)
            acc_ref[at_row, at_col, :] += result.reshape(PH, PW, channels)
            dens_ref[patch] += lax.dot_general(
                rows.astype(BF16), cols.astype(BF16), (((1,), (1,)), ((), ())), preferred_element_type=F32
            )
        return unused

    lax.fori_loop(0, got_ref.shape[0], tile, 0)
    for k in range(orbits):
        for out_ref, way, band in ((up[k], 1, 0), (down[k], -1, 1)):
            rows = acc_ref[pl.ds(stripe_at(k, way) * SR + band * PH, PH)].astype(BF16)
            out_ref[0 : PH * TC, :] = rows.reshape(PH * TC, channels)
        bands = []
        for band in range(SR // PH):
            first = (stripe_at(k, 1) * (SR // PH) + band) * ACROSS
            bands.append(jnp.concatenate([dens_ref[first + c] for c in range(ACROSS)], axis=1))
        up[k][PH * TC :, :] = jnp.concatenate(bands, axis=0).astype(BF16)


def weights_kernel(most, got_ref, out_ref):
    base = most * got_ref.shape[2]

    def tile(t, unused):
        metas = got_ref[t, base:, :].astype(F32)
        for n in range(most):
            rows, cols = factors(metas[n * META : (n + 1) * META], True)
            out_ref[t * most + n] = outer(rows, cols).T.astype(BF16)
        return unused

    lax.fori_loop(0, got_ref.shape[0], tile, 0)


def grid_kernel(own0_ref, sum0_ref, own1_ref, sum1_ref, weight_ref, out_ref):
    channels = out_ref.shape[2]
    tail = slice(PH * TC, PH * TC + SR)
    density = (own0_ref[tail, :].astype(F32) + sum0_ref[tail, :].astype(F32)).T
    for i in range(SR):
        own_ref, sum_ref = (own0_ref, sum0_ref) if i < PH else (own1_ref, sum1_ref)
        at = slice(i % PH * TC, (i % PH + 1) * TC)
        spread = own_ref[at, :].astype(F32) + sum_ref[at, :].astype(F32)
        d = jnp.broadcast_to(density[:, i : i + 1], (TC, channels))
        out_ref[i] = (spread / jnp.maximum(d, 1.0) + weight_ref[...] * (d / (1.0 + d))).astype(BF16)


def conv_kernel(
    x_ref, up_ref, down_ref, left_ref, right_ref, w1_ref, b1_ref, w2_ref, b2_ref,
    out_ref, out0_ref, out1_ref, wide_ref, x16_ref, first_ref, wc1_ref, wc2_ref,
):
    channels = out_ref.shape[2]
    width = x16_ref.shape[1]
    for a in range(3):
        for b in range(3):
            at = (slice(a * channels, (a + 1) * channels), slice(b * channels, (b + 1) * channels))
            wc1_ref[at] = w1_ref[a, b]
            wc2_ref[at] = w2_ref[a, b]
    body = slice(PAD, PAD + TC)
    wide_ref[...] = jnp.zeros(wide_ref.shape, F32)
    wide_ref[0:2, body] = up_ref[...].astype(F32)
    wide_ref[2 : 2 + SR, body] = x_ref[...].astype(F32)
    wide_ref[2 + SR :, body] = down_ref[...].astype(F32)
    wide_ref[:, PAD - 2 : PAD] = left_ref[...].astype(F32)
    wide_ref[:, PAD + TC : PAD + TC + 2] = right_ref[...].astype(F32)
    x16_ref[...] = wide_ref[...].astype(BF16)

    def taps(source, first, count, weights):
        rows = [source[pl.ds(first + a, count)].reshape(count * width, channels) for a in range(3)]
        all_taps = jnp.dot(jnp.concatenate(rows, axis=1), weights[...], preferred_element_type=F32)
        return (
            pltpu.roll(all_taps[:, :channels], 1, 0)
            + all_taps[:, channels : 2 * channels]
            + pltpu.roll(all_taps[:, 2 * channels :], count * width - 1, 0)
        )

    at_row, at_col = lax.axis_index(("orbits", "rows")), lax.axis_index("cols")
    col = lax.broadcasted_iota(jnp.int32, (width, channels), 0)
    first_col = jnp.where(at_col > 0, PAD - 1, PAD)
    last_col = jnp.where(at_col < lax.axis_size("cols") - 1, PAD + TC, PAD + TC - 1)
    inside = (col >= first_col) & (col <= last_col)
    first_row = jnp.where(at_row > 0, 0, 1)
    last_row = jnp.where(at_row < lax.axis_size(("orbits", "rows")) - 1, SR + 1, SR)
    count = (SR + 2) // 3

    def first_rows(i, unused):
        value = silu(taps(x16_ref, i * count, count, wc1_ref) + b1_ref[...])
        for r in range(count):
            row = i * count + r
            keep = inside & (row >= first_row) & (row <= last_row)
            first_ref[row] = jnp.where(keep, value[r * width : (r + 1) * width], 0.0).astype(BF16)
        return unused

    lax.fori_loop(0, 3, first_rows, 0)
    again = PH

    def second_rows(i, band_ref):
        values = taps(first_ref, i * again, again, wc2_ref) + b2_ref[...]
        for r in range(again):
            row = i * again + r
            value = values[r * width + PAD : r * width + PAD + TC] + x_ref[row].astype(F32)
            out_ref[row] = value.astype(BF16)
            band_ref[r] = value.astype(BF16)

    second_rows(0, out0_ref)
    second_rows(1, out1_ref)


def read_kernel(orbits, most, patch_ref, weights_ref, *refs):
    up, down, (out_ref, grid_ref) = refs[:orbits], refs[orbits : 2 * orbits], refs[2 * orbits :]
    size = out_ref.shape[2]
    for k in range(orbits):
        for piece_ref, way, band in ((up[k], 1, 0), (down[k], -1, 1)):
            grid_ref[pl.ds(stripe_at(orbits - 1 - k, -way) * SR + band * PH, PH)] = piece_ref[...]

    def tile(t, unused):
        for n in range(most):
            at_row, at_col = place(patch_ref[t * most + n])
            values = grid_ref[at_row, at_col, :].reshape(PH * PW, grid_ref.shape[2])
            result = jnp.dot(weights_ref[t * most + n], values, preferred_element_type=F32)
            out_ref[t, n * size : (n + 1) * size, :] = result.astype(BF16)
        return unused

    lax.fori_loop(0, out_ref.shape[0], tile, 0)


def final_kernel(tile_ref, feat_ref, got_ref, out_ref, count_ref):
    blocks, size, _ = feat_ref.shape
    clear(count_ref)
    per = 4

    def chunk(c, unused):
        for k in range(per):
            b = c * per + k
            t, n = next_slot(tile_ref, count_ref, b)
            mine = got_ref[t, pl.ds(pl.multiple_of(n * size, size), size), :]
            out_ref[b] = (feat_ref[b].astype(F32) + mine.astype(F32)).astype(BF16)
        return unused

    lax.fori_loop(0, blocks // per, chunk, 0)


def shifts(axis):
    size = lax.axis_size(axis)
    up = [(i, i + 1) for i in range(size - 1)]
    return up, [(j, i) for i, j in up]


def halo(x, axis, dim, width):
    up, down = shifts(axis)
    length = x.shape[dim]
    before = lax.ppermute(lax.slice_in_dim(x, length - width, length, axis=dim), axis, up)
    after = lax.ppermute(lax.slice_in_dim(x, 0, width, axis=dim), axis, down)
    return before, after


def turn(x, way):
    size = lax.axis_size("orbits")
    return lax.ppermute(x, "orbits", [(i, (i + way) % size) for i in range(size)])


def ring_sum(stripes, way):
    total = stripes[0]
    for k in range(1, len(stripes)):
        total = turn(total, way)
        if k < len(stripes) - 1:
            total = total + stripes[k]
    return total


def ring_gather(x, way):
    pieces = [x]
    for _ in range(lax.axis_size("orbits") - 1):
        pieces.append(turn(pieces[-1], way))
    return pieces


def local(
    obs_feat, obs_offset, obs_cells, block_tile, block_patch, w_embed, b_embed, w_proj, b_proj,
    density_weight, w_first, b_first, w_second, b_second,
):
    channels = obs_feat.shape[1]
    blocks = block_tile.shape[0]
    size = obs_feat.shape[0] // blocks
    plane = ("rows", "cols")
    tiles = lax.axis_size(plane)
    orbits = lax.axis_size("orbits")
    most = max(2, 2 * blocks // tiles)
    slots = tiles * most
    height = orbits * SR
    patches = height // PH * ACROSS
    length = most * size
    meta_rows = max(16, most * META)
    chunks = blocks // 4
    counts = pltpu.SMEM((tiles,), jnp.int32)
    shape = jax.ShapeDtypeStruct
    bias = lambda b: b.reshape(1, channels)
    exchange = lambda x: lax.all_to_all(x, plane, split_axis=0, concat_axis=0, tiled=True)
    vmem = lambda a: pltpu.VMEM(a.shape, a.dtype)

    b_embed, b_proj = bias(b_embed), bias(b_proj)
    features, send = call(
        embed_kernel,
        [HBM] * 9,
        [VMEM] * 2,
        (shape((blocks, size, channels), BF16), shape((tiles, length + meta_rows, channels), BF16)),
        [
            pltpu.SMEM((blocks,), jnp.int32),
            pltpu.SMEM((blocks,), jnp.int32),
            vmem(obs_offset),
            pltpu.VMEM((8, obs_cells.shape[1]), jnp.int32),
            vmem(obs_feat),
            vmem(w_embed),
            vmem(b_embed),
            vmem(w_proj),
            vmem(b_proj),
            counts,
            pltpu.VMEM((slots * META, size), F32),
            pltpu.SemaphoreType.DMA((8,)),
            pltpu.SemaphoreType.DMA((chunks,)),
        ],
        6 * obs_feat.size * channels,
        8 * obs_feat.size,
        block_tile, block_patch, obs_offset, obs_cells, obs_feat, w_embed, b_embed, w_proj, b_proj,
        limit=LARGE,
    )
    got = exchange(send)

    flops = 2 * slots * size * channels * PH * PW
    band_shape = shape((PH * TC, channels), BF16)
    dense_shape = shape((PH * TC + SR, channels), BF16)
    *bands, patch_of = call(
        functools.partial(spread_kernel, orbits, most),
        [VMEM],
        [VMEM] * (2 * orbits) + [SMEM],
        [dense_shape] * orbits + [band_shape] * orbits + [shape((slots,), jnp.int32)],
        [pltpu.VMEM((height, TC, channels), F32), pltpu.VMEM((patches, PH, PW), F32)],
        flops,
        8 * slots * size * channels,
        got,
    )
    bands0, bands1 = bands[:orbits], bands[orbits:]
    sum0, sum1 = ring_sum(bands0, 1), ring_sum(bands1, -1)
    weights = call(
        functools.partial(weights_kernel, most),
        [VMEM],
        VMEM,
        shape((slots, size, PH * PW), BF16),
        [],
        flops,
        4 * slots * size * channels,
        got,
    )
    grid_in = call(
        grid_kernel,
        [VMEM] * 5,
        VMEM,
        shape((SR, TC, channels), BF16),
        [],
        10000000,
        8 * SR * TC * channels,
        bands0[-1], sum0, bands1[-1], sum1, bias(density_weight),
    )

    above, below = halo(grid_in, ("orbits", "rows"), 0, 2)
    extended = jnp.concatenate(
        [
            jnp.concatenate([above[:, c], grid_in[:, c], below[:, c]], axis=0)
            for c in (slice(0, 2), slice(TC - 2, TC))
        ],
        axis=1,
    )
    left, right = halo(extended, "cols", 1, 2)
    width = TC + 2 * PAD
    grid_out, band0, band1 = call(
        conv_kernel,
        [VMEM] * 9,
        [VMEM] * 3,
        [shape((SR, TC, channels), BF16)] + [shape((PH, TC, channels), BF16)] * 2,
        [
            pltpu.VMEM((SR + 4, width, channels), F32),
            pltpu.VMEM((SR + 4, width, channels), BF16),
            pltpu.VMEM((SR + 2, width, channels), BF16),
            pltpu.VMEM((3 * channels, 3 * channels), BF16),
            pltpu.VMEM((3 * channels, 3 * channels), BF16),
        ],
        4 * 9 * SR * TC * channels * channels,
        8 * grid_in.size,
        grid_in, above, below, left, right, w_first, bias(b_first), w_second, bias(b_second),
    )

    readings = call(
        functools.partial(read_kernel, orbits, most),
        [SMEM, VMEM] + [VMEM] * (2 * orbits),
        VMEM,
        shape((tiles, length, channels), BF16),
        [pltpu.VMEM((height, TC, channels), BF16)],
        flops,
        8 * slots * size * channels,
        patch_of, weights, *ring_gather(band0, 1), *ring_gather(band1, -1),
    )
    back = exchange(readings)
    obs_out = call(
        final_kernel,
        [SMEM] + [VMEM] * 2,
        VMEM,
        shape((blocks, size, channels), BF16),
        [counts],
        1000000,
        8 * obs_feat.size,
        block_tile, features, back,
    )
    return obs_out.reshape(obs_feat.shape), grid_out


def solution(mesh):
    spread_out = ("orbits", "rows", "cols")
    in_specs = (
        P(spread_out, None),
        P(None, spread_out),
        P(None, spread_out),
        P(spread_out),
        P(spread_out),
    ) + (P(),) * 9
    out_specs = (P(spread_out, None), P(("orbits", "rows"), "cols", None))
    return jax.shard_map(local, mesh=mesh, in_specs=in_specs, out_specs=out_specs, check_vma=False)
```

time: 205 us -> 175 us (0.85)
  Pallas kernels: 51.9 us -> 22 us
  blocking collectives: 40.2 us -> 62.3 us
  starting transfers between devices: 39.2 us -> 23 us
  local copies, waits for them, and re-layouts: 4.68 us -> 0.07 us
  other arithmetic: 3.18 us -> 0.33 us
  waiting for transfers between devices: 64.3 us -> 66.5 us
    pallas_call x9 -> x7, Pallas kernels: 51.9 us -> 22 us  [call(): pl.pallas_call(kernel, in_specs=in_specs, out_specs=out_specs, out_shape=...]
    all_to_all x2, blocking collectives: 40.2 us -> 62.3 us  [local(): lax.all_to_all(x, plane, split_axis=0, concat_axis=0, tiled=True)]
    ppermute x12, starting transfers between devices: 22.8 us -> 14.6 us  [turn(): lax.ppermute(x, 'orbits', [(i, (i + way) % size) for i in range(size)])]
    all_to_all x2 -> x0, starting transfers between devices: 7.12 us -> none  [local(): lax.all_to_all(x, plane, split_axis=0, concat_axis=0, tiled=True)]
    unnamed x30 -> x14, local copies, waits for them, and re-layouts: 2.99 us -> 0.03 us
    add x4, other arithmetic: 3.14 us -> 0.29 us  [ring_sum(): total = total + stripes[k]]
    ppermute x12, waiting for transfers between devices: 58.6 us -> 61.4 us  [turn(): lax.ppermute(x, 'orbits', [(i, (i + way) % size) for i in range(size)])]
  transfers between devices with their start and end apart: 18 -> 16, of which waited for: 14 -> 14; matrix products, arithmetic and copies ran while one was open for 2% -> 0% of each run, Pallas kernels for 10% -> 1%
where the time goes in v4:
time: 175 us
  waiting for transfers between devices  66.5 us (38%)
  blocking collectives  62.3 us (36%)
  starting transfers between devices  23 us (13%)
  Pallas kernels  22 us (13%)
    all_to_all x2, blocking collectives, local(): lax.all_to_all(x, plane, split_axis=0, concat_axis=0, tiled=True)  62.3 us
    ppermute x12, waiting for transfers between devices, turn(): lax.ppermute(x, 'orbits', [(i, (i + way) % size) for i in range(size)])  61.4 us
    pallas_call x7, Pallas kernels, call(): pl.pallas_call(kernel, in_specs=in_specs, out_specs=out_specs, out_shape=...  22 us
    ppermute x12, starting transfers between devices, turn(): lax.ppermute(x, 'orbits', [(i, (i + way) % size) for i in range(size)])  14.6 us
    ppermute x2, starting transfers between devices, halo(): lax.ppermute(lax.slice_in_dim(x, length - width, length, axis=dim), axis,...  5.84 us
    ppermute x2, waiting for transfers between devices, halo(): after = lax.ppermute(lax.slice_in_dim(x, 0, width, axis=dim), axis, down)  3.51 us
  transfers between devices with their start and end apart: 16, of which 14 were waited for; matrix products, arithmetic and copies ran while one was open for 0% of the time, Pallas kernels for 1%

profile of v4, /device:TPU:0, one launch (start us, length us, event | category | flops | bytes accessed | tf_op | source)
XLA Modules:
  0.0 175.1 jit_solution(17056571993547468472)
XLA Ops:
  0.6 5.9 %shard_map.149 = (bf16[32,128,128]{2,1,0:T(8,128)(2,1)}, bf16[8,1056,128]{2,1,0:T(8,128)(2,1)}) custom-call(s32[32]{0:T(128)} %tile_ref.1, s32[32]{0:T(128)} %patch_hbm.1, bf16[2,4096]{1,0:T(2,128)(2,1)} %offset_hbm.1, s32[16,4096]{1,0:T(8,128)} %cells_hbm.1, bf16[4096,128]{1,0:T(8,128)(2,1)} %x_hbm.1, bf16[128,128]{1,0:T(8,128)(2,1)} %we_hbm.1, ...), custom_call_target="tpu_custom_call" | custom-call | flops 402653184 | bytes 4194304 | tf_op jit(solution)/shard_map/pallas_call | solution.py:30
  6.5 32.7 %all_to_all.10.got_ref = bf16[8,1056,128]{2,1,0:T(8,128)(2,1)S(1)} all-to-all(bf16[8,1056,128]{2,1,0:T(8,128)(2,1)} %get-tuple-element.17), channel_id=1, replica_groups=mesh['orbits'=4,'rows'=2,'cols'=4] {'rows','cols'}, dimensions={0} | all-to-all | bytes 4325376 | tf_op jit(solution)/shard_map/all_to_all | solution.py:364
  39.2 4.0 %shard_map.150 = (bf16[1040,128]{1,0:T(8,128)(2,1)S(1)}, bf16[1040,128]{1,0:T(8,128)(2,1)S(1)}, bf16[1040,128]{1,0:T(8,128)(2,1)S(1)}, bf16[1040,128]{1,0:T(8,12...) custom-call(bf16[8,1056,128]{2,1,0:T(8,128)(2,1)S(1)} %all_to_all.10, ...), custom_call_target="tpu_custom_call" | custom-call | flops 536870912 | bytes 8388608 | tf_op jit(solution)/shard_map/pallas_call | solution.py:30
  43.2 1.6 collective-permute-start
  44.8 2.2 %collective-permute-start.3 = (bf16[1024,128]{1,0:T(8,128)(2,1)S(1)}, bf16[1024,128]{1,0:T(8,128)(2,1)S(1)}, u32[]{:S(2)}, u32[]{:S(2)}) collective-permute-start(bf16[1024,128]{1,0:T(8,128)(2,1)S(1)} %get-tuple-element.24), channel_id=1, source_target_pairs={{0,24},{8,0},{16,8},{24,16},{1,25},{9,1},{17,9},{25,17},{2,26},{10... | collective-permute-start | bytes 786440 | tf_op jit(solution)/shard_map/ppermute | solution.py:325
  47.1 7.3 %collective-permute-done = bf16[1040,128]{1,0:T(8,128)(2,1)S(1)} collective-permute-done((bf16[1040,128]{1,0:T(8,128)(2,1)S(1)}, bf16[1040,128]{1,0:T(8,128)(2,1)S(1)}, u32[]{:S(2)}, u32[]{:S(2)}) %collective-permute-start) | collective-permute-done | bytes 266272 | tf_op jit(solution)/shard_map/ppermute | solution.py:325
  54.4 0.1 add.12
  54.5 0.1 collective-permute-start.1
  54.5 4.3 %collective-permute-done.3 = bf16[1024,128]{1,0:T(8,128)(2,1)S(1)} collective-permute-done((bf16[1024,128]{1,0:T(8,128)(2,1)S(1)}, bf16[1024,128]{1,0:T(8,128)(2,1)S(1)}, u32[]{:S(2)}, u32[]{:S(2)}) %collective-permute-start.3) | collective-permute-done | bytes 262176 | tf_op jit(solution)/shard_map/ppermute | solution.py:325
  58.8 0.1 add.14
  58.9 2.9 %collective-permute-start.4 = (bf16[1024,128]{1,0:T(8,128)(2,1)S(1)}, bf16[1024,128]{1,0:T(8,128)(2,1)S(1)}, u32[]{:S(2)}, u32[]{:S(2)}) collective-permute-start(bf16[1024,128]{1,0:T(8,128)(2,1)S(1)} %add.14), channel_id=1, source_target_pairs={{0,24},{8,0},{16,8},{24,16},{1,25},{9,1},{17,9},{25,17},{2,26},{10... | collective-permute-start | bytes 786440 | tf_op jit(solution)/shard_map/ppermute | solution.py:325
  61.7 5.1 %collective-permute-done.1 = bf16[1040,128]{1,0:T(8,128)(2,1)S(1)} collective-permute-done((bf16[1040,128]{1,0:T(8,128)(2,1)S(1)}, bf16[1040,128]{1,0:T(8,128)(2,1)S(1)}, u32[]{:S(2)}, u32[]{:S(2)}) %collective-permute-start.1) | collective-permute-done | bytes 266272 | tf_op jit(solution)/shard_map/ppermute | solution.py:325
  66.9 0.1 add.13
  66.9 1.2 collective-permute-start.2
  68.1 4.3 %collective-permute-done.4 = bf16[1024,128]{1,0:T(8,128)(2,1)S(1)} collective-permute-done((bf16[1024,128]{1,0:T(8,128)(2,1)S(1)}, bf16[1024,128]{1,0:T(8,128)(2,1)S(1)}, u32[]{:S(2)}, u32[]{:S(2)}) %collective-permute-start.4) | collective-permute-done | bytes 262176 | tf_op jit(solution)/shard_map/ppermute | solution.py:325
  72.5 0.1 add.15
  72.5 0.5 collective-permute-start.5
  73.1 9.6 %collective-permute-done.5.sum1_ref = bf16[1024,128]{1,0:T(8,128)(2,1)S(1)} collective-permute-done((bf16[1024,128]{1,0:T(8,128)(2,1)S(1)}, bf16[1024,128]{1,0:T(8,128)(2,1)S(1)}, u32[]{:S(2)}, u32[]{:S(2)}) %collective-permute-start.5) | collective-permute-done | bytes 262176 | tf_op jit(solution)/shard_map/ppermute | solution.py:325
  82.7 0.0 collective-permute-done.2.sum0_ref
  82.7 0.5 shard_map.152.x_ref
  83.2 1.3 collective-permute-start.7
  84.5 4.5 %collective-permute-start.6 = (bf16[2,128,128]{2,1,0:T(8,128)(2,1)S(1)}, bf16[2,128,128]{2,1,0:T(8,128)(2,1)S(1)}, u32[]{:S(2)}, u32[]{:S(2)}) collective-permute-start(bf16[2,128,128]{2,1,0:T(8,128)(2,1)S(1)} %get-tuple-element.33), channel_id=1, source_target_pairs={{0,4},{4,8},{8,12},{12,16},{16,20},{20,24},{24,28},{1,5},{5,9},{9,... | collective-permute-start | bytes 196616 | tf_op jit(solution)/shard_map/ppermute | solution.py:318
  89.1 0.3 collective-permute-done.7.down_ref
  89.4 1.6 collective-permute-done.6.up_ref
  91.0 1.3 collective-permute-start.8
  92.3 1.3 collective-permute-start.9
  93.6 0.0 collective-permute-done.8.left_ref
  93.7 3.2 %collective-permute-done.9.right_ref = bf16[20,2,128]{2,1,0:T(2,128)(2,1)S(1)} collective-permute-done((bf16[20,2,128]{2,1,0:T(2,128)(2,1)S(1)}, bf16[20,2,128]{2,1,0:T(2,128)(2,1)S(1)}, u32[]{:S(2)}, u32[]{:S(2)}) %collective-permute-start.9) | collective-permute-done | bytes 10272 | tf_op jit(solution)/shard_map/ppermute | solution.py:319
  96.9 0.0 copy-done.3
  96.9 4.4 %shard_map.153 = (bf16[16,128,128]{2,1,0:T(8,128)(2,1)}, bf16[8,128,128]{2,1,0:T(8,128)(2,1)S(1)}, bf16[8,128,128]{2,1,0:T(8,128)(2,1)S(1)}) custom-call(bf16[16,128,128]{2,1,0:T(8,128)(2,1)S(1)} %shard_map.152.x_ref, bf16[2,128,128]{2,1,0:T(8,128)(2,1)S(1)} %collective-permute-done.6.up_ref, bf16[2,128,128]{2,1,0:T(8,128)(2,1)S(1)} %collective-permute-done.7.down_ref, ...), custom_call_target="tpu_custom_call" | custom-call | flops 1207959552 | bytes 2097152 | tf_op jit(solution)/shard_map/pallas_call | solution.py:30
  101.3 2.8 %collective-permute-start.10 = (bf16[8,128,128]{2,1,0:T(8,128)(2,1)S(1)}, bf16[8,128,128]{2,1,0:T(8,128)(2,1)S(1)}, u32[]{:S(2)}, u32[]{:S(2)}) collective-permute-start(bf16[8,128,128]{2,1,0:T(8,128)(2,1)S(1)} %get-tuple-element.27.refs_0_), channel_id=1, source_target_pairs={{0,8},{8,16},{16,24},{24,0},{1,9},{9,17},{17,25},{25,1},{2,10},{10... | collective-permute-start | bytes 786440 | tf_op jit(solution)/shard_map/ppermute | solution.py:325
  104.1 1.0 collective-permute-start.13
  105.1 5.8 %collective-permute-done.10.refs_1_ = bf16[8,128,128]{2,1,0:T(8,128)(2,1)S(1)} collective-permute-done((bf16[8,128,128]{2,1,0:T(8,128)(2,1)S(1)}, bf16[8,128,128]{2,1,0:T(8,128)(2,1)S(1)}, u32[]{:S(2)}, u32[]{:S(2)}) %collective-permute-start.10) | collective-permute-done | bytes 262176 | tf_op jit(solution)/shard_map/ppermute | solution.py:325
  110.9 0.9 collective-permute-start.11
  111.8 7.3 %collective-permute-done.13.refs_5_ = bf16[8,128,128]{2,1,0:T(8,128)(2,1)S(1)} collective-permute-done((bf16[8,128,128]{2,1,0:T(8,128)(2,1)S(1)}, bf16[8,128,128]{2,1,0:T(8,128)(2,1)S(1)}, u32[]{:S(2)}, u32[]{:S(2)}) %collective-permute-start.13) | collective-permute-done | bytes 262176 | tf_op jit(solution)/shard_map/ppermute | solution.py:325
  119.1 0.3 collective-permute-start.14
  119.3 2.7 %collective-permute-done.11.refs_2_ = bf16[8,128,128]{2,1,0:T(8,128)(2,1)S(1)} collective-permute-done((bf16[8,128,128]{2,1,0:T(8,128)(2,1)S(1)}, bf16[8,128,128]{2,1,0:T(8,128)(2,1)S(1)}, u32[]{:S(2)}, u32[]{:S(2)}) %collective-permute-start.11) | collective-permute-done | bytes 262176 | tf_op jit(solution)/shard_map/ppermute | solution.py:325
  122.0 1.1 collective-permute-start.12
  123.1 7.6 %collective-permute-done.14.refs_6_ = bf16[8,128,128]{2,1,0:T(8,128)(2,1)S(1)} collective-permute-done((bf16[8,128,128]{2,1,0:T(8,128)(2,1)S(1)}, bf16[8,128,128]{2,1,0:T(8,128)(2,1)S(1)}, u32[]{:S(2)}, u32[]{:S(2)}) %collective-permute-start.14) | collective-permute-done | bytes 262176 | tf_op jit(solution)/shard_map/ppermute | solution.py:325
  130.7 0.0 collective-permute-start.15
  130.7 2.3 %shard_map.151.weights_ref = bf16[64,128,256]{2,1,0:T(8,128)(2,1)S(1)} custom-call(bf16[8,1056,128]{2,1,0:T(8,128)(2,1)S(1)} %all_to_all.10.got_ref), custom_call_target="tpu_custom_call" | custom-call | flops 536870912 | bytes 4194304 | tf_op jit(solution)/shard_map/pallas_call | solution.py:30
  133.0 0.3 collective-permute-done.12.refs_3_
  133.3 7.1 %collective-permute-done.15.refs_7_ = bf16[8,128,128]{2,1,0:T(8,128)(2,1)S(1)} collective-permute-done((bf16[8,128,128]{2,1,0:T(8,128)(2,1)S(1)}, bf16[8,128,128]{2,1,0:T(8,128)(2,1)S(1)}, u32[]{:S(2)}, u32[]{:S(2)}) %collective-permute-start.15) | collective-permute-done | bytes 262176 | tf_op jit(solution)/shard_map/ppermute | solution.py:325
  140.4 3.1 %shard_map.154 = bf16[8,1024,128]{2,1,0:T(8,128)(2,1)S(1)} custom-call(s32[64]{0:T(128)S(1)} %get-tuple-element.18.patch_ref, bf16[64,128,256]{2,1,0:T(8,128)(2,1)S(1)} %shard_map.151.weights_ref, bf16[8,128,128]{2,1,0:T(8,128)(2,1)S(1)} %get-tuple-element.27.refs_0_, bf16[8,128,128]{2,1,0:T(8,128)(2,1)S(1)} %collective-permute-done.10.refs_1_, ...), custom_call_target="tpu_custom_call" | custom-call | flops 536870912 | bytes 8388608 | tf_op jit(solution)/shard_map/pallas_call | solution.py:30
  143.6 0.0 copy-start
  143.6 0.0 copy-start.2
  143.6 29.6 %all_to_all.11.got_ref = bf16[8,1024,128]{2,1,0:T(8,128)(2,1)S(1)} all-to-all(bf16[8,1024,128]{2,1,0:T(8,128)(2,1)S(1)} %shard_map.154), channel_id=1, replica_groups=mesh['orbits'=4,'rows'=2,'cols'=4] {'rows','cols'}, dimensions={0} | all-to-all | bytes 4194304 | tf_op jit(solution)/shard_map/all_to_all | solution.py:364
  173.2 1.8 %shard_map.155 = bf16[32,128,128]{2,1,0:T(8,128)(2,1)} custom-call(s32[32]{0:T(128)S(1)} %copy-done.2, bf16[32,128,128]{2,1,0:T(8,128)(2,1)S(1)} %copy-done, bf16[8,1024,128]{2,1,0:T(8,128)(2,1)S(1)} %all_to_all.11.got_ref), custom_call_target="tpu_custom_call" | custom-call | flops 1000000 | bytes 4194304 | tf_op jit(solution)/shard_map/pallas_call | solution.py:30
  (17 shorter events, 0.1 us)
Async XLA Ops:
  39.2 43.5 %copy-start.1 = (f32[128]{0:T(128)S(1)}, f32[128]{0:T(128)}, u32[]{:S(2)}) copy-start(f32[128]{0:T(128)} %param.23) | copy-start | bytes 1540
  43.2 11.2 %collective-permute-start = (bf16[1040,128]{1,0:T(8,128)(2,1)S(1)}, bf16[1040,128]{1,0:T(8,128)(2,1)S(1)}, u32[]{:S(2)}, u32[]{:S(2)}) collective-permute-start(bf16[1040,128]{1,0:T(8,128)(2,1)S(1)} %get-tuple-element.20), channel_id=1, source_target_pairs={{0,8},{8,16},{16,24},{24,0},{1,9},{9,17},{17,25},{25,1},{2,10},{10... | collective-permute-start | bytes 798728 | tf_op jit(solution)/shard_map/ppermute | solution.py:325
  44.8 14.0 %collective-permute-start.3 = (bf16[1024,128]{1,0:T(8,128)(2,1)S(1)}, bf16[1024,128]{1,0:T(8,128)(2,1)S(1)}, u32[]{:S(2)}, u32[]{:S(2)}) collective-permute-start(bf16[1024,128]{1,0:T(8,128)(2,1)S(1)} %get-tuple-element.24), channel_id=1, source_target_pairs={{0,24},{8,0},{16,8},{24,16},{1,25},{9,1},{17,9},{25,17},{2,26},{10... | collective-permute-start | bytes 786440 | tf_op jit(solution)/shard_map/ppermute | solution.py:325
  54.5 12.4 %collective-permute-start.1 = (bf16[1040,128]{1,0:T(8,128)(2,1)S(1)}, bf16[1040,128]{1,0:T(8,128)(2,1)S(1)}, u32[]{:S(2)}, u32[]{:S(2)}) collective-permute-start(bf16[1040,128]{1,0:T(8,128)(2,1)S(1)} %add.12), channel_id=1, source_target_pairs={{0,8},{8,16},{16,24},{24,0},{1,9},{9,17},{17,25},{25,1},{2,10},{10... | collective-permute-start | bytes 798728 | tf_op jit(solution)/shard_map/ppermute | solution.py:325
  58.8 38.1 %copy-start.3 = (bf16[3,3,128,128]{3,2,1,0:T(8,128)(2,1)S(1)}, bf16[3,3,128,128]{3,2,1,0:T(8,128)(2,1)}, u32[]{:S(2)}) copy-start(bf16[3,3,128,128]{3,2,1,0:T(8,128)(2,1)} %w1_ref.1) | copy-start | bytes 884740
  58.8 38.1 %copy-start.4 = (bf16[3,3,128,128]{3,2,1,0:T(8,128)(2,1)S(1)}, bf16[3,3,128,128]{3,2,1,0:T(8,128)(2,1)}, u32[]{:S(2)}) copy-start(bf16[3,3,128,128]{3,2,1,0:T(8,128)(2,1)} %w2_ref.1) | copy-start | bytes 884740
  58.8 38.1 %copy-start.5 = (f32[128]{0:T(128)S(1)}, f32[128]{0:T(128)}, u32[]{:S(2)}) copy-start(f32[128]{0:T(128)} %param.25) | copy-start | bytes 1540
  58.8 38.1 %copy-start.6 = (f32[128]{0:T(128)S(1)}, f32[128]{0:T(128)}, u32[]{:S(2)}) copy-start(f32[128]{0:T(128)} %param.27) | copy-start | bytes 1540
  58.9 13.6 %collective-permute-start.4 = (bf16[1024,128]{1,0:T(8,128)(2,1)S(1)}, bf16[1024,128]{1,0:T(8,128)(2,1)S(1)}, u32[]{:S(2)}, u32[]{:S(2)}) collective-permute-start(bf16[1024,128]{1,0:T(8,128)(2,1)S(1)} %add.14), channel_id=1, source_target_pairs={{0,24},{8,0},{16,8},{24,16},{1,25},{9,1},{17,9},{25,17},{2,26},{10... | collective-permute-start | bytes 786440 | tf_op jit(solution)/shard_map/ppermute | solution.py:325
  66.9 15.7 %collective-permute-start.2 = (bf16[1040,128]{1,0:T(8,128)(2,1)S(1)}, bf16[1040,128]{1,0:T(8,128)(2,1)S(1)}, u32[]{:S(2)}, u32[]{:S(2)}) collective-permute-start(bf16[1040,128]{1,0:T(8,128)(2,1)S(1)} %add.13), channel_id=1, source_target_pairs={{0,8},{8,16},{16,24},{24,0},{1,9},{9,17},{17,25},{25,1},{2,10},{10... | collective-permute-start | bytes 798728 | tf_op jit(solution)/shard_map/ppermute | solution.py:325
  72.5 10.1 %collective-permute-start.5 = (bf16[1024,128]{1,0:T(8,128)(2,1)S(1)}, bf16[1024,128]{1,0:T(8,128)(2,1)S(1)}, u32[]{:S(2)}, u32[]{:S(2)}) collective-permute-start(bf16[1024,128]{1,0:T(8,128)(2,1)S(1)} %add.15), channel_id=1, source_target_pairs={{0,24},{8,0},{16,8},{24,16},{1,25},{9,1},{17,9},{25,17},{2,26},{10... | collective-permute-start | bytes 786440 | tf_op jit(solution)/shard_map/ppermute | solution.py:325
  83.2 6.2 %collective-permute-start.7 = (bf16[2,128,128]{2,1,0:T(8,128)(2,1)S(1)}, bf16[2,128,128]{2,1,0:T(8,128)(2,1)S(1)}, u32[]{:S(2)}, u32[]{:S(2)}) collective-permute-start(bf16[2,128,128]{2,1,0:T(8,128)(2,1)S(1)} %get-tuple-element.32), channel_id=1, source_target_pairs={{4,0},{8,4},{12,8},{16,12},{20,16},{24,20},{28,24},{5,1},{9,5},{13... | collective-permute-start | bytes 196616 | tf_op jit(solution)/shard_map/ppermute | solution.py:319
  84.5 6.4 %collective-permute-start.6 = (bf16[2,128,128]{2,1,0:T(8,128)(2,1)S(1)}, bf16[2,128,128]{2,1,0:T(8,128)(2,1)S(1)}, u32[]{:S(2)}, u32[]{:S(2)}) collective-permute-start(bf16[2,128,128]{2,1,0:T(8,128)(2,1)S(1)} %get-tuple-element.33), channel_id=1, source_target_pairs={{0,4},{4,8},{8,12},{12,16},{16,20},{20,24},{24,28},{1,5},{5,9},{9,... | collective-permute-start | bytes 196616 | tf_op jit(solution)/shard_map/ppermute | solution.py:318
  91.0 2.6 %collective-permute-start.8 = (bf16[20,2,128]{2,1,0:T(2,128)(2,1)S(1)}, bf16[20,2,128]{2,1,0:T(2,128)(2,1)S(1)}, u32[]{:S(2)}, u32[]{:S(2)}) collective-permute-start(bf16[20,2,128]{2,1,0:T(2,128)(2,1)S(1)} %pad_maximum_fusion), channel_id=1, source_target_pairs={{0,1},{1,2},{2,3},{4,5},{5,6},{6,7},{8,9},{9,10},{10,11},{12,13},{... | collective-permute-start | bytes 30728 | tf_op jit(solution)/shard_map/ppermute | solution.py:318
  92.3 4.5 %collective-permute-start.9 = (bf16[20,2,128]{2,1,0:T(2,128)(2,1)S(1)}, bf16[20,2,128]{2,1,0:T(2,128)(2,1)S(1)}, u32[]{:S(2)}, u32[]{:S(2)}) collective-permute-start(bf16[20,2,128]{2,1,0:T(2,128)(2,1)S(1)} %pad_maximum_fusion.1), channel_id=1, source_target_pairs={{1,0},{2,1},{3,2},{5,4},{6,5},{7,6},{9,8},{10,9},{11,10},{13,12},{... | collective-permute-start | bytes 30728 | tf_op jit(solution)/shard_map/ppermute | solution.py:319
  101.3 9.6 %collective-permute-start.10 = (bf16[8,128,128]{2,1,0:T(8,128)(2,1)S(1)}, bf16[8,128,128]{2,1,0:T(8,128)(2,1)S(1)}, u32[]{:S(2)}, u32[]{:S(2)}) collective-permute-start(bf16[8,128,128]{2,1,0:T(8,128)(2,1)S(1)} %get-tuple-element.27.refs_0_), channel_id=1, source_target_pairs={{0,8},{8,16},{16,24},{24,0},{1,9},{9,17},{17,25},{25,1},{2,10},{10... | collective-permute-start | bytes 786440 | tf_op jit(solution)/shard_map/ppermute | solution.py:325
  104.1 15.0 %collective-permute-start.13 = (bf16[8,128,128]{2,1,0:T(8,128)(2,1)S(1)}, bf16[8,128,128]{2,1,0:T(8,128)(2,1)S(1)}, u32[]{:S(2)}, u32[]{:S(2)}) collective-permute-start(bf16[8,128,128]{2,1,0:T(8,128)(2,1)S(1)} %get-tuple-element.28.refs_4_), channel_id=1, source_target_pairs={{0,24},{8,0},{16,8},{24,16},{1,25},{9,1},{17,9},{25,17},{2,26},{10... | collective-permute-start | bytes 786440 | tf_op jit(solution)/shard_map/ppermute | solution.py:325
  110.9 11.1 %collective-permute-start.11 = (bf16[8,128,128]{2,1,0:T(8,128)(2,1)S(1)}, bf16[8,128,128]{2,1,0:T(8,128)(2,1)S(1)}, u32[]{:S(2)}, u32[]{:S(2)}) collective-permute-start(bf16[8,128,128]{2,1,0:T(8,128)(2,1)S(1)} %collective-permute-done.10.refs_1_), channel_id=1, source_target_pairs={{0,8},{8,16},{16,24},{24,0},{1,9},{9,17},{17,25},{25,1},{2,10},{10... | collective-permute-start | bytes 786440 | tf_op jit(solution)/shard_map/ppermute | solution.py:325
  119.1 11.6 %collective-permute-start.14 = (bf16[8,128,128]{2,1,0:T(8,128)(2,1)S(1)}, bf16[8,128,128]{2,1,0:T(8,128)(2,1)S(1)}, u32[]{:S(2)}, u32[]{:S(2)}) collective-permute-start(bf16[8,128,128]{2,1,0:T(8,128)(2,1)S(1)} %collective-permute-done.13.refs_5_), channel_id=1, source_target_pairs={{0,24},{8,0},{16,8},{24,16},{1,25},{9,1},{17,9},{25,17},{2,26},{10... | collective-permute-start | bytes 786440 | tf_op jit(solution)/shard_map/ppermute | solution.py:325
  122.0 11.3 %collective-permute-start.12 = (bf16[8,128,128]{2,1,0:T(8,128)(2,1)S(1)}, bf16[8,128,128]{2,1,0:T(8,128)(2,1)S(1)}, u32[]{:S(2)}, u32[]{:S(2)}) collective-permute-start(bf16[8,128,128]{2,1,0:T(8,128)(2,1)S(1)} %collective-permute-done.11.refs_2_), channel_id=1, source_target_pairs={{0,8},{8,16},{16,24},{24,0},{1,9},{9,17},{17,25},{25,1},{2,10},{10... | collective-permute-start | bytes 786440 | tf_op jit(solution)/shard_map/ppermute | solution.py:325
  130.7 9.7 %collective-permute-start.15 = (bf16[8,128,128]{2,1,0:T(8,128)(2,1)S(1)}, bf16[8,128,128]{2,1,0:T(8,128)(2,1)S(1)}, u32[]{:S(2)}, u32[]{:S(2)}) collective-permute-start(bf16[8,128,128]{2,1,0:T(8,128)(2,1)S(1)} %collective-permute-done.14.refs_6_), channel_id=1, source_target_pairs={{0,24},{8,0},{16,8},{24,16},{1,25},{9,1},{17,9},{25,17},{2,26},{10... | collective-permute-start | bytes 786440 | tf_op jit(solution)/shard_map/ppermute | solution.py:325
  143.6 29.7 %copy-start = (bf16[32,128,128]{2,1,0:T(8,128)(2,1)S(1)}, bf16[32,128,128]{2,1,0:T(8,128)(2,1)}, u32[]{:S(2)}) copy-start(bf16[32,128,128]{2,1,0:T(8,128)(2,1)} %get-tuple-element.16.feat_ref) | copy-start | bytes 3145732
  143.6 29.6 %copy-start.2 = (s32[32]{0:T(128)S(1)}, s32[32]{0:T(128)}, u32[]{:S(2)}) copy-start(s32[32]{0:T(128)} %tile_ref.1) | copy-start | bytes 388

commit v5 on v4

--- a/solution.py
+++ b/solution.py
@@ -15,6 +15,11 @@
 SIDE = 4
 PAD = 8
 META = 4
+EDGE = 2
+EARLY = (0, 1, SR - 2, SR - 1)
+LATE = tuple(r for r in range(SR) if r not in EARLY)
+FULL = len(EARLY) * TC
+CELLS = -(-len(LATE) * 2 * EDGE // 16) * 16
 ACROSS = TC // PW
 F32 = jnp.float32
 BF16 = jnp.bfloat16
@@ -176,14 +181,21 @@
 
     lax.fori_loop(0, got_ref.shape[0], tile, 0)
     for k in range(orbits):
-        for out_ref, way, band in ((up[k], 1, 0), (down[k], -1, 1)):
-            rows = acc_ref[pl.ds(stripe_at(k, way) * SR + band * PH, PH)].astype(BF16)
-            out_ref[0 : PH * TC, :] = rows.reshape(PH * TC, channels)
+        for out_ref, way, rows in ((up[k], 1, EARLY), (down[k], -1, LATE)):
+            first = stripe_at(k, way) * SR
+            for i, r in enumerate(rows):
+                out_ref[i * TC : (i + 1) * TC, :] = acc_ref[first + r].astype(BF16)
+        first = stripe_at(k, 1) * SR
         bands = []
         for band in range(SR // PH):
-            first = (stripe_at(k, 1) * (SR // PH) + band) * ACROSS
-            bands.append(jnp.concatenate([dens_ref[first + c] for c in range(ACROSS)], axis=1))
-        up[k][PH * TC :, :] = jnp.concatenate(bands, axis=0).astype(BF16)
+            at = (stripe_at(k, 1) * (SR // PH) + band) * ACROSS
+            bands.append(jnp.concatenate([dens_ref[at + c] for c in range(ACROSS)], axis=1))
+        up[k][FULL : FULL + SR, :] = jnp.concatenate(bands, axis=0).astype(BF16)
+        cells = [acc_ref[first + r, at] for r in LATE for at in (slice(0, EDGE), slice(TC - EDGE, TC))]
+        spare = CELLS - len(LATE) * 2 * EDGE
+        if spare:
+            cells.append(jnp.zeros((spare, channels), F32))
+        up[k][FULL + SR :, :] = jnp.concatenate(cells, axis=0).astype(BF16)
 
 
 def weights_kernel(most, got_ref, out_ref):
@@ -199,16 +211,45 @@
     lax.fori_loop(0, got_ref.shape[0], tile, 0)
 
 
+def grid_values(spread, density, weight):
+    return (spread / jnp.maximum(density, 1.0) + weight * (density / (1.0 + density))).astype(BF16)
+
+
+def densities(own_ref, sum_ref):
+    tail = slice(FULL, FULL + SR)
+    columns = (own_ref[tail, :].astype(F32) + sum_ref[tail, :].astype(F32)).T
+    return lambda r: jnp.broadcast_to(columns[:, r : r + 1], (TC, own_ref.shape[1]))
+
+
+def edge_kernel(own_ref, sum_ref, weight_ref, top_ref, bottom_ref, left_ref, right_ref):
+    density = densities(own_ref, sum_ref)
+    weight = weight_ref[...]
+    low, high = slice(0, EDGE), slice(TC - EDGE, TC)
+    cells = own_ref[FULL + SR :, :].astype(F32) + sum_ref[FULL + SR :, :].astype(F32)
+    for r in range(SR):
+        d = density(r)
+        if r in EARLY:
+            at = slice(EARLY.index(r) * TC, (EARLY.index(r) + 1) * TC)
+            spread = own_ref[at, :].astype(F32) + sum_ref[at, :].astype(F32)
+            row = grid_values(spread, d, weight)
+            if r < EDGE:
+                top_ref[r] = row
+            if r >= SR - EDGE:
+                bottom_ref[r - (SR - EDGE)] = row
+            left_ref[r], right_ref[r] = row[low], row[high]
+        else:
+            at = LATE.index(r) * 2 * EDGE
+            left_ref[r] = grid_values(cells[at : at + EDGE], d[low], weight)
+            right_ref[r] = grid_values(cells[at + EDGE : at + 2 * EDGE], d[high], weight)
+
+
 def grid_kernel(own0_ref, sum0_ref, own1_ref, sum1_ref, weight_ref, out_ref):
-    channels = out_ref.shape[2]
-    tail = slice(PH * TC, PH * TC + SR)
-    density = (own0_ref[tail, :].astype(F32) + sum0_ref[tail, :].astype(F32)).T
-    for i in range(SR):
-        own_ref, sum_ref = (own0_ref, sum0_ref) if i < PH else (own1_ref, sum1_ref)
-        at = slice(i % PH * TC, (i % PH + 1) * TC)
-        spread = own_ref[at, :].astype(F32) + sum_ref[at, :].astype(F32)
-        d = jnp.broadcast_to(density[:, i : i + 1], (TC, channels))
-        out_ref[i] = (spread / jnp.maximum(d, 1.0) + weight_ref[...] * (d / (1.0 + d))).astype(BF16)
+    density = densities(own0_ref, sum0_ref)
+    for own_ref, sum_ref, rows in ((own0_ref, sum0_ref, EARLY), (own1_ref, sum1_ref, LATE)):
+        for i, r in enumerate(rows):
+            at = slice(i * TC, (i + 1) * TC)
+            spread = own_ref[at, :].astype(F32) + sum_ref[at, :].astype(F32)
+            out_ref[r] = grid_values(spread, density(r), weight_ref[...])
 
 
 def conv_kernel(
@@ -312,12 +353,9 @@
     return up, [(j, i) for i, j in up]
 
 
-def halo(x, axis, dim, width):
+def halo(first, last, axis):
     up, down = shifts(axis)
-    length = x.shape[dim]
-    before = lax.ppermute(lax.slice_in_dim(x, length - width, length, axis=dim), axis, up)
-    after = lax.ppermute(lax.slice_in_dim(x, 0, width, axis=dim), axis, down)
-    return before, after
+    return lax.ppermute(last, axis, up), lax.ppermute(first, axis, down)
 
 
 def turn(x, way):
@@ -393,13 +431,13 @@
     got = exchange(send)
 
     flops = 2 * slots * size * channels * PH * PW
-    band_shape = shape((PH * TC, channels), BF16)
-    dense_shape = shape((PH * TC + SR, channels), BF16)
+    early_shape = shape((FULL + SR + CELLS, channels), BF16)
+    late_shape = shape((len(LATE) * TC, channels), BF16)
     *bands, patch_of = call(
         functools.partial(spread_kernel, orbits, most),
         [VMEM],
         [VMEM] * (2 * orbits) + [SMEM],
-        [dense_shape] * orbits + [band_shape] * orbits + [shape((slots,), jnp.int32)],
+        [early_shape] * orbits + [late_shape] * orbits + [shape((slots,), jnp.int32)],
         [pltpu.VMEM((height, TC, channels), F32), pltpu.VMEM((patches, PH, PW), F32)],
         flops,
         8 * slots * size * channels,
@@ -417,6 +455,22 @@
         4 * slots * size * channels,
         got,
     )
+    density_weight = bias(density_weight)
+    rows_shape, cols_shape = shape((EDGE, TC, channels), BF16), shape((SR, EDGE, channels), BF16)
+    top, bottom, left, right = call(
+        edge_kernel,
+        [VMEM] * 3,
+        [VMEM] * 4,
+        [rows_shape] * 2 + [cols_shape] * 2,
+        [],
+        10000000,
+        4 * SR * TC * channels,
+        bands0[-1], sum0, density_weight,
+    )
+    above, below = halo(top, bottom, ("orbits", "rows"))
+    left = jnp.concatenate([above[:, :EDGE], left, below[:, :EDGE]], axis=0)
+    right = jnp.concatenate([above[:, TC - EDGE :], right, below[:, TC - EDGE :]], axis=0)
+    left, right = halo(left, right, "cols")
     grid_in = call(
         grid_kernel,
         [VMEM] * 5,
@@ -425,18 +479,9 @@
         [],
         10000000,
         8 * SR * TC * channels,
-        bands0[-1], sum0, bands1[-1], sum1, bias(density_weight),
-    )
-
-    above, below = halo(grid_in, ("orbits", "rows"), 0, 2)
-    extended = jnp.concatenate(
-        [
-            jnp.concatenate([above[:, c], grid_in[:, c], below[:, c]], axis=0)
-            for c in (slice(0, 2), slice(TC - 2, TC))
-        ],
-        axis=1,
-    )
-    left, right = halo(extended, "cols", 1, 2)
+        bands0[-1], sum0, bands1[-1], sum1, density_weight,
+    )
+
     width = TC + 2 * PAD
     grid_out, band0, band1 = call(
         conv_kernel,

time: 175 us -> 168 us (0.960)
  waiting for transfers between devices: 66.5 us -> 57.7 us
    ppermute x12, waiting for transfers between devices: 61.4 us -> 56.6 us  [turn(): lax.ppermute(x, 'orbits', [(i, (i + way) % size) for i in range(size)])]
    ppermute x4, waiting for transfers between devices: 5.12 us -> 1.07 us  [halo(): return (lax.ppermute(last, axis, up), lax.ppermute(first, axis, down))]
    pallas_call x7 -> x8, Pallas kernels: 22 us -> 22.4 us  [call(): pl.pallas_call(kernel, in_specs=in_specs, out_specs=out_specs, out_shape=...]
  transfers between devices with their start and end apart: 16 -> 16, of which waited for: 14 -> 12; matrix products, arithmetic and copies ran while one was open for 0% -> 0% of each run, Pallas kernels for 1% -> 2%
where the time goes in v5:
time: 168 us
  blocking collectives  62 us (37%)
  waiting for transfers between devices  57.7 us (34%)
  starting transfers between devices  24.5 us (15%)
  Pallas kernels  22.4 us (13%)
    all_to_all x2, blocking collectives, local(): lax.all_to_all(x, plane, split_axis=0, concat_axis=0, tiled=True)  62 us
    ppermute x12, waiting for transfers between devices, turn(): lax.ppermute(x, 'orbits', [(i, (i + way) % size) for i in range(size)])  56.6 us
    pallas_call x8, Pallas kernels, call(): pl.pallas_call(kernel, in_specs=in_specs, out_specs=out_specs, out_shape=...  22.4 us
    ppermute x12, starting transfers between devices, turn(): lax.ppermute(x, 'orbits', [(i, (i + way) % size) for i in range(size)])  16.1 us
    ppermute x4, starting transfers between devices, halo(): return (lax.ppermute(last, axis, up), lax.ppermute(first, axis, down))  8.42 us
  transfers between devices with their start and end apart: 16, of which 12 were waited for; matrix products, arithmetic and copies ran while one was open for 0% of the time, Pallas kernels for 2%

profile of v5, /device:TPU:0, one launch (start us, length us, event | category | flops | bytes accessed | tf_op | source)
XLA Modules:
  0.0 167.9 jit_solution(18253141980556639326)
XLA Ops:
  0.6 5.9 %shard_map.149 = (bf16[32,128,128]{2,1,0:T(8,128)(2,1)}, bf16[8,1056,128]{2,1,0:T(8,128)(2,1)}) custom-call(s32[32]{0:T(128)} %tile_ref.1, s32[32]{0:T(128)} %patch_hbm.1, bf16[2,4096]{1,0:T(2,128)(2,1)} %offset_hbm.1, s32[16,4096]{1,0:T(8,128)} %cells_hbm.1, bf16[4096,128]{1,0:T(8,128)(2,1)} %x_hbm.1, bf16[128,128]{1,0:T(8,128)(2,1)} %we_hbm.1, ...), custom_call_target="tpu_custom_call" | custom-call | flops 402653184 | bytes 4194304 | tf_op jit(solution)/shard_map/pallas_call | solution.py:35
  6.5 32.7 %all_to_all.10.got_ref = bf16[8,1056,128]{2,1,0:T(8,128)(2,1)S(1)} all-to-all(bf16[8,1056,128]{2,1,0:T(8,128)(2,1)} %get-tuple-element.21), channel_id=1, replica_groups=mesh['orbits'=4,'rows'=2,'cols'=4] {'rows','cols'}, dimensions={0} | all-to-all | bytes 4325376 | tf_op jit(solution)/shard_map/all_to_all | solution.py:402
  39.2 4.1 %shard_map.150 = (bf16[576,128]{1,0:T(8,128)(2,1)S(1)}, bf16[576,128]{1,0:T(8,128)(2,1)S(1)}, bf16[576,128]{1,0:T(8,128)(2,1)S(1)}, bf16[576,128]{1,0:T(8,128)(2...) custom-call(bf16[8,1056,128]{2,1,0:T(8,128)(2,1)S(1)} %all_to_all.10, ...), custom_call_target="tpu_custom_call" | custom-call | flops 536870912 | bytes 8388608 | tf_op jit(solution)/shard_map/pallas_call | solution.py:35
  43.3 3.7 %collective-permute-start.3 = (bf16[1536,128]{1,0:T(8,128)(2,1)S(1)}, bf16[1536,128]{1,0:T(8,128)(2,1)S(1)}, u32[]{:S(2)}, u32[]{:S(2)}) collective-permute-start(bf16[1536,128]{1,0:T(8,128)(2,1)S(1)} %get-tuple-element.28), channel_id=1, source_target_pairs={{0,24},{8,0},{16,8},{24,16},{1,25},{9,1},{17,9},{25,17},{2,26},{10... | collective-permute-start | bytes 1179656 | tf_op jit(solution)/shard_map/ppermute | solution.py:363
  46.9 0.0 collective-permute-start
  46.9 12.3 %collective-permute-done = bf16[576,128]{1,0:T(8,128)(2,1)S(1)} collective-permute-done((bf16[576,128]{1,0:T(8,128)(2,1)S(1)}, bf16[576,128]{1,0:T(8,128)(2,1)S(1)}, u32[]{:S(2)}, u32[]{:S(2)}) %collective-permute-start) | collective-permute-done | bytes 147488 | tf_op jit(solution)/shard_map/ppermute | solution.py:363
  59.3 1.7 collective-permute-start.1
  61.0 5.3 %collective-permute-done.1 = bf16[576,128]{1,0:T(8,128)(2,1)S(1)} collective-permute-done((bf16[576,128]{1,0:T(8,128)(2,1)S(1)}, bf16[576,128]{1,0:T(8,128)(2,1)S(1)}, u32[]{:S(2)}, u32[]{:S(2)}) %collective-permute-start.1) | collective-permute-done | bytes 147488 | tf_op jit(solution)/shard_map/ppermute | solution.py:363
  66.4 0.1 collective-permute-start.2
  66.4 0.0 collective-permute-done.3
  66.4 0.0 copy-start.3
  66.5 0.0 copy-start.4
  66.5 0.0 copy-start.5
  66.5 0.0 copy-start.6
  66.5 0.1 add.14
  66.6 3.8 %collective-permute-start.4 = (bf16[1536,128]{1,0:T(8,128)(2,1)S(1)}, bf16[1536,128]{1,0:T(8,128)(2,1)S(1)}, u32[]{:S(2)}, u32[]{:S(2)}) collective-permute-start(bf16[1536,128]{1,0:T(8,128)(2,1)S(1)} %add.14), channel_id=1, source_target_pairs={{0,24},{8,0},{16,8},{24,16},{1,25},{9,1},{17,9},{25,17},{2,26},{10... | collective-permute-start | bytes 1179656 | tf_op jit(solution)/shard_map/ppermute | solution.py:363
  70.4 4.6 %collective-permute-done.2.sum0_ref.sum_ref = bf16[576,128]{1,0:T(8,128)(2,1)S(1)} collective-permute-done((bf16[576,128]{1,0:T(8,128)(2,1)S(1)}, bf16[576,128]{1,0:T(8,128)(2,1)S(1)}, u32[]{:S(2)}, u32[]{:S(2)}) %collective-permute-start.2) | collective-permute-done | bytes 147488 | tf_op jit(solution)/shard_map/ppermute | solution.py:363
  75.0 0.3 shard_map.153
  75.3 1.3 collective-permute-start.7
  76.6 4.5 %collective-permute-start.6 = (bf16[2,128,128]{2,1,0:T(8,128)(2,1)S(1)}, bf16[2,128,128]{2,1,0:T(8,128)(2,1)S(1)}, u32[]{:S(2)}, u32[]{:S(2)}) collective-permute-start(bf16[2,128,128]{2,1,0:T(8,128)(2,1)S(1)} %get-tuple-element.31), channel_id=1, source_target_pairs={{0,4},{4,8},{8,12},{12,16},{16,20},{20,24},{24,28},{1,5},{5,9},{9,... | collective-permute-start | bytes 196616 | tf_op jit(solution)/shard_map/ppermute | solution.py:358
  81.2 0.3 collective-permute-done.7.down_ref
  81.5 0.0 collective-permute-done.4
  81.5 0.1 add.15
  81.6 0.7 collective-permute-start.5
  82.3 0.8 collective-permute-done.6.up_ref
  83.1 1.3 collective-permute-start.8
  84.4 1.3 collective-permute-start.9
  85.7 3.7 %collective-permute-done.5.sum1_ref = bf16[1536,128]{1,0:T(8,128)(2,1)S(1)} collective-permute-done((bf16[1536,128]{1,0:T(8,128)(2,1)S(1)}, bf16[1536,128]{1,0:T(8,128)(2,1)S(1)}, u32[]{:S(2)}, u32[]{:S(2)}) %collective-permute-start.5) | collective-permute-done | bytes 393248 | tf_op jit(solution)/shard_map/ppermute | solution.py:363
  89.4 0.5 shard_map.152.x_ref
  90.0 0.0 collective-permute-done.8.left_ref
  90.0 0.0 collective-permute-done.9.right_ref
  90.0 4.4 %shard_map.154 = (bf16[16,128,128]{2,1,0:T(8,128)(2,1)}, bf16[8,128,128]{2,1,0:T(8,128)(2,1)S(1)}, bf16[8,128,128]{2,1,0:T(8,128)(2,1)S(1)}) custom-call(bf16[16,128,128]{2,1,0:T(8,128)(2,1)S(1)} %shard_map.152.x_ref, bf16[2,128,128]{2,1,0:T(8,128)(2,1)S(1)} %collective-permute-done.6.up_ref, bf16[2,128,128]{2,1,0:T(8,128)(2,1)S(1)} %collective-permute-done.7.down_ref, ...), custom_call_target="tpu_custom_call" | custom-call | flops 1207959552 | bytes 2097152 | tf_op jit(solution)/shard_map/pallas_call | solution.py:35
  94.4 2.5 %collective-permute-start.10 = (bf16[8,128,128]{2,1,0:T(8,128)(2,1)S(1)}, bf16[8,128,128]{2,1,0:T(8,128)(2,1)S(1)}, u32[]{:S(2)}, u32[]{:S(2)}) collective-permute-start(bf16[8,128,128]{2,1,0:T(8,128)(2,1)S(1)} %get-tuple-element.35.refs_0_), channel_id=1, source_target_pairs={{0,8},{8,16},{16,24},{24,0},{1,9},{9,17},{17,25},{25,1},{2,10},{10... | collective-permute-start | bytes 786440 | tf_op jit(solution)/shard_map/ppermute | solution.py:363
  96.9 1.3 collective-permute-start.13
  98.2 7.2 %collective-permute-done.10.refs_1_ = bf16[8,128,128]{2,1,0:T(8,128)(2,1)S(1)} collective-permute-done((bf16[8,128,128]{2,1,0:T(8,128)(2,1)S(1)}, bf16[8,128,128]{2,1,0:T(8,128)(2,1)S(1)}, u32[]{:S(2)}, u32[]{:S(2)}) %collective-permute-start.10) | collective-permute-done | bytes 262176 | tf_op jit(solution)/shard_map/ppermute | solution.py:363
  105.5 5.4 %collective-permute-done.13.refs_5_ = bf16[8,128,128]{2,1,0:T(8,128)(2,1)S(1)} collective-permute-done((bf16[8,128,128]{2,1,0:T(8,128)(2,1)S(1)}, bf16[8,128,128]{2,1,0:T(8,128)(2,1)S(1)}, u32[]{:S(2)}, u32[]{:S(2)}) %collective-permute-start.13) | collective-permute-done | bytes 262176 | tf_op jit(solution)/shard_map/ppermute | solution.py:363
  110.9 1.3 collective-permute-start.14
  112.1 4.6 %collective-permute-done.11.refs_2_ = bf16[8,128,128]{2,1,0:T(8,128)(2,1)S(1)} collective-permute-done((bf16[8,128,128]{2,1,0:T(8,128)(2,1)S(1)}, bf16[8,128,128]{2,1,0:T(8,128)(2,1)S(1)}, u32[]{:S(2)}, u32[]{:S(2)}) %collective-permute-start.11) | collective-permute-done | bytes 262176 | tf_op jit(solution)/shard_map/ppermute | solution.py:363
  116.8 5.5 %collective-permute-done.14.refs_6_ = bf16[8,128,128]{2,1,0:T(8,128)(2,1)S(1)} collective-permute-done((bf16[8,128,128]{2,1,0:T(8,128)(2,1)S(1)}, bf16[8,128,128]{2,1,0:T(8,128)(2,1)S(1)}, u32[]{:S(2)}, u32[]{:S(2)}) %collective-permute-start.14) | collective-permute-done | bytes 262176 | tf_op jit(solution)/shard_map/ppermute | solution.py:363
  122.3 1.1 collective-permute-start.15
  123.4 2.3 %shard_map.151.weights_ref = bf16[64,128,256]{2,1,0:T(8,128)(2,1)S(1)} custom-call(bf16[8,1056,128]{2,1,0:T(8,128)(2,1)S(1)} %all_to_all.10.got_ref), custom_call_target="tpu_custom_call" | custom-call | flops 536870912 | bytes 4194304 | tf_op jit(solution)/shard_map/pallas_call | solution.py:35
  125.7 2.4 %collective-permute-done.12.refs_3_ = bf16[8,128,128]{2,1,0:T(8,128)(2,1)S(1)} collective-permute-done((bf16[8,128,128]{2,1,0:T(8,128)(2,1)S(1)}, bf16[8,128,128]{2,1,0:T(8,128)(2,1)S(1)}, u32[]{:S(2)}, u32[]{:S(2)}) %collective-permute-start.12) | collective-permute-done | bytes 262176 | tf_op jit(solution)/shard_map/ppermute | solution.py:363
  128.0 5.5 %collective-permute-done.15.refs_7_ = bf16[8,128,128]{2,1,0:T(8,128)(2,1)S(1)} collective-permute-done((bf16[8,128,128]{2,1,0:T(8,128)(2,1)S(1)}, bf16[8,128,128]{2,1,0:T(8,128)(2,1)S(1)}, u32[]{:S(2)}, u32[]{:S(2)}) %collective-permute-start.15) | collective-permute-done | bytes 262176 | tf_op jit(solution)/shard_map/ppermute | solution.py:363
  133.6 3.1 %shard_map.155 = bf16[8,1024,128]{2,1,0:T(8,128)(2,1)S(1)} custom-call(s32[64]{0:T(128)S(1)} %get-tuple-element.22.patch_ref, bf16[64,128,256]{2,1,0:T(8,128)(2,1)S(1)} %shard_map.151.weights_ref, bf16[8,128,128]{2,1,0:T(8,128)(2,1)S(1)} %get-tuple-element.35.refs_0_, bf16[8,128,128]{2,1,0:T(8,128)(2,1)S(1)} %collective-permute-done.10.refs_1_, ...), custom_call_target="tpu_custom_call" | custom-call | flops 536870912 | bytes 8388608 | tf_op jit(solution)/shard_map/pallas_call | solution.py:35
  136.7 0.0 copy-start
  136.7 0.0 copy-start.2
  136.7 29.4 %all_to_all.11.got_ref = bf16[8,1024,128]{2,1,0:T(8,128)(2,1)S(1)} all-to-all(bf16[8,1024,128]{2,1,0:T(8,128)(2,1)S(1)} %shard_map.155), channel_id=1, replica_groups=mesh['orbits'=4,'rows'=2,'cols'=4] {'rows','cols'}, dimensions={0} | all-to-all | bytes 4194304 | tf_op jit(solution)/shard_map/all_to_all | solution.py:402
  166.1 1.8 %shard_map.156 = bf16[32,128,128]{2,1,0:T(8,128)(2,1)} custom-call(s32[32]{0:T(128)S(1)} %copy-done.2, bf16[32,128,128]{2,1,0:T(8,128)(2,1)S(1)} %copy-done, bf16[8,1024,128]{2,1,0:T(8,128)(2,1)S(1)} %all_to_all.11.got_ref), custom_call_target="tpu_custom_call" | custom-call | flops 1000000 | bytes 4194304 | tf_op jit(solution)/shard_map/pallas_call | solution.py:35
  (16 shorter events, 0.2 us)
Async XLA Ops:
  39.2 35.9 %copy-start.1 = (f32[128]{0:T(128)S(1)}, f32[128]{0:T(128)}, u32[]{:S(2)}) copy-start(f32[128]{0:T(128)} %param.23) | copy-start | bytes 1540
  43.3 23.1 %collective-permute-start.3 = (bf16[1536,128]{1,0:T(8,128)(2,1)S(1)}, bf16[1536,128]{1,0:T(8,128)(2,1)S(1)}, u32[]{:S(2)}, u32[]{:S(2)}) collective-permute-start(bf16[1536,128]{1,0:T(8,128)(2,1)S(1)} %get-tuple-element.28), channel_id=1, source_target_pairs={{0,24},{8,0},{16,8},{24,16},{1,25},{9,1},{17,9},{25,17},{2,26},{10... | collective-permute-start | bytes 1179656 | tf_op jit(solution)/shard_map/ppermute | solution.py:363
  46.9 12.3 %collective-permute-start = (bf16[576,128]{1,0:T(8,128)(2,1)S(1)}, bf16[576,128]{1,0:T(8,128)(2,1)S(1)}, u32[]{:S(2)}, u32[]{:S(2)}) collective-permute-start(bf16[576,128]{1,0:T(8,128)(2,1)S(1)} %get-tuple-element.24), channel_id=1, source_target_pairs={{0,8},{8,16},{16,24},{24,0},{1,9},{9,17},{17,25},{25,1},{2,10},{10... | collective-permute-start | bytes 442376 | tf_op jit(solution)/shard_map/ppermute | solution.py:363
  59.3 7.0 %collective-permute-start.1 = (bf16[576,128]{1,0:T(8,128)(2,1)S(1)}, bf16[576,128]{1,0:T(8,128)(2,1)S(1)}, u32[]{:S(2)}, u32[]{:S(2)}) collective-permute-start(bf16[576,128]{1,0:T(8,128)(2,1)S(1)} %add.12), channel_id=1, source_target_pairs={{0,8},{8,16},{16,24},{24,0},{1,9},{9,17},{17,25},{25,1},{2,10},{10... | collective-permute-start | bytes 442376 | tf_op jit(solution)/shard_map/ppermute | solution.py:363
  66.4 8.6 %collective-permute-start.2 = (bf16[576,128]{1,0:T(8,128)(2,1)S(1)}, bf16[576,128]{1,0:T(8,128)(2,1)S(1)}, u32[]{:S(2)}, u32[]{:S(2)}) collective-permute-start(bf16[576,128]{1,0:T(8,128)(2,1)S(1)} %add.13), channel_id=1, source_target_pairs={{0,8},{8,16},{16,24},{24,0},{1,9},{9,17},{17,25},{25,1},{2,10},{10... | collective-permute-start | bytes 442376 | tf_op jit(solution)/shard_map/ppermute | solution.py:363
  66.4 23.5 %copy-start.3 = (bf16[3,3,128,128]{3,2,1,0:T(8,128)(2,1)S(1)}, bf16[3,3,128,128]{3,2,1,0:T(8,128)(2,1)}, u32[]{:S(2)}) copy-start(bf16[3,3,128,128]{3,2,1,0:T(8,128)(2,1)} %w1_ref.1) | copy-start | bytes 884740
  66.5 23.5 %copy-start.4 = (bf16[3,3,128,128]{3,2,1,0:T(8,128)(2,1)S(1)}, bf16[3,3,128,128]{3,2,1,0:T(8,128)(2,1)}, u32[]{:S(2)}) copy-start(bf16[3,3,128,128]{3,2,1,0:T(8,128)(2,1)} %w2_ref.1) | copy-start | bytes 884740
  66.5 23.5 %copy-start.5 = (f32[128]{0:T(128)S(1)}, f32[128]{0:T(128)}, u32[]{:S(2)}) copy-start(f32[128]{0:T(128)} %param.25) | copy-start | bytes 1540
  66.5 23.5 %copy-start.6 = (f32[128]{0:T(128)S(1)}, f32[128]{0:T(128)}, u32[]{:S(2)}) copy-start(f32[128]{0:T(128)} %param.27) | copy-start | bytes 1540
  66.6 14.9 %collective-permute-start.4 = (bf16[1536,128]{1,0:T(8,128)(2,1)S(1)}, bf16[1536,128]{1,0:T(8,128)(2,1)S(1)}, u32[]{:S(2)}, u32[]{:S(2)}) collective-permute-start(bf16[1536,128]{1,0:T(8,128)(2,1)S(1)} %add.14), channel_id=1, source_target_pairs={{0,24},{8,0},{16,8},{24,16},{1,25},{9,1},{17,9},{25,17},{2,26},{10... | collective-permute-start | bytes 1179656 | tf_op jit(solution)/shard_map/ppermute | solution.py:363
  75.3 6.2 %collective-permute-start.7 = (bf16[2,128,128]{2,1,0:T(8,128)(2,1)S(1)}, bf16[2,128,128]{2,1,0:T(8,128)(2,1)S(1)}, u32[]{:S(2)}, u32[]{:S(2)}) collective-permute-start(bf16[2,128,128]{2,1,0:T(8,128)(2,1)S(1)} %get-tuple-element.32), channel_id=1, source_target_pairs={{4,0},{8,4},{12,8},{16,12},{20,16},{24,20},{28,24},{5,1},{9,5},{13... | collective-permute-start | bytes 196616 | tf_op jit(solution)/shard_map/ppermute | solution.py:358
  76.6 6.4 %collective-permute-start.6 = (bf16[2,128,128]{2,1,0:T(8,128)(2,1)S(1)}, bf16[2,128,128]{2,1,0:T(8,128)(2,1)S(1)}, u32[]{:S(2)}, u32[]{:S(2)}) collective-permute-start(bf16[2,128,128]{2,1,0:T(8,128)(2,1)S(1)} %get-tuple-element.31), channel_id=1, source_target_pairs={{0,4},{4,8},{8,12},{12,16},{16,20},{20,24},{24,28},{1,5},{5,9},{9,... | collective-permute-start | bytes 196616 | tf_op jit(solution)/shard_map/ppermute | solution.py:358
  81.6 7.8 %collective-permute-start.5 = (bf16[1536,128]{1,0:T(8,128)(2,1)S(1)}, bf16[1536,128]{1,0:T(8,128)(2,1)S(1)}, u32[]{:S(2)}, u32[]{:S(2)}) collective-permute-start(bf16[1536,128]{1,0:T(8,128)(2,1)S(1)} %add.15), channel_id=1, source_target_pairs={{0,24},{8,0},{16,8},{24,16},{1,25},{9,1},{17,9},{25,17},{2,26},{10... | collective-permute-start | bytes 1179656 | tf_op jit(solution)/shard_map/ppermute | solution.py:363
  83.1 6.9 %collective-permute-start.8 = (bf16[20,2,128]{2,1,0:T(2,128)(2,1)S(1)}, bf16[20,2,128]{2,1,0:T(2,128)(2,1)S(1)}, u32[]{:S(2)}, u32[]{:S(2)}) collective-permute-start(bf16[20,2,128]{2,1,0:T(2,128)(2,1)S(1)} %pad_maximum_fusion), channel_id=1, source_target_pairs={{0,1},{1,2},{2,3},{4,5},{5,6},{6,7},{8,9},{9,10},{10,11},{12,13},{... | collective-permute-start | bytes 30728 | tf_op jit(solution)/shard_map/ppermute | solution.py:358
  84.4 5.6 %collective-permute-start.9 = (bf16[20,2,128]{2,1,0:T(2,128)(2,1)S(1)}, bf16[20,2,128]{2,1,0:T(2,128)(2,1)S(1)}, u32[]{:S(2)}, u32[]{:S(2)}) collective-permute-start(bf16[20,2,128]{2,1,0:T(2,128)(2,1)S(1)} %pad_maximum_fusion.1), channel_id=1, source_target_pairs={{1,0},{2,1},{3,2},{5,4},{6,5},{7,6},{9,8},{10,9},{11,10},{13,12},{... | collective-permute-start | bytes 30728 | tf_op jit(solution)/shard_map/ppermute | solution.py:358
  94.4 11.1 %collective-permute-start.10 = (bf16[8,128,128]{2,1,0:T(8,128)(2,1)S(1)}, bf16[8,128,128]{2,1,0:T(8,128)(2,1)S(1)}, u32[]{:S(2)}, u32[]{:S(2)}) collective-permute-start(bf16[8,128,128]{2,1,0:T(8,128)(2,1)S(1)} %get-tuple-element.35.refs_0_), channel_id=1, source_target_pairs={{0,8},{8,16},{16,24},{24,0},{1,9},{9,17},{17,25},{25,1},{2,10},{10... | collective-permute-start | bytes 786440 | tf_op jit(solution)/shard_map/ppermute | solution.py:363
  96.9 14.0 %collective-permute-start.13 = (bf16[8,128,128]{2,1,0:T(8,128)(2,1)S(1)}, bf16[8,128,128]{2,1,0:T(8,128)(2,1)S(1)}, u32[]{:S(2)}, u32[]{:S(2)}) collective-permute-start(bf16[8,128,128]{2,1,0:T(8,128)(2,1)S(1)} %get-tuple-element.36.refs_4_), channel_id=1, source_target_pairs={{0,24},{8,0},{16,8},{24,16},{1,25},{9,1},{17,9},{25,17},{2,26},{10... | collective-permute-start | bytes 786440 | tf_op jit(solution)/shard_map/ppermute | solution.py:363
  105.5 11.3 %collective-permute-start.11 = (bf16[8,128,128]{2,1,0:T(8,128)(2,1)S(1)}, bf16[8,128,128]{2,1,0:T(8,128)(2,1)S(1)}, u32[]{:S(2)}, u32[]{:S(2)}) collective-permute-start(bf16[8,128,128]{2,1,0:T(8,128)(2,1)S(1)} %collective-permute-done.10.refs_1_), channel_id=1, source_target_pairs={{0,8},{8,16},{16,24},{24,0},{1,9},{9,17},{17,25},{25,1},{2,10},{10... | collective-permute-start | bytes 786440 | tf_op jit(solution)/shard_map/ppermute | solution.py:363
  110.9 11.4 %collective-permute-start.14 = (bf16[8,128,128]{2,1,0:T(8,128)(2,1)S(1)}, bf16[8,128,128]{2,1,0:T(8,128)(2,1)S(1)}, u32[]{:S(2)}, u32[]{:S(2)}) collective-permute-start(bf16[8,128,128]{2,1,0:T(8,128)(2,1)S(1)} %collective-permute-done.13.refs_5_), channel_id=1, source_target_pairs={{0,24},{8,0},{16,8},{24,16},{1,25},{9,1},{17,9},{25,17},{2,26},{10... | collective-permute-start | bytes 786440 | tf_op jit(solution)/shard_map/ppermute | solution.py:363
  116.7 11.3 %collective-permute-start.12 = (bf16[8,128,128]{2,1,0:T(8,128)(2,1)S(1)}, bf16[8,128,128]{2,1,0:T(8,128)(2,1)S(1)}, u32[]{:S(2)}, u32[]{:S(2)}) collective-permute-start(bf16[8,128,128]{2,1,0:T(8,128)(2,1)S(1)} %collective-permute-done.11.refs_2_), channel_id=1, source_target_pairs={{0,8},{8,16},{16,24},{24,0},{1,9},{9,17},{17,25},{25,1},{2,10},{10... | collective-permute-start | bytes 786440 | tf_op jit(solution)/shard_map/ppermute | solution.py:363
  122.3 11.3 %collective-permute-start.15 = (bf16[8,128,128]{2,1,0:T(8,128)(2,1)S(1)}, bf16[8,128,128]{2,1,0:T(8,128)(2,1)S(1)}, u32[]{:S(2)}, u32[]{:S(2)}) collective-permute-start(bf16[8,128,128]{2,1,0:T(8,128)(2,1)S(1)} %collective-permute-done.14.refs_6_), channel_id=1, source_target_pairs={{0,24},{8,0},{16,8},{24,16},{1,25},{9,1},{17,9},{25,17},{2,26},{10... | collective-permute-start | bytes 786440 | tf_op jit(solution)/shard_map/ppermute | solution.py:363
  136.7 29.4 %copy-start = (bf16[32,128,128]{2,1,0:T(8,128)(2,1)S(1)}, bf16[32,128,128]{2,1,0:T(8,128)(2,1)}, u32[]{:S(2)}) copy-start(bf16[32,128,128]{2,1,0:T(8,128)(2,1)} %get-tuple-element.20.feat_ref) | copy-start | bytes 3145732
  136.7 29.4 %copy-start.2 = (s32[32]{0:T(128)S(1)}, s32[32]{0:T(128)}, u32[]{:S(2)}) copy-start(s32[32]{0:T(128)} %tile_ref.1) | copy-start | bytes 388

commit v6 on v5

--- a/solution.py
+++ b/solution.py
@@ -62,62 +62,97 @@
 
 def embed_kernel(
     tile_hbm, patch_hbm, offset_hbm, cells_hbm, x_hbm, we_hbm, be_hbm, wp_hbm, bp_hbm,
-    feat_ref, send_ref,
-    tile_ref, patch_ref, offset_ref, cells_ref, x_ref, we_ref, be_ref, wp_ref, bp_ref,
-    count_ref, meta_ref, sems, x_sems,
+    feat_hbm, send_hbm,
+    tile_ref, patch_ref, offset_ref, cells_ref, x_ref, we_ref, be_ref, wp_ref, bp_ref, feat_ref,
+    zero_ref, count_ref, slot_ref, meta_ref, meta16_ref, sems, x_sems, feat_sems, send_sems,
 ):
     blocks, size, channels = feat_ref.shape
     chunks = x_sems.shape[0]
     per = blocks // chunks
-    tiles = send_ref.shape[0]
-    meta_rows = meta_ref.shape[0] // tiles
-    base = meta_rows // META * size
+    tiles, meta_rows = meta16_ref.shape[0], meta_ref.shape[0] // meta16_ref.shape[0]
+    most = meta_rows // META
+    base = most * size
     pairs = (
-        (we_hbm, we_ref), (be_hbm, be_ref), (wp_hbm, wp_ref), (bp_hbm, bp_ref), (tile_hbm, tile_ref),
-        (patch_hbm, patch_ref), (offset_hbm, offset_ref), (cells_hbm.at[0:8], cells_ref),
+        (tile_hbm, tile_ref), (patch_hbm, patch_ref), (offset_hbm, offset_ref), (cells_hbm.at[0:8], cells_ref),
+        (we_hbm, we_ref), (be_hbm, be_ref), (wp_hbm, wp_ref), (bp_hbm, bp_ref),
     )
     copies = [pltpu.make_async_copy(a, b, sems.at[i]) for i, (a, b) in enumerate(pairs)]
 
+    def rows_of(c):
+        return pl.ds(pl.multiple_of(c * per * size, per * size), per * size)
+
     def fetch(c):
-        rows = pl.ds(pl.multiple_of(c * per * size, per * size), per * size)
-        return pltpu.make_async_copy(x_hbm.at[rows], x_ref.at[rows], x_sems.at[c])
+        return pltpu.make_async_copy(x_hbm.at[rows_of(c)], x_ref.at[rows_of(c)], x_sems.at[c])
+
+    def keep(c):
+        at = pl.ds(c * per, per)
+        return pltpu.make_async_copy(feat_ref.at[at], feat_hbm.at[at], feat_sems.at[c])
+
+    def send(source, slot):
+        rows = pl.ds(pl.multiple_of(lax.rem(slot, most) * size, size), size)
+        return pltpu.make_async_copy(source, send_hbm.at[slot // most, rows], send_sems.at[slot])
 
     for copy in copies:
         copy.start()
     for c in range(chunks):
         fetch(c).start()
+    zero_ref[...] = jnp.zeros(zero_ref.shape, BF16)
     clear(count_ref)
-    send_ref[...] = jnp.zeros(send_ref.shape, BF16)
     row = lax.broadcasted_iota(jnp.int32, meta_ref.shape, 0) % META
     meta_ref[...] = jnp.where(row == 2, -65536.0, 0.0)
-    for copy in copies:
+    copies[0].wait()
+    for b in range(blocks):
+        t, n = next_slot(tile_ref, count_ref, b)
+        slot_ref[b] = t * most + n
+    for t in range(tiles):
+        for n in range(most):
+
+            @pl.when(n >= count_ref[t])
+            def _():
+                send(zero_ref, t * most + n).start()
+
+    for copy in copies[4:]:
         copy.wait()
 
     def chunk(c, unused):
         fetch(c).wait()
-        rows = pl.ds(pl.multiple_of(c * per * size, per * size), per * size)
-        hidden = silu(jnp.dot(x_ref[rows, :], we_ref[...], preferred_element_type=F32) + be_ref[...])
+        hidden = silu(jnp.dot(x_ref[rows_of(c), :], we_ref[...], preferred_element_type=F32) + be_ref[...])
         out = jnp.dot(hidden.astype(BF16), wp_ref[...], preferred_element_type=F32) + bp_ref[...]
-        out = out.astype(BF16)
-        feat_ref[pl.ds(c * per, per)] = out.reshape(per, size, channels)
+        feat_ref[pl.ds(c * per, per)] = out.astype(BF16).reshape(per, size, channels)
+        keep(c).start()
         for k in range(per):
             b = c * per + k
-            t, n = next_slot(tile_ref, count_ref, b)
-            send_ref[t, pl.ds(pl.multiple_of(n * size, size), size), :] = out[k * size : (k + 1) * size]
-            first = t * meta_rows + n * META
-            obs = pl.ds(pl.multiple_of(b * size, size), size)
-            meta_ref[pl.ds(first, 2), :] = offset_ref[:, obs].astype(F32)
-            meta_ref[pl.ds(first + 2, 1), :] = cells_ref[0:1, obs].astype(F32)
-            meta_ref[pl.ds(first + 3, 1), :] = jnp.full((1, size), patch_ref[b], jnp.int32).astype(F32)
+            send(feat_ref.at[b], slot_ref[b]).start()
         return unused
 
     lax.fori_loop(0, chunks, chunk, 0)
-    extra = send_ref.shape[1] - base - meta_rows
+    for copy in copies[1:4]:
+        copy.wait()
+    for b in range(blocks):
+        first = slot_ref[b] * META
+        obs = slice(b * size, (b + 1) * size)
+        meta_ref[pl.ds(first, 2), :] = offset_ref[:, obs].astype(F32)
+        meta_ref[pl.ds(first + 2, 1), :] = cells_ref[0:1, obs].astype(F32)
+        meta_ref[pl.ds(first + 3, 1), :] = jnp.full((1, size), patch_ref[b], jnp.int32).astype(F32)
+    extra = meta16_ref.shape[1] - meta_rows
     for t in range(tiles):
         rows = meta_ref[t * meta_rows : (t + 1) * meta_rows, :]
         if extra:
             rows = jnp.concatenate([rows, jnp.zeros((extra, size), F32)], axis=0)
-        send_ref[t, base:, :] = rows.astype(BF16)
+        meta16_ref[t] = rows.astype(BF16)
+    described = pltpu.make_async_copy(
+        meta16_ref, send_hbm.at[:, pl.ds(base, meta16_ref.shape[1])], sems.at[len(copies)]
+    )
+    described.start()
+
+    def finish(c, unused):
+        keep(c).wait()
+        return unused
+
+    lax.fori_loop(0, chunks, finish, 0)
+    for slot in range(tiles * most):
+        send(zero_ref, slot).wait()
+    described.wait()
 
 
 def factors(meta, normal):
@@ -331,10 +366,15 @@
     lax.fori_loop(0, out_ref.shape[0], tile, 0)
 
 
-def final_kernel(tile_ref, feat_ref, got_ref, out_ref, count_ref):
+def final_kernel(tile_ref, feat_ref, got_ref, out_hbm, out_ref, count_ref, sems):
     blocks, size, _ = feat_ref.shape
+    chunks = sems.shape[0]
+    per = blocks // chunks
     clear(count_ref)
-    per = 4
+
+    def give(c):
+        at = pl.ds(c * per, per)
+        return pltpu.make_async_copy(out_ref.at[at], out_hbm.at[at], sems.at[c])
 
     def chunk(c, unused):
         for k in range(per):
@@ -342,9 +382,12 @@
             t, n = next_slot(tile_ref, count_ref, b)
             mine = got_ref[t, pl.ds(pl.multiple_of(n * size, size), size), :]
             out_ref[b] = (feat_ref[b].astype(F32) + mine.astype(F32)).astype(BF16)
-        return unused
-
-    lax.fori_loop(0, blocks // per, chunk, 0)
+        give(c).start()
+        return unused
+
+    lax.fori_loop(0, chunks, chunk, 0)
+    for c in range(chunks):
+        give(c).wait()
 
 
 def shifts(axis):
@@ -395,7 +438,7 @@
     patches = height // PH * ACROSS
     length = most * size
     meta_rows = max(16, most * META)
-    chunks = blocks // 4
+    chunks = blocks // 8
     counts = pltpu.SMEM((tiles,), jnp.int32)
     shape = jax.ShapeDtypeStruct
     bias = lambda b: b.reshape(1, channels)
@@ -406,7 +449,7 @@
     features, send = call(
         embed_kernel,
         [HBM] * 9,
-        [VMEM] * 2,
+        [HBM] * 2,
         (shape((blocks, size, channels), BF16), shape((tiles, length + meta_rows, channels), BF16)),
         [
             pltpu.SMEM((blocks,), jnp.int32),
@@ -418,10 +461,16 @@
             vmem(b_embed),
             vmem(w_proj),
             vmem(b_proj),
+            pltpu.VMEM((blocks, size, channels), BF16),
+            pltpu.VMEM((size, channels), BF16),
             counts,
+            pltpu.SMEM((blocks,), jnp.int32),
             pltpu.VMEM((slots * META, size), F32),
-            pltpu.SemaphoreType.DMA((8,)),
+            pltpu.VMEM((tiles, meta_rows, size), BF16),
+            pltpu.SemaphoreType.DMA((9,)),
             pltpu.SemaphoreType.DMA((chunks,)),
+            pltpu.SemaphoreType.DMA((chunks,)),
+            pltpu.SemaphoreType.DMA((slots,)),
         ],
         6 * obs_feat.size * channels,
         8 * obs_feat.size,
@@ -514,9 +563,9 @@
     obs_out = call(
         final_kernel,
         [SMEM] + [VMEM] * 2,
-        VMEM,
+        HBM,
         shape((blocks, size, channels), BF16),
-        [counts],
+        [pltpu.VMEM((blocks, size, channels), BF16), counts, pltpu.SemaphoreType.DMA((chunks,))],
         1000000,
         8 * obs_feat.size,
         block_tile, features, back,

time: 168 us -> 166 us (0.988)
  Pallas kernels: 22.4 us -> 20.6 us
    pallas_call x8, Pallas kernels: 22.4 us -> 20.6 us  [call(): pl.pallas_call(kernel, in_specs=in_specs, out_specs=out_specs, out_shape=...]
where the time goes in v6:
time: 166 us
  blocking collectives  62.1 us (37%)
  waiting for transfers between devices  57.7 us (35%)
  starting transfers between devices  24.5 us (15%)
  Pallas kernels  20.6 us (12%)
    all_to_all x2, blocking collectives, local(): lax.all_to_all(x, plane, split_axis=0, concat_axis=0, tiled=True)  62.1 us
    ppermute x12, waiting for transfers between devices, turn(): lax.ppermute(x, 'orbits', [(i, (i + way) % size) for i in range(size)])  56.6 us
    pallas_call x8, Pallas kernels, call(): pl.pallas_call(kernel, in_specs=in_specs, out_specs=out_specs, out_shape=...  20.6 us
    ppermute x12, starting transfers between devices, turn(): lax.ppermute(x, 'orbits', [(i, (i + way) % size) for i in range(size)])  16.1 us
    ppermute x4, starting transfers between devices, halo(): return (lax.ppermute(last, axis, up), lax.ppermute(first, axis, down))  8.42 us
  transfers between devices with their start and end apart: 16, of which 12 were waited for; matrix products, arithmetic and copies ran while one was open for 0% of the time, Pallas kernels for 2%

profile of v6, /device:TPU:0, one launch (start us, length us, event | category | flops | bytes accessed | tf_op | source)
XLA Modules:
  0.0 166.1 jit_solution(12900520460802538157)
XLA Ops:
  0.6 4.3 %shard_map.149 = (bf16[32,128,128]{2,1,0:T(8,128)(2,1)}, bf16[8,1056,128]{2,1,0:T(8,128)(2,1)}) custom-call(s32[32]{0:T(128)} %tile_ref.1, s32[32]{0:T(128)} %patch_hbm.1, bf16[2,4096]{1,0:T(2,128)(2,1)} %offset_hbm.1, s32[16,4096]{1,0:T(8,128)} %cells_hbm.1, bf16[4096,128]{1,0:T(8,128)(2,1)} %x_hbm.1, bf16[128,128]{1,0:T(8,128)(2,1)} %we_hbm.1, ...), custom_call_target="tpu_custom_call" | custom-call | flops 402653184 | bytes 4194304 | tf_op jit(solution)/shard_map/pallas_call | solution.py:35
  4.9 32.7 %all_to_all.10.got_ref = bf16[8,1056,128]{2,1,0:T(8,128)(2,1)S(1)} all-to-all(bf16[8,1056,128]{2,1,0:T(8,128)(2,1)} %get-tuple-element.21), channel_id=1, replica_groups=mesh['orbits'=4,'rows'=2,'cols'=4] {'rows','cols'}, dimensions={0} | all-to-all | bytes 4325376 | tf_op jit(solution)/shard_map/all_to_all | solution.py:445
  37.6 4.1 %shard_map.150 = (bf16[576,128]{1,0:T(8,128)(2,1)S(1)}, bf16[576,128]{1,0:T(8,128)(2,1)S(1)}, bf16[576,128]{1,0:T(8,128)(2,1)S(1)}, bf16[576,128]{1,0:T(8,128)(2...) custom-call(bf16[8,1056,128]{2,1,0:T(8,128)(2,1)S(1)} %all_to_all.10, ...), custom_call_target="tpu_custom_call" | custom-call | flops 536870912 | bytes 8388608 | tf_op jit(solution)/shard_map/pallas_call | solution.py:35
  41.7 3.6 %collective-permute-start.3 = (bf16[1536,128]{1,0:T(8,128)(2,1)S(1)}, bf16[1536,128]{1,0:T(8,128)(2,1)S(1)}, u32[]{:S(2)}, u32[]{:S(2)}) collective-permute-start(bf16[1536,128]{1,0:T(8,128)(2,1)S(1)} %get-tuple-element.28), channel_id=1, source_target_pairs={{0,24},{8,0},{16,8},{24,16},{1,25},{9,1},{17,9},{25,17},{2,26},{10... | collective-permute-start | bytes 1179656 | tf_op jit(solution)/shard_map/ppermute | solution.py:406
  45.3 0.0 collective-permute-start
  45.4 12.3 %collective-permute-done = bf16[576,128]{1,0:T(8,128)(2,1)S(1)} collective-permute-done((bf16[576,128]{1,0:T(8,128)(2,1)S(1)}, bf16[576,128]{1,0:T(8,128)(2,1)S(1)}, u32[]{:S(2)}, u32[]{:S(2)}) %collective-permute-start) | collective-permute-done | bytes 147488 | tf_op jit(solution)/shard_map/ppermute | solution.py:406
  57.7 1.7 %collective-permute-start.1 = (bf16[576,128]{1,0:T(8,128)(2,1)S(1)}, bf16[576,128]{1,0:T(8,128)(2,1)S(1)}, u32[]{:S(2)}, u32[]{:S(2)}) collective-permute-start(bf16[576,128]{1,0:T(8,128)(2,1)S(1)} %add.12), channel_id=1, source_target_pairs={{0,8},{8,16},{16,24},{24,0},{1,9},{9,17},{17,25},{25,1},{2,10},{10... | collective-permute-start | bytes 442376 | tf_op jit(solution)/shard_map/ppermute | solution.py:406
  59.4 5.3 %collective-permute-done.1 = bf16[576,128]{1,0:T(8,128)(2,1)S(1)} collective-permute-done((bf16[576,128]{1,0:T(8,128)(2,1)S(1)}, bf16[576,128]{1,0:T(8,128)(2,1)S(1)}, u32[]{:S(2)}, u32[]{:S(2)}) %collective-permute-start.1) | collective-permute-done | bytes 147488 | tf_op jit(solution)/shard_map/ppermute | solution.py:406
  64.8 0.1 collective-permute-start.2
  64.8 0.0 collective-permute-done.3
  64.9 0.0 copy-start.3
  64.9 0.0 copy-start.4
  64.9 0.0 copy-start.5
  64.9 0.0 copy-start.6
  64.9 0.1 add.14
  65.0 3.8 %collective-permute-start.4 = (bf16[1536,128]{1,0:T(8,128)(2,1)S(1)}, bf16[1536,128]{1,0:T(8,128)(2,1)S(1)}, u32[]{:S(2)}, u32[]{:S(2)}) collective-permute-start(bf16[1536,128]{1,0:T(8,128)(2,1)S(1)} %add.14), channel_id=1, source_target_pairs={{0,24},{8,0},{16,8},{24,16},{1,25},{9,1},{17,9},{25,17},{2,26},{10... | collective-permute-start | bytes 1179656 | tf_op jit(solution)/shard_map/ppermute | solution.py:406
  68.8 4.6 %collective-permute-done.2.sum0_ref.sum_ref = bf16[576,128]{1,0:T(8,128)(2,1)S(1)} collective-permute-done((bf16[576,128]{1,0:T(8,128)(2,1)S(1)}, bf16[576,128]{1,0:T(8,128)(2,1)S(1)}, u32[]{:S(2)}, u32[]{:S(2)}) %collective-permute-start.2) | collective-permute-done | bytes 147488 | tf_op jit(solution)/shard_map/ppermute | solution.py:406
  73.4 0.3 shard_map.153
  73.7 1.3 collective-permute-start.7
  75.0 4.5 %collective-permute-start.6 = (bf16[2,128,128]{2,1,0:T(8,128)(2,1)S(1)}, bf16[2,128,128]{2,1,0:T(8,128)(2,1)S(1)}, u32[]{:S(2)}, u32[]{:S(2)}) collective-permute-start(bf16[2,128,128]{2,1,0:T(8,128)(2,1)S(1)} %get-tuple-element.31), channel_id=1, source_target_pairs={{0,4},{4,8},{8,12},{12,16},{16,20},{20,24},{24,28},{1,5},{5,9},{9,... | collective-permute-start | bytes 196616 | tf_op jit(solution)/shard_map/ppermute | solution.py:401
  79.6 0.3 collective-permute-done.7.down_ref
  79.9 0.0 collective-permute-done.4
  79.9 0.1 add.15
  80.0 0.7 collective-permute-start.5
  80.7 0.8 collective-permute-done.6.up_ref
  81.5 1.3 collective-permute-start.8
  82.8 1.3 collective-permute-start.9
  84.1 3.7 %collective-permute-done.5.sum1_ref = bf16[1536,128]{1,0:T(8,128)(2,1)S(1)} collective-permute-done((bf16[1536,128]{1,0:T(8,128)(2,1)S(1)}, bf16[1536,128]{1,0:T(8,128)(2,1)S(1)}, u32[]{:S(2)}, u32[]{:S(2)}) %collective-permute-start.5) | collective-permute-done | bytes 393248 | tf_op jit(solution)/shard_map/ppermute | solution.py:406
  87.8 0.5 shard_map.152.x_ref
  88.4 0.0 collective-permute-done.8.left_ref
  88.4 0.0 collective-permute-done.9.right_ref
  88.4 4.4 %shard_map.154 = (bf16[16,128,128]{2,1,0:T(8,128)(2,1)}, bf16[8,128,128]{2,1,0:T(8,128)(2,1)S(1)}, bf16[8,128,128]{2,1,0:T(8,128)(2,1)S(1)}) custom-call(bf16[16,128,128]{2,1,0:T(8,128)(2,1)S(1)} %shard_map.152.x_ref, bf16[2,128,128]{2,1,0:T(8,128)(2,1)S(1)} %collective-permute-done.6.up_ref, bf16[2,128,128]{2,1,0:T(8,128)(2,1)S(1)} %collective-permute-done.7.down_ref, ...), custom_call_target="tpu_custom_call" | custom-call | flops 1207959552 | bytes 2097152 | tf_op jit(solution)/shard_map/pallas_call | solution.py:35
  92.8 2.5 %collective-permute-start.10 = (bf16[8,128,128]{2,1,0:T(8,128)(2,1)S(1)}, bf16[8,128,128]{2,1,0:T(8,128)(2,1)S(1)}, u32[]{:S(2)}, u32[]{:S(2)}) collective-permute-start(bf16[8,128,128]{2,1,0:T(8,128)(2,1)S(1)} %get-tuple-element.35.refs_0_), channel_id=1, source_target_pairs={{0,8},{8,16},{16,24},{24,0},{1,9},{9,17},{17,25},{25,1},{2,10},{10... | collective-permute-start | bytes 786440 | tf_op jit(solution)/shard_map/ppermute | solution.py:406
  95.3 1.3 collective-permute-start.13
  96.6 7.2 %collective-permute-done.10.refs_1_ = bf16[8,128,128]{2,1,0:T(8,128)(2,1)S(1)} collective-permute-done((bf16[8,128,128]{2,1,0:T(8,128)(2,1)S(1)}, bf16[8,128,128]{2,1,0:T(8,128)(2,1)S(1)}, u32[]{:S(2)}, u32[]{:S(2)}) %collective-permute-start.10) | collective-permute-done | bytes 262176 | tf_op jit(solution)/shard_map/ppermute | solution.py:406
  103.9 5.4 %collective-permute-done.13.refs_5_ = bf16[8,128,128]{2,1,0:T(8,128)(2,1)S(1)} collective-permute-done((bf16[8,128,128]{2,1,0:T(8,128)(2,1)S(1)}, bf16[8,128,128]{2,1,0:T(8,128)(2,1)S(1)}, u32[]{:S(2)}, u32[]{:S(2)}) %collective-permute-start.13) | collective-permute-done | bytes 262176 | tf_op jit(solution)/shard_map/ppermute | solution.py:406
  109.3 1.3 collective-permute-start.14
  110.5 4.6 %collective-permute-done.11.refs_2_ = bf16[8,128,128]{2,1,0:T(8,128)(2,1)S(1)} collective-permute-done((bf16[8,128,128]{2,1,0:T(8,128)(2,1)S(1)}, bf16[8,128,128]{2,1,0:T(8,128)(2,1)S(1)}, u32[]{:S(2)}, u32[]{:S(2)}) %collective-permute-start.11) | collective-permute-done | bytes 262176 | tf_op jit(solution)/shard_map/ppermute | solution.py:406
  115.1 5.5 %collective-permute-done.14.refs_6_ = bf16[8,128,128]{2,1,0:T(8,128)(2,1)S(1)} collective-permute-done((bf16[8,128,128]{2,1,0:T(8,128)(2,1)S(1)}, bf16[8,128,128]{2,1,0:T(8,128)(2,1)S(1)}, u32[]{:S(2)}, u32[]{:S(2)}) %collective-permute-start.14) | collective-permute-done | bytes 262176 | tf_op jit(solution)/shard_map/ppermute | solution.py:406
  120.7 1.1 collective-permute-start.15
  121.8 2.3 %shard_map.151.weights_ref = bf16[64,128,256]{2,1,0:T(8,128)(2,1)S(1)} custom-call(bf16[8,1056,128]{2,1,0:T(8,128)(2,1)S(1)} %all_to_all.10.got_ref), custom_call_target="tpu_custom_call" | custom-call | flops 536870912 | bytes 4194304 | tf_op jit(solution)/shard_map/pallas_call | solution.py:35
  124.1 2.3 %collective-permute-done.12.refs_3_ = bf16[8,128,128]{2,1,0:T(8,128)(2,1)S(1)} collective-permute-done((bf16[8,128,128]{2,1,0:T(8,128)(2,1)S(1)}, bf16[8,128,128]{2,1,0:T(8,128)(2,1)S(1)}, u32[]{:S(2)}, u32[]{:S(2)}) %collective-permute-start.12) | collective-permute-done | bytes 262176 | tf_op jit(solution)/shard_map/ppermute | solution.py:406
  126.4 5.5 %collective-permute-done.15.refs_7_ = bf16[8,128,128]{2,1,0:T(8,128)(2,1)S(1)} collective-permute-done((bf16[8,128,128]{2,1,0:T(8,128)(2,1)S(1)}, bf16[8,128,128]{2,1,0:T(8,128)(2,1)S(1)}, u32[]{:S(2)}, u32[]{:S(2)}) %collective-permute-start.15) | collective-permute-done | bytes 262176 | tf_op jit(solution)/shard_map/ppermute | solution.py:406
  131.9 3.1 %shard_map.155 = bf16[8,1024,128]{2,1,0:T(8,128)(2,1)S(1)} custom-call(s32[64]{0:T(128)S(1)} %get-tuple-element.22.patch_ref, bf16[64,128,256]{2,1,0:T(8,128)(2,1)S(1)} %shard_map.151.weights_ref, bf16[8,128,128]{2,1,0:T(8,128)(2,1)S(1)} %get-tuple-element.35.refs_0_, bf16[8,128,128]{2,1,0:T(8,128)(2,1)S(1)} %collective-permute-done.10.refs_1_, ...), custom_call_target="tpu_custom_call" | custom-call | flops 536870912 | bytes 8388608 | tf_op jit(solution)/shard_map/pallas_call | solution.py:35
  135.1 0.0 copy-start
  135.1 0.0 copy-start.2
  135.1 29.4 %all_to_all.11.got_ref = bf16[8,1024,128]{2,1,0:T(8,128)(2,1)S(1)} all-to-all(bf16[8,1024,128]{2,1,0:T(8,128)(2,1)S(1)} %shard_map.155), channel_id=1, replica_groups=mesh['orbits'=4,'rows'=2,'cols'=4] {'rows','cols'}, dimensions={0} | all-to-all | bytes 4194304 | tf_op jit(solution)/shard_map/all_to_all | solution.py:445
  164.5 1.6 shard_map.156
  (16 shorter events, 0.2 us)
Async XLA Ops:
  37.6 35.9 %copy-start.1 = (f32[128]{0:T(128)S(1)}, f32[128]{0:T(128)}, u32[]{:S(2)}) copy-start(f32[128]{0:T(128)} %param.23) | copy-start | bytes 1540
  41.7 23.1 %collective-permute-start.3 = (bf16[1536,128]{1,0:T(8,128)(2,1)S(1)}, bf16[1536,128]{1,0:T(8,128)(2,1)S(1)}, u32[]{:S(2)}, u32[]{:S(2)}) collective-permute-start(bf16[1536,128]{1,0:T(8,128)(2,1)S(1)} %get-tuple-element.28), channel_id=1, source_target_pairs={{0,24},{8,0},{16,8},{24,16},{1,25},{9,1},{17,9},{25,17},{2,26},{10... | collective-permute-start | bytes 1179656 | tf_op jit(solution)/shard_map/ppermute | solution.py:406
  45.3 12.3 %collective-permute-start = (bf16[576,128]{1,0:T(8,128)(2,1)S(1)}, bf16[576,128]{1,0:T(8,128)(2,1)S(1)}, u32[]{:S(2)}, u32[]{:S(2)}) collective-permute-start(bf16[576,128]{1,0:T(8,128)(2,1)S(1)} %get-tuple-element.24), channel_id=1, source_target_pairs={{0,8},{8,16},{16,24},{24,0},{1,9},{9,17},{17,25},{25,1},{2,10},{10... | collective-permute-start | bytes 442376 | tf_op jit(solution)/shard_map/ppermute | solution.py:406
  57.7 7.0 %collective-permute-start.1 = (bf16[576,128]{1,0:T(8,128)(2,1)S(1)}, bf16[576,128]{1,0:T(8,128)(2,1)S(1)}, u32[]{:S(2)}, u32[]{:S(2)}) collective-permute-start(bf16[576,128]{1,0:T(8,128)(2,1)S(1)} %add.12), channel_id=1, source_target_pairs={{0,8},{8,16},{16,24},{24,0},{1,9},{9,17},{17,25},{25,1},{2,10},{10... | collective-permute-start | bytes 442376 | tf_op jit(solution)/shard_map/ppermute | solution.py:406
  64.8 8.6 %collective-permute-start.2 = (bf16[576,128]{1,0:T(8,128)(2,1)S(1)}, bf16[576,128]{1,0:T(8,128)(2,1)S(1)}, u32[]{:S(2)}, u32[]{:S(2)}) collective-permute-start(bf16[576,128]{1,0:T(8,128)(2,1)S(1)} %add.13), channel_id=1, source_target_pairs={{0,8},{8,16},{16,24},{24,0},{1,9},{9,17},{17,25},{25,1},{2,10},{10... | collective-permute-start | bytes 442376 | tf_op jit(solution)/shard_map/ppermute | solution.py:406
  64.9 23.5 %copy-start.3 = (bf16[3,3,128,128]{3,2,1,0:T(8,128)(2,1)S(1)}, bf16[3,3,128,128]{3,2,1,0:T(8,128)(2,1)}, u32[]{:S(2)}) copy-start(bf16[3,3,128,128]{3,2,1,0:T(8,128)(2,1)} %w1_ref.1) | copy-start | bytes 884740
  64.9 23.5 %copy-start.4 = (bf16[3,3,128,128]{3,2,1,0:T(8,128)(2,1)S(1)}, bf16[3,3,128,128]{3,2,1,0:T(8,128)(2,1)}, u32[]{:S(2)}) copy-start(bf16[3,3,128,128]{3,2,1,0:T(8,128)(2,1)} %w2_ref.1) | copy-start | bytes 884740
  64.9 23.5 %copy-start.5 = (f32[128]{0:T(128)S(1)}, f32[128]{0:T(128)}, u32[]{:S(2)}) copy-start(f32[128]{0:T(128)} %param.25) | copy-start | bytes 1540
  64.9 23.5 %copy-start.6 = (f32[128]{0:T(128)S(1)}, f32[128]{0:T(128)}, u32[]{:S(2)}) copy-start(f32[128]{0:T(128)} %param.27) | copy-start | bytes 1540
  65.0 14.9 %collective-permute-start.4 = (bf16[1536,128]{1,0:T(8,128)(2,1)S(1)}, bf16[1536,128]{1,0:T(8,128)(2,1)S(1)}, u32[]{:S(2)}, u32[]{:S(2)}) collective-permute-start(bf16[1536,128]{1,0:T(8,128)(2,1)S(1)} %add.14), channel_id=1, source_target_pairs={{0,24},{8,0},{16,8},{24,16},{1,25},{9,1},{17,9},{25,17},{2,26},{10... | collective-permute-start | bytes 1179656 | tf_op jit(solution)/shard_map/ppermute | solution.py:406
  73.7 6.2 %collective-permute-start.7 = (bf16[2,128,128]{2,1,0:T(8,128)(2,1)S(1)}, bf16[2,128,128]{2,1,0:T(8,128)(2,1)S(1)}, u32[]{:S(2)}, u32[]{:S(2)}) collective-permute-start(bf16[2,128,128]{2,1,0:T(8,128)(2,1)S(1)} %get-tuple-element.32), channel_id=1, source_target_pairs={{4,0},{8,4},{12,8},{16,12},{20,16},{24,20},{28,24},{5,1},{9,5},{13... | collective-permute-start | bytes 196616 | tf_op jit(solution)/shard_map/ppermute | solution.py:401
  75.0 6.4 %collective-permute-start.6 = (bf16[2,128,128]{2,1,0:T(8,128)(2,1)S(1)}, bf16[2,128,128]{2,1,0:T(8,128)(2,1)S(1)}, u32[]{:S(2)}, u32[]{:S(2)}) collective-permute-start(bf16[2,128,128]{2,1,0:T(8,128)(2,1)S(1)} %get-tuple-element.31), channel_id=1, source_target_pairs={{0,4},{4,8},{8,12},{12,16},{16,20},{20,24},{24,28},{1,5},{5,9},{9,... | collective-permute-start | bytes 196616 | tf_op jit(solution)/shard_map/ppermute | solution.py:401
  80.0 7.8 %collective-permute-start.5 = (bf16[1536,128]{1,0:T(8,128)(2,1)S(1)}, bf16[1536,128]{1,0:T(8,128)(2,1)S(1)}, u32[]{:S(2)}, u32[]{:S(2)}) collective-permute-start(bf16[1536,128]{1,0:T(8,128)(2,1)S(1)} %add.15), channel_id=1, source_target_pairs={{0,24},{8,0},{16,8},{24,16},{1,25},{9,1},{17,9},{25,17},{2,26},{10... | collective-permute-start | bytes 1179656 | tf_op jit(solution)/shard_map/ppermute | solution.py:406
  81.5 6.9 %collective-permute-start.8 = (bf16[20,2,128]{2,1,0:T(2,128)(2,1)S(1)}, bf16[20,2,128]{2,1,0:T(2,128)(2,1)S(1)}, u32[]{:S(2)}, u32[]{:S(2)}) collective-permute-start(bf16[20,2,128]{2,1,0:T(2,128)(2,1)S(1)} %pad_maximum_fusion), channel_id=1, source_target_pairs={{0,1},{1,2},{2,3},{4,5},{5,6},{6,7},{8,9},{9,10},{10,11},{12,13},{... | collective-permute-start | bytes 30728 | tf_op jit(solution)/shard_map/ppermute | solution.py:401
  82.8 5.6 %collective-permute-start.9 = (bf16[20,2,128]{2,1,0:T(2,128)(2,1)S(1)}, bf16[20,2,128]{2,1,0:T(2,128)(2,1)S(1)}, u32[]{:S(2)}, u32[]{:S(2)}) collective-permute-start(bf16[20,2,128]{2,1,0:T(2,128)(2,1)S(1)} %pad_maximum_fusion.1), channel_id=1, source_target_pairs={{1,0},{2,1},{3,2},{5,4},{6,5},{7,6},{9,8},{10,9},{11,10},{13,12},{... | collective-permute-start | bytes 30728 | tf_op jit(solution)/shard_map/ppermute | solution.py:401
  92.8 11.1 %collective-permute-start.10 = (bf16[8,128,128]{2,1,0:T(8,128)(2,1)S(1)}, bf16[8,128,128]{2,1,0:T(8,128)(2,1)S(1)}, u32[]{:S(2)}, u32[]{:S(2)}) collective-permute-start(bf16[8,128,128]{2,1,0:T(8,128)(2,1)S(1)} %get-tuple-element.35.refs_0_), channel_id=1, source_target_pairs={{0,8},{8,16},{16,24},{24,0},{1,9},{9,17},{17,25},{25,1},{2,10},{10... | collective-permute-start | bytes 786440 | tf_op jit(solution)/shard_map/ppermute | solution.py:406
  95.3 14.0 %collective-permute-start.13 = (bf16[8,128,128]{2,1,0:T(8,128)(2,1)S(1)}, bf16[8,128,128]{2,1,0:T(8,128)(2,1)S(1)}, u32[]{:S(2)}, u32[]{:S(2)}) collective-permute-start(bf16[8,128,128]{2,1,0:T(8,128)(2,1)S(1)} %get-tuple-element.36.refs_4_), channel_id=1, source_target_pairs={{0,24},{8,0},{16,8},{24,16},{1,25},{9,1},{17,9},{25,17},{2,26},{10... | collective-permute-start | bytes 786440 | tf_op jit(solution)/shard_map/ppermute | solution.py:406
  103.9 11.3 %collective-permute-start.11 = (bf16[8,128,128]{2,1,0:T(8,128)(2,1)S(1)}, bf16[8,128,128]{2,1,0:T(8,128)(2,1)S(1)}, u32[]{:S(2)}, u32[]{:S(2)}) collective-permute-start(bf16[8,128,128]{2,1,0:T(8,128)(2,1)S(1)} %collective-permute-done.10.refs_1_), channel_id=1, source_target_pairs={{0,8},{8,16},{16,24},{24,0},{1,9},{9,17},{17,25},{25,1},{2,10},{10... | collective-permute-start | bytes 786440 | tf_op jit(solution)/shard_map/ppermute | solution.py:406
  109.3 11.4 %collective-permute-start.14 = (bf16[8,128,128]{2,1,0:T(8,128)(2,1)S(1)}, bf16[8,128,128]{2,1,0:T(8,128)(2,1)S(1)}, u32[]{:S(2)}, u32[]{:S(2)}) collective-permute-start(bf16[8,128,128]{2,1,0:T(8,128)(2,1)S(1)} %collective-permute-done.13.refs_5_), channel_id=1, source_target_pairs={{0,24},{8,0},{16,8},{24,16},{1,25},{9,1},{17,9},{25,17},{2,26},{10... | collective-permute-start | bytes 786440 | tf_op jit(solution)/shard_map/ppermute | solution.py:406
  115.1 11.3 %collective-permute-start.12 = (bf16[8,128,128]{2,1,0:T(8,128)(2,1)S(1)}, bf16[8,128,128]{2,1,0:T(8,128)(2,1)S(1)}, u32[]{:S(2)}, u32[]{:S(2)}) collective-permute-start(bf16[8,128,128]{2,1,0:T(8,128)(2,1)S(1)} %collective-permute-done.11.refs_2_), channel_id=1, source_target_pairs={{0,8},{8,16},{16,24},{24,0},{1,9},{9,17},{17,25},{25,1},{2,10},{10... | collective-permute-start | bytes 786440 | tf_op jit(solution)/shard_map/ppermute | solution.py:406
  120.7 11.3 %collective-permute-start.15 = (bf16[8,128,128]{2,1,0:T(8,128)(2,1)S(1)}, bf16[8,128,128]{2,1,0:T(8,128)(2,1)S(1)}, u32[]{:S(2)}, u32[]{:S(2)}) collective-permute-start(bf16[8,128,128]{2,1,0:T(8,128)(2,1)S(1)} %collective-permute-done.14.refs_6_), channel_id=1, source_target_pairs={{0,24},{8,0},{16,8},{24,16},{1,25},{9,1},{17,9},{25,17},{2,26},{10... | collective-permute-start | bytes 786440 | tf_op jit(solution)/shard_map/ppermute | solution.py:406
  135.1 29.4 %copy-start = (bf16[32,128,128]{2,1,0:T(8,128)(2,1)S(1)}, bf16[32,128,128]{2,1,0:T(8,128)(2,1)}, u32[]{:S(2)}) copy-start(bf16[32,128,128]{2,1,0:T(8,128)(2,1)} %get-tuple-element.20.feat_ref) | copy-start | bytes 3145732
  135.1 29.4 %copy-start.2 = (s32[32]{0:T(128)S(1)}, s32[32]{0:T(128)}, u32[]{:S(2)}) copy-start(s32[32]{0:T(128)} %tile_ref.1) | copy-start | bytes 388

commit v7 on v6

--- a/solution.py
+++ b/solution.py
@@ -15,6 +15,8 @@
 SIDE = 4
 PAD = 8
 META = 4
+BANDS = SR // PH
+GROUP = 4
 EDGE = 2
 EARLY = (0, 1, SR - 2, SR - 1)
 LATE = tuple(r for r in range(SR) if r not in EARLY)
@@ -99,7 +101,7 @@
     zero_ref[...] = jnp.zeros(zero_ref.shape, BF16)
     clear(count_ref)
     row = lax.broadcasted_iota(jnp.int32, meta_ref.shape, 0) % META
-    meta_ref[...] = jnp.where(row == 2, -65536.0, 0.0)
+    meta_ref[...] = jnp.where(row == 2, -65536.0, jnp.where(row == 3, -1.0, 0.0))
     copies[0].wait()
     for b in range(blocks):
         t, n = next_slot(tile_ref, count_ref, b)
@@ -191,46 +193,90 @@
     return lax.rem(lax.axis_index("orbits") + way * (orbits - 1 - k) + orbits * orbits, orbits)
 
 
-def spread_kernel(orbits, most, got_ref, *refs):
-    up, down, (patch_ref, acc_ref, dens_ref) = refs[:orbits], refs[orbits : 2 * orbits], refs[2 * orbits :]
+def choose(list_ref, patch_ref, wanted):
+    def look(slot, count):
+        patch = patch_ref[slot]
+        list_ref[count] = slot
+        return count + jnp.where((patch >= 0) & wanted(jnp.maximum(patch, 0)), 1, 0)
+
+    return lax.fori_loop(0, patch_ref.shape[0], look, 0, unroll=8)
+
+
+def for_chosen(list_ref, count, spare, body):
+    for j in range(GROUP):
+        list_ref[count + j] = spare
+
+    def some(i, unused):
+        for j in range(GROUP):
+            body(list_ref[i * GROUP + j])
+        return unused
+
+    lax.fori_loop(0, (count + GROUP - 1) // GROUP, some, 0)
+
+
+def odd_distance(stripe):
+    return lax.rem(stripe + lax.axis_index("orbits"), 2) == 1
+
+
+def spread_kernel(orbits, most, leading, *refs):
+    ks = range(0 if leading else 1, orbits, 2)
+    if leading:
+        got_ref, *refs = refs
+    else:
+        patch_ref, got_ref, *refs = refs
+    outs, refs = refs[: 2 * len(ks)], refs[2 * len(ks) :]
+    if leading:
+        patch_ref, *refs = refs
+    acc_ref, dens_ref, meta_ref, list_ref = refs
     size, channels = got_ref.shape[2], acc_ref.shape[2]
+    tiles, slots = got_ref.shape[0], patch_ref.shape[0]
+    base, rows_of = most * size, most * META
     acc_ref[...] = jnp.zeros(acc_ref.shape, F32)
     dens_ref[...] = jnp.zeros(dens_ref.shape, F32)
-    base = most * size
-
-    def tile(t, unused):
-        metas = got_ref[t, base:, :].astype(F32)
-        patches = [jnp.max(metas[n * META + 3 : n * META + 4, :]).astype(jnp.int32) for n in range(most)]
-        for n in range(most):
-            patch = patches[n]
-            patch_ref[t * most + n] = patch
-            rows, cols = factors(metas[n * META : (n + 1) * META], False)
-            values = got_ref[t, n * size : (n + 1) * size, :]
-            result = jnp.dot(outer(rows, cols).astype(BF16), values, preferred_element_type=F32)
-            at_row, at_col = place(patch)
-            acc_ref[at_row, at_col, :] += result.reshape(PH, PW, channels)
-            dens_ref[patch] += lax.dot_general(
-                rows.astype(BF16), cols.astype(BF16), (((1,), (1,)), ((), ())), preferred_element_type=F32
-            )
-        return unused
-
-    lax.fori_loop(0, got_ref.shape[0], tile, 0)
-    for k in range(orbits):
-        for out_ref, way, rows in ((up[k], 1, EARLY), (down[k], -1, LATE)):
-            first = stripe_at(k, way) * SR
+    for t in range(tiles):
+        metas = got_ref[t, base:, :].astype(F32)[:rows_of]
+        meta_ref[t * rows_of : (t + 1) * rows_of, :] = metas
+        if leading:
+            for n in range(most):
+                patch_ref[t * most + n] = jnp.max(metas[n * META + 3 : n * META + 4, :]).astype(jnp.int32)
+    meta_ref[slots * META :, :] = jnp.full((meta_ref.shape[0] - slots * META, size), -65536.0, F32)
+    per = BANDS * ACROSS
+    count = choose(list_ref, patch_ref, lambda patch: odd_distance(patch // per) == leading)
+
+    def add(slot):
+        real = jnp.minimum(slot, slots - 1)
+        patch = jnp.maximum(patch_ref[real], 0)
+        metas = meta_ref[pl.ds(slot * META, META), :]
+        rows, cols = factors(metas, False)
+        values = got_ref[real // most, pl.ds(pl.multiple_of(lax.rem(real, most) * size, size), size), :]
+        result = jnp.dot(outer(rows, cols).astype(BF16), values, preferred_element_type=F32)
+        band = patch // ACROSS
+        at_row = band // BANDS // 2 * SR + lax.rem(band, BANDS) * PH
+        at_col = pl.ds(pl.multiple_of(lax.rem(patch, ACROSS) * PW, PW), PW)
+        acc_ref[pl.ds(at_row, PH), at_col, :] += result.reshape(PH, PW, channels)
+        dens_ref[patch] += lax.dot_general(
+            rows.astype(BF16), cols.astype(BF16), (((1,), (1,)), ((), ())), preferred_element_type=F32
+        )
+
+    for_chosen(list_ref, count, slots, add)
+    for j, k in enumerate(ks):
+        for out_ref, way, rows in ((outs[2 * j], 1, EARLY), (outs[2 * j + 1], -1, LATE)):
+            first = stripe_at(k, way) // 2 * SR
             for i, r in enumerate(rows):
                 out_ref[i * TC : (i + 1) * TC, :] = acc_ref[first + r].astype(BF16)
-        first = stripe_at(k, 1) * SR
+        out_ref = outs[2 * j]
+        stripe = stripe_at(k, 1)
+        first = stripe // 2 * SR
         bands = []
-        for band in range(SR // PH):
-            at = (stripe_at(k, 1) * (SR // PH) + band) * ACROSS
+        for band in range(BANDS):
+            at = (stripe * BANDS + band) * ACROSS
             bands.append(jnp.concatenate([dens_ref[at + c] for c in range(ACROSS)], axis=1))
-        up[k][FULL : FULL + SR, :] = jnp.concatenate(bands, axis=0).astype(BF16)
+        out_ref[FULL : FULL + SR, :] = jnp.concatenate(bands, axis=0).astype(BF16)
         cells = [acc_ref[first + r, at] for r in LATE for at in (slice(0, EDGE), slice(TC - EDGE, TC))]
         spare = CELLS - len(LATE) * 2 * EDGE
         if spare:
             cells.append(jnp.zeros((spare, channels), F32))
-        up[k][FULL + SR :, :] = jnp.concatenate(cells, axis=0).astype(BF16)
+        out_ref[FULL + SR :, :] = jnp.concatenate(cells, axis=0).astype(BF16)
 
 
 def weights_kernel(most, got_ref, out_ref):
@@ -287,11 +333,13 @@
             out_ref[r] = grid_values(spread, density(r), weight_ref[...])
 
 
-def conv_kernel(
-    x_ref, up_ref, down_ref, left_ref, right_ref, w1_ref, b1_ref, w2_ref, b2_ref,
-    out_ref, out0_ref, out1_ref, wide_ref, x16_ref, first_ref, wc1_ref, wc2_ref,
-):
-    channels = out_ref.shape[2]
+def conv_kernel(upper, x_ref, halo_ref, left_ref, right_ref, w1_ref, b1_ref, w2_ref, b2_ref, *refs):
+    if upper:
+        band_ref, *refs = refs
+    else:
+        above_ref, out_ref, band_ref, *refs = refs
+    wide_ref, x16_ref, first_ref, wc1_ref, wc2_ref = refs
+    channels = x_ref.shape[2]
     width = x16_ref.shape[1]
     for a in range(3):
         for b in range(3):
@@ -299,16 +347,19 @@
             wc1_ref[at] = w1_ref[a, b]
             wc2_ref[at] = w2_ref[a, b]
     body = slice(PAD, PAD + TC)
+    start = 0 if upper else SR - PH
+    outer_rows, inner_rows = (slice(0, EDGE), slice(EDGE, None)) if upper else (slice(PH + EDGE, None), slice(0, PH + EDGE))
     wide_ref[...] = jnp.zeros(wide_ref.shape, F32)
-    wide_ref[0:2, body] = up_ref[...].astype(F32)
-    wide_ref[2 : 2 + SR, body] = x_ref[...].astype(F32)
-    wide_ref[2 + SR :, body] = down_ref[...].astype(F32)
-    wide_ref[:, PAD - 2 : PAD] = left_ref[...].astype(F32)
-    wide_ref[:, PAD + TC : PAD + TC + 2] = right_ref[...].astype(F32)
+    wide_ref[outer_rows, body] = halo_ref[...].astype(F32)
+    inner = x_ref[0 : PH + EDGE] if upper else x_ref[SR - PH - EDGE :]
+    wide_ref[inner_rows, body] = inner.astype(F32)
+    sides = slice(start, start + PH + 2 * EDGE)
+    wide_ref[:, PAD - EDGE : PAD] = left_ref[sides].astype(F32)
+    wide_ref[:, PAD + TC : PAD + TC + EDGE] = right_ref[sides].astype(F32)
     x16_ref[...] = wide_ref[...].astype(BF16)
 
     def taps(source, first, count, weights):
-        rows = [source[pl.ds(first + a, count)].reshape(count * width, channels) for a in range(3)]
+        rows = [source[first + a : first + a + count].reshape(count * width, channels) for a in range(3)]
         all_taps = jnp.dot(jnp.concatenate(rows, axis=1), weights[...], preferred_element_type=F32)
         return (
             pltpu.roll(all_taps[:, :channels], 1, 0)
@@ -321,49 +372,59 @@
     first_col = jnp.where(at_col > 0, PAD - 1, PAD)
     last_col = jnp.where(at_col < lax.axis_size("cols") - 1, PAD + TC, PAD + TC - 1)
     inside = (col >= first_col) & (col <= last_col)
-    first_row = jnp.where(at_row > 0, 0, 1)
-    last_row = jnp.where(at_row < lax.axis_size(("orbits", "rows")) - 1, SR + 1, SR)
-    count = (SR + 2) // 3
-
-    def first_rows(i, unused):
+    if upper:
+        edge, has_edge = 0, at_row > 0
+    else:
+        edge, has_edge = PH + 1, at_row < lax.axis_size(("orbits", "rows")) - 1
+    count = (PH + 2) // 2
+    for i in range(2):
         value = silu(taps(x16_ref, i * count, count, wc1_ref) + b1_ref[...])
         for r in range(count):
             row = i * count + r
-            keep = inside & (row >= first_row) & (row <= last_row)
+            keep = inside & has_edge if row == edge else inside
             first_ref[row] = jnp.where(keep, value[r * width : (r + 1) * width], 0.0).astype(BF16)
-        return unused
-
-    lax.fori_loop(0, 3, first_rows, 0)
-    again = PH
-
-    def second_rows(i, band_ref):
-        values = taps(first_ref, i * again, again, wc2_ref) + b2_ref[...]
-        for r in range(again):
-            row = i * again + r
-            value = values[r * width + PAD : r * width + PAD + TC] + x_ref[row].astype(F32)
-            out_ref[row] = value.astype(BF16)
-            band_ref[r] = value.astype(BF16)
-
-    second_rows(0, out0_ref)
-    second_rows(1, out1_ref)
-
-
-def read_kernel(orbits, most, patch_ref, weights_ref, *refs):
-    up, down, (out_ref, grid_ref) = refs[:orbits], refs[orbits : 2 * orbits], refs[2 * orbits :]
+    values = taps(first_ref, 0, PH, wc2_ref) + b2_ref[...]
+    for r in range(PH):
+        value = values[r * width + PAD : r * width + PAD + TC] + x_ref[start + r].astype(F32)
+        band_ref[r] = value.astype(BF16)
+        if not upper:
+            out_ref[start + r] = value.astype(BF16)
+    if not upper:
+        out_ref[:start] = above_ref[...]
+
+
+def arrives_last(orbits, patch):
+    band = patch // ACROSS
+    stripe = band // BANDS
+    return jnp.where(
+        lax.rem(band, BANDS) == 0, stripe == stripe_at(0, -1), stripe == stripe_at(0, 1)
+    )
+
+
+def read_kernel(orbits, most, last, patch_ref, weights_ref, *refs):
+    if last:
+        up_ref, down_ref, before_ref, out_ref, grid_ref, list_ref = refs
+        out_ref[...] = before_ref[...]
+        grid_ref[0:PH], grid_ref[PH : 2 * PH] = up_ref[...], down_ref[...]
+    else:
+        count = orbits - 1
+        up, down, (out_ref, grid_ref, list_ref) = refs[:count], refs[count : 2 * count], refs[2 * count :]
+        for k in range(count):
+            for piece_ref, way, band in ((up[k], 1, 0), (down[k], -1, 1)):
+                grid_ref[pl.ds(stripe_at(orbits - 1 - k, -way) * SR + band * PH, PH)] = piece_ref[...]
+        out_ref[...] = jnp.zeros(out_ref.shape, BF16)
     size = out_ref.shape[2]
-    for k in range(orbits):
-        for piece_ref, way, band in ((up[k], 1, 0), (down[k], -1, 1)):
-            grid_ref[pl.ds(stripe_at(orbits - 1 - k, -way) * SR + band * PH, PH)] = piece_ref[...]
-
-    def tile(t, unused):
-        for n in range(most):
-            at_row, at_col = place(patch_ref[t * most + n])
-            values = grid_ref[at_row, at_col, :].reshape(PH * PW, grid_ref.shape[2])
-            result = jnp.dot(weights_ref[t * most + n], values, preferred_element_type=F32)
-            out_ref[t, n * size : (n + 1) * size, :] = result.astype(BF16)
-        return unused
-
-    lax.fori_loop(0, out_ref.shape[0], tile, 0)
+    count = choose(list_ref, patch_ref, lambda patch: arrives_last(orbits, patch) == last)
+
+    def read(slot):
+        patch = jnp.maximum(patch_ref[slot], 0)
+        at_row, at_col = place(lax.rem(patch, BANDS * ACROSS) if last else patch)
+        values = grid_ref[at_row, at_col, :].reshape(PH * PW, grid_ref.shape[2])
+        result = jnp.dot(weights_ref[slot], values, preferred_element_type=F32)
+        at = pl.ds(pl.multiple_of(lax.rem(slot, most) * size, size), size)
+        out_ref[slot // most, at, :] = result.astype(BF16)
+
+    for_chosen(list_ref, count, list_ref[jnp.maximum(count - 1, 0)], read)
 
 
 def final_kernel(tile_ref, feat_ref, got_ref, out_hbm, out_ref, count_ref, sems):
@@ -482,17 +543,36 @@
     flops = 2 * slots * size * channels * PH * PW
     early_shape = shape((FULL + SR + CELLS, channels), BF16)
     late_shape = shape((len(LATE) * TC, channels), BF16)
-    *bands, patch_of = call(
-        functools.partial(spread_kernel, orbits, most),
+    steps = orbits // 2
+    spread_shapes = [early_shape, late_shape] * steps
+    spread_scratch = [
+        pltpu.VMEM((steps * SR, TC, channels), F32),
+        pltpu.VMEM((patches, PH, PW), F32),
+        pltpu.VMEM((slots * META + 8, size), F32),
+        pltpu.SMEM((slots + GROUP,), jnp.int32),
+    ]
+    *leading, patch_of = call(
+        functools.partial(spread_kernel, orbits, most, True),
         [VMEM],
-        [VMEM] * (2 * orbits) + [SMEM],
-        [early_shape] * orbits + [late_shape] * orbits + [shape((slots,), jnp.int32)],
-        [pltpu.VMEM((height, TC, channels), F32), pltpu.VMEM((patches, PH, PW), F32)],
-        flops,
-        8 * slots * size * channels,
+        [VMEM] * (2 * steps) + [SMEM],
+        spread_shapes + [shape((slots,), jnp.int32)],
+        spread_scratch,
+        flops // 2,
+        4 * slots * size * channels,
         got,
     )
-    bands0, bands1 = bands[:orbits], bands[orbits:]
+    others = call(
+        functools.partial(spread_kernel, orbits, most, False),
+        [SMEM, VMEM],
+        [VMEM] * (2 * steps),
+        spread_shapes,
+        spread_scratch,
+        flops // 2,
+        4 * slots * size * channels,
+        patch_of, got,
+    )
+    bands0 = [a for pair in zip(leading[0::2], others[0::2]) for a in pair]
+    bands1 = [a for pair in zip(leading[1::2], others[1::2]) for a in pair]
     sum0, sum1 = ring_sum(bands0, 1), ring_sum(bands1, -1)
     weights = call(
         functools.partial(weights_kernel, most),
@@ -532,32 +612,59 @@
     )
 
     width = TC + 2 * PAD
-    grid_out, band0, band1 = call(
-        conv_kernel,
+    conv_args = (w_first, bias(b_first), w_second, bias(b_second))
+    conv_scratch = [
+        pltpu.VMEM((PH + 4, width, channels), F32),
+        pltpu.VMEM((PH + 4, width, channels), BF16),
+        pltpu.VMEM((PH + 2, width, channels), BF16),
+        pltpu.VMEM((3 * channels, 3 * channels), BF16),
+        pltpu.VMEM((3 * channels, 3 * channels), BF16),
+    ]
+    conv_flops = 2 * 9 * SR * TC * channels * channels
+    band_shape = shape((PH, TC, channels), BF16)
+    band0 = call(
+        functools.partial(conv_kernel, True),
+        [VMEM] * 8,
+        VMEM,
+        band_shape,
+        conv_scratch,
+        conv_flops,
+        4 * grid_in.size,
+        grid_in, above, left, right, *conv_args,
+    )
+    grid_out, band1 = call(
+        functools.partial(conv_kernel, False),
         [VMEM] * 9,
-        [VMEM] * 3,
-        [shape((SR, TC, channels), BF16)] + [shape((PH, TC, channels), BF16)] * 2,
-        [
-            pltpu.VMEM((SR + 4, width, channels), F32),
-            pltpu.VMEM((SR + 4, width, channels), BF16),
-            pltpu.VMEM((SR + 2, width, channels), BF16),
-            pltpu.VMEM((3 * channels, 3 * channels), BF16),
-            pltpu.VMEM((3 * channels, 3 * channels), BF16),
-        ],
-        4 * 9 * SR * TC * channels * channels,
-        8 * grid_in.size,
-        grid_in, above, below, left, right, w_first, bias(b_first), w_second, bias(b_second),
-    )
-
+        [VMEM] * 2,
+        (shape((SR, TC, channels), BF16), band_shape),
+        conv_scratch,
+        conv_flops,
+        4 * grid_in.size,
+        grid_in, below, left, right, *conv_args, band0,
+    )
+
+    up, down = ring_gather(band0, 1), ring_gather(band1, -1)
+    read_shape = shape((tiles, length, channels), BF16)
+    slot_list = pltpu.SMEM((slots + GROUP,), jnp.int32)
     readings = call(
-        functools.partial(read_kernel, orbits, most),
-        [SMEM, VMEM] + [VMEM] * (2 * orbits),
+        functools.partial(read_kernel, orbits, most, False),
+        [SMEM, VMEM] + [VMEM] * (2 * orbits - 2),
         VMEM,
-        shape((tiles, length, channels), BF16),
-        [pltpu.VMEM((height, TC, channels), BF16)],
+        read_shape,
+        [pltpu.VMEM((height, TC, channels), BF16), slot_list],
         flops,
         8 * slots * size * channels,
-        patch_of, weights, *ring_gather(band0, 1), *ring_gather(band1, -1),
+        patch_of, weights, *up[:-1], *down[:-1],
+    )
+    readings = call(
+        functools.partial(read_kernel, orbits, most, True),
+        [SMEM, VMEM, VMEM, VMEM, VMEM],
+        VMEM,
+        read_shape,
+        [pltpu.VMEM((2 * PH, TC, channels), BF16), slot_list],
+        flops // 4,
+        2 * slots * size * channels,
+        patch_of, weights, up[-1], down[-1], readings,
     )
     back = exchange(readings)
     obs_out = call(

time: 166 us -> 166 us (level); the launches traced: 166 us -> 170 us
  starting transfers between devices: 24.5 us -> 37 us
  waiting for transfers between devices: 57.7 us -> 46.1 us
  Pallas kernels: 20.6 us -> 22.6 us
    ppermute x12, starting transfers between devices: 16.1 us -> 31.5 us  [turn(): lax.ppermute(x, 'orbits', [(i, (i + way) % size) for i in range(size)])]
    ppermute x12, waiting for transfers between devices: 56.6 us -> 45 us  [turn(): lax.ppermute(x, 'orbits', [(i, (i + way) % size) for i in range(size)])]
    ppermute x4, starting transfers between devices: 8.42 us -> 5.45 us  [halo(): return (lax.ppermute(last, axis, up), lax.ppermute(first, axis, down))]
    pallas_call x8 -> x11, Pallas kernels: 20.6 us -> 22.6 us  [call(): pl.pallas_call(kernel, in_specs=in_specs, out_specs=out_specs, out_shape=...]
  transfers between devices with their start and end apart: 16 -> 16, of which waited for: 12 -> 13; matrix products, arithmetic and copies ran while one was open for 0% -> 0% of each run, Pallas kernels for 2% -> 5%
where the time goes in v7:
time: 166 us; the launch traced here: 170 us
  blocking collectives  62.6 us (38%)
  waiting for transfers between devices  46.1 us (28%)
  starting transfers between devices  37 us (22%)
  Pallas kernels  22.6 us (14%)
    all_to_all x2, blocking collectives, local(): lax.all_to_all(x, plane, split_axis=0, concat_axis=0, tiled=True)  62.6 us
    ppermute x12, waiting for transfers between devices, turn(): lax.ppermute(x, 'orbits', [(i, (i + way) % size) for i in range(size)])  45 us
    ppermute x12, starting transfers between devices, turn(): lax.ppermute(x, 'orbits', [(i, (i + way) % size) for i in range(size)])  31.5 us
    pallas_call x11, Pallas kernels, call(): pl.pallas_call(kernel, in_specs=in_specs, out_specs=out_specs, out_shape=...  22.6 us
    ppermute x4, starting transfers between devices, halo(): return (lax.ppermute(last, axis, up), lax.ppermute(first, axis, down))  5.45 us
  transfers between devices with their start and end apart: 16, of which 13 were waited for; matrix products, arithmetic and copies ran while one was open for 0% of the time, Pallas kernels for 5%

profile of v7, /device:TPU:0, one launch (start us, length us, event | category | flops | bytes accessed | tf_op | source)
XLA Modules:
  0.0 169.5 jit_solution(6219647236156374413)
XLA Ops:
  0.6 4.3 %shard_map.149 = (bf16[32,128,128]{2,1,0:T(8,128)(2,1)}, bf16[8,1056,128]{2,1,0:T(8,128)(2,1)}) custom-call(s32[32]{0:T(128)} %tile_ref.1, s32[32]{0:T(128)} %patch_hbm.1, bf16[2,4096]{1,0:T(2,128)(2,1)} %offset_hbm.1, s32[16,4096]{1,0:T(8,128)} %cells_hbm.1, bf16[4096,128]{1,0:T(8,128)(2,1)} %x_hbm.1, bf16[128,128]{1,0:T(8,128)(2,1)} %we_hbm.1, ...), custom_call_target="tpu_custom_call" | custom-call | flops 402653184 | bytes 4194304 | tf_op jit(solution)/shard_map/pallas_call | solution.py:37
  4.9 32.7 %all_to_all.10.refs_0_.got_ref.refs_1_ = bf16[8,1056,128]{2,1,0:T(8,128)(2,1)S(1)} all-to-all(bf16[8,1056,128]{2,1,0:T(8,128)(2,1)} %get-tuple-element.20), channel_id=1, replica_groups=mesh['orbits'=4,'rows'=2,'cols'=4] {'rows','cols'}, dimensions={0} | all-to-all | bytes 4325376 | tf_op jit(solution)/shard_map/all_to_all | solution.py:506
  37.6 2.5 %shard_map.150 = (bf16[576,128]{1,0:T(8,128)(2,1)S(1)}, bf16[1536,128]{1,0:T(8,128)(2,1)S(1)}, bf16[576,128]{1,0:T(8,128)(2,1)S(1)}, bf16[1536,128]{1,0:T(8,128)(2,1)S(1)}, s32[64]{0:T(128)S(1)}) custom-call(bf16[8,1056,128]{2,1,0:T(8,128)(2,1)S(1)} %all_to_all.10.refs_0_.got_ref.refs_1_), custom_call_target="tpu_custom_call" | custom-call | flops 268435456 | bytes 4194304 | tf_op jit(solution)/shard_map/pallas_call | solution.py:37
  40.1 0.0 copy-start.1
  40.1 4.4 %collective-permute-start.3 = (bf16[1536,128]{1,0:T(8,128)(2,1)S(1)}, bf16[1536,128]{1,0:T(8,128)(2,1)S(1)}, u32[]{:S(2)}, u32[]{:S(2)}) collective-permute-start(bf16[1536,128]{1,0:T(8,128)(2,1)S(1)} %get-tuple-element.27), channel_id=1, source_target_pairs={{0,24},{8,0},{16,8},{24,16},{1,25},{9,1},{17,9},{25,17},{2,26},{10... | collective-permute-start | bytes 1179656 | tf_op jit(solution)/shard_map/ppermute | solution.py:467
  44.6 2.2 %shard_map.152 = (bf16[576,128]{1,0:T(8,128)(2,1)S(1)}, bf16[1536,128]{1,0:T(8,128)(2,1)S(1)}, bf16[576,128]{1,0:T(8,128)(2,1)S(1)}, bf16[1536,128]{1,0:T(8,128)(2,1)S(1)}) custom-call(s32[64]{0:T(128)S(1)} %get-tuple-element.21.refs_0_.patch_ref, bf16[8,1056,128]{2,1,0:T(8,128)(2,1)S(1)} %all_to_all.10.refs_0_.got_ref.refs_1_), custom_call_target="tpu_custom_call" | custom-call | flops 268435456 | bytes 4194304 | tf_op jit(solution)/shard_map/pallas_call | solution.py:37
  46.7 10.0 %collective-permute-done = bf16[576,128]{1,0:T(8,128)(2,1)S(1)} collective-permute-done((bf16[576,128]{1,0:T(8,128)(2,1)S(1)}, bf16[576,128]{1,0:T(8,128)(2,1)S(1)}, u32[]{:S(2)}, u32[]{:S(2)}) %collective-permute-start) | collective-permute-done | bytes 147488 | tf_op jit(solution)/shard_map/ppermute | solution.py:467
  56.8 1.8 %collective-permute-start.1 = (bf16[576,128]{1,0:T(8,128)(2,1)S(1)}, bf16[576,128]{1,0:T(8,128)(2,1)S(1)}, u32[]{:S(2)}, u32[]{:S(2)}) collective-permute-start(bf16[576,128]{1,0:T(8,128)(2,1)S(1)} %add.12), channel_id=1, source_target_pairs={{0,8},{8,16},{16,24},{24,0},{1,9},{9,17},{17,25},{25,1},{2,10},{10... | collective-permute-start | bytes 442376 | tf_op jit(solution)/shard_map/ppermute | solution.py:467
  58.6 5.2 %collective-permute-done.1 = bf16[576,128]{1,0:T(8,128)(2,1)S(1)} collective-permute-done((bf16[576,128]{1,0:T(8,128)(2,1)S(1)}, bf16[576,128]{1,0:T(8,128)(2,1)S(1)}, u32[]{:S(2)}, u32[]{:S(2)}) %collective-permute-start.1) | collective-permute-done | bytes 147488 | tf_op jit(solution)/shard_map/ppermute | solution.py:467
  63.8 0.1 collective-permute-start.2
  63.9 0.0 copy-start.3
  63.9 0.0 copy-start.4
  63.9 0.0 copy-start.5
  63.9 0.0 copy-start.6
  63.9 0.1 add.14
  64.1 3.8 %collective-permute-start.4 = (bf16[1536,128]{1,0:T(8,128)(2,1)S(1)}, bf16[1536,128]{1,0:T(8,128)(2,1)S(1)}, u32[]{:S(2)}, u32[]{:S(2)}) collective-permute-start(bf16[1536,128]{1,0:T(8,128)(2,1)S(1)} %add.14), channel_id=1, source_target_pairs={{0,24},{8,0},{16,8},{24,16},{1,25},{9,1},{17,9},{25,17},{2,26},{10... | collective-permute-start | bytes 1179656 | tf_op jit(solution)/shard_map/ppermute | solution.py:467
  67.9 4.6 %collective-permute-done.2.sum0_ref.sum_ref = bf16[576,128]{1,0:T(8,128)(2,1)S(1)} collective-permute-done((bf16[576,128]{1,0:T(8,128)(2,1)S(1)}, bf16[576,128]{1,0:T(8,128)(2,1)S(1)}, u32[]{:S(2)}, u32[]{:S(2)}) %collective-permute-start.2) | collective-permute-done | bytes 147488 | tf_op jit(solution)/shard_map/ppermute | solution.py:467
  72.5 0.3 shard_map.154
  72.8 1.6 collective-permute-start.6
  74.4 1.3 collective-permute-start.7
  75.7 0.6 collective-permute-done.6.halo_ref
  76.2 0.8 collective-permute-done.4
  77.0 0.1 add.15
  77.1 2.9 %collective-permute-start.5 = (bf16[1536,128]{1,0:T(8,128)(2,1)S(1)}, bf16[1536,128]{1,0:T(8,128)(2,1)S(1)}, u32[]{:S(2)}, u32[]{:S(2)}) collective-permute-start(bf16[1536,128]{1,0:T(8,128)(2,1)S(1)} %add.15), channel_id=1, source_target_pairs={{0,24},{8,0},{16,8},{24,16},{1,25},{9,1},{17,9},{25,17},{2,26},{10... | collective-permute-start | bytes 1179656 | tf_op jit(solution)/shard_map/ppermute | solution.py:467
  80.0 0.5 collective-permute-done.7.halo_ref
  80.5 1.3 collective-permute-start.8
  81.9 1.3 collective-permute-start.9
  83.2 4.8 %collective-permute-done.5.sum1_ref = bf16[1536,128]{1,0:T(8,128)(2,1)S(1)} collective-permute-done((bf16[1536,128]{1,0:T(8,128)(2,1)S(1)}, bf16[1536,128]{1,0:T(8,128)(2,1)S(1)}, u32[]{:S(2)}, u32[]{:S(2)}) %collective-permute-start.5) | collective-permute-done | bytes 393248 | tf_op jit(solution)/shard_map/ppermute | solution.py:467
  88.0 0.5 shard_map.153.x_ref
  88.6 1.6 shard_map.155.refs_0_
  90.2 2.4 %shard_map.156 = (bf16[16,128,128]{2,1,0:T(8,128)(2,1)}, bf16[8,128,128]{2,1,0:T(8,128)(2,1)S(1)}) custom-call(bf16[16,128,128]{2,1,0:T(8,128)(2,1)S(1)} %shard_map.153.x_ref, bf16[2,128,128]{2,1,0:T(8,128)(2,1)S(1)} %collective-permute-done.7.halo_ref, bf16[20,2,128]{2,1,0:T(2,128)(2,1)S(1)} %collective-permute-done.8.left_ref, ...), custom_call_target="tpu_custom_call" | custom-call | flops 603979776 | bytes 1048576 | tf_op jit(solution)/shard_map/pallas_call | solution.py:37
  92.6 8.2 %collective-permute-start.13 = (bf16[8,128,128]{2,1,0:T(8,128)(2,1)S(1)}, bf16[8,128,128]{2,1,0:T(8,128)(2,1)S(1)}, u32[]{:S(2)}, u32[]{:S(2)}) collective-permute-start(bf16[8,128,128]{2,1,0:T(8,128)(2,1)S(1)} %get-tuple-element.34.refs_3_), channel_id=1, source_target_pairs={{0,24},{8,0},{16,8},{24,16},{1,25},{9,1},{17,9},{25,17},{2,26},{10... | collective-permute-start | bytes 786440 | tf_op jit(solution)/shard_map/ppermute | solution.py:467
  100.8 5.3 %collective-permute-done.13.refs_4_ = bf16[8,128,128]{2,1,0:T(8,128)(2,1)S(1)} collective-permute-done((bf16[8,128,128]{2,1,0:T(8,128)(2,1)S(1)}, bf16[8,128,128]{2,1,0:T(8,128)(2,1)S(1)}, u32[]{:S(2)}, u32[]{:S(2)}) %collective-permute-start.13) | collective-permute-done | bytes 262176 | tf_op jit(solution)/shard_map/ppermute | solution.py:467
  106.1 4.4 %collective-permute-start.14 = (bf16[8,128,128]{2,1,0:T(8,128)(2,1)S(1)}, bf16[8,128,128]{2,1,0:T(8,128)(2,1)S(1)}, u32[]{:S(2)}, u32[]{:S(2)}) collective-permute-start(bf16[8,128,128]{2,1,0:T(8,128)(2,1)S(1)} %collective-permute-done.13.refs_4_), channel_id=1, source_target_pairs={{0,24},{8,0},{16,8},{24,16},{1,25},{9,1},{17,9},{25,17},{2,26},{10... | collective-permute-start | bytes 786440 | tf_op jit(solution)/shard_map/ppermute | solution.py:467
  110.5 1.5 collective-permute-done.10.refs_1_
  112.0 2.2 %collective-permute-start.11 = (bf16[8,128,128]{2,1,0:T(8,128)(2,1)S(1)}, bf16[8,128,128]{2,1,0:T(8,128)(2,1)S(1)}, u32[]{:S(2)}, u32[]{:S(2)}) collective-permute-start(bf16[8,128,128]{2,1,0:T(8,128)(2,1)S(1)} %collective-permute-done.10.refs_1_), channel_id=1, source_target_pairs={{0,8},{8,16},{16,24},{24,0},{1,9},{9,17},{17,25},{25,1},{2,10},{10... | collective-permute-start | bytes 786440 | tf_op jit(solution)/shard_map/ppermute | solution.py:467
  114.2 6.0 %collective-permute-done.14.refs_5_ = bf16[8,128,128]{2,1,0:T(8,128)(2,1)S(1)} collective-permute-done((bf16[8,128,128]{2,1,0:T(8,128)(2,1)S(1)}, bf16[8,128,128]{2,1,0:T(8,128)(2,1)S(1)}, u32[]{:S(2)}, u32[]{:S(2)}) %collective-permute-start.14) | collective-permute-done | bytes 262176 | tf_op jit(solution)/shard_map/ppermute | solution.py:467
  120.2 1.5 collective-permute-start.15
  121.8 1.7 collective-permute-done.11.refs_2_
  123.4 2.0 %collective-permute-start.12 = (bf16[8,128,128]{2,1,0:T(8,128)(2,1)S(1)}, bf16[8,128,128]{2,1,0:T(8,128)(2,1)S(1)}, u32[]{:S(2)}, u32[]{:S(2)}) collective-permute-start(bf16[8,128,128]{2,1,0:T(8,128)(2,1)S(1)} %collective-permute-done.11.refs_2_), channel_id=1, source_target_pairs={{0,8},{8,16},{16,24},{24,0},{1,9},{9,17},{17,25},{25,1},{2,10},{10... | collective-permute-start | bytes 786440 | tf_op jit(solution)/shard_map/ppermute | solution.py:467
  125.5 2.3 %shard_map.151.weights_ref = bf16[64,128,256]{2,1,0:T(8,128)(2,1)S(1)} custom-call(bf16[8,1056,128]{2,1,0:T(8,128)(2,1)S(1)} %all_to_all.10.refs_0_.got_ref.refs_1_), custom_call_target="tpu_custom_call" | custom-call | flops 536870912 | bytes 4194304 | tf_op jit(solution)/shard_map/pallas_call | solution.py:37
  127.7 2.9 %shard_map.157.refs_2_ = bf16[8,1024,128]{2,1,0:T(8,128)(2,1)S(1)} custom-call(s32[64]{0:T(128)S(1)} %get-tuple-element.21.refs_0_.patch_ref, bf16[64,128,256]{2,1,0:T(8,128)(2,1)S(1)} %shard_map.151.weights_ref, bf16[8,128,128]{2,1,0:T(8,128)(2,1)S(1)} %shard_map.155.refs_0_, bf16[8,128,128]{2,1,0:T(8,128)(2,1)S(1)} %collective-permute-done.10.refs_1_, ...), custom_call_target="tpu_custom_call" | custom-call | flops 536870912 | bytes 8388608 | tf_op jit(solution)/shard_map/pallas_call | solution.py:37
  130.7 0.3 collective-permute-done.15.refs_1_
  131.0 4.9 %collective-permute-done.12.refs_0_ = bf16[8,128,128]{2,1,0:T(8,128)(2,1)S(1)} collective-permute-done((bf16[8,128,128]{2,1,0:T(8,128)(2,1)S(1)}, bf16[8,128,128]{2,1,0:T(8,128)(2,1)S(1)}, u32[]{:S(2)}, u32[]{:S(2)}) %collective-permute-start.12) | collective-permute-done | bytes 262176 | tf_op jit(solution)/shard_map/ppermute | solution.py:467
  135.9 2.0 %shard_map.158 = bf16[8,1024,128]{2,1,0:T(8,128)(2,1)S(1)} custom-call(s32[64]{0:T(128)S(1)} %get-tuple-element.21.refs_0_.patch_ref, bf16[64,128,256]{2,1,0:T(8,128)(2,1)S(1)} %shard_map.151.weights_ref, bf16[8,128,128]{2,1,0:T(8,128)(2,1)S(1)} %collective-permute-done.12.refs_0_, bf16[8,128,128]{2,1,0:T(8,128)(2,1)S(1)} %collective-permute-done.15.refs_1_, ...), custom_call_target="tpu_custom_call" | custom-call | flops 134217728 | bytes 2097152 | tf_op jit(solution)/shard_map/pallas_call | solution.py:37
  137.9 0.0 copy-start
  137.9 30.0 %all_to_all.11.got_ref = bf16[8,1024,128]{2,1,0:T(8,128)(2,1)S(1)} all-to-all(bf16[8,1024,128]{2,1,0:T(8,128)(2,1)S(1)} %shard_map.158), channel_id=1, replica_groups=mesh['orbits'=4,'rows'=2,'cols'=4] {'rows','cols'}, dimensions={0} | all-to-all | bytes 4194304 | tf_op jit(solution)/shard_map/all_to_all | solution.py:506
  167.9 1.6 shard_map.159
  (19 shorter events, 0.2 us)
Async XLA Ops:
  40.1 32.4 %copy-start.1 = (f32[128]{0:T(128)S(1)}, f32[128]{0:T(128)}, u32[]{:S(2)}) copy-start(f32[128]{0:T(128)} %param.23) | copy-start | bytes 1540
  40.1 23.8 %collective-permute-start.3 = (bf16[1536,128]{1,0:T(8,128)(2,1)S(1)}, bf16[1536,128]{1,0:T(8,128)(2,1)S(1)}, u32[]{:S(2)}, u32[]{:S(2)}) collective-permute-start(bf16[1536,128]{1,0:T(8,128)(2,1)S(1)} %get-tuple-element.27), channel_id=1, source_target_pairs={{0,24},{8,0},{16,8},{24,16},{1,25},{9,1},{17,9},{25,17},{2,26},{10... | collective-permute-start | bytes 1179656 | tf_op jit(solution)/shard_map/ppermute | solution.py:467
  44.6 12.2 %collective-permute-start = (bf16[576,128]{1,0:T(8,128)(2,1)S(1)}, bf16[576,128]{1,0:T(8,128)(2,1)S(1)}, u32[]{:S(2)}, u32[]{:S(2)}) collective-permute-start(bf16[576,128]{1,0:T(8,128)(2,1)S(1)} %get-tuple-element.23), channel_id=1, source_target_pairs={{0,8},{8,16},{16,24},{24,0},{1,9},{9,17},{17,25},{25,1},{2,10},{10... | collective-permute-start | bytes 442376 | tf_op jit(solution)/shard_map/ppermute | solution.py:467
  56.8 7.0 %collective-permute-start.1 = (bf16[576,128]{1,0:T(8,128)(2,1)S(1)}, bf16[576,128]{1,0:T(8,128)(2,1)S(1)}, u32[]{:S(2)}, u32[]{:S(2)}) collective-permute-start(bf16[576,128]{1,0:T(8,128)(2,1)S(1)} %add.12), channel_id=1, source_target_pairs={{0,8},{8,16},{16,24},{24,0},{1,9},{9,17},{17,25},{25,1},{2,10},{10... | collective-permute-start | bytes 442376 | tf_op jit(solution)/shard_map/ppermute | solution.py:467
  63.8 8.6 %collective-permute-start.2 = (bf16[576,128]{1,0:T(8,128)(2,1)S(1)}, bf16[576,128]{1,0:T(8,128)(2,1)S(1)}, u32[]{:S(2)}, u32[]{:S(2)}) collective-permute-start(bf16[576,128]{1,0:T(8,128)(2,1)S(1)} %add.13), channel_id=1, source_target_pairs={{0,8},{8,16},{16,24},{24,0},{1,9},{9,17},{17,25},{25,1},{2,10},{10... | collective-permute-start | bytes 442376 | tf_op jit(solution)/shard_map/ppermute | solution.py:467
  63.9 24.6 %copy-start.3 = (bf16[3,3,128,128]{3,2,1,0:T(8,128)(2,1)S(1)}, bf16[3,3,128,128]{3,2,1,0:T(8,128)(2,1)}, u32[]{:S(2)}) copy-start(bf16[3,3,128,128]{3,2,1,0:T(8,128)(2,1)} %w1_ref.3) | copy-start | bytes 884740
  63.9 24.6 %copy-start.4 = (bf16[3,3,128,128]{3,2,1,0:T(8,128)(2,1)S(1)}, bf16[3,3,128,128]{3,2,1,0:T(8,128)(2,1)}, u32[]{:S(2)}) copy-start(bf16[3,3,128,128]{3,2,1,0:T(8,128)(2,1)} %w2_ref.3) | copy-start | bytes 884740
  63.9 24.6 %copy-start.5 = (f32[128]{0:T(128)S(1)}, f32[128]{0:T(128)}, u32[]{:S(2)}) copy-start(f32[128]{0:T(128)} %param.25) | copy-start | bytes 1540
  63.9 24.6 %copy-start.6 = (f32[128]{0:T(128)S(1)}, f32[128]{0:T(128)}, u32[]{:S(2)}) copy-start(f32[128]{0:T(128)} %param.27) | copy-start | bytes 1540
  64.1 12.9 %collective-permute-start.4 = (bf16[1536,128]{1,0:T(8,128)(2,1)S(1)}, bf16[1536,128]{1,0:T(8,128)(2,1)S(1)}, u32[]{:S(2)}, u32[]{:S(2)}) collective-permute-start(bf16[1536,128]{1,0:T(8,128)(2,1)S(1)} %add.14), channel_id=1, source_target_pairs={{0,24},{8,0},{16,8},{24,16},{1,25},{9,1},{17,9},{25,17},{2,26},{10... | collective-permute-start | bytes 1179656 | tf_op jit(solution)/shard_map/ppermute | solution.py:467
  72.8 3.5 %collective-permute-start.6 = (bf16[2,128,128]{2,1,0:T(8,128)(2,1)S(1)}, bf16[2,128,128]{2,1,0:T(8,128)(2,1)S(1)}, u32[]{:S(2)}, u32[]{:S(2)}) collective-permute-start(bf16[2,128,128]{2,1,0:T(8,128)(2,1)S(1)} %get-tuple-element.30), channel_id=1, source_target_pairs={{0,4},{4,8},{8,12},{12,16},{16,20},{20,24},{24,28},{1,5},{5,9},{9,... | collective-permute-start | bytes 196616 | tf_op jit(solution)/shard_map/ppermute | solution.py:462
  74.4 6.2 %collective-permute-start.7 = (bf16[2,128,128]{2,1,0:T(8,128)(2,1)S(1)}, bf16[2,128,128]{2,1,0:T(8,128)(2,1)S(1)}, u32[]{:S(2)}, u32[]{:S(2)}) collective-permute-start(bf16[2,128,128]{2,1,0:T(8,128)(2,1)S(1)} %get-tuple-element.32), channel_id=1, source_target_pairs={{4,0},{8,4},{12,8},{16,12},{20,16},{24,20},{28,24},{5,1},{9,5},{13... | collective-permute-start | bytes 196616 | tf_op jit(solution)/shard_map/ppermute | solution.py:462
  77.1 10.9 %collective-permute-start.5 = (bf16[1536,128]{1,0:T(8,128)(2,1)S(1)}, bf16[1536,128]{1,0:T(8,128)(2,1)S(1)}, u32[]{:S(2)}, u32[]{:S(2)}) collective-permute-start(bf16[1536,128]{1,0:T(8,128)(2,1)S(1)} %add.15), channel_id=1, source_target_pairs={{0,24},{8,0},{16,8},{24,16},{1,25},{9,1},{17,9},{25,17},{2,26},{10... | collective-permute-start | bytes 1179656 | tf_op jit(solution)/shard_map/ppermute | solution.py:467
  80.5 8.0 %collective-permute-start.8 = (bf16[20,2,128]{2,1,0:T(2,128)(2,1)S(1)}, bf16[20,2,128]{2,1,0:T(2,128)(2,1)S(1)}, u32[]{:S(2)}, u32[]{:S(2)}) collective-permute-start(bf16[20,2,128]{2,1,0:T(2,128)(2,1)S(1)} %pad_maximum_fusion), channel_id=1, source_target_pairs={{0,1},{1,2},{2,3},{4,5},{5,6},{6,7},{8,9},{9,10},{10,11},{12,13},{... | collective-permute-start | bytes 30728 | tf_op jit(solution)/shard_map/ppermute | solution.py:462
  81.9 6.7 %collective-permute-start.9 = (bf16[20,2,128]{2,1,0:T(2,128)(2,1)S(1)}, bf16[20,2,128]{2,1,0:T(2,128)(2,1)S(1)}, u32[]{:S(2)}, u32[]{:S(2)}) collective-permute-start(bf16[20,2,128]{2,1,0:T(2,128)(2,1)S(1)} %pad_maximum_fusion.1), channel_id=1, source_target_pairs={{1,0},{2,1},{3,2},{5,4},{6,5},{7,6},{9,8},{10,9},{11,10},{13,12},{... | collective-permute-start | bytes 30728 | tf_op jit(solution)/shard_map/ppermute | solution.py:462
  92.6 13.5 %collective-permute-start.13 = (bf16[8,128,128]{2,1,0:T(8,128)(2,1)S(1)}, bf16[8,128,128]{2,1,0:T(8,128)(2,1)S(1)}, u32[]{:S(2)}, u32[]{:S(2)}) collective-permute-start(bf16[8,128,128]{2,1,0:T(8,128)(2,1)S(1)} %get-tuple-element.34.refs_3_), channel_id=1, source_target_pairs={{0,24},{8,0},{16,8},{24,16},{1,25},{9,1},{17,9},{25,17},{2,26},{10... | collective-permute-start | bytes 786440 | tf_op jit(solution)/shard_map/ppermute | solution.py:467
  100.8 11.2 %collective-permute-start.10 = (bf16[8,128,128]{2,1,0:T(8,128)(2,1)S(1)}, bf16[8,128,128]{2,1,0:T(8,128)(2,1)S(1)}, u32[]{:S(2)}, u32[]{:S(2)}) collective-permute-start(bf16[8,128,128]{2,1,0:T(8,128)(2,1)S(1)} %shard_map.155.refs_0_), channel_id=1, source_target_pairs={{0,8},{8,16},{16,24},{24,0},{1,9},{9,17},{17,25},{25,1},{2,10},{10... | collective-permute-start | bytes 786440 | tf_op jit(solution)/shard_map/ppermute | solution.py:467
  106.1 14.1 %collective-permute-start.14 = (bf16[8,128,128]{2,1,0:T(8,128)(2,1)S(1)}, bf16[8,128,128]{2,1,0:T(8,128)(2,1)S(1)}, u32[]{:S(2)}, u32[]{:S(2)}) collective-permute-start(bf16[8,128,128]{2,1,0:T(8,128)(2,1)S(1)} %collective-permute-done.13.refs_4_), channel_id=1, source_target_pairs={{0,24},{8,0},{16,8},{24,16},{1,25},{9,1},{17,9},{25,17},{2,26},{10... | collective-permute-start | bytes 786440 | tf_op jit(solution)/shard_map/ppermute | solution.py:467
  112.0 11.4 %collective-permute-start.11 = (bf16[8,128,128]{2,1,0:T(8,128)(2,1)S(1)}, bf16[8,128,128]{2,1,0:T(8,128)(2,1)S(1)}, u32[]{:S(2)}, u32[]{:S(2)}) collective-permute-start(bf16[8,128,128]{2,1,0:T(8,128)(2,1)S(1)} %collective-permute-done.10.refs_1_), channel_id=1, source_target_pairs={{0,8},{8,16},{16,24},{24,0},{1,9},{9,17},{17,25},{25,1},{2,10},{10... | collective-permute-start | bytes 786440 | tf_op jit(solution)/shard_map/ppermute | solution.py:467
  120.2 10.7 %collective-permute-start.15 = (bf16[8,128,128]{2,1,0:T(8,128)(2,1)S(1)}, bf16[8,128,128]{2,1,0:T(8,128)(2,1)S(1)}, u32[]{:S(2)}, u32[]{:S(2)}) collective-permute-start(bf16[8,128,128]{2,1,0:T(8,128)(2,1)S(1)} %collective-permute-done.14.refs_5_), channel_id=1, source_target_pairs={{0,24},{8,0},{16,8},{24,16},{1,25},{9,1},{17,9},{25,17},{2,26},{10... | collective-permute-start | bytes 786440 | tf_op jit(solution)/shard_map/ppermute | solution.py:467
  123.4 12.5 %collective-permute-start.12 = (bf16[8,128,128]{2,1,0:T(8,128)(2,1)S(1)}, bf16[8,128,128]{2,1,0:T(8,128)(2,1)S(1)}, u32[]{:S(2)}, u32[]{:S(2)}) collective-permute-start(bf16[8,128,128]{2,1,0:T(8,128)(2,1)S(1)} %collective-permute-done.11.refs_2_), channel_id=1, source_target_pairs={{0,8},{8,16},{16,24},{24,0},{1,9},{9,17},{17,25},{25,1},{2,10},{10... | collective-permute-start | bytes 786440 | tf_op jit(solution)/shard_map/ppermute | solution.py:467
  137.9 30.0 %copy-start = (bf16[32,128,128]{2,1,0:T(8,128)(2,1)S(1)}, bf16[32,128,128]{2,1,0:T(8,128)(2,1)}, u32[]{:S(2)}) copy-start(bf16[32,128,128]{2,1,0:T(8,128)(2,1)} %get-tuple-element.19.feat_ref) | copy-start | bytes 3145732
  137.9 30.0 %copy-start.2 = (s32[32]{0:T(128)S(1)}, s32[32]{0:T(128)}, u32[]{:S(2)}) copy-start(s32[32]{0:T(128)} %tile_ref.1) | copy-start | bytes 388

commit v8 on v6

--- a/solution.py
+++ b/solution.py
@@ -15,8 +15,10 @@
 SIDE = 4
 PAD = 8
 META = 4
+BANDS = SR // PH
+GROUP = 8
 EDGE = 2
-EARLY = (0, 1, SR - 2, SR - 1)
+EARLY = (0, 1, SR - 2, SR - 1, 2, 3, 4)
 LATE = tuple(r for r in range(SR) if r not in EARLY)
 FULL = len(EARLY) * TC
 CELLS = -(-len(LATE) * 2 * EDGE // 16) * 16
@@ -31,13 +33,14 @@
 LARGE = 56 * 1024 * 1024
 
 
-def call(kernel, in_specs, out_specs, out_shape, scratch, flops, moved, *args, limit=LIMIT):
+def call(kernel, in_specs, out_specs, out_shape, scratch, flops, moved, *args, limit=LIMIT, aliases={}):
     return pl.pallas_call(
         kernel,
         in_specs=in_specs,
         out_specs=out_specs,
         out_shape=out_shape,
         scratch_shapes=scratch,
+        input_output_aliases=aliases,
         compiler_params=pltpu.CompilerParams(vmem_limit_bytes=limit),
         cost_estimate=pl.CostEstimate(flops=flops, bytes_accessed=moved, transcendentals=0),
     )(*args)
@@ -99,7 +102,7 @@
     zero_ref[...] = jnp.zeros(zero_ref.shape, BF16)
     clear(count_ref)
     row = lax.broadcasted_iota(jnp.int32, meta_ref.shape, 0) % META
-    meta_ref[...] = jnp.where(row == 2, -65536.0, 0.0)
+    meta_ref[...] = jnp.where(row == 2, -65536.0, jnp.where(row == 3, -1.0, 0.0))
     copies[0].wait()
     for b in range(blocks):
         t, n = next_slot(tile_ref, count_ref, b)
@@ -202,8 +205,8 @@
         metas = got_ref[t, base:, :].astype(F32)
         patches = [jnp.max(metas[n * META + 3 : n * META + 4, :]).astype(jnp.int32) for n in range(most)]
         for n in range(most):
-            patch = patches[n]
-            patch_ref[t * most + n] = patch
+            patch_ref[t * most + n] = patches[n]
+            patch = jnp.maximum(patches[n], 0)
             rows, cols = factors(metas[n * META : (n + 1) * META], False)
             values = got_ref[t, n * size : (n + 1) * size, :]
             result = jnp.dot(outer(rows, cols).astype(BF16), values, preferred_element_type=F32)
@@ -214,7 +217,7 @@
             )
         return unused
 
-    lax.fori_loop(0, got_ref.shape[0], tile, 0)
+    lax.fori_loop(0, got_ref.shape[0], tile, 0, unroll=4)
     for k in range(orbits):
         for out_ref, way, rows in ((up[k], 1, EARLY), (down[k], -1, LATE)):
             first = stripe_at(k, way) * SR
@@ -278,17 +281,9 @@
             right_ref[r] = grid_values(cells[at + EDGE : at + 2 * EDGE], d[high], weight)
 
 
-def grid_kernel(own0_ref, sum0_ref, own1_ref, sum1_ref, weight_ref, out_ref):
-    density = densities(own0_ref, sum0_ref)
-    for own_ref, sum_ref, rows in ((own0_ref, sum0_ref, EARLY), (own1_ref, sum1_ref, LATE)):
-        for i, r in enumerate(rows):
-            at = slice(i * TC, (i + 1) * TC)
-            spread = own_ref[at, :].astype(F32) + sum_ref[at, :].astype(F32)
-            out_ref[r] = grid_values(spread, density(r), weight_ref[...])
-
-
 def conv_kernel(
-    x_ref, up_ref, down_ref, left_ref, right_ref, w1_ref, b1_ref, w2_ref, b2_ref,
+    own0_ref, sum0_ref, own1_ref, sum1_ref, weight_ref, up_ref, down_ref, left_ref, right_ref,
+    w1_ref, b1_ref, w2_ref, b2_ref,
     out_ref, out0_ref, out1_ref, wide_ref, x16_ref, first_ref, wc1_ref, wc2_ref,
 ):
     channels = out_ref.shape[2]
@@ -296,24 +291,40 @@
     for a in range(3):
         for b in range(3):
             at = (slice(a * channels, (a + 1) * channels), slice(b * channels, (b + 1) * channels))
+            if a == 2 and b == 2:
+                at = (slice(channels, 2 * channels), slice(3 * channels, None))
             wc1_ref[at] = w1_ref[a, b]
             wc2_ref[at] = w2_ref[a, b]
+    spare = (slice(0, channels), slice(3 * channels, None))
+    wc1_ref[spare] = jnp.zeros((channels, channels), BF16)
+    wc2_ref[spare] = jnp.zeros((channels, channels), BF16)
     body = slice(PAD, PAD + TC)
-    wide_ref[...] = jnp.zeros(wide_ref.shape, F32)
-    wide_ref[0:2, body] = up_ref[...].astype(F32)
-    wide_ref[2 : 2 + SR, body] = x_ref[...].astype(F32)
-    wide_ref[2 + SR :, body] = down_ref[...].astype(F32)
-    wide_ref[:, PAD - 2 : PAD] = left_ref[...].astype(F32)
-    wide_ref[:, PAD + TC : PAD + TC + 2] = right_ref[...].astype(F32)
+    wide_ref[:, :PAD] = jnp.zeros((wide_ref.shape[0], PAD, channels), F32)
+    wide_ref[:, PAD + TC :] = jnp.zeros((wide_ref.shape[0], PAD, channels), F32)
+    density = densities(own0_ref, sum0_ref)
+    for own_ref, sum_ref, rows in ((own0_ref, sum0_ref, EARLY), (own1_ref, sum1_ref, LATE)):
+        for i, r in enumerate(rows):
+            at = slice(i * TC, (i + 1) * TC)
+            spread = own_ref[at, :].astype(F32) + sum_ref[at, :].astype(F32)
+            wide_ref[EDGE + r, body] = grid_values(spread, density(r), weight_ref[...]).astype(F32)
+    wide_ref[0:EDGE, body] = up_ref[...].astype(F32)
+    wide_ref[EDGE + SR :, body] = down_ref[...].astype(F32)
+    wide_ref[:, PAD - EDGE : PAD] = left_ref[...].astype(F32)
+    wide_ref[:, PAD + TC : PAD + TC + EDGE] = right_ref[...].astype(F32)
     x16_ref[...] = wide_ref[...].astype(BF16)
 
     def taps(source, first, count, weights):
         rows = [source[pl.ds(first + a, count)].reshape(count * width, channels) for a in range(3)]
-        all_taps = jnp.dot(jnp.concatenate(rows, axis=1), weights[...], preferred_element_type=F32)
+        near = jnp.dot(jnp.concatenate(rows, axis=1), weights[:, : 2 * channels], preferred_element_type=F32)
+        more = [source[pl.ds(first + a, count + 1)].reshape((count + 1) * width, channels) for a in range(2)]
+        far = jnp.dot(
+            jnp.concatenate(more, axis=1), weights[: 2 * channels, 2 * channels :], preferred_element_type=F32
+        )
+        right = far[: count * width, :channels] + far[width:, channels:]
         return (
-            pltpu.roll(all_taps[:, :channels], 1, 0)
-            + all_taps[:, channels : 2 * channels]
-            + pltpu.roll(all_taps[:, 2 * channels :], count * width - 1, 0)
+            pltpu.roll(near[:, :channels], 1, 0)
+            + near[:, channels:]
+            + pltpu.roll(right, count * width - 1, 0)
         )
 
     at_row, at_col = lax.axis_index(("orbits", "rows")), lax.axis_index("cols")
@@ -323,7 +334,7 @@
     inside = (col >= first_col) & (col <= last_col)
     first_row = jnp.where(at_row > 0, 0, 1)
     last_row = jnp.where(at_row < lax.axis_size(("orbits", "rows")) - 1, SR + 1, SR)
-    count = (SR + 2) // 3
+    count = (SR + 2) // 2
 
     def first_rows(i, unused):
         value = silu(taps(x16_ref, i * count, count, wc1_ref) + b1_ref[...])
@@ -333,14 +344,14 @@
             first_ref[row] = jnp.where(keep, value[r * width : (r + 1) * width], 0.0).astype(BF16)
         return unused
 
-    lax.fori_loop(0, 3, first_rows, 0)
+    lax.fori_loop(0, 2, first_rows, 0)
     again = PH
 
     def second_rows(i, band_ref):
         values = taps(first_ref, i * again, again, wc2_ref) + b2_ref[...]
         for r in range(again):
             row = i * again + r
-            value = values[r * width + PAD : r * width + PAD + TC] + x_ref[row].astype(F32)
+            value = values[r * width + PAD : r * width + PAD + TC] + wide_ref[row + EDGE, body]
             out_ref[row] = value.astype(BF16)
             band_ref[r] = value.astype(BF16)
 
@@ -348,22 +359,77 @@
     second_rows(1, out1_ref)
 
 
+def arrives_last(patch):
+    band = patch // ACROSS
+    stripe = band // BANDS
+    return jnp.where(lax.rem(band, BANDS) == 0, stripe == stripe_at(0, -1), stripe == stripe_at(0, 1))
+
+
+def read_slot(grid_ref, weights_ref, slot, patch):
+    at_row, at_col = place(jnp.maximum(patch, 0))
+    values = grid_ref[at_row, at_col, :].reshape(PH * PW, grid_ref.shape[2])
+    return jnp.dot(weights_ref[slot], values, preferred_element_type=F32).astype(BF16)
+
+
 def read_kernel(orbits, most, patch_ref, weights_ref, *refs):
-    up, down, (out_ref, grid_ref) = refs[:orbits], refs[orbits : 2 * orbits], refs[2 * orbits :]
-    size = out_ref.shape[2]
-    for k in range(orbits):
+    count = orbits - 1
+    up, down, (out_ref, list_ref, grid_ref) = refs[:count], refs[count : 2 * count], refs[2 * count :]
+    size, slots = out_ref.shape[2], patch_ref.shape[0]
+    grid_ref[...] = jnp.zeros(grid_ref.shape, BF16)
+    for k in range(count):
         for piece_ref, way, band in ((up[k], 1, 0), (down[k], -1, 1)):
             grid_ref[pl.ds(stripe_at(orbits - 1 - k, -way) * SR + band * PH, PH)] = piece_ref[...]
 
     def tile(t, unused):
         for n in range(most):
-            at_row, at_col = place(patch_ref[t * most + n])
-            values = grid_ref[at_row, at_col, :].reshape(PH * PW, grid_ref.shape[2])
-            result = jnp.dot(weights_ref[t * most + n], values, preferred_element_type=F32)
-            out_ref[t, n * size : (n + 1) * size, :] = result.astype(BF16)
+            slot = t * most + n
+            out_ref[t, n * size : (n + 1) * size, :] = read_slot(grid_ref, weights_ref, slot, patch_ref[slot])
         return unused
 
     lax.fori_loop(0, out_ref.shape[0], tile, 0)
+
+    def look(slot, late):
+        list_ref[late] = slot
+        patch = patch_ref[slot]
+        return late + jnp.where((patch >= 0) & arrives_last(jnp.maximum(patch, 0)), 1, 0)
+
+    late = lax.fori_loop(0, slots, look, 0, unroll=8)
+    for j in range(GROUP):
+        list_ref[late + j] = 0
+    list_ref[slots + GROUP] = late
+
+
+def late_kernel(most, patch_ref, list_ref, weights_ref, up_ref, down_ref, _, out_hbm, grid_ref, result_ref, sems):
+    size, slots = result_ref.shape[1], patch_ref.shape[0]
+    grid_ref[0:PH], grid_ref[PH:] = up_ref[...], down_ref[...]
+    late = list_ref[slots + GROUP]
+
+    def give(i):
+        slot = list_ref[i]
+        rows = pl.ds(pl.multiple_of(lax.rem(slot, most) * size, size), size)
+        return pltpu.make_async_copy(result_ref.at[i], out_hbm.at[slot // most, rows], sems.at[i])
+
+    def some(c, unused):
+        for j in range(GROUP):
+            i = c * GROUP + j
+            slot = list_ref[i]
+            patch = lax.rem(jnp.maximum(patch_ref[slot], 0), BANDS * ACROSS)
+            result_ref[i] = read_slot(grid_ref, weights_ref, slot, patch)
+        for j in range(GROUP):
+            i = c * GROUP + j
+
+            @pl.when(i < late)
+            def _():
+                give(i).start()
+
+        return unused
+
+    def finish(i, unused):
+        give(i).wait()
+        return unused
+
+    lax.fori_loop(0, (late + GROUP - 1) // GROUP, some, 0)
+    lax.fori_loop(0, late, finish, 0)
 
 
 def final_kernel(tile_ref, feat_ref, got_ref, out_hbm, out_ref, count_ref, sems):
@@ -406,13 +472,29 @@
     return lax.ppermute(x, "orbits", [(i, (i + way) % size) for i in range(size)])
 
 
-def ring_sum(stripes, way):
-    total = stripes[0]
-    for k in range(1, len(stripes)):
+TIES = {2: 1}
+
+
+def ring_sums(leading, following):
+    orbits = len(leading)
+    first, second = leading[0], following[0]
+    done = 0
+
+    def step(total, stripes, k, way):
         total = turn(total, way)
-        if k < len(stripes) - 1:
-            total = total + stripes[k]
-    return total
+        return total + stripes[k] if k < orbits - 1 else total
+
+    for k in range(1, orbits):
+        first = step(first, leading, k, 1)
+        while done < TIES.get(k, 0):
+            done += 1
+            second = step(second, following, done, -1)
+        if k in TIES:
+            first, second = lax.optimization_barrier((first, second))
+    while done < orbits - 1:
+        done += 1
+        second = step(second, following, done, -1)
+    return first, second
 
 
 def ring_gather(x, way):
@@ -493,7 +575,7 @@
         got,
     )
     bands0, bands1 = bands[:orbits], bands[orbits:]
-    sum0, sum1 = ring_sum(bands0, 1), ring_sum(bands1, -1)
+    sum0, sum1 = ring_sums(bands0, bands1)
     weights = call(
         functools.partial(weights_kernel, most),
         [VMEM],
@@ -520,44 +602,51 @@
     left = jnp.concatenate([above[:, :EDGE], left, below[:, :EDGE]], axis=0)
     right = jnp.concatenate([above[:, TC - EDGE :], right, below[:, TC - EDGE :]], axis=0)
     left, right = halo(left, right, "cols")
-    grid_in = call(
-        grid_kernel,
-        [VMEM] * 5,
-        VMEM,
-        shape((SR, TC, channels), BF16),
-        [],
-        10000000,
-        8 * SR * TC * channels,
-        bands0[-1], sum0, bands1[-1], sum1, density_weight,
-    )
-
+    sum1, weights = lax.optimization_barrier((sum1, weights))
     width = TC + 2 * PAD
     grid_out, band0, band1 = call(
         conv_kernel,
-        [VMEM] * 9,
+        [VMEM] * 13,
         [VMEM] * 3,
         [shape((SR, TC, channels), BF16)] + [shape((PH, TC, channels), BF16)] * 2,
         [
             pltpu.VMEM((SR + 4, width, channels), F32),
             pltpu.VMEM((SR + 4, width, channels), BF16),
             pltpu.VMEM((SR + 2, width, channels), BF16),
-            pltpu.VMEM((3 * channels, 3 * channels), BF16),
-            pltpu.VMEM((3 * channels, 3 * channels), BF16),
+            pltpu.VMEM((3 * channels, 4 * channels), BF16),
+            pltpu.VMEM((3 * channels, 4 * channels), BF16),
         ],
         4 * 9 * SR * TC * channels * channels,
-        8 * grid_in.size,
-        grid_in, above, below, left, right, w_first, bias(b_first), w_second, bias(b_second),
-    )
-
-    readings = call(
+        8 * SR * TC * channels,
+        bands0[-1], sum0, bands1[-1], sum1, density_weight, above, below, left, right, w_first, bias(b_first), w_second, bias(b_second),
+    )
+
+    up, down = ring_gather(band0, 1), ring_gather(band1, -1)
+    read_shape = shape((tiles, length, channels), BF16)
+    readings, late = call(
         functools.partial(read_kernel, orbits, most),
-        [SMEM, VMEM] + [VMEM] * (2 * orbits),
-        VMEM,
-        shape((tiles, length, channels), BF16),
+        [SMEM] + [VMEM] * (2 * orbits - 1),
+        [VMEM, SMEM],
+        (read_shape, shape((slots + GROUP + 1,), jnp.int32)),
         [pltpu.VMEM((height, TC, channels), BF16)],
         flops,
         8 * slots * size * channels,
-        patch_of, weights, *ring_gather(band0, 1), *ring_gather(band1, -1),
+        patch_of, weights, *up[:-1], *down[:-1],
+    )
+    readings = call(
+        functools.partial(late_kernel, most),
+        [SMEM] * 2 + [VMEM] * 3 + [HBM],
+        HBM,
+        read_shape,
+        [
+            pltpu.VMEM((BANDS * PH, TC, channels), BF16),
+            pltpu.VMEM((slots + GROUP, size, channels), BF16),
+            pltpu.SemaphoreType.DMA((slots + GROUP,)),
+        ],
+        flops // 4,
+        2 * slots * size * channels,
+        patch_of, late, weights, up[-1], down[-1], readings,
+        aliases={5: 0},
     )
     back = exchange(readings)
     obs_out = call(

time: 166 us -> 166 us (level)
  starting transfers between devices: 24.5 us -> 36.2 us
  waiting for transfers between devices: 57.7 us -> 46.3 us
  Pallas kernels: 20.6 us -> 22.6 us
    ppermute x12, starting transfers between devices: 16.1 us -> 29.7 us  [turn(): lax.ppermute(x, 'orbits', [(i, (i + way) % size) for i in range(size)])]
    ppermute x12, waiting for transfers between devices: 56.6 us -> 43 us  [turn(): lax.ppermute(x, 'orbits', [(i, (i + way) % size) for i in range(size)])]
    ppermute x4, waiting for transfers between devices: 1.07 us -> 3.29 us  [halo(): return (lax.ppermute(last, axis, up), lax.ppermute(first, axis, down))]
    pallas_call x8, Pallas kernels: 20.6 us -> 22.6 us  [call(): pl.pallas_call(kernel, in_specs=in_specs, out_specs=out_specs, out_shape=...]
    ppermute x4, starting transfers between devices: 8.42 us -> 6.47 us  [halo(): return (lax.ppermute(last, axis, up), lax.ppermute(first, axis, down))]
  transfers between devices with their start and end apart: 16 -> 16, of which waited for: 12 -> 10; matrix products, arithmetic and copies ran while one was open for 0% -> 0% of each run, Pallas kernels for 2% -> 4%
where the time goes in v8:
time: 166 us; the launch traced here: 168 us
  blocking collectives  61.2 us (37%)
  waiting for transfers between devices  46.3 us (28%)
  starting transfers between devices  36.2 us (22%)
  Pallas kernels  22.6 us (14%)
    all_to_all x2, blocking collectives, local(): lax.all_to_all(x, plane, split_axis=0, concat_axis=0, tiled=True)  61.2 us
    ppermute x12, waiting for transfers between devices, turn(): lax.ppermute(x, 'orbits', [(i, (i + way) % size) for i in range(size)])  43 us
    ppermute x12, starting transfers between devices, turn(): lax.ppermute(x, 'orbits', [(i, (i + way) % size) for i in range(size)])  29.7 us
    pallas_call x8, Pallas kernels, call(): pl.pallas_call(kernel, in_specs=in_specs, out_specs=out_specs, out_shape=...  22.6 us
    ppermute x4, starting transfers between devices, halo(): return (lax.ppermute(last, axis, up), lax.ppermute(first, axis, down))  6.47 us
  transfers between devices with their start and end apart: 16, of which 10 were waited for; matrix products, arithmetic and copies ran while one was open for 0% of the time, Pallas kernels for 4%

profile of v8, /device:TPU:0, one launch (start us, length us, event | category | flops | bytes accessed | tf_op | source)
XLA Modules:
  0.0 167.6 jit_solution(5764168479746824597)
XLA Ops:
  0.6 4.3 %shard_map.149 = (bf16[32,128,128]{2,1,0:T(8,128)(2,1)}, bf16[8,1056,128]{2,1,0:T(8,128)(2,1)}) custom-call(s32[32]{0:T(128)} %tile_ref.1, s32[32]{0:T(128)} %patch_hbm.1, bf16[2,4096]{1,0:T(2,128)(2,1)} %offset_hbm.1, s32[16,4096]{1,0:T(8,128)} %cells_hbm.1, bf16[4096,128]{1,0:T(8,128)(2,1)} %x_hbm.1, bf16[128,128]{1,0:T(8,128)(2,1)} %we_hbm.1, ...), custom_call_target="tpu_custom_call" | custom-call | flops 402653184 | bytes 4194304 | tf_op jit(solution)/shard_map/pallas_call | solution.py:37
  4.9 32.7 %all_to_all.10.got_ref = bf16[8,1056,128]{2,1,0:T(8,128)(2,1)S(1)} all-to-all(bf16[8,1056,128]{2,1,0:T(8,128)(2,1)} %get-tuple-element.27), channel_id=1, replica_groups=mesh['orbits'=4,'rows'=2,'cols'=4] {'rows','cols'}, dimensions={0} | all-to-all | bytes 4325376 | tf_op jit(solution)/shard_map/all_to_all | solution.py:527
  37.6 3.2 %shard_map.150 = (bf16[960,128]{1,0:T(8,128)(2,1)S(1)}, bf16[960,128]{1,0:T(8,128)(2,1)S(1)}, bf16[960,128]{1,0:T(8,128)(2,1)S(1)}, bf16[960,128]{1,0:T(8,128)(2...) custom-call(bf16[8,1056,128]{2,1,0:T(8,128)(2,1)S(1)} %all_to_all.10, ...), custom_call_target="tpu_custom_call" | custom-call | flops 536870912 | bytes 8388608 | tf_op jit(solution)/shard_map/pallas_call | solution.py:37
  40.8 1.6 collective-permute-start
  42.4 2.2 %collective-permute-start.2 = (bf16[1152,128]{1,0:T(8,128)(2,1)S(1)}, bf16[1152,128]{1,0:T(8,128)(2,1)S(1)}, u32[]{:S(2)}, u32[]{:S(2)}) collective-permute-start(bf16[1152,128]{1,0:T(8,128)(2,1)S(1)} %get-tuple-element.32), channel_id=1, source_target_pairs={{0,24},{8,0},{16,8},{24,16},{1,25},{9,1},{17,9},{25,17},{2,26},{10... | collective-permute-start | bytes 884744 | tf_op jit(solution)/shard_map/ppermute | solution.py:472
  44.7 6.9 %collective-permute-done = bf16[960,128]{1,0:T(8,128)(2,1)S(1)} collective-permute-done((bf16[960,128]{1,0:T(8,128)(2,1)S(1)}, bf16[960,128]{1,0:T(8,128)(2,1)S(1)}, u32[]{:S(2)}, u32[]{:S(2)}) %collective-permute-start) | collective-permute-done | bytes 245792 | tf_op jit(solution)/shard_map/ppermute | solution.py:472
  51.6 0.1 add.12
  51.6 0.1 collective-permute-start.1
  51.7 5.0 %collective-permute-done.2 = bf16[1152,128]{1,0:T(8,128)(2,1)S(1)} collective-permute-done((bf16[1152,128]{1,0:T(8,128)(2,1)S(1)}, bf16[1152,128]{1,0:T(8,128)(2,1)S(1)}, u32[]{:S(2)}, u32[]{:S(2)}) %collective-permute-start.2) | collective-permute-done | bytes 294944 | tf_op jit(solution)/shard_map/ppermute | solution.py:472
  56.7 0.1 add.14
  56.8 5.2 %collective-permute-done.1 = bf16[960,128]{1,0:T(8,128)(2,1)S(1)} collective-permute-done((bf16[960,128]{1,0:T(8,128)(2,1)S(1)}, bf16[960,128]{1,0:T(8,128)(2,1)S(1)}, u32[]{:S(2)}, u32[]{:S(2)}) %collective-permute-start.1) | collective-permute-done | bytes 245792 | tf_op jit(solution)/shard_map/ppermute | solution.py:472
  61.9 0.1 add.13
  62.0 0.1 collective-permute-start.5
  62.1 3.8 %collective-permute-start.3 = (bf16[1152,128]{1,0:T(8,128)(2,1)S(1)}, bf16[1152,128]{1,0:T(8,128)(2,1)S(1)}, u32[]{:S(2)}, u32[]{:S(2)}) collective-permute-start(bf16[1152,128]{1,0:T(8,128)(2,1)S(1)} %add.14), channel_id=1, source_target_pairs={{0,24},{8,0},{16,8},{24,16},{1,25},{9,1},{17,9},{25,17},{2,26},{10... | collective-permute-start | bytes 884744 | tf_op jit(solution)/shard_map/ppermute | solution.py:472
  65.9 6.9 %collective-permute-done.5.sum_ref.sum0_ref = bf16[960,128]{1,0:T(8,128)(2,1)S(1)} collective-permute-done((bf16[960,128]{1,0:T(8,128)(2,1)S(1)}, bf16[960,128]{1,0:T(8,128)(2,1)S(1)}, u32[]{:S(2)}, u32[]{:S(2)}) %collective-permute-start.5) | collective-permute-done | bytes 245792 | tf_op jit(solution)/shard_map/ppermute | solution.py:472
  72.8 0.3 shard_map.152
  73.1 2.5 %collective-permute-start.6 = (bf16[2,128,128]{2,1,0:T(8,128)(2,1)S(1)}, bf16[2,128,128]{2,1,0:T(8,128)(2,1)S(1)}, u32[]{:S(2)}, u32[]{:S(2)}) collective-permute-start(bf16[2,128,128]{2,1,0:T(8,128)(2,1)S(1)} %get-tuple-element.41), channel_id=1, source_target_pairs={{0,4},{4,8},{8,12},{12,16},{16,20},{20,24},{24,28},{1,5},{5,9},{9,... | collective-permute-start | bytes 196616 | tf_op jit(solution)/shard_map/ppermute | solution.py:467
  75.6 1.3 collective-permute-start.7
  76.9 0.0 collective-permute-done.3
  76.9 0.1 add.15
  77.0 2.7 %collective-permute-start.4 = (bf16[1152,128]{1,0:T(8,128)(2,1)S(1)}, bf16[1152,128]{1,0:T(8,128)(2,1)S(1)}, u32[]{:S(2)}, u32[]{:S(2)}) collective-permute-start(bf16[1152,128]{1,0:T(8,128)(2,1)S(1)} %add.15), channel_id=1, source_target_pairs={{0,24},{8,0},{16,8},{24,16},{1,25},{9,1},{17,9},{25,17},{2,26},{10... | collective-permute-start | bytes 884744 | tf_op jit(solution)/shard_map/ppermute | solution.py:472
  79.7 0.0 collective-permute-done.6.up_ref
  79.7 3.3 %collective-permute-done.7.down_ref = bf16[2,128,128]{2,1,0:T(8,128)(2,1)S(1)} collective-permute-done((bf16[2,128,128]{2,1,0:T(8,128)(2,1)S(1)}, bf16[2,128,128]{2,1,0:T(8,128)(2,1)S(1)}, u32[]{:S(2)}, u32[]{:S(2)}) %collective-permute-start.7) | collective-permute-done | bytes 65568 | tf_op jit(solution)/shard_map/ppermute | solution.py:467
  83.0 1.3 collective-permute-start.8
  84.3 0.0 copy-start.3
  84.3 0.0 copy-start.4
  84.3 0.0 copy-start.5
  84.4 0.0 copy-start.6
  84.4 1.4 collective-permute-start.9
  85.8 2.3 %shard_map.151.weights_ref = bf16[64,128,256]{2,1,0:T(8,128)(2,1)S(1)} custom-call(bf16[8,1056,128]{2,1,0:T(8,128)(2,1)S(1)} %all_to_all.10.got_ref), custom_call_target="tpu_custom_call" | custom-call | flops 536870912 | bytes 4194304 | tf_op jit(solution)/shard_map/pallas_call | solution.py:37
  88.1 0.0 collective-permute-done.4.sum1_ref
  88.1 4.4 %shard_map.153 = (bf16[16,128,128]{2,1,0:T(8,128)(2,1)}, bf16[8,128,128]{2,1,0:T(8,128)(2,1)S(1)}, bf16[8,128,128]{2,1,0:T(8,128)(2,1)S(1)}) custom-call(bf16[960,128]{1,0:T(8,128)(2,1)S(1)} %get-tuple-element.37.own_ref.own0_ref, bf16[960,128]{1,0:T(8,128)(2,1)S(1)} %collective-permute-done.5.sum_ref.sum0_ref, ...), custom_call_target="tpu_custom_call" | custom-call | flops 1207959552 | bytes 2097152 | tf_op jit(solution)/shard_map/pallas_call | solution.py:37
  92.5 3.8 %collective-permute-start.10 = (bf16[8,128,128]{2,1,0:T(8,128)(2,1)S(1)}, bf16[8,128,128]{2,1,0:T(8,128)(2,1)S(1)}, u32[]{:S(2)}, u32[]{:S(2)}) collective-permute-start(bf16[8,128,128]{2,1,0:T(8,128)(2,1)S(1)} %get-tuple-element.45.refs_0_), channel_id=1, source_target_pairs={{0,8},{8,16},{16,24},{24,0},{1,9},{9,17},{17,25},{25,1},{2,10},{10... | collective-permute-start | bytes 786440 | tf_op jit(solution)/shard_map/ppermute | solution.py:472
  96.4 6.7 %collective-permute-done.10.refs_1_ = bf16[8,128,128]{2,1,0:T(8,128)(2,1)S(1)} collective-permute-done((bf16[8,128,128]{2,1,0:T(8,128)(2,1)S(1)}, bf16[8,128,128]{2,1,0:T(8,128)(2,1)S(1)}, u32[]{:S(2)}, u32[]{:S(2)}) %collective-permute-start.10) | collective-permute-done | bytes 262176 | tf_op jit(solution)/shard_map/ppermute | solution.py:472
  103.1 2.5 %collective-permute-start.11 = (bf16[8,128,128]{2,1,0:T(8,128)(2,1)S(1)}, bf16[8,128,128]{2,1,0:T(8,128)(2,1)S(1)}, u32[]{:S(2)}, u32[]{:S(2)}) collective-permute-start(bf16[8,128,128]{2,1,0:T(8,128)(2,1)S(1)} %collective-permute-done.10.refs_1_), channel_id=1, source_target_pairs={{0,8},{8,16},{16,24},{24,0},{1,9},{9,17},{17,25},{25,1},{2,10},{10... | collective-permute-start | bytes 786440 | tf_op jit(solution)/shard_map/ppermute | solution.py:472
  105.6 4.1 %collective-permute-done.12.refs_4_ = bf16[8,128,128]{2,1,0:T(8,128)(2,1)S(1)} collective-permute-done((bf16[8,128,128]{2,1,0:T(8,128)(2,1)S(1)}, bf16[8,128,128]{2,1,0:T(8,128)(2,1)S(1)}, u32[]{:S(2)}, u32[]{:S(2)}) %collective-permute-start.12) | collective-permute-done | bytes 262176 | tf_op jit(solution)/shard_map/ppermute | solution.py:472
  109.7 3.3 %collective-permute-start.13 = (bf16[8,128,128]{2,1,0:T(8,128)(2,1)S(1)}, bf16[8,128,128]{2,1,0:T(8,128)(2,1)S(1)}, u32[]{:S(2)}, u32[]{:S(2)}) collective-permute-start(bf16[8,128,128]{2,1,0:T(8,128)(2,1)S(1)} %collective-permute-done.12.refs_4_), channel_id=1, source_target_pairs={{0,24},{8,0},{16,8},{24,16},{1,25},{9,1},{17,9},{25,17},{2,26},{10... | collective-permute-start | bytes 786440 | tf_op jit(solution)/shard_map/ppermute | solution.py:472
  113.0 1.3 collective-permute-done.11.refs_2_
  114.4 7.7 %collective-permute-start.14 = (bf16[8,128,128]{2,1,0:T(8,128)(2,1)S(1)}, bf16[8,128,128]{2,1,0:T(8,128)(2,1)S(1)}, u32[]{:S(2)}, u32[]{:S(2)}) collective-permute-start(bf16[8,128,128]{2,1,0:T(8,128)(2,1)S(1)} %collective-permute-done.11.refs_2_), channel_id=1, source_target_pairs={{0,8},{8,16},{16,24},{24,0},{1,9},{9,17},{17,25},{25,1},{2,10},{10... | collective-permute-start | bytes 786440 | tf_op jit(solution)/shard_map/ppermute | solution.py:472
  122.0 1.9 %collective-permute-start.15 = (bf16[8,128,128]{2,1,0:T(8,128)(2,1)S(1)}, bf16[8,128,128]{2,1,0:T(8,128)(2,1)S(1)}, u32[]{:S(2)}, u32[]{:S(2)}) collective-permute-start(bf16[8,128,128]{2,1,0:T(8,128)(2,1)S(1)} %collective-permute-done.13.refs_5_), channel_id=1, source_target_pairs={{0,24},{8,0},{16,8},{24,16},{1,25},{9,1},{17,9},{25,17},{2,26},{10... | collective-permute-start | bytes 786440 | tf_op jit(solution)/shard_map/ppermute | solution.py:472
  124.0 4.8 %shard_map.154 = (bf16[8,1024,128]{2,1,0:T(8,128)(2,1)S(1)}, s32[73]{0:T(128)S(1)}) custom-call(s32[64]{0:T(128)S(1)} %get-tuple-element.28.patch_ref, bf16[64,128,256]{2,1,0:T(8,128)(2,1)S(1)} %shard_map.151.weights_ref, bf16[8,128,128]{2,1,0:T(8,128)(2,1)S(1)} %get-tuple-element.45.refs_0_, bf16[8,128,128]{2,1,0:T(8,128)(2,1)S(1)} %collective-permute-done.10.refs_1_, ...), custom_call_target="tpu_custom_call" | custom-call | flops 536870912 | bytes 8388608 | tf_op jit(solution)/shard_map/pallas_call | solution.py:37
  128.8 2.4 %collective-permute-done.14.up_ref = bf16[8,128,128]{2,1,0:T(8,128)(2,1)S(1)} collective-permute-done((bf16[8,128,128]{2,1,0:T(8,128)(2,1)S(1)}, bf16[8,128,128]{2,1,0:T(8,128)(2,1)S(1)}, u32[]{:S(2)}, u32[]{:S(2)}) %collective-permute-start.14) | collective-permute-done | bytes 262176 | tf_op jit(solution)/shard_map/ppermute | solution.py:472
  131.2 4.5 %collective-permute-done.15.down_ref = bf16[8,128,128]{2,1,0:T(8,128)(2,1)S(1)} collective-permute-done((bf16[8,128,128]{2,1,0:T(8,128)(2,1)S(1)}, bf16[8,128,128]{2,1,0:T(8,128)(2,1)S(1)}, u32[]{:S(2)}, u32[]{:S(2)}) %collective-permute-start.15) | collective-permute-done | bytes 262176 | tf_op jit(solution)/shard_map/ppermute | solution.py:472
  135.6 1.8 %shard_map.155 = bf16[8,1024,128]{2,1,0:T(8,128)(2,1)S(1)} custom-call(s32[64]{0:T(128)S(1)} %get-tuple-element.28.patch_ref, s32[73]{0:T(128)S(1)} %get-tuple-element.47.list_ref, bf16[64,128,256]{2,1,0:T(8,128)(2,1)S(1)} %shard_map.151.weights_ref, bf16[8,128,128]{2,1,0:T(8,128)(2,1)S(1)} %collective-permute-done.14.up_ref, ...), custom_call_target="tpu_custom_call", output_to_operand_aliasing={{}: (5, {})} | custom-call | flops 134217728 | bytes 2097152 | tf_op jit(solution)/shard_map/pallas_call | solution.py:37
  137.4 0.0 copy-start
  137.4 0.0 copy-start.2
  137.4 28.6 %all_to_all.11.got_ref = bf16[8,1024,128]{2,1,0:T(8,128)(2,1)S(1)} all-to-all(bf16[8,1024,128]{2,1,0:T(8,128)(2,1)S(1)} %shard_map.155), channel_id=1, replica_groups=mesh['orbits'=4,'rows'=2,'cols'=4] {'rows','cols'}, dimensions={0} | all-to-all | bytes 4194304 | tf_op jit(solution)/shard_map/all_to_all | solution.py:527
  166.0 1.6 shard_map.156
  (16 shorter events, 0.1 us)
Async XLA Ops:
  37.6 35.3 %copy-start.1 = (f32[128]{0:T(128)S(1)}, f32[128]{0:T(128)}, u32[]{:S(2)}) copy-start(f32[128]{0:T(128)} %param.23) | copy-start | bytes 1540
  40.8 10.8 %collective-permute-start = (bf16[960,128]{1,0:T(8,128)(2,1)S(1)}, bf16[960,128]{1,0:T(8,128)(2,1)S(1)}, u32[]{:S(2)}, u32[]{:S(2)}) collective-permute-start(bf16[960,128]{1,0:T(8,128)(2,1)S(1)} %get-tuple-element.29), channel_id=1, source_target_pairs={{0,8},{8,16},{16,24},{24,0},{1,9},{9,17},{17,25},{25,1},{2,10},{10... | collective-permute-start | bytes 737288 | tf_op jit(solution)/shard_map/ppermute | solution.py:472
  42.4 14.2 %collective-permute-start.2 = (bf16[1152,128]{1,0:T(8,128)(2,1)S(1)}, bf16[1152,128]{1,0:T(8,128)(2,1)S(1)}, u32[]{:S(2)}, u32[]{:S(2)}) collective-permute-start(bf16[1152,128]{1,0:T(8,128)(2,1)S(1)} %get-tuple-element.32), channel_id=1, source_target_pairs={{0,24},{8,0},{16,8},{24,16},{1,25},{9,1},{17,9},{25,17},{2,26},{10... | collective-permute-start | bytes 884744 | tf_op jit(solution)/shard_map/ppermute | solution.py:472
  51.6 10.3 %collective-permute-start.1 = (bf16[960,128]{1,0:T(8,128)(2,1)S(1)}, bf16[960,128]{1,0:T(8,128)(2,1)S(1)}, u32[]{:S(2)}, u32[]{:S(2)}) collective-permute-start(bf16[960,128]{1,0:T(8,128)(2,1)S(1)} %add.12), channel_id=1, source_target_pairs={{0,8},{8,16},{16,24},{24,0},{1,9},{9,17},{17,25},{25,1},{2,10},{10... | collective-permute-start | bytes 737288 | tf_op jit(solution)/shard_map/ppermute | solution.py:472
  62.0 10.8 %collective-permute-start.5 = (bf16[960,128]{1,0:T(8,128)(2,1)S(1)}, bf16[960,128]{1,0:T(8,128)(2,1)S(1)}, u32[]{:S(2)}, u32[]{:S(2)}) collective-permute-start(bf16[960,128]{1,0:T(8,128)(2,1)S(1)} %add.13), channel_id=1, source_target_pairs={{0,8},{8,16},{16,24},{24,0},{1,9},{9,17},{17,25},{25,1},{2,10},{10... | collective-permute-start | bytes 737288 | tf_op jit(solution)/shard_map/ppermute | solution.py:472
  62.1 14.8 %collective-permute-start.3 = (bf16[1152,128]{1,0:T(8,128)(2,1)S(1)}, bf16[1152,128]{1,0:T(8,128)(2,1)S(1)}, u32[]{:S(2)}, u32[]{:S(2)}) collective-permute-start(bf16[1152,128]{1,0:T(8,128)(2,1)S(1)} %add.14), channel_id=1, source_target_pairs={{0,24},{8,0},{16,8},{24,16},{1,25},{9,1},{17,9},{25,17},{2,26},{10... | collective-permute-start | bytes 884744 | tf_op jit(solution)/shard_map/ppermute | solution.py:472
  73.1 6.5 %collective-permute-start.6 = (bf16[2,128,128]{2,1,0:T(8,128)(2,1)S(1)}, bf16[2,128,128]{2,1,0:T(8,128)(2,1)S(1)}, u32[]{:S(2)}, u32[]{:S(2)}) collective-permute-start(bf16[2,128,128]{2,1,0:T(8,128)(2,1)S(1)} %get-tuple-element.41), channel_id=1, source_target_pairs={{0,4},{4,8},{8,12},{12,16},{16,20},{20,24},{24,28},{1,5},{5,9},{9,... | collective-permute-start | bytes 196616 | tf_op jit(solution)/shard_map/ppermute | solution.py:467
  75.6 7.4 %collective-permute-start.7 = (bf16[2,128,128]{2,1,0:T(8,128)(2,1)S(1)}, bf16[2,128,128]{2,1,0:T(8,128)(2,1)S(1)}, u32[]{:S(2)}, u32[]{:S(2)}) collective-permute-start(bf16[2,128,128]{2,1,0:T(8,128)(2,1)S(1)} %get-tuple-element.42), channel_id=1, source_target_pairs={{4,0},{8,4},{12,8},{16,12},{20,16},{24,20},{28,24},{5,1},{9,5},{13... | collective-permute-start | bytes 196616 | tf_op jit(solution)/shard_map/ppermute | solution.py:467
  77.0 11.1 %collective-permute-start.4 = (bf16[1152,128]{1,0:T(8,128)(2,1)S(1)}, bf16[1152,128]{1,0:T(8,128)(2,1)S(1)}, u32[]{:S(2)}, u32[]{:S(2)}) collective-permute-start(bf16[1152,128]{1,0:T(8,128)(2,1)S(1)} %add.15), channel_id=1, source_target_pairs={{0,24},{8,0},{16,8},{24,16},{1,25},{9,1},{17,9},{25,17},{2,26},{10... | collective-permute-start | bytes 884744 | tf_op jit(solution)/shard_map/ppermute | solution.py:472
  83.0 5.1 %collective-permute-start.8 = (bf16[20,2,128]{2,1,0:T(2,128)(2,1)S(1)}, bf16[20,2,128]{2,1,0:T(2,128)(2,1)S(1)}, u32[]{:S(2)}, u32[]{:S(2)}) collective-permute-start(bf16[20,2,128]{2,1,0:T(2,128)(2,1)S(1)} %pad_maximum_fusion), channel_id=1, source_target_pairs={{0,1},{1,2},{2,3},{4,5},{5,6},{6,7},{8,9},{9,10},{10,11},{12,13},{... | collective-permute-start | bytes 30728 | tf_op jit(solution)/shard_map/ppermute | solution.py:467
  84.3 3.8 %copy-start.3 = (bf16[3,3,128,128]{3,2,1,0:T(8,128)(2,1)S(1)}, bf16[3,3,128,128]{3,2,1,0:T(8,128)(2,1)}, u32[]{:S(2)}) copy-start(bf16[3,3,128,128]{3,2,1,0:T(8,128)(2,1)} %w1_ref.1) | copy-start | bytes 884740
  84.3 3.8 %copy-start.4 = (bf16[3,3,128,128]{3,2,1,0:T(8,128)(2,1)S(1)}, bf16[3,3,128,128]{3,2,1,0:T(8,128)(2,1)}, u32[]{:S(2)}) copy-start(bf16[3,3,128,128]{3,2,1,0:T(8,128)(2,1)} %w2_ref.1) | copy-start | bytes 884740
  84.3 3.8 %copy-start.5 = (f32[128]{0:T(128)S(1)}, f32[128]{0:T(128)}, u32[]{:S(2)}) copy-start(f32[128]{0:T(128)} %param.25) | copy-start | bytes 1540
  84.4 3.8 %copy-start.6 = (f32[128]{0:T(128)S(1)}, f32[128]{0:T(128)}, u32[]{:S(2)}) copy-start(f32[128]{0:T(128)} %param.27) | copy-start | bytes 1540
  84.4 3.7 %collective-permute-start.9 = (bf16[20,2,128]{2,1,0:T(2,128)(2,1)S(1)}, bf16[20,2,128]{2,1,0:T(2,128)(2,1)S(1)}, u32[]{:S(2)}, u32[]{:S(2)}) collective-permute-start(bf16[20,2,128]{2,1,0:T(2,128)(2,1)S(1)} %pad_maximum_fusion.1), channel_id=1, source_target_pairs={{1,0},{2,1},{3,2},{5,4},{6,5},{7,6},{9,8},{10,9},{11,10},{13,12},{... | collective-permute-start | bytes 30728 | tf_op jit(solution)/shard_map/ppermute | solution.py:467
  92.5 10.6 %collective-permute-start.10 = (bf16[8,128,128]{2,1,0:T(8,128)(2,1)S(1)}, bf16[8,128,128]{2,1,0:T(8,128)(2,1)S(1)}, u32[]{:S(2)}, u32[]{:S(2)}) collective-permute-start(bf16[8,128,128]{2,1,0:T(8,128)(2,1)S(1)} %get-tuple-element.45.refs_0_), channel_id=1, source_target_pairs={{0,8},{8,16},{16,24},{24,0},{1,9},{9,17},{17,25},{25,1},{2,10},{10... | collective-permute-start | bytes 786440 | tf_op jit(solution)/shard_map/ppermute | solution.py:472
  96.4 13.3 %collective-permute-start.12 = (bf16[8,128,128]{2,1,0:T(8,128)(2,1)S(1)}, bf16[8,128,128]{2,1,0:T(8,128)(2,1)S(1)}, u32[]{:S(2)}, u32[]{:S(2)}) collective-permute-start(bf16[8,128,128]{2,1,0:T(8,128)(2,1)S(1)} %get-tuple-element.46.refs_3_), channel_id=1, source_target_pairs={{0,24},{8,0},{16,8},{24,16},{1,25},{9,1},{17,9},{25,17},{2,26},{10... | collective-permute-start | bytes 786440 | tf_op jit(solution)/shard_map/ppermute | solution.py:472
  103.1 11.3 %collective-permute-start.11 = (bf16[8,128,128]{2,1,0:T(8,128)(2,1)S(1)}, bf16[8,128,128]{2,1,0:T(8,128)(2,1)S(1)}, u32[]{:S(2)}, u32[]{:S(2)}) collective-permute-start(bf16[8,128,128]{2,1,0:T(8,128)(2,1)S(1)} %collective-permute-done.10.refs_1_), channel_id=1, source_target_pairs={{0,8},{8,16},{16,24},{24,0},{1,9},{9,17},{17,25},{25,1},{2,10},{10... | collective-permute-start | bytes 786440 | tf_op jit(solution)/shard_map/ppermute | solution.py:472
  109.7 12.4 %collective-permute-start.13 = (bf16[8,128,128]{2,1,0:T(8,128)(2,1)S(1)}, bf16[8,128,128]{2,1,0:T(8,128)(2,1)S(1)}, u32[]{:S(2)}, u32[]{:S(2)}) collective-permute-start(bf16[8,128,128]{2,1,0:T(8,128)(2,1)S(1)} %collective-permute-done.12.refs_4_), channel_id=1, source_target_pairs={{0,24},{8,0},{16,8},{24,16},{1,25},{9,1},{17,9},{25,17},{2,26},{10... | collective-permute-start | bytes 786440 | tf_op jit(solution)/shard_map/ppermute | solution.py:472
  114.4 16.8 %collective-permute-start.14 = (bf16[8,128,128]{2,1,0:T(8,128)(2,1)S(1)}, bf16[8,128,128]{2,1,0:T(8,128)(2,1)S(1)}, u32[]{:S(2)}, u32[]{:S(2)}) collective-permute-start(bf16[8,128,128]{2,1,0:T(8,128)(2,1)S(1)} %collective-permute-done.11.refs_2_), channel_id=1, source_target_pairs={{0,8},{8,16},{16,24},{24,0},{1,9},{9,17},{17,25},{25,1},{2,10},{10... | collective-permute-start | bytes 786440 | tf_op jit(solution)/shard_map/ppermute | solution.py:472
  122.0 13.6 %collective-permute-start.15 = (bf16[8,128,128]{2,1,0:T(8,128)(2,1)S(1)}, bf16[8,128,128]{2,1,0:T(8,128)(2,1)S(1)}, u32[]{:S(2)}, u32[]{:S(2)}) collective-permute-start(bf16[8,128,128]{2,1,0:T(8,128)(2,1)S(1)} %collective-permute-done.13.refs_5_), channel_id=1, source_target_pairs={{0,24},{8,0},{16,8},{24,16},{1,25},{9,1},{17,9},{25,17},{2,26},{10... | collective-permute-start | bytes 786440 | tf_op jit(solution)/shard_map/ppermute | solution.py:472
  137.4 28.6 %copy-start = (bf16[32,128,128]{2,1,0:T(8,128)(2,1)S(1)}, bf16[32,128,128]{2,1,0:T(8,128)(2,1)}, u32[]{:S(2)}) copy-start(bf16[32,128,128]{2,1,0:T(8,128)(2,1)} %get-tuple-element.26.feat_ref) | copy-start | bytes 3145732
  137.4 28.6 %copy-start.2 = (s32[32]{0:T(128)S(1)}, s32[32]{0:T(128)}, u32[]{:S(2)}) copy-start(s32[32]{0:T(128)} %tile_ref.1) | copy-start | bytes 388

commit v9 on v8

--- a/solution.py
+++ b/solution.py
@@ -64,7 +64,7 @@
 
 
 def embed_kernel(
-    tile_hbm, patch_hbm, offset_hbm, cells_hbm, x_hbm, we_hbm, be_hbm, wp_hbm, bp_hbm,
+    most, tile_hbm, patch_hbm, offset_hbm, cells_hbm, x_hbm, we_hbm, be_hbm, wp_hbm, bp_hbm,
     feat_hbm, send_hbm,
     tile_ref, patch_ref, offset_ref, cells_ref, x_ref, we_ref, be_ref, wp_ref, bp_ref, feat_ref,
     zero_ref, count_ref, slot_ref, meta_ref, meta16_ref, sems, x_sems, feat_sems, send_sems,
@@ -72,9 +72,7 @@
     blocks, size, channels = feat_ref.shape
     chunks = x_sems.shape[0]
     per = blocks // chunks
-    tiles, meta_rows = meta16_ref.shape[0], meta_ref.shape[0] // meta16_ref.shape[0]
-    most = meta_rows // META
-    base = most * size
+    tiles, meta_rows, base = meta16_ref.shape[0], most * META, most * size
     pairs = (
         (tile_hbm, tile_ref), (patch_hbm, patch_ref), (offset_hbm, offset_ref), (cells_hbm.at[0:8], cells_ref),
         (we_hbm, we_ref), (be_hbm, be_ref), (wp_hbm, wp_ref), (bp_hbm, bp_ref),
@@ -529,7 +527,7 @@
 
     b_embed, b_proj = bias(b_embed), bias(b_proj)
     features, send = call(
-        embed_kernel,
+        functools.partial(embed_kernel, most),
         [HBM] * 9,
         [HBM] * 2,
         (shape((blocks, size, channels), BF16), shape((tiles, length + meta_rows, channels), BF16)),
@@ -547,7 +545,7 @@
             pltpu.VMEM((size, channels), BF16),
             counts,
             pltpu.SMEM((blocks,), jnp.int32),
-            pltpu.VMEM((slots * META, size), F32),
+            pltpu.VMEM((slots * META + 8, size), F32),
             pltpu.VMEM((tiles, meta_rows, size), BF16),
             pltpu.SemaphoreType.DMA((9,)),
             pltpu.SemaphoreType.DMA((chunks,)),

time: 166 us -> 164 us (0.988); the launches traced: 168 us -> 163 us
  starting transfers between devices: 36.2 us -> 22.3 us
  waiting for transfers between devices: 46.3 us -> 55.5 us
    ppermute x12, starting transfers between devices: 29.7 us -> 15.8 us  [turn(): lax.ppermute(x, 'orbits', [(i, (i + way) % size) for i in range(size)])]
    ppermute x12, waiting for transfers between devices: 43 us -> 52.8 us  [turn(): lax.ppermute(x, 'orbits', [(i, (i + way) % size) for i in range(size)])]
  transfers between devices with their start and end apart: 16 -> 16, of which waited for: 10 -> 11; matrix products, arithmetic and copies ran while one was open for 0% -> 0% of each run, Pallas kernels for 4% -> 4%
where the time goes in v9:
time: 164 us; the launch traced here: 163 us
  blocking collectives  61.2 us (37%)
  waiting for transfers between devices  55.5 us (34%)
  Pallas kernels  22.8 us (14%)
  starting transfers between devices  22.3 us (14%)
    all_to_all x2, blocking collectives, local(): lax.all_to_all(x, plane, split_axis=0, concat_axis=0, tiled=True)  61.2 us
    ppermute x12, waiting for transfers between devices, turn(): lax.ppermute(x, 'orbits', [(i, (i + way) % size) for i in range(size)])  52.8 us
    pallas_call x8, Pallas kernels, call(): pl.pallas_call(kernel, in_specs=in_specs, out_specs=out_specs, out_shape=...  22.8 us
    ppermute x12, starting transfers between devices, turn(): lax.ppermute(x, 'orbits', [(i, (i + way) % size) for i in range(size)])  15.8 us
    ppermute x4, starting transfers between devices, halo(): return (lax.ppermute(last, axis, up), lax.ppermute(first, axis, down))  6.48 us
  transfers between devices with their start and end apart: 16, of which 11 were waited for; matrix products, arithmetic and copies ran while one was open for 0% of the time, Pallas kernels for 4%

profile of v9, /device:TPU:0, one launch (start us, length us, event | category | flops | bytes accessed | tf_op | source)
XLA Modules:
  0.0 163.1 jit_solution(3898528192894505521)
XLA Ops:
  0.6 4.3 %shard_map.149 = (bf16[32,128,128]{2,1,0:T(8,128)(2,1)}, bf16[8,1056,128]{2,1,0:T(8,128)(2,1)}) custom-call(s32[32]{0:T(128)} %tile_ref.1, s32[32]{0:T(128)} %patch_hbm.1, bf16[2,4096]{1,0:T(2,128)(2,1)} %offset_hbm.1, s32[16,4096]{1,0:T(8,128)} %cells_hbm.1, bf16[4096,128]{1,0:T(8,128)(2,1)} %x_hbm.1, bf16[128,128]{1,0:T(8,128)(2,1)} %we_hbm.1, ...), custom_call_target="tpu_custom_call" | custom-call | flops 402653184 | bytes 4194304 | tf_op jit(solution)/shard_map/pallas_call | solution.py:37
  4.9 32.7 %all_to_all.10.got_ref = bf16[8,1056,128]{2,1,0:T(8,128)(2,1)S(1)} all-to-all(bf16[8,1056,128]{2,1,0:T(8,128)(2,1)} %get-tuple-element.27), channel_id=1, replica_groups=mesh['orbits'=4,'rows'=2,'cols'=4] {'rows','cols'}, dimensions={0} | all-to-all | bytes 4325376 | tf_op jit(solution)/shard_map/all_to_all | solution.py:525
  37.6 3.2 %shard_map.150 = (bf16[960,128]{1,0:T(8,128)(2,1)S(1)}, bf16[960,128]{1,0:T(8,128)(2,1)S(1)}, bf16[960,128]{1,0:T(8,128)(2,1)S(1)}, bf16[960,128]{1,0:T(8,128)(2...) custom-call(bf16[8,1056,128]{2,1,0:T(8,128)(2,1)S(1)} %all_to_all.10, ...), custom_call_target="tpu_custom_call" | custom-call | flops 536870912 | bytes 8388608 | tf_op jit(solution)/shard_map/pallas_call | solution.py:37
  40.8 1.6 %collective-permute-start = (bf16[960,128]{1,0:T(8,128)(2,1)S(1)}, bf16[960,128]{1,0:T(8,128)(2,1)S(1)}, u32[]{:S(2)}, u32[]{:S(2)}) collective-permute-start(bf16[960,128]{1,0:T(8,128)(2,1)S(1)} %get-tuple-element.29), channel_id=1, source_target_pairs={{0,8},{8,16},{16,24},{24,0},{1,9},{9,17},{17,25},{25,1},{2,10},{10... | collective-permute-start | bytes 737288 | tf_op jit(solution)/shard_map/ppermute | solution.py:470
  42.4 2.2 %collective-permute-start.2 = (bf16[1152,128]{1,0:T(8,128)(2,1)S(1)}, bf16[1152,128]{1,0:T(8,128)(2,1)S(1)}, u32[]{:S(2)}, u32[]{:S(2)}) collective-permute-start(bf16[1152,128]{1,0:T(8,128)(2,1)S(1)} %get-tuple-element.32), channel_id=1, source_target_pairs={{0,24},{8,0},{16,8},{24,16},{1,25},{9,1},{17,9},{25,17},{2,26},{10... | collective-permute-start | bytes 884744 | tf_op jit(solution)/shard_map/ppermute | solution.py:470
  44.7 6.9 %collective-permute-done = bf16[960,128]{1,0:T(8,128)(2,1)S(1)} collective-permute-done((bf16[960,128]{1,0:T(8,128)(2,1)S(1)}, bf16[960,128]{1,0:T(8,128)(2,1)S(1)}, u32[]{:S(2)}, u32[]{:S(2)}) %collective-permute-start) | collective-permute-done | bytes 245792 | tf_op jit(solution)/shard_map/ppermute | solution.py:470
  51.6 0.1 add.12
  51.6 0.1 collective-permute-start.1
  51.7 5.0 %collective-permute-done.2 = bf16[1152,128]{1,0:T(8,128)(2,1)S(1)} collective-permute-done((bf16[1152,128]{1,0:T(8,128)(2,1)S(1)}, bf16[1152,128]{1,0:T(8,128)(2,1)S(1)}, u32[]{:S(2)}, u32[]{:S(2)}) %collective-permute-start.2) | collective-permute-done | bytes 294944 | tf_op jit(solution)/shard_map/ppermute | solution.py:470
  56.7 0.1 add.14
  56.7 5.2 %collective-permute-done.1 = bf16[960,128]{1,0:T(8,128)(2,1)S(1)} collective-permute-done((bf16[960,128]{1,0:T(8,128)(2,1)S(1)}, bf16[960,128]{1,0:T(8,128)(2,1)S(1)}, u32[]{:S(2)}, u32[]{:S(2)}) %collective-permute-start.1) | collective-permute-done | bytes 245792 | tf_op jit(solution)/shard_map/ppermute | solution.py:470
  61.9 0.1 add.13
  62.0 0.1 collective-permute-start.5
  62.1 3.8 %collective-permute-start.3 = (bf16[1152,128]{1,0:T(8,128)(2,1)S(1)}, bf16[1152,128]{1,0:T(8,128)(2,1)S(1)}, u32[]{:S(2)}, u32[]{:S(2)}) collective-permute-start(bf16[1152,128]{1,0:T(8,128)(2,1)S(1)} %add.14), channel_id=1, source_target_pairs={{0,24},{8,0},{16,8},{24,16},{1,25},{9,1},{17,9},{25,17},{2,26},{10... | collective-permute-start | bytes 884744 | tf_op jit(solution)/shard_map/ppermute | solution.py:470
  65.9 6.9 %collective-permute-done.5.sum_ref.sum0_ref = bf16[960,128]{1,0:T(8,128)(2,1)S(1)} collective-permute-done((bf16[960,128]{1,0:T(8,128)(2,1)S(1)}, bf16[960,128]{1,0:T(8,128)(2,1)S(1)}, u32[]{:S(2)}, u32[]{:S(2)}) %collective-permute-start.5) | collective-permute-done | bytes 245792 | tf_op jit(solution)/shard_map/ppermute | solution.py:470
  72.8 0.3 shard_map.152
  73.1 2.5 %collective-permute-start.6 = (bf16[2,128,128]{2,1,0:T(8,128)(2,1)S(1)}, bf16[2,128,128]{2,1,0:T(8,128)(2,1)S(1)}, u32[]{:S(2)}, u32[]{:S(2)}) collective-permute-start(bf16[2,128,128]{2,1,0:T(8,128)(2,1)S(1)} %get-tuple-element.41), channel_id=1, source_target_pairs={{0,4},{4,8},{8,12},{12,16},{16,20},{20,24},{24,28},{1,5},{5,9},{9,... | collective-permute-start | bytes 196616 | tf_op jit(solution)/shard_map/ppermute | solution.py:465
  75.6 1.3 collective-permute-start.7
  76.9 0.0 collective-permute-done.3
  76.9 0.1 add.15
  77.0 2.5 %collective-permute-start.4 = (bf16[1152,128]{1,0:T(8,128)(2,1)S(1)}, bf16[1152,128]{1,0:T(8,128)(2,1)S(1)}, u32[]{:S(2)}, u32[]{:S(2)}) collective-permute-start(bf16[1152,128]{1,0:T(8,128)(2,1)S(1)} %add.15), channel_id=1, source_target_pairs={{0,24},{8,0},{16,8},{24,16},{1,25},{9,1},{17,9},{25,17},{2,26},{10... | collective-permute-start | bytes 884744 | tf_op jit(solution)/shard_map/ppermute | solution.py:470
  79.5 2.3 %collective-permute-done.7.down_ref = bf16[2,128,128]{2,1,0:T(8,128)(2,1)S(1)} collective-permute-done((bf16[2,128,128]{2,1,0:T(8,128)(2,1)S(1)}, bf16[2,128,128]{2,1,0:T(8,128)(2,1)S(1)}, u32[]{:S(2)}, u32[]{:S(2)}) %collective-permute-start.7) | collective-permute-done | bytes 65568 | tf_op jit(solution)/shard_map/ppermute | solution.py:465
  81.8 1.3 collective-permute-start.8
  83.1 0.0 copy-start.3
  83.1 0.0 copy-start.4
  83.2 0.0 copy-start.5
  83.2 0.0 copy-start.6
  83.2 1.4 collective-permute-start.9
  84.6 2.3 %shard_map.151.weights_ref = bf16[64,128,256]{2,1,0:T(8,128)(2,1)S(1)} custom-call(bf16[8,1056,128]{2,1,0:T(8,128)(2,1)S(1)} %all_to_all.10.got_ref), custom_call_target="tpu_custom_call" | custom-call | flops 536870912 | bytes 4194304 | tf_op jit(solution)/shard_map/pallas_call | solution.py:37
  86.9 0.0 collective-permute-done.4.sum1_ref
  86.9 0.4 collective-permute-done.9.right_ref
  87.4 4.4 %shard_map.153 = (bf16[16,128,128]{2,1,0:T(8,128)(2,1)}, bf16[8,128,128]{2,1,0:T(8,128)(2,1)S(1)}, bf16[8,128,128]{2,1,0:T(8,128)(2,1)S(1)}) custom-call(bf16[960,128]{1,0:T(8,128)(2,1)S(1)} %get-tuple-element.37.own_ref.own0_ref, bf16[960,128]{1,0:T(8,128)(2,1)S(1)} %collective-permute-done.5.sum_ref.sum0_ref, ...), custom_call_target="tpu_custom_call" | custom-call | flops 1207959552 | bytes 2097152 | tf_op jit(solution)/shard_map/pallas_call | solution.py:37
  91.8 0.0 collective-permute-start.10
  91.8 3.8 %collective-permute-start.12 = (bf16[8,128,128]{2,1,0:T(8,128)(2,1)S(1)}, bf16[8,128,128]{2,1,0:T(8,128)(2,1)S(1)}, u32[]{:S(2)}, u32[]{:S(2)}) collective-permute-start(bf16[8,128,128]{2,1,0:T(8,128)(2,1)S(1)} %get-tuple-element.46.refs_3_), channel_id=1, source_target_pairs={{0,24},{8,0},{16,8},{24,16},{1,25},{9,1},{17,9},{25,17},{2,26},{10... | collective-permute-start | bytes 786440 | tf_op jit(solution)/shard_map/ppermute | solution.py:470
  95.6 5.8 %collective-permute-done.10.refs_1_ = bf16[8,128,128]{2,1,0:T(8,128)(2,1)S(1)} collective-permute-done((bf16[8,128,128]{2,1,0:T(8,128)(2,1)S(1)}, bf16[8,128,128]{2,1,0:T(8,128)(2,1)S(1)}, u32[]{:S(2)}, u32[]{:S(2)}) %collective-permute-start.10) | collective-permute-done | bytes 262176 | tf_op jit(solution)/shard_map/ppermute | solution.py:470
  101.4 3.6 %collective-permute-done.12.refs_4_ = bf16[8,128,128]{2,1,0:T(8,128)(2,1)S(1)} collective-permute-done((bf16[8,128,128]{2,1,0:T(8,128)(2,1)S(1)}, bf16[8,128,128]{2,1,0:T(8,128)(2,1)S(1)}, u32[]{:S(2)}, u32[]{:S(2)}) %collective-permute-start.12) | collective-permute-done | bytes 262176 | tf_op jit(solution)/shard_map/ppermute | solution.py:470
  105.0 1.7 %collective-permute-start.13 = (bf16[8,128,128]{2,1,0:T(8,128)(2,1)S(1)}, bf16[8,128,128]{2,1,0:T(8,128)(2,1)S(1)}, u32[]{:S(2)}, u32[]{:S(2)}) collective-permute-start(bf16[8,128,128]{2,1,0:T(8,128)(2,1)S(1)} %collective-permute-done.12.refs_4_), channel_id=1, source_target_pairs={{0,24},{8,0},{16,8},{24,16},{1,25},{9,1},{17,9},{25,17},{2,26},{10... | collective-permute-start | bytes 786440 | tf_op jit(solution)/shard_map/ppermute | solution.py:470
  106.8 5.9 %collective-permute-done.11.refs_2_ = bf16[8,128,128]{2,1,0:T(8,128)(2,1)S(1)} collective-permute-done((bf16[8,128,128]{2,1,0:T(8,128)(2,1)S(1)}, bf16[8,128,128]{2,1,0:T(8,128)(2,1)S(1)}, u32[]{:S(2)}, u32[]{:S(2)}) %collective-permute-start.11) | collective-permute-done | bytes 262176 | tf_op jit(solution)/shard_map/ppermute | solution.py:470
  112.7 0.0 collective-permute-start.14
  112.7 6.7 %collective-permute-done.13.refs_5_ = bf16[8,128,128]{2,1,0:T(8,128)(2,1)S(1)} collective-permute-done((bf16[8,128,128]{2,1,0:T(8,128)(2,1)S(1)}, bf16[8,128,128]{2,1,0:T(8,128)(2,1)S(1)}, u32[]{:S(2)}, u32[]{:S(2)}) %collective-permute-start.13) | collective-permute-done | bytes 262176 | tf_op jit(solution)/shard_map/ppermute | solution.py:470
  119.4 0.0 collective-permute-start.15
  119.4 4.8 %shard_map.154 = (bf16[8,1024,128]{2,1,0:T(8,128)(2,1)S(1)}, s32[73]{0:T(128)S(1)}) custom-call(s32[64]{0:T(128)S(1)} %get-tuple-element.28.patch_ref, bf16[64,128,256]{2,1,0:T(8,128)(2,1)S(1)} %shard_map.151.weights_ref, bf16[8,128,128]{2,1,0:T(8,128)(2,1)S(1)} %get-tuple-element.45.refs_0_, bf16[8,128,128]{2,1,0:T(8,128)(2,1)S(1)} %collective-permute-done.10.refs_1_, ...), custom_call_target="tpu_custom_call" | custom-call | flops 536870912 | bytes 8388608 | tf_op jit(solution)/shard_map/pallas_call | solution.py:37
  124.2 6.7 %collective-permute-done.15.down_ref = bf16[8,128,128]{2,1,0:T(8,128)(2,1)S(1)} collective-permute-done((bf16[8,128,128]{2,1,0:T(8,128)(2,1)S(1)}, bf16[8,128,128]{2,1,0:T(8,128)(2,1)S(1)}, u32[]{:S(2)}, u32[]{:S(2)}) %collective-permute-start.15) | collective-permute-done | bytes 262176 | tf_op jit(solution)/shard_map/ppermute | solution.py:470
  130.9 2.0 %shard_map.155 = bf16[8,1024,128]{2,1,0:T(8,128)(2,1)S(1)} custom-call(s32[64]{0:T(128)S(1)} %get-tuple-element.28.patch_ref, s32[73]{0:T(128)S(1)} %get-tuple-element.47.list_ref, bf16[64,128,256]{2,1,0:T(8,128)(2,1)S(1)} %shard_map.151.weights_ref, bf16[8,128,128]{2,1,0:T(8,128)(2,1)S(1)} %collective-permute-done.14.up_ref, ...), custom_call_target="tpu_custom_call", output_to_operand_aliasing={{}: (5, {})} | custom-call | flops 134217728 | bytes 2097152 | tf_op jit(solution)/shard_map/pallas_call | solution.py:37
  132.9 0.0 copy-start
  132.9 0.0 copy-start.2
  132.9 28.6 %all_to_all.11.got_ref = bf16[8,1024,128]{2,1,0:T(8,128)(2,1)S(1)} all-to-all(bf16[8,1024,128]{2,1,0:T(8,128)(2,1)S(1)} %shard_map.155), channel_id=1, replica_groups=mesh['orbits'=4,'rows'=2,'cols'=4] {'rows','cols'}, dimensions={0} | all-to-all | bytes 4194304 | tf_op jit(solution)/shard_map/all_to_all | solution.py:525
  161.5 1.6 shard_map.156
  (16 shorter events, 0.1 us)
Async XLA Ops:
  37.6 35.2 %copy-start.1 = (f32[128]{0:T(128)S(1)}, f32[128]{0:T(128)}, u32[]{:S(2)}) copy-start(f32[128]{0:T(128)} %param.23) | copy-start | bytes 1540
  40.8 10.7 %collective-permute-start = (bf16[960,128]{1,0:T(8,128)(2,1)S(1)}, bf16[960,128]{1,0:T(8,128)(2,1)S(1)}, u32[]{:S(2)}, u32[]{:S(2)}) collective-permute-start(bf16[960,128]{1,0:T(8,128)(2,1)S(1)} %get-tuple-element.29), channel_id=1, source_target_pairs={{0,8},{8,16},{16,24},{24,0},{1,9},{9,17},{17,25},{25,1},{2,10},{10... | collective-permute-start | bytes 737288 | tf_op jit(solution)/shard_map/ppermute | solution.py:470
  42.4 14.2 %collective-permute-start.2 = (bf16[1152,128]{1,0:T(8,128)(2,1)S(1)}, bf16[1152,128]{1,0:T(8,128)(2,1)S(1)}, u32[]{:S(2)}, u32[]{:S(2)}) collective-permute-start(bf16[1152,128]{1,0:T(8,128)(2,1)S(1)} %get-tuple-element.32), channel_id=1, source_target_pairs={{0,24},{8,0},{16,8},{24,16},{1,25},{9,1},{17,9},{25,17},{2,26},{10... | collective-permute-start | bytes 884744 | tf_op jit(solution)/shard_map/ppermute | solution.py:470
  51.6 10.3 %collective-permute-start.1 = (bf16[960,128]{1,0:T(8,128)(2,1)S(1)}, bf16[960,128]{1,0:T(8,128)(2,1)S(1)}, u32[]{:S(2)}, u32[]{:S(2)}) collective-permute-start(bf16[960,128]{1,0:T(8,128)(2,1)S(1)} %add.12), channel_id=1, source_target_pairs={{0,8},{8,16},{16,24},{24,0},{1,9},{9,17},{17,25},{25,1},{2,10},{10... | collective-permute-start | bytes 737288 | tf_op jit(solution)/shard_map/ppermute | solution.py:470
  62.0 10.8 %collective-permute-start.5 = (bf16[960,128]{1,0:T(8,128)(2,1)S(1)}, bf16[960,128]{1,0:T(8,128)(2,1)S(1)}, u32[]{:S(2)}, u32[]{:S(2)}) collective-permute-start(bf16[960,128]{1,0:T(8,128)(2,1)S(1)} %add.13), channel_id=1, source_target_pairs={{0,8},{8,16},{16,24},{24,0},{1,9},{9,17},{17,25},{25,1},{2,10},{10... | collective-permute-start | bytes 737288 | tf_op jit(solution)/shard_map/ppermute | solution.py:470
  62.1 14.8 %collective-permute-start.3 = (bf16[1152,128]{1,0:T(8,128)(2,1)S(1)}, bf16[1152,128]{1,0:T(8,128)(2,1)S(1)}, u32[]{:S(2)}, u32[]{:S(2)}) collective-permute-start(bf16[1152,128]{1,0:T(8,128)(2,1)S(1)} %add.14), channel_id=1, source_target_pairs={{0,24},{8,0},{16,8},{24,16},{1,25},{9,1},{17,9},{25,17},{2,26},{10... | collective-permute-start | bytes 884744 | tf_op jit(solution)/shard_map/ppermute | solution.py:470
  73.1 6.4 %collective-permute-start.6 = (bf16[2,128,128]{2,1,0:T(8,128)(2,1)S(1)}, bf16[2,128,128]{2,1,0:T(8,128)(2,1)S(1)}, u32[]{:S(2)}, u32[]{:S(2)}) collective-permute-start(bf16[2,128,128]{2,1,0:T(8,128)(2,1)S(1)} %get-tuple-element.41), channel_id=1, source_target_pairs={{0,4},{4,8},{8,12},{12,16},{16,20},{20,24},{24,28},{1,5},{5,9},{9,... | collective-permute-start | bytes 196616 | tf_op jit(solution)/shard_map/ppermute | solution.py:465
  75.6 6.2 %collective-permute-start.7 = (bf16[2,128,128]{2,1,0:T(8,128)(2,1)S(1)}, bf16[2,128,128]{2,1,0:T(8,128)(2,1)S(1)}, u32[]{:S(2)}, u32[]{:S(2)}) collective-permute-start(bf16[2,128,128]{2,1,0:T(8,128)(2,1)S(1)} %get-tuple-element.42), channel_id=1, source_target_pairs={{4,0},{8,4},{12,8},{16,12},{20,16},{24,20},{28,24},{5,1},{9,5},{13... | collective-permute-start | bytes 196616 | tf_op jit(solution)/shard_map/ppermute | solution.py:465
  77.0 9.9 %collective-permute-start.4 = (bf16[1152,128]{1,0:T(8,128)(2,1)S(1)}, bf16[1152,128]{1,0:T(8,128)(2,1)S(1)}, u32[]{:S(2)}, u32[]{:S(2)}) collective-permute-start(bf16[1152,128]{1,0:T(8,128)(2,1)S(1)} %add.15), channel_id=1, source_target_pairs={{0,24},{8,0},{16,8},{24,16},{1,25},{9,1},{17,9},{25,17},{2,26},{10... | collective-permute-start | bytes 884744 | tf_op jit(solution)/shard_map/ppermute | solution.py:470
  81.8 5.1 %collective-permute-start.8 = (bf16[20,2,128]{2,1,0:T(2,128)(2,1)S(1)}, bf16[20,2,128]{2,1,0:T(2,128)(2,1)S(1)}, u32[]{:S(2)}, u32[]{:S(2)}) collective-permute-start(bf16[20,2,128]{2,1,0:T(2,128)(2,1)S(1)} %pad_maximum_fusion), channel_id=1, source_target_pairs={{0,1},{1,2},{2,3},{4,5},{5,6},{6,7},{8,9},{9,10},{10,11},{12,13},{... | collective-permute-start | bytes 30728 | tf_op jit(solution)/shard_map/ppermute | solution.py:465
  83.1 4.2 %copy-start.3 = (bf16[3,3,128,128]{3,2,1,0:T(8,128)(2,1)S(1)}, bf16[3,3,128,128]{3,2,1,0:T(8,128)(2,1)}, u32[]{:S(2)}) copy-start(bf16[3,3,128,128]{3,2,1,0:T(8,128)(2,1)} %w1_ref.1) | copy-start | bytes 884740
  83.1 4.2 %copy-start.4 = (bf16[3,3,128,128]{3,2,1,0:T(8,128)(2,1)S(1)}, bf16[3,3,128,128]{3,2,1,0:T(8,128)(2,1)}, u32[]{:S(2)}) copy-start(bf16[3,3,128,128]{3,2,1,0:T(8,128)(2,1)} %w2_ref.1) | copy-start | bytes 884740
  83.2 4.2 %copy-start.5 = (f32[128]{0:T(128)S(1)}, f32[128]{0:T(128)}, u32[]{:S(2)}) copy-start(f32[128]{0:T(128)} %param.25) | copy-start | bytes 1540
  83.2 4.2 %copy-start.6 = (f32[128]{0:T(128)S(1)}, f32[128]{0:T(128)}, u32[]{:S(2)}) copy-start(f32[128]{0:T(128)} %param.27) | copy-start | bytes 1540
  83.2 4.2 %collective-permute-start.9 = (bf16[20,2,128]{2,1,0:T(2,128)(2,1)S(1)}, bf16[20,2,128]{2,1,0:T(2,128)(2,1)S(1)}, u32[]{:S(2)}, u32[]{:S(2)}) collective-permute-start(bf16[20,2,128]{2,1,0:T(2,128)(2,1)S(1)} %pad_maximum_fusion.1), channel_id=1, source_target_pairs={{1,0},{2,1},{3,2},{5,4},{6,5},{7,6},{9,8},{10,9},{11,10},{13,12},{... | collective-permute-start | bytes 30728 | tf_op jit(solution)/shard_map/ppermute | solution.py:465
  91.8 9.7 %collective-permute-start.10 = (bf16[8,128,128]{2,1,0:T(8,128)(2,1)S(1)}, bf16[8,128,128]{2,1,0:T(8,128)(2,1)S(1)}, u32[]{:S(2)}, u32[]{:S(2)}) collective-permute-start(bf16[8,128,128]{2,1,0:T(8,128)(2,1)S(1)} %get-tuple-element.45.refs_0_), channel_id=1, source_target_pairs={{0,8},{8,16},{16,24},{24,0},{1,9},{9,17},{17,25},{25,1},{2,10},{10... | collective-permute-start | bytes 786440 | tf_op jit(solution)/shard_map/ppermute | solution.py:470
  91.8 13.3 %collective-permute-start.12 = (bf16[8,128,128]{2,1,0:T(8,128)(2,1)S(1)}, bf16[8,128,128]{2,1,0:T(8,128)(2,1)S(1)}, u32[]{:S(2)}, u32[]{:S(2)}) collective-permute-start(bf16[8,128,128]{2,1,0:T(8,128)(2,1)S(1)} %get-tuple-element.46.refs_3_), channel_id=1, source_target_pairs={{0,24},{8,0},{16,8},{24,16},{1,25},{9,1},{17,9},{25,17},{2,26},{10... | collective-permute-start | bytes 786440 | tf_op jit(solution)/shard_map/ppermute | solution.py:470
  101.4 11.3 %collective-permute-start.11 = (bf16[8,128,128]{2,1,0:T(8,128)(2,1)S(1)}, bf16[8,128,128]{2,1,0:T(8,128)(2,1)S(1)}, u32[]{:S(2)}, u32[]{:S(2)}) collective-permute-start(bf16[8,128,128]{2,1,0:T(8,128)(2,1)S(1)} %collective-permute-done.10.refs_1_), channel_id=1, source_target_pairs={{0,8},{8,16},{16,24},{24,0},{1,9},{9,17},{17,25},{25,1},{2,10},{10... | collective-permute-start | bytes 786440 | tf_op jit(solution)/shard_map/ppermute | solution.py:470
  105.0 14.4 %collective-permute-start.13 = (bf16[8,128,128]{2,1,0:T(8,128)(2,1)S(1)}, bf16[8,128,128]{2,1,0:T(8,128)(2,1)S(1)}, u32[]{:S(2)}, u32[]{:S(2)}) collective-permute-start(bf16[8,128,128]{2,1,0:T(8,128)(2,1)S(1)} %collective-permute-done.12.refs_4_), channel_id=1, source_target_pairs={{0,24},{8,0},{16,8},{24,16},{1,25},{9,1},{17,9},{25,17},{2,26},{10... | collective-permute-start | bytes 786440 | tf_op jit(solution)/shard_map/ppermute | solution.py:470
  112.7 11.5 %collective-permute-start.14 = (bf16[8,128,128]{2,1,0:T(8,128)(2,1)S(1)}, bf16[8,128,128]{2,1,0:T(8,128)(2,1)S(1)}, u32[]{:S(2)}, u32[]{:S(2)}) collective-permute-start(bf16[8,128,128]{2,1,0:T(8,128)(2,1)S(1)} %collective-permute-done.11.refs_2_), channel_id=1, source_target_pairs={{0,8},{8,16},{16,24},{24,0},{1,9},{9,17},{17,25},{25,1},{2,10},{10... | collective-permute-start | bytes 786440 | tf_op jit(solution)/shard_map/ppermute | solution.py:470
  119.4 11.5 %collective-permute-start.15 = (bf16[8,128,128]{2,1,0:T(8,128)(2,1)S(1)}, bf16[8,128,128]{2,1,0:T(8,128)(2,1)S(1)}, u32[]{:S(2)}, u32[]{:S(2)}) collective-permute-start(bf16[8,128,128]{2,1,0:T(8,128)(2,1)S(1)} %collective-permute-done.13.refs_5_), channel_id=1, source_target_pairs={{0,24},{8,0},{16,8},{24,16},{1,25},{9,1},{17,9},{25,17},{2,26},{10... | collective-permute-start | bytes 786440 | tf_op jit(solution)/shard_map/ppermute | solution.py:470
  132.9 28.6 %copy-start = (bf16[32,128,128]{2,1,0:T(8,128)(2,1)S(1)}, bf16[32,128,128]{2,1,0:T(8,128)(2,1)}, u32[]{:S(2)}) copy-start(bf16[32,128,128]{2,1,0:T(8,128)(2,1)} %get-tuple-element.26.feat_ref) | copy-start | bytes 3145732
  132.9 28.6 %copy-start.2 = (s32[32]{0:T(128)S(1)}, s32[32]{0:T(128)}, u32[]{:S(2)}) copy-start(s32[32]{0:T(128)} %tile_ref.1) | copy-start | bytes 388

commit v10 on v9

--- a/solution.py
+++ b/solution.py
@@ -342,7 +342,7 @@
             first_ref[row] = jnp.where(keep, value[r * width : (r + 1) * width], 0.0).astype(BF16)
         return unused
 
-    lax.fori_loop(0, 2, first_rows, 0)
+    lax.fori_loop(0, 2, first_rows, 0, unroll=True)
     again = PH
 
     def second_rows(i, band_ref):

time: 164 us -> 163 us (level)
  transfers between devices with their start and end apart: 16 -> 16, of which waited for: 11 -> 11; matrix products, arithmetic and copies ran while one was open for 0% -> 0% of each run, Pallas kernels for 4% -> 5%
where the time goes in v10:
time: 163 us
  blocking collectives  61.2 us (38%)
  waiting for transfers between devices  55.5 us (34%)
  Pallas kernels  22.6 us (14%)
  starting transfers between devices  22.3 us (14%)
    all_to_all x2, blocking collectives, local(): lax.all_to_all(x, plane, split_axis=0, concat_axis=0, tiled=True)  61.2 us
    ppermute x12, waiting for transfers between devices, turn(): lax.ppermute(x, 'orbits', [(i, (i + way) % size) for i in range(size)])  52.8 us
    pallas_call x8, Pallas kernels, call(): pl.pallas_call(kernel, in_specs=in_specs, out_specs=out_specs, out_shape=...  22.6 us
    ppermute x12, starting transfers between devices, turn(): lax.ppermute(x, 'orbits', [(i, (i + way) % size) for i in range(size)])  15.9 us
    ppermute x4, starting transfers between devices, halo(): return (lax.ppermute(last, axis, up), lax.ppermute(first, axis, down))  6.48 us
  transfers between devices with their start and end apart: 16, of which 11 were waited for; matrix products, arithmetic and copies ran while one was open for 0% of the time, Pallas kernels for 5%

profile of v10, /device:TPU:0, one launch (start us, length us, event | category | flops | bytes accessed | tf_op | source)
XLA Modules:
  0.0 162.9 jit_solution(15379815289875713122)
XLA Ops:
  0.6 4.3 %shard_map.149 = (bf16[32,128,128]{2,1,0:T(8,128)(2,1)}, bf16[8,1056,128]{2,1,0:T(8,128)(2,1)}) custom-call(s32[32]{0:T(128)} %tile_ref.1, s32[32]{0:T(128)} %patch_hbm.1, bf16[2,4096]{1,0:T(2,128)(2,1)} %offset_hbm.1, s32[16,4096]{1,0:T(8,128)} %cells_hbm.1, bf16[4096,128]{1,0:T(8,128)(2,1)} %x_hbm.1, bf16[128,128]{1,0:T(8,128)(2,1)} %we_hbm.1, ...), custom_call_target="tpu_custom_call" | custom-call | flops 402653184 | bytes 4194304 | tf_op jit(solution)/shard_map/pallas_call | solution.py:37
  4.9 32.7 %all_to_all.10.got_ref = bf16[8,1056,128]{2,1,0:T(8,128)(2,1)S(1)} all-to-all(bf16[8,1056,128]{2,1,0:T(8,128)(2,1)} %get-tuple-element.27), channel_id=1, replica_groups=mesh['orbits'=4,'rows'=2,'cols'=4] {'rows','cols'}, dimensions={0} | all-to-all | bytes 4325376 | tf_op jit(solution)/shard_map/all_to_all | solution.py:525
  37.6 3.2 %shard_map.150 = (bf16[960,128]{1,0:T(8,128)(2,1)S(1)}, bf16[960,128]{1,0:T(8,128)(2,1)S(1)}, bf16[960,128]{1,0:T(8,128)(2,1)S(1)}, bf16[960,128]{1,0:T(8,128)(2...) custom-call(bf16[8,1056,128]{2,1,0:T(8,128)(2,1)S(1)} %all_to_all.10, ...), custom_call_target="tpu_custom_call" | custom-call | flops 536870912 | bytes 8388608 | tf_op jit(solution)/shard_map/pallas_call | solution.py:37
  40.8 1.6 %collective-permute-start = (bf16[960,128]{1,0:T(8,128)(2,1)S(1)}, bf16[960,128]{1,0:T(8,128)(2,1)S(1)}, u32[]{:S(2)}, u32[]{:S(2)}) collective-permute-start(bf16[960,128]{1,0:T(8,128)(2,1)S(1)} %get-tuple-element.29), channel_id=1, source_target_pairs={{0,8},{8,16},{16,24},{24,0},{1,9},{9,17},{17,25},{25,1},{2,10},{10... | collective-permute-start | bytes 737288 | tf_op jit(solution)/shard_map/ppermute | solution.py:470
  42.4 2.2 %collective-permute-start.2 = (bf16[1152,128]{1,0:T(8,128)(2,1)S(1)}, bf16[1152,128]{1,0:T(8,128)(2,1)S(1)}, u32[]{:S(2)}, u32[]{:S(2)}) collective-permute-start(bf16[1152,128]{1,0:T(8,128)(2,1)S(1)} %get-tuple-element.32), channel_id=1, source_target_pairs={{0,24},{8,0},{16,8},{24,16},{1,25},{9,1},{17,9},{25,17},{2,26},{10... | collective-permute-start | bytes 884744 | tf_op jit(solution)/shard_map/ppermute | solution.py:470
  44.7 6.9 %collective-permute-done = bf16[960,128]{1,0:T(8,128)(2,1)S(1)} collective-permute-done((bf16[960,128]{1,0:T(8,128)(2,1)S(1)}, bf16[960,128]{1,0:T(8,128)(2,1)S(1)}, u32[]{:S(2)}, u32[]{:S(2)}) %collective-permute-start) | collective-permute-done | bytes 245792 | tf_op jit(solution)/shard_map/ppermute | solution.py:470
  51.6 0.1 add.12
  51.6 0.1 collective-permute-start.1
  51.7 5.0 %collective-permute-done.2 = bf16[1152,128]{1,0:T(8,128)(2,1)S(1)} collective-permute-done((bf16[1152,128]{1,0:T(8,128)(2,1)S(1)}, bf16[1152,128]{1,0:T(8,128)(2,1)S(1)}, u32[]{:S(2)}, u32[]{:S(2)}) %collective-permute-start.2) | collective-permute-done | bytes 294944 | tf_op jit(solution)/shard_map/ppermute | solution.py:470
  56.7 0.1 add.14
  56.7 5.2 %collective-permute-done.1 = bf16[960,128]{1,0:T(8,128)(2,1)S(1)} collective-permute-done((bf16[960,128]{1,0:T(8,128)(2,1)S(1)}, bf16[960,128]{1,0:T(8,128)(2,1)S(1)}, u32[]{:S(2)}, u32[]{:S(2)}) %collective-permute-start.1) | collective-permute-done | bytes 245792 | tf_op jit(solution)/shard_map/ppermute | solution.py:470
  61.9 0.1 add.13
  62.0 0.1 collective-permute-start.5
  62.1 3.8 %collective-permute-start.3 = (bf16[1152,128]{1,0:T(8,128)(2,1)S(1)}, bf16[1152,128]{1,0:T(8,128)(2,1)S(1)}, u32[]{:S(2)}, u32[]{:S(2)}) collective-permute-start(bf16[1152,128]{1,0:T(8,128)(2,1)S(1)} %add.14), channel_id=1, source_target_pairs={{0,24},{8,0},{16,8},{24,16},{1,25},{9,1},{17,9},{25,17},{2,26},{10... | collective-permute-start | bytes 884744 | tf_op jit(solution)/shard_map/ppermute | solution.py:470
  65.9 6.9 %collective-permute-done.5.sum_ref.sum0_ref = bf16[960,128]{1,0:T(8,128)(2,1)S(1)} collective-permute-done((bf16[960,128]{1,0:T(8,128)(2,1)S(1)}, bf16[960,128]{1,0:T(8,128)(2,1)S(1)}, u32[]{:S(2)}, u32[]{:S(2)}) %collective-permute-start.5) | collective-permute-done | bytes 245792 | tf_op jit(solution)/shard_map/ppermute | solution.py:470
  72.8 0.3 shard_map.152
  73.1 2.5 %collective-permute-start.6 = (bf16[2,128,128]{2,1,0:T(8,128)(2,1)S(1)}, bf16[2,128,128]{2,1,0:T(8,128)(2,1)S(1)}, u32[]{:S(2)}, u32[]{:S(2)}) collective-permute-start(bf16[2,128,128]{2,1,0:T(8,128)(2,1)S(1)} %get-tuple-element.41), channel_id=1, source_target_pairs={{0,4},{4,8},{8,12},{12,16},{16,20},{20,24},{24,28},{1,5},{5,9},{9,... | collective-permute-start | bytes 196616 | tf_op jit(solution)/shard_map/ppermute | solution.py:465
  75.6 1.3 collective-permute-start.7
  76.9 0.0 collective-permute-done.3
  76.9 0.1 add.15
  77.0 2.5 %collective-permute-start.4 = (bf16[1152,128]{1,0:T(8,128)(2,1)S(1)}, bf16[1152,128]{1,0:T(8,128)(2,1)S(1)}, u32[]{:S(2)}, u32[]{:S(2)}) collective-permute-start(bf16[1152,128]{1,0:T(8,128)(2,1)S(1)} %add.15), channel_id=1, source_target_pairs={{0,24},{8,0},{16,8},{24,16},{1,25},{9,1},{17,9},{25,17},{2,26},{10... | collective-permute-start | bytes 884744 | tf_op jit(solution)/shard_map/ppermute | solution.py:470
  79.5 0.0 collective-permute-done.6.up_ref
  79.5 2.3 %collective-permute-done.7.down_ref = bf16[2,128,128]{2,1,0:T(8,128)(2,1)S(1)} collective-permute-done((bf16[2,128,128]{2,1,0:T(8,128)(2,1)S(1)}, bf16[2,128,128]{2,1,0:T(8,128)(2,1)S(1)}, u32[]{:S(2)}, u32[]{:S(2)}) %collective-permute-start.7) | collective-permute-done | bytes 65568 | tf_op jit(solution)/shard_map/ppermute | solution.py:465
  81.8 1.3 collective-permute-start.8
  83.1 0.0 copy-start.3
  83.1 0.0 copy-start.4
  83.2 0.0 copy-start.5
  83.2 0.0 copy-start.6
  83.2 1.4 collective-permute-start.9
  84.6 2.3 %shard_map.151.weights_ref = bf16[64,128,256]{2,1,0:T(8,128)(2,1)S(1)} custom-call(bf16[8,1056,128]{2,1,0:T(8,128)(2,1)S(1)} %all_to_all.10.got_ref), custom_call_target="tpu_custom_call" | custom-call | flops 536870912 | bytes 4194304 | tf_op jit(solution)/shard_map/pallas_call | solution.py:37
  86.9 0.0 collective-permute-done.8.left_ref
  86.9 0.4 collective-permute-done.9.right_ref
  87.4 3.6 %shard_map.153 = (bf16[16,128,128]{2,1,0:T(8,128)(2,1)}, bf16[8,128,128]{2,1,0:T(8,128)(2,1)S(1)}, bf16[8,128,128]{2,1,0:T(8,128)(2,1)S(1)}) custom-call(bf16[960,128]{1,0:T(8,128)(2,1)S(1)} %get-tuple-element.37.own_ref.own0_ref, bf16[960,128]{1,0:T(8,128)(2,1)S(1)} %collective-permute-done.5.sum_ref.sum0_ref, ...), custom_call_target="tpu_custom_call" | custom-call | flops 1207959552 | bytes 2097152 | tf_op jit(solution)/shard_map/pallas_call | solution.py:37
  91.0 3.8 %collective-permute-start.12 = (bf16[8,128,128]{2,1,0:T(8,128)(2,1)S(1)}, bf16[8,128,128]{2,1,0:T(8,128)(2,1)S(1)}, u32[]{:S(2)}, u32[]{:S(2)}) collective-permute-start(bf16[8,128,128]{2,1,0:T(8,128)(2,1)S(1)} %get-tuple-element.46.refs_3_), channel_id=1, source_target_pairs={{0,24},{8,0},{16,8},{24,16},{1,25},{9,1},{17,9},{25,17},{2,26},{10... | collective-permute-start | bytes 786440 | tf_op jit(solution)/shard_map/ppermute | solution.py:470
  94.8 5.8 %collective-permute-done.10.refs_1_ = bf16[8,128,128]{2,1,0:T(8,128)(2,1)S(1)} collective-permute-done((bf16[8,128,128]{2,1,0:T(8,128)(2,1)S(1)}, bf16[8,128,128]{2,1,0:T(8,128)(2,1)S(1)}, u32[]{:S(2)}, u32[]{:S(2)}) %collective-permute-start.10) | collective-permute-done | bytes 262176 | tf_op jit(solution)/shard_map/ppermute | solution.py:470
  100.6 0.0 collective-permute-start.11
  100.6 3.6 %collective-permute-done.12.refs_4_ = bf16[8,128,128]{2,1,0:T(8,128)(2,1)S(1)} collective-permute-done((bf16[8,128,128]{2,1,0:T(8,128)(2,1)S(1)}, bf16[8,128,128]{2,1,0:T(8,128)(2,1)S(1)}, u32[]{:S(2)}, u32[]{:S(2)}) %collective-permute-start.12) | collective-permute-done | bytes 262176 | tf_op jit(solution)/shard_map/ppermute | solution.py:470
  104.3 1.7 %collective-permute-start.13 = (bf16[8,128,128]{2,1,0:T(8,128)(2,1)S(1)}, bf16[8,128,128]{2,1,0:T(8,128)(2,1)S(1)}, u32[]{:S(2)}, u32[]{:S(2)}) collective-permute-start(bf16[8,128,128]{2,1,0:T(8,128)(2,1)S(1)} %collective-permute-done.12.refs_4_), channel_id=1, source_target_pairs={{0,24},{8,0},{16,8},{24,16},{1,25},{9,1},{17,9},{25,17},{2,26},{10... | collective-permute-start | bytes 786440 | tf_op jit(solution)/shard_map/ppermute | solution.py:470
  106.0 5.9 %collective-permute-done.11.refs_2_ = bf16[8,128,128]{2,1,0:T(8,128)(2,1)S(1)} collective-permute-done((bf16[8,128,128]{2,1,0:T(8,128)(2,1)S(1)}, bf16[8,128,128]{2,1,0:T(8,128)(2,1)S(1)}, u32[]{:S(2)}, u32[]{:S(2)}) %collective-permute-start.11) | collective-permute-done | bytes 262176 | tf_op jit(solution)/shard_map/ppermute | solution.py:470
  111.9 6.7 %collective-permute-done.13.refs_5_ = bf16[8,128,128]{2,1,0:T(8,128)(2,1)S(1)} collective-permute-done((bf16[8,128,128]{2,1,0:T(8,128)(2,1)S(1)}, bf16[8,128,128]{2,1,0:T(8,128)(2,1)S(1)}, u32[]{:S(2)}, u32[]{:S(2)}) %collective-permute-start.13) | collective-permute-done | bytes 262176 | tf_op jit(solution)/shard_map/ppermute | solution.py:470
  118.6 0.0 collective-permute-start.15
  118.6 4.8 %shard_map.154 = (bf16[8,1024,128]{2,1,0:T(8,128)(2,1)S(1)}, s32[73]{0:T(128)S(1)}) custom-call(s32[64]{0:T(128)S(1)} %get-tuple-element.28.patch_ref, bf16[64,128,256]{2,1,0:T(8,128)(2,1)S(1)} %shard_map.151.weights_ref, bf16[8,128,128]{2,1,0:T(8,128)(2,1)S(1)} %get-tuple-element.45.refs_0_, bf16[8,128,128]{2,1,0:T(8,128)(2,1)S(1)} %collective-permute-done.10.refs_1_, ...), custom_call_target="tpu_custom_call" | custom-call | flops 536870912 | bytes 8388608 | tf_op jit(solution)/shard_map/pallas_call | solution.py:37
  123.4 6.7 %collective-permute-done.15.down_ref = bf16[8,128,128]{2,1,0:T(8,128)(2,1)S(1)} collective-permute-done((bf16[8,128,128]{2,1,0:T(8,128)(2,1)S(1)}, bf16[8,128,128]{2,1,0:T(8,128)(2,1)S(1)}, u32[]{:S(2)}, u32[]{:S(2)}) %collective-permute-start.15) | collective-permute-done | bytes 262176 | tf_op jit(solution)/shard_map/ppermute | solution.py:470
  130.1 2.5 %shard_map.155 = bf16[8,1024,128]{2,1,0:T(8,128)(2,1)S(1)} custom-call(s32[64]{0:T(128)S(1)} %get-tuple-element.28.patch_ref, s32[73]{0:T(128)S(1)} %get-tuple-element.47.list_ref, bf16[64,128,256]{2,1,0:T(8,128)(2,1)S(1)} %shard_map.151.weights_ref, bf16[8,128,128]{2,1,0:T(8,128)(2,1)S(1)} %collective-permute-done.14.up_ref, ...), custom_call_target="tpu_custom_call", output_to_operand_aliasing={{}: (5, {})} | custom-call | flops 134217728 | bytes 2097152 | tf_op jit(solution)/shard_map/pallas_call | solution.py:37
  132.7 0.0 copy-start
  132.7 0.0 copy-start.2
  132.7 28.6 %all_to_all.11.got_ref = bf16[8,1024,128]{2,1,0:T(8,128)(2,1)S(1)} all-to-all(bf16[8,1024,128]{2,1,0:T(8,128)(2,1)S(1)} %shard_map.155), channel_id=1, replica_groups=mesh['orbits'=4,'rows'=2,'cols'=4] {'rows','cols'}, dimensions={0} | all-to-all | bytes 4194304 | tf_op jit(solution)/shard_map/all_to_all | solution.py:525
  161.3 1.6 shard_map.156
  (16 shorter events, 0.1 us)
Async XLA Ops:
  37.6 35.3 %copy-start.1 = (f32[128]{0:T(128)S(1)}, f32[128]{0:T(128)}, u32[]{:S(2)}) copy-start(f32[128]{0:T(128)} %param.23) | copy-start | bytes 1540
  40.8 10.7 %collective-permute-start = (bf16[960,128]{1,0:T(8,128)(2,1)S(1)}, bf16[960,128]{1,0:T(8,128)(2,1)S(1)}, u32[]{:S(2)}, u32[]{:S(2)}) collective-permute-start(bf16[960,128]{1,0:T(8,128)(2,1)S(1)} %get-tuple-element.29), channel_id=1, source_target_pairs={{0,8},{8,16},{16,24},{24,0},{1,9},{9,17},{17,25},{25,1},{2,10},{10... | collective-permute-start | bytes 737288 | tf_op jit(solution)/shard_map/ppermute | solution.py:470
  42.4 14.2 %collective-permute-start.2 = (bf16[1152,128]{1,0:T(8,128)(2,1)S(1)}, bf16[1152,128]{1,0:T(8,128)(2,1)S(1)}, u32[]{:S(2)}, u32[]{:S(2)}) collective-permute-start(bf16[1152,128]{1,0:T(8,128)(2,1)S(1)} %get-tuple-element.32), channel_id=1, source_target_pairs={{0,24},{8,0},{16,8},{24,16},{1,25},{9,1},{17,9},{25,17},{2,26},{10... | collective-permute-start | bytes 884744 | tf_op jit(solution)/shard_map/ppermute | solution.py:470
  51.6 10.3 %collective-permute-start.1 = (bf16[960,128]{1,0:T(8,128)(2,1)S(1)}, bf16[960,128]{1,0:T(8,128)(2,1)S(1)}, u32[]{:S(2)}, u32[]{:S(2)}) collective-permute-start(bf16[960,128]{1,0:T(8,128)(2,1)S(1)} %add.12), channel_id=1, source_target_pairs={{0,8},{8,16},{16,24},{24,0},{1,9},{9,17},{17,25},{25,1},{2,10},{10... | collective-permute-start | bytes 737288 | tf_op jit(solution)/shard_map/ppermute | solution.py:470
  62.0 10.8 %collective-permute-start.5 = (bf16[960,128]{1,0:T(8,128)(2,1)S(1)}, bf16[960,128]{1,0:T(8,128)(2,1)S(1)}, u32[]{:S(2)}, u32[]{:S(2)}) collective-permute-start(bf16[960,128]{1,0:T(8,128)(2,1)S(1)} %add.13), channel_id=1, source_target_pairs={{0,8},{8,16},{16,24},{24,0},{1,9},{9,17},{17,25},{25,1},{2,10},{10... | collective-permute-start | bytes 737288 | tf_op jit(solution)/shard_map/ppermute | solution.py:470
  62.1 14.8 %collective-permute-start.3 = (bf16[1152,128]{1,0:T(8,128)(2,1)S(1)}, bf16[1152,128]{1,0:T(8,128)(2,1)S(1)}, u32[]{:S(2)}, u32[]{:S(2)}) collective-permute-start(bf16[1152,128]{1,0:T(8,128)(2,1)S(1)} %add.14), channel_id=1, source_target_pairs={{0,24},{8,0},{16,8},{24,16},{1,25},{9,1},{17,9},{25,17},{2,26},{10... | collective-permute-start | bytes 884744 | tf_op jit(solution)/shard_map/ppermute | solution.py:470
  73.1 6.4 %collective-permute-start.6 = (bf16[2,128,128]{2,1,0:T(8,128)(2,1)S(1)}, bf16[2,128,128]{2,1,0:T(8,128)(2,1)S(1)}, u32[]{:S(2)}, u32[]{:S(2)}) collective-permute-start(bf16[2,128,128]{2,1,0:T(8,128)(2,1)S(1)} %get-tuple-element.41), channel_id=1, source_target_pairs={{0,4},{4,8},{8,12},{12,16},{16,20},{20,24},{24,28},{1,5},{5,9},{9,... | collective-permute-start | bytes 196616 | tf_op jit(solution)/shard_map/ppermute | solution.py:465
  75.6 6.2 %collective-permute-start.7 = (bf16[2,128,128]{2,1,0:T(8,128)(2,1)S(1)}, bf16[2,128,128]{2,1,0:T(8,128)(2,1)S(1)}, u32[]{:S(2)}, u32[]{:S(2)}) collective-permute-start(bf16[2,128,128]{2,1,0:T(8,128)(2,1)S(1)} %get-tuple-element.42), channel_id=1, source_target_pairs={{4,0},{8,4},{12,8},{16,12},{20,16},{24,20},{28,24},{5,1},{9,5},{13... | collective-permute-start | bytes 196616 | tf_op jit(solution)/shard_map/ppermute | solution.py:465
  77.0 9.9 %collective-permute-start.4 = (bf16[1152,128]{1,0:T(8,128)(2,1)S(1)}, bf16[1152,128]{1,0:T(8,128)(2,1)S(1)}, u32[]{:S(2)}, u32[]{:S(2)}) collective-permute-start(bf16[1152,128]{1,0:T(8,128)(2,1)S(1)} %add.15), channel_id=1, source_target_pairs={{0,24},{8,0},{16,8},{24,16},{1,25},{9,1},{17,9},{25,17},{2,26},{10... | collective-permute-start | bytes 884744 | tf_op jit(solution)/shard_map/ppermute | solution.py:470
  81.8 5.1 %collective-permute-start.8 = (bf16[20,2,128]{2,1,0:T(2,128)(2,1)S(1)}, bf16[20,2,128]{2,1,0:T(2,128)(2,1)S(1)}, u32[]{:S(2)}, u32[]{:S(2)}) collective-permute-start(bf16[20,2,128]{2,1,0:T(2,128)(2,1)S(1)} %pad_maximum_fusion), channel_id=1, source_target_pairs={{0,1},{1,2},{2,3},{4,5},{5,6},{6,7},{8,9},{9,10},{10,11},{12,13},{... | collective-permute-start | bytes 30728 | tf_op jit(solution)/shard_map/ppermute | solution.py:465
  83.1 4.2 %copy-start.3 = (bf16[3,3,128,128]{3,2,1,0:T(8,128)(2,1)S(1)}, bf16[3,3,128,128]{3,2,1,0:T(8,128)(2,1)}, u32[]{:S(2)}) copy-start(bf16[3,3,128,128]{3,2,1,0:T(8,128)(2,1)} %w1_ref.1) | copy-start | bytes 884740
  83.1 4.2 %copy-start.4 = (bf16[3,3,128,128]{3,2,1,0:T(8,128)(2,1)S(1)}, bf16[3,3,128,128]{3,2,1,0:T(8,128)(2,1)}, u32[]{:S(2)}) copy-start(bf16[3,3,128,128]{3,2,1,0:T(8,128)(2,1)} %w2_ref.1) | copy-start | bytes 884740
  83.2 4.2 %copy-start.5 = (f32[128]{0:T(128)S(1)}, f32[128]{0:T(128)}, u32[]{:S(2)}) copy-start(f32[128]{0:T(128)} %param.25) | copy-start | bytes 1540
  83.2 4.2 %copy-start.6 = (f32[128]{0:T(128)S(1)}, f32[128]{0:T(128)}, u32[]{:S(2)}) copy-start(f32[128]{0:T(128)} %param.27) | copy-start | bytes 1540
  83.2 4.2 %collective-permute-start.9 = (bf16[20,2,128]{2,1,0:T(2,128)(2,1)S(1)}, bf16[20,2,128]{2,1,0:T(2,128)(2,1)S(1)}, u32[]{:S(2)}, u32[]{:S(2)}) collective-permute-start(bf16[20,2,128]{2,1,0:T(2,128)(2,1)S(1)} %pad_maximum_fusion.1), channel_id=1, source_target_pairs={{1,0},{2,1},{3,2},{5,4},{6,5},{7,6},{9,8},{10,9},{11,10},{13,12},{... | collective-permute-start | bytes 30728 | tf_op jit(solution)/shard_map/ppermute | solution.py:465
  91.0 9.7 %collective-permute-start.10 = (bf16[8,128,128]{2,1,0:T(8,128)(2,1)S(1)}, bf16[8,128,128]{2,1,0:T(8,128)(2,1)S(1)}, u32[]{:S(2)}, u32[]{:S(2)}) collective-permute-start(bf16[8,128,128]{2,1,0:T(8,128)(2,1)S(1)} %get-tuple-element.45.refs_0_), channel_id=1, source_target_pairs={{0,8},{8,16},{16,24},{24,0},{1,9},{9,17},{17,25},{25,1},{2,10},{10... | collective-permute-start | bytes 786440 | tf_op jit(solution)/shard_map/ppermute | solution.py:470
  91.0 13.3 %collective-permute-start.12 = (bf16[8,128,128]{2,1,0:T(8,128)(2,1)S(1)}, bf16[8,128,128]{2,1,0:T(8,128)(2,1)S(1)}, u32[]{:S(2)}, u32[]{:S(2)}) collective-permute-start(bf16[8,128,128]{2,1,0:T(8,128)(2,1)S(1)} %get-tuple-element.46.refs_3_), channel_id=1, source_target_pairs={{0,24},{8,0},{16,8},{24,16},{1,25},{9,1},{17,9},{25,17},{2,26},{10... | collective-permute-start | bytes 786440 | tf_op jit(solution)/shard_map/ppermute | solution.py:470
  100.6 11.3 %collective-permute-start.11 = (bf16[8,128,128]{2,1,0:T(8,128)(2,1)S(1)}, bf16[8,128,128]{2,1,0:T(8,128)(2,1)S(1)}, u32[]{:S(2)}, u32[]{:S(2)}) collective-permute-start(bf16[8,128,128]{2,1,0:T(8,128)(2,1)S(1)} %collective-permute-done.10.refs_1_), channel_id=1, source_target_pairs={{0,8},{8,16},{16,24},{24,0},{1,9},{9,17},{17,25},{25,1},{2,10},{10... | collective-permute-start | bytes 786440 | tf_op jit(solution)/shard_map/ppermute | solution.py:470
  104.3 14.4 %collective-permute-start.13 = (bf16[8,128,128]{2,1,0:T(8,128)(2,1)S(1)}, bf16[8,128,128]{2,1,0:T(8,128)(2,1)S(1)}, u32[]{:S(2)}, u32[]{:S(2)}) collective-permute-start(bf16[8,128,128]{2,1,0:T(8,128)(2,1)S(1)} %collective-permute-done.12.refs_4_), channel_id=1, source_target_pairs={{0,24},{8,0},{16,8},{24,16},{1,25},{9,1},{17,9},{25,17},{2,26},{10... | collective-permute-start | bytes 786440 | tf_op jit(solution)/shard_map/ppermute | solution.py:470
  111.9 11.5 %collective-permute-start.14 = (bf16[8,128,128]{2,1,0:T(8,128)(2,1)S(1)}, bf16[8,128,128]{2,1,0:T(8,128)(2,1)S(1)}, u32[]{:S(2)}, u32[]{:S(2)}) collective-permute-start(bf16[8,128,128]{2,1,0:T(8,128)(2,1)S(1)} %collective-permute-done.11.refs_2_), channel_id=1, source_target_pairs={{0,8},{8,16},{16,24},{24,0},{1,9},{9,17},{17,25},{25,1},{2,10},{10... | collective-permute-start | bytes 786440 | tf_op jit(solution)/shard_map/ppermute | solution.py:470
  118.6 11.5 %collective-permute-start.15 = (bf16[8,128,128]{2,1,0:T(8,128)(2,1)S(1)}, bf16[8,128,128]{2,1,0:T(8,128)(2,1)S(1)}, u32[]{:S(2)}, u32[]{:S(2)}) collective-permute-start(bf16[8,128,128]{2,1,0:T(8,128)(2,1)S(1)} %collective-permute-done.13.refs_5_), channel_id=1, source_target_pairs={{0,24},{8,0},{16,8},{24,16},{1,25},{9,1},{17,9},{25,17},{2,26},{10... | collective-permute-start | bytes 786440 | tf_op jit(solution)/shard_map/ppermute | solution.py:470
  132.7 28.6 %copy-start = (bf16[32,128,128]{2,1,0:T(8,128)(2,1)S(1)}, bf16[32,128,128]{2,1,0:T(8,128)(2,1)}, u32[]{:S(2)}) copy-start(bf16[32,128,128]{2,1,0:T(8,128)(2,1)} %get-tuple-element.26.feat_ref) | copy-start | bytes 3145732
  132.7 28.6 %copy-start.2 = (s32[32]{0:T(128)S(1)}, s32[32]{0:T(128)}, u32[]{:S(2)}) copy-start(s32[32]{0:T(128)} %tile_ref.1) | copy-start | bytes 388
